TPU v7x, 32 devices: a whole 2x2x4 slice. The times are simulated.
32 devices in a mesh: row: 8 (over y, x, core), col: 4 (over z).
Axes of the slice: x: 2, y: 2, z: 4, core: 2. Of those that a mesh axis runs over, the one named last changes fastest.
Arguments:
- inverse_front: float32 [16384, 16384], P('row', 'col'), may hold values from -0.09375 to 0.09375
- factor: float32 [4096, 1024], P('row'), may hold values from -1.2 to 1.2
- unit_lower: float32 [2, 512, 512], replicated, may hold values from -0.25 to 0.25
- pivot_inverse: float32 [2, 512], replicated, may hold values from 0.5 to 4
- tile_list: int32 [2, 16], replicated, may hold values from 0 to 63, as said below
- tile_valid: int32 [2, 16], replicated, may hold values from 0 to 1, as said below
Outputs:
- inverse_column: float32 [16384, 1024], P('row')
- diagonal_block: float32 [2, 512, 512], replicated
Inputs may be any that keep to these rules, and one draw needn't show every extreme that they name: `tile_list`: each row names 16 different tile rows of the front in increasing order, exactly 2 of them among each aligned group of 8 tile rows, and the last tile row is always among them. `tile_valid`: each row holds at least one 1.
All inputs are finite; a program needn't handle non-finite values.
Results may differ from a plain program's by a relative error of at most 0.0001.
Values sent between devices are 32-bit elements; how exact they have to be, the bound alone decides.
No kernel may reach another device: no remote copies, remote signals or barrier semaphores. Data moves between devices by JAX's collectives and lax.ppermute only.
A program may use at most 256 MiB of HBM per device.

v0:
```python
import jax
import jax.numpy as jnp
from jax import lax
from jax.sharding import PartitionSpec as P

B = 256
W = 512
NS = 2
NA = 16


def from_root(block, axis, owner):
    block = jnp.where(lax.axis_index(axis) == owner, block, jnp.zeros_like(block))
    return lax.psum(block, axis)


def inner_left(left, right):
    return lax.dot_general(
        left,
        right,
        (((0,), (0,)), ((), ())),
        precision=lax.Precision.HIGHEST,
        preferred_element_type=jnp.float32,
    )


def shards(inverse_front, factor, unit_lower, pivot_inverse, tile_list, tile_valid):
    row_count = lax.axis_size("row")
    col_count = lax.axis_size("col")
    row_span, col_span = inverse_front.shape
    row_index = lax.axis_index("row")
    col_index = lax.axis_index("col")
    identity = jnp.eye(W, dtype=jnp.float32)
    inverses = [jnp.tril(unit_lower[member], -1) + identity for member in range(NS)]

    def normalize(slab):
        return jnp.concatenate(
            [
                jnp.dot(
                    slab[:, member * W : (member + 1) * W],
                    inverses[member],
                    precision=lax.Precision.HIGHEST,
                    preferred_element_type=jnp.float32,
                )
                for member in range(NS)
            ],
            axis=1,
        )

    normalized = lax.all_gather(normalize(factor), "row", axis=0, tiled=True)
    slot_tiles = normalized.reshape(NA, B, NS, W)

    def place_tiles(first, number):
        global_tile = first + jnp.arange(number, dtype=jnp.int32)
        onehot = (
            (tile_list[:, None, :] == global_tile[None, :, None]) & (tile_valid[:, None, :] > 0)
        ).astype(jnp.float32)
        placed = jnp.einsum("sta,absw->tbsw", onehot, slot_tiles, precision=lax.Precision.HIGHEST)
        return (placed.reshape(number * B, NS * W), jnp.sum(onehot, axis=2))

    row_factor, row_chosen = place_tiles(row_index * (row_span // B), row_span // B)
    col_factor, col_chosen = place_tiles(col_index * (col_span // B), col_span // B)
    row_global = row_index * row_span + jnp.arange(row_span, dtype=jnp.int32)
    col_global = col_index * col_span + jnp.arange(col_span, dtype=jnp.int32)
    lower_part = jnp.where(row_global[:, None] >= col_global[None, :], inverse_front, 0.0)
    lower_prod = jnp.dot(
        lower_part, col_factor, precision=lax.Precision.HIGHEST, preferred_element_type=jnp.float32
    )
    strict = jnp.where(row_global[:, None] > col_global[None, :], inverse_front, 0.0)
    mirror_prod = inner_left(strict, row_factor)
    row_total = lax.psum(lower_prod, "col")
    col_total = lax.psum(mirror_prod, "row")
    grid_ratio = row_count // col_count
    offset = row_index % grid_ratio * row_span
    own_piece = lax.dynamic_slice_in_dim(col_total, offset, row_span, 0)
    mirrored = from_root(own_piece, "col", row_index // grid_ratio)
    keep_rows = jnp.repeat(row_chosen, B, axis=1)
    keep_mask = jnp.repeat(keep_rows.T, W, axis=1)
    column = -(row_total + mirrored) * keep_mask
    base_block = jnp.stack(
        [
            jnp.dot(
                inverses[member].T * pivot_inverse[member][None, :],
                inverses[member],
                precision=lax.Precision.HIGHEST,
                preferred_element_type=jnp.float32,
            )
            for member in range(NS)
        ]
    )
    diag_terms = jnp.stack(
        [
            inner_left(
                row_factor[:, member * W : (member + 1) * W],
                column[:, member * W : (member + 1) * W],
            )
            for member in range(NS)
        ]
    )
    diag_total = lax.psum(diag_terms, "row")
    diagonal_block = base_block - diag_total
    return (column, diagonal_block)


def solution(mesh):
    in_specs = (P("row", "col"), P("row", None), P(), P(), P(), P())
    out_specs = (P("row", None), P())
    return jax.shard_map(shards, mesh=mesh, in_specs=in_specs, out_specs=out_specs, check_vma=False)
```

profile of v0, /device:TPU:0, one launch (start us, length us, event | category | flops | bytes accessed | tf_op | source)
XLA Modules:
  0.0 1138.7 jit_solution(14625596206540926153)
XLA Ops:
  7.2 0.0 copy-start.6
  7.2 0.0 all-gather.2.cloned.1.call-start
  7.2 0.0 copy-start.3
  7.2 5.1 convolution_bitcast_fusion.2
  12.4 0.0 copy-done.3
  12.4 5.1 convolution_bitcast_fusion.3
  17.5 1.5 pad_maximum_fusion
  19.0 0.0 all-gather.2.cloned.1.call-update
  19.0 0.3 all-reduce.4.cloned.1.call-start
  19.3 0.0 copy-done.6
  19.4 92.4 %all-gather.2.cloned.1.call-done = f32[4096,1024]{0,1:T(8,128)} async-done(((f32[512,1024]{0,1:T(8,128)}), f32[4096,1024]{0,1:T(8,128)}) %all-gather.2.cloned.1.call-update) | async-done | bytes 16777232 | tf_op jit(solution)/shard_map/all_gather | solution.py:50
  111.7 15.7 %copy.21 = f32[128,8,16,256]{3,2,1,0:T(8,128)} copy(f32[128,8,16,256]{3,1,2,0:T(8,128)} %bitcast.78) | data formatting | bytes 33554432
  127.5 20.3 %copy.14 = f32[16,256,2,512]{3,0,1,2:T(8,128)} copy(f32[16,256,2,512]{1,0,3,2:T(8,128)} %bitcast.70) | data formatting | bytes 33554432 | tf_op jit(solution)/shard_map/reshape | solution.py:51
  147.7 0.0 copy-done.2
  147.7 11.9 %convolution_bitcast_fusion.1 = f32[8,256,2,512]{3,0,1,2:T(8,128)} fusion(f32[16,256,2,512]{3,0,1,2:T(8,128)} %copy.14, s32[2,16]{1,0:T(2,128)S(1)} %copy-done.2, s32[8]{0:T(128)S(1)} %iota_add_fusion.3, pred[2,16]{1,0:T(4,128)(4,1)S(1)} %broadcast_compare_fusion), kind=kOutput, calls=%fused_computation.21 | convolution fusion | flops 402653696 | bytes 25166016 | tf_op jit(solution)/shard_map/sta,absw->tbsw/dot_general | solution.py:58
  159.6 10.5 copy.17
  170.1 10.7 copy.23
  180.8 221.8 %fusion = f32[4096,1024]{1,0:T(8,128)} fusion(f32[2048,1024]{0,1:T(8,128)} %bitcast.72, f32[2048,4096]{1,0:T(8,128)} %param.6, s32[4096]{0:T(1024)S(1)} %iota_add_fusion, s32[2048]{0:T(1024)S(1)} %iota_add_fusion.1), kind=kOutput, calls=%fused_computation | convolution fusion | flops 103095992320 | bytes 58744832 | tf_op jit(solution)/shard_map/dot_general | solution.py:18
  402.6 0.0 all-reduce.4.cloned.1.call-update
  402.6 0.0 all-reduce.8.cloned.1.call-start
  402.7 16.4 %convolution_bitcast_fusion = f32[16,256,2,512]{3,0,1,2:T(8,128)} fusion(f32[16,256,2,512]{3,0,1,2:T(8,128)} %copy.14, s32[2,16]{1,0:T(2,128)S(1)} %copy-done.2, s32[16]{0:T(128)S(1)} %iota_add_fusion.4, pred[2,16]{1,0:T(4,128)(4,1)S(1)} %broadcast_compare_fusion), kind=kOutput, calls=%fused_computation.14 | convolution fusion | flops 805307392 | bytes 33554656 | tf_op jit(solution)/shard_map/sta,absw->tbsw/dot_general | solution.py:58
  419.2 20.5 %copy.15 = f32[16,256,2,512]{1,0,3,2:T(8,128)} copy(f32[16,256,2,512]{3,0,1,2:T(8,128)} %convolution_bitcast_fusion) | data formatting | bytes 33554432 | tf_op jit(solution)/shard_map/sta,absw->tbsw/transpose | solution.py:58
  439.6 21.1 %copy.22 = f32[128,8,16,256]{3,1,2,0:T(8,128)} copy(f32[128,8,16,256]{3,2,1,0:T(8,128)} %bitcast.71) | data formatting | bytes 33554432
  460.7 159.9 %all-reduce.4.cloned.1.call-done = f32[4096,1024]{1,0:T(8,128)} async-done(((f32[4096,1024]{1,0:T(8,128)}), f32[4096,1024]{1,0:T(8,128)}) %all-reduce.4.cloned.1.call-update) | async-done | bytes 16777232 | tf_op jit(solution)/shard_map/psum | solution.py:72
  620.6 123.2 %select_add_fusion = f32[2048,1024]{1,0:T(8,128)} fusion(f32[4096,1024]{1,0:T(8,128)} %all-reduce.4.cloned.1.call-done, s32[]{:T(128)S(6)} %select_n.43, f32[4096,1024]{0,1:T(8,128)} %bitcast.79, f32[2048,4096]{1,0:T(8,128)} %param.6, s32[4096]{0:T(1024)S(1)} %iota_add_fusion, s32[2048]{0:T(1024)S(1)} %iota_add_fusion.1, pred[]{:T(512)S(6)} %eq.40), kind=kOutput, calls=%fused_computation.13 | convolution fusion | flops 103100186624 | bytes 67133448 | tf_op jit(solution)/shard_map/dot_general | solution.py:66
  743.8 0.0 all-reduce.8.cloned.1.call-update
  743.8 0.0 all-reduce.6.cloned.1.call-start
  743.9 0.2 convert_reduce_fusion
  744.0 0.1 copy.18
  744.1 0.1 broadcast_in_dim.32
  744.2 3.0 broadcast_in_dim.33
  747.2 5.5 copy.24
  752.7 282.1 %all-reduce.8.cloned.1.call-done = f32[2048,1024]{1,0:T(8,128)} async-done(((f32[2048,1024]{1,0:T(8,128)}), f32[2048,1024]{1,0:T(8,128)}) %all-reduce.8.cloned.1.call-update) | async-done | bytes 8388624 | tf_op jit(solution)/shard_map/psum | solution.py:71
  1034.8 12.2 %negate_multiply_fusion = f32[2048,1024]{1,0:T(8,128)} fusion(f32[2048,1024]{1,0:T(8,128)} %bitcast.75, f32[2048,1024]{1,0:T(8,128)} %all-reduce.8.cloned.1.call-done), kind=kLoop, calls=%fused_computation.12 | loop fusion | flops 4194304 | bytes 25165824 | tf_op jit(solution)/shard_map/mul | solution.py:79
  1047.0 9.4 fusion.30
  1056.5 0.0 copy-done
  1056.5 0.0 copy-start.5
  1056.5 0.0 copy-start.1
  1056.5 0.0 copy-start.4
  1056.5 9.5 fusion.35
  1066.0 1.5 pad_maximum_fusion.1
  1067.5 0.0 all-reduce.6.cloned.1.call-update
  1067.5 0.0 copy-done.5
  1067.5 0.0 copy-done.1
  1067.6 2.3 fusion.24
  1069.9 3.3 fusion.27
  1073.2 54.9 %all-reduce.6.cloned.1.call-done = f32[2,512,512]{2,1,0:T(8,128)} async-done(((f32[2,512,512]{2,1,0:T(8,128)}), f32[2,512,512]{2,1,0:T(8,128)}) %all-reduce.6.cloned.1.call-update) | async-done | bytes 2097168 | tf_op jit(solution)/shard_map/psum | solution.py:100
  1128.1 3.7 maximum_subtract_fusion
  (10 shorter events, 0.0 us)
Async XLA Ops:
  7.2 12.2 %copy-start.6 = (s32[2,16]{1,0:T(2,128)S(1)}, s32[2,16]{1,0:T(2,128)}, u32[]{:S(2)}) copy-start(s32[2,16]{1,0:T(2,128)} %param.11) | copy-start | bytes 388
  7.2 104.6 %all-gather.2.cloned.1.call-start = ((), (), s32[]{:S(2)}) async-start(), calls=%async_computation | async-start | bytes 18874368 | tf_op jit(solution)/shard_map/all_gather | solution.py:50
  7.2 5.1 copy-start.3
  19.0 601.6 %all-reduce.4.cloned.1.call-start = ((), (), s32[]{:S(2)}) async-start(), calls=%async_computation.1 | async-start | bytes 33554432 | tf_op jit(solution)/shard_map/psum | solution.py:72
  127.5 20.3 %copy-start.2 = (s32[2,16]{1,0:T(2,128)S(1)}, s32[2,16]{1,0:T(2,128)}, u32[]{:S(2)}) copy-start(s32[2,16]{1,0:T(2,128)} %param.10) | copy-start | bytes 388
  402.6 632.2 %all-reduce.8.cloned.1.call-start = ((), (), s32[]{:S(2)}) async-start(), calls=%async_computation.3 | async-start | bytes 16777216 | tf_op jit(solution)/shard_map/psum | solution.py:71
  743.8 384.3 %all-reduce.6.cloned.1.call-start = ((), (), s32[]{:S(2)}) async-start(), calls=%async_computation.2 | async-start | bytes 4194304 | tf_op jit(solution)/shard_map/psum | solution.py:100
  1047.0 9.4 copy-start
  1056.5 11.1 copy-start.5
  1056.5 11.1 copy-start.1
  1056.5 11.1 copy-start.4
Sparse Core Ops, SparseCore 0:
  19.2 92.5 all-gather.1
  402.8 217.8 all-reduce.3
  743.9 290.8 all-reduce.7
  1067.6 60.4 all-reduce.5
where the time goes:
time: 1150 us; the launch traced here: 1140 us
  waiting for transfers between devices  589 us (51%)
  matrix products  408 us (35%)
  local copies, waits for them, and re-layouts  107 us (9%)
  other arithmetic  19 us (2%)
  between operations  14.4 us (1%)
    psum x1, waiting for transfers between devices, shards(): row_total = lax.psum(lower_prod, 'col')  282 us
    dot_general x3, matrix products, inner_left(): lax.dot_general(left, right, (((0,), (0,)), ((), ())), precision=lax.Prec...  241 us
    psum x1, waiting for transfers between devices, shards(): col_total = lax.psum(mirror_prod, 'row')  160 us
    dot_general x1, matrix products, shards(): jnp.dot(lower_part, col_factor, precision=lax.Precision.HIGHEST, preferre...  123 us
    all_gather x1, waiting for transfers between devices, shards(): normalized = lax.all_gather(normalize(factor), 'row', axis=0, tiled=True)  92.4 us
    psum x1, waiting for transfers between devices, shards(): diag_total = lax.psum(diag_terms, 'row')  54.9 us
    unnamed x18, local copies, waits for them, and re-layouts  53 us
    transpose x2, local copies, waits for them, and re-layouts, place_tiles(): jnp.einsum('sta,absw->tbsw', onehot, slot_tiles, precision=lax.Precision....  30.9 us
  transfers between devices with their start and end apart: 4, of which 4 were waited for; matrix products, arithmetic and copies ran while one was open for 6% of the time, Pallas kernels for 0%

commit v1 on v0

v1 whole, which is shorter than its diff:
```python
import functools

import jax
import jax.numpy as jnp
from jax import lax
from jax.experimental import pallas as pl
from jax.experimental.pallas import tpu as pltpu
from jax.sharding import PartitionSpec as P

F32 = jnp.float32
BF16 = jnp.bfloat16
VMEM = pltpu.MemorySpace.VMEM
SMEM = pltpu.MemorySpace.SMEM
PARAMS = pltpu.CompilerParams(vmem_limit_bytes=48 * 1024 * 1024)


def vmem(count):
    return [pl.BlockSpec(memory_space=VMEM)] * count


def smem(count):
    return [pl.BlockSpec(memory_space=SMEM)] * count


def split(x):
    high = x.astype(BF16)
    return high, (x - high.astype(F32)).astype(BF16)


def product(left, right, contract=1):
    def one(a, b):
        return lax.dot_general(a, b, (((contract,), (0,)), ((), ())), preferred_element_type=F32)

    return one(left[0], right[1]) + one(left[1], right[0]) + one(left[0], right[0])


def unit_inverse(ref, member):
    lower = ref[member]
    row = lax.broadcasted_iota(jnp.int32, lower.shape, 0)
    col = lax.broadcasted_iota(jnp.int32, lower.shape, 1)
    return jnp.where(row > col, lower, jnp.where(row == col, 1.0, 0.0).astype(F32))


class Plan:
    def __init__(self, front, factor, unit_lower, tile_list):
        self.rows, self.cols = lax.axis_size("row"), lax.axis_size("col")
        self.lanes = self.rows // self.cols
        self.members, self.width, _ = unit_lower.shape
        self.na = tile_list.shape[1] // self.rows
        self.tile = factor.shape[0] // self.na
        self.nb = self.na * self.lanes
        self.row_tiles = front.shape[0] // self.tile
        self.col_tiles = front.shape[1] // self.tile
        self.depth = factor.shape[0]
        bits = [1 << i for i in range((self.cols - 1).bit_length())]
        self.orders = [
            bits[lane % len(bits):] + bits[:lane % len(bits)] for lane in range(self.lanes)
        ]
        self.steps = len(bits)

    def device(self, chip, lane, col):
        return (chip * self.lanes + lane) * self.cols + col

    def tree(self, step):
        pairs = []
        for col in range(self.cols):
            for lane, order in enumerate(self.orders):
                held, later = [0], [0]
                for bit in order[:step]:
                    held = held + [x ^ bit for x in held]
                for bit in order[step + 1:]:
                    later = later + [x ^ bit for x in later]
                for offset in held:
                    child = col ^ offset ^ order[step]
                    if any(child ^ x > col for x in later):
                        pairs.append(
                            (self.device(col ^ offset, lane, col), self.device(child, lane, col))
                        )
        return pairs

    def received(self, step):
        row, col = lax.axis_index("row"), lax.axis_index("col")
        offset = (row // self.lanes) ^ col
        got = False
        for lane, order in enumerate(self.orders):
            later = sum(order[step + 1:])
            here = ((offset & order[step]) != 0) & ((offset & later) == 0)
            got = got | (here & (row % self.lanes == lane))
        return got

    def swap(self, x, shift):
        pairs = []
        for row in range(self.rows):
            chip, lane = divmod(row, self.lanes)
            pairs.append((chip * self.lanes + (lane + shift) % self.lanes, row))
        return lax.ppermute(x, "row", pairs)

    def spread(self, x):
        for step in range(self.steps):
            got = lax.ppermute(x, ("row", "col"), self.tree(step))
            x = jnp.where(self.received(step), got, x)
        return x

    def collect(self, x):
        for step in reversed(range(self.steps)):
            pairs = [(child, parent) for parent, child in self.tree(step)]
            x = x + lax.ppermute(x, ("row", "col"), pairs)
        return x

    def line_sum(self, x):
        count, half = self.cols, self.cols // 2
        place = lax.axis_index("col")
        for i in range(half - 1):
            x = x + lax.ppermute(x, "col", [(i, i + 1), (count - 1 - i, count - 2 - i)])
        x = x + lax.ppermute(x, "col", [(half - 1, half), (half, half - 1)])
        for i in range(half - 1):
            got = lax.ppermute(x, "col", [(half - 1 - i, half - 2 - i), (half + i, half + i + 1)])
            x = jnp.where((place == half - 2 - i) | (place == half + i + 1), got, x)
        return x


def gather_kernel(plan, member, tiles_ref, valid_ref, front, factor, high, low, *rest):
    mirror, (buffer, sems) = rest[:plan.lanes], rest[plan.lanes:]
    size, na, nb = plan.tile, plan.na, plan.nb
    row, col = lax.axis_index("row"), lax.axis_index("col")
    lane = lax.rem(row, plan.lanes)
    row_slots = [row * na + a for a in range(na)]
    col_slots = [
        col * nb + lax.rem(lane + b // na, plan.lanes) * na + b % na for b in range(nb)
    ]
    copies = []
    for a in range(na):
        for b in range(nb):
            i = jnp.clip(tiles_ref[member, row_slots[a]] - row * plan.row_tiles, 0, plan.row_tiles - 1)
            j = jnp.clip(tiles_ref[member, col_slots[b]] - col * plan.col_tiles, 0, plan.col_tiles - 1)
            copy = pltpu.make_async_copy(
                front.at[
                    pl.ds(pl.multiple_of(i * size, size), size),
                    pl.ds(pl.multiple_of(j * size, size), size),
                ],
                buffer.at[a, b],
                sems.at[a, b],
            )
            copy.start()
            copies.append(copy)
    right = split(factor[...])
    local_row = lax.broadcasted_iota(jnp.int32, (size, size), 0)
    local_col = lax.broadcasted_iota(jnp.int32, (size, size), 1)
    for a in range(na):
        for b in range(nb):
            copies[a * nb + b].wait()
            live = (valid_ref[member, row_slots[a]] > 0) & (valid_ref[member, col_slots[b]] > 0)
            ahead = (tiles_ref[member, row_slots[a]] - tiles_ref[member, col_slots[b]]) * size
            gap = local_row - local_col + ahead
            x = buffer[a, b]
            x = jnp.where(gap > 0, x, jnp.where(gap == 0, 0.5 * x, 0.0))
            x = jnp.where(live, x, 0.0)
            x_high, x_low = split(x)
            high[a * size:(a + 1) * size, b * size:(b + 1) * size] = x_high
            low[a * size:(a + 1) * size, b * size:(b + 1) * size] = x_low
    for b in range(nb):
        left = (high[:, b * size:(b + 1) * size], low[:, b * size:(b + 1) * size])
        first = b % na * size
        mirror[b // na][first:first + size, :] = product(left, right, contract=0)


def forward_kernel(plan, high, low, factor, *rest):
    parts, (total, cross) = rest[:plan.lanes], rest[plan.lanes:]
    size, depth = plan.tile, plan.depth
    right = [split(part[...]) for part in parts]
    for a in range(plan.na):
        rows = slice(a * size, (a + 1) * size)
        total[rows, :] = sum(
            product(
                (high[rows, i * depth:(i + 1) * depth], low[rows, i * depth:(i + 1) * depth]),
                right[i],
            )
            for i in range(plan.lanes)
        )
    cross[...] = product(split(factor[...]), split(total[...]), contract=0)


def place_kernel(plan, tiles_ref, unit_ref, *rest):
    sums, (out, stack, sem) = rest[:plan.members], rest[plan.members:]
    size, width = plan.tile, plan.width
    row = lax.axis_index("row")
    for member in range(plan.members):
        right = split(unit_inverse(unit_ref, member))
        stack[member, plan.na] = jnp.zeros((size, width), F32)
        for a in range(plan.na):
            left = split(sums[member][a * size:(a + 1) * size, :])
            stack[member, a] = -product(left, right)
        copies = []
        for t in range(plan.row_tiles):
            slot = jnp.int32(plan.na)
            for a in range(plan.na):
                slot = jnp.where(
                    tiles_ref[member, row * plan.na + a] == row * plan.row_tiles + t, a, slot
                )
            copy = pltpu.make_async_copy(
                stack.at[member, slot],
                out.at[t * size:(t + 1) * size, member * width:(member + 1) * width],
                sem.at[member, t],
            )
            copy.start()
            copies.append(copy)
        if member == plan.members - 1:
            last = copies
        else:
            for copy in copies:
                copy.wait()
    for copy in last:
        copy.wait()


def diagonal_kernel(plan, cross, pivot, unit_ref, out):
    width = plan.width
    row = lax.broadcasted_iota(jnp.int32, (width, width), 0)
    col = lax.broadcasted_iota(jnp.int32, (width, width), 1)
    for member in range(plan.members):
        inverse = split(unit_inverse(unit_ref, member))
        x = cross[member]
        x = jnp.where(row == col, pivot[member:member + 1, :], 0.0) + x + x.T
        half = product(split(x), inverse)
        out[member] = product(inverse, split(half), contract=0)


def shards(inverse_front, factor, unit_lower, pivot_inverse, tile_list, tile_valid):
    plan = Plan(inverse_front, factor, unit_lower, tile_list)
    width, depth, lanes = plan.width, plan.depth, plan.lanes
    row, col = lax.axis_index("row"), lax.axis_index("col")
    on_diagonal = row // lanes == col
    flops = 6 * depth * depth * lanes * width
    sums, crosses = [], []
    for member in range(plan.members):
        own = factor[:, member * width:(member + 1) * width]
        high, low, *mirror = pl.pallas_call(
            functools.partial(gather_kernel, plan, member),
            in_specs=smem(2) + [pl.BlockSpec(memory_space=pl.ANY)] + vmem(1),
            out_specs=vmem(2 + lanes),
            out_shape=[jax.ShapeDtypeStruct((depth, depth * lanes), BF16)] * 2
            + [jax.ShapeDtypeStruct((depth, width), F32)] * lanes,
            scratch_shapes=[
                pltpu.VMEM((plan.na, plan.nb, plan.tile, plan.tile), F32),
                pltpu.SemaphoreType.DMA((plan.na, plan.nb)),
            ],
            compiler_params=PARAMS,
            cost_estimate=pl.CostEstimate(flops=flops, bytes_accessed=8 << 20, transcendentals=0),
            name="gather_mirror",
        )(tile_list, tile_valid, inverse_front, own)
        back = mirror[0]
        for shift in range(1, lanes):
            back = back + plan.swap(mirror[lanes - shift], shift)
        back = plan.collect(back)
        held = plan.spread(own)
        parts = [held] + [plan.swap(held, shift) for shift in range(1, lanes)]
        total, cross = pl.pallas_call(
            functools.partial(forward_kernel, plan),
            in_specs=vmem(3 + lanes),
            out_specs=vmem(2),
            out_shape=[
                jax.ShapeDtypeStruct((depth, width), F32),
                jax.ShapeDtypeStruct((width, width), F32),
            ],
            compiler_params=PARAMS,
            cost_estimate=pl.CostEstimate(flops=flops, bytes_accessed=8 << 20, transcendentals=0),
            name="forward",
        )(high, low, own, *parts)
        sums.append(plan.line_sum(total + jnp.where(on_diagonal, back, 0.0)))
        crosses.append(cross)
    column = pl.pallas_call(
        functools.partial(place_kernel, plan),
        in_specs=smem(1) + vmem(1 + plan.members),
        out_specs=pl.BlockSpec(memory_space=pl.ANY),
        out_shape=jax.ShapeDtypeStruct((inverse_front.shape[0], factor.shape[1]), F32),
        scratch_shapes=[
            pltpu.VMEM((plan.members, plan.na + 1, plan.tile, width), F32),
            pltpu.SemaphoreType.DMA((plan.members, plan.row_tiles)),
        ],
        compiler_params=PARAMS,
        name="place",
    )(tile_list, unit_lower, *sums)
    cross = lax.psum(jnp.stack(crosses), ("row", "col"))
    diagonal = pl.pallas_call(
        functools.partial(diagonal_kernel, plan),
        in_specs=vmem(3),
        out_specs=vmem(1)[0],
        out_shape=jax.ShapeDtypeStruct(unit_lower.shape, F32),
        compiler_params=PARAMS,
        name="diagonal",
    )(cross, pivot_inverse, unit_lower)
    return (column, diagonal)


def solution(mesh):
    in_specs = (P("row", "col"), P("row", None), P(), P(), P(), P())
    out_specs = (P("row", None), P())
    return jax.shard_map(shards, mesh=mesh, in_specs=in_specs, out_specs=out_specs, check_vma=False)
```

time: 1150 us -> 299 us (0.26)
  matrix products: 408 us -> 0 us
  waiting for transfers between devices: 589 us -> 183 us
  local copies, waits for them, and re-layouts: 107 us -> 6.11 us
  starting transfers between devices: 0.38 us -> 36 us
  Pallas kernels: 0 us -> 29.6 us
    dot_general x10 -> x0, matrix products: 408 us -> none  [the longest x3 241 us: inner_left(): lax.dot_general(left, right, (((0,), (0,)), ((), ())), precision=lax.Prec...]
    psum x3 -> x1, waiting for transfers between devices: 497 us -> 133 us  [shards(): cross = lax.psum(jnp.stack(crosses), ('row', 'col'))]
    all_gather x1 -> x0, waiting for transfers between devices: 92.4 us -> none  [shards(): normalized = lax.all_gather(normalize(factor), 'row', axis=0, tiled=True)]
    ppermute x0 -> x18, waiting for transfers between devices: none -> 50.1 us  [the longest x2 30 us: line_sum(): x = x + lax.ppermute(x, 'col', [(i, i + 1), (count - 1 - i, count - 2 - i)])]
    unnamed x18 -> x28, local copies, waits for them, and re-layouts: 53 us -> 4.81 us
    ppermute x0 -> x18, starting transfers between devices: none -> 36 us  [the longest x4 15.6 us: spread(): got = lax.ppermute(x, ('row', 'col'), self.tree(step))]
    transpose x2 -> x0, local copies, waits for them, and re-layouts: 30.9 us -> none  [place_tiles(): jnp.einsum('sta,absw->tbsw', onehot, slot_tiles, precision=lax.Precision....]
    pallas_call x0 -> x6, Pallas kernels: none -> 29.6 us  [the longest x2 9.28 us: shards(): pl.pallas_call(functools.partial(gather_kernel, plan, member), in_specs=s...]
  transfers between devices with their start and end apart: 4 -> 19, of which waited for: 4 -> 8; matrix products, arithmetic and copies ran while one was open for 6% -> 9% of each run, Pallas kernels for 0% -> 8%
where the time goes in v1:
time: 299 us
  waiting for transfers between devices  183 us (61%)
  starting transfers between devices  36 us (12%)
  Pallas kernels  29.6 us (10%)
  other arithmetic  29.5 us (10%)
  between operations  14.4 us (5%)
  local copies, waits for them, and re-layouts  6.11 us (2%)
    psum x1, waiting for transfers between devices, shards(): cross = lax.psum(jnp.stack(crosses), ('row', 'col'))  133 us
    ppermute x2, waiting for transfers between devices, line_sum(): x = x + lax.ppermute(x, 'col', [(i, i + 1), (count - 1 - i, count - 2 - i)])  30 us
    ppermute x4, starting transfers between devices, spread(): got = lax.ppermute(x, ('row', 'col'), self.tree(step))  15.6 us
    ppermute x4, waiting for transfers between devices, spread(): got = lax.ppermute(x, ('row', 'col'), self.tree(step))  13.5 us
    pallas_call x2, Pallas kernels, shards(): pl.pallas_call(functools.partial(gather_kernel, plan, member), in_specs=s...  9.28 us
    pallas_call x2, Pallas kernels, shards(): pl.pallas_call(functools.partial(forward_kernel, plan), in_specs=vmem(3 +...  8.56 us
    ppermute x2, starting transfers between devices, line_sum(): x = x + lax.ppermute(x, 'col', [(i, i + 1), (count - 1 - i, count - 2 - i)])  6.91 us
    pallas_call x1, Pallas kernels, shards(): pl.pallas_call(functools.partial(place_kernel, plan), in_specs=smem(1) +...  6.76 us
  transfers between devices with their start and end apart: 19, of which 8 were waited for; matrix products, arithmetic and copies ran while one was open for 9% of the time, Pallas kernels for 8%

profile of v1, /device:TPU:0, one launch (start us, length us, event | category | flops | bytes accessed | tf_op | source)
XLA Modules:
  0.0 298.6 jit_solution(11471285718799868646)
XLA Ops:
  7.2 1.3 slice.7.factor
  8.5 5.8 %collective-permute-start.9 = (f32[512,512]{1,0:T(8,128)S(1)}, f32[512,512]{1,0:T(8,128)}, u32[]{:S(2)}, u32[]{:S(2)}) collective-permute-start(f32[512,512]{1,0:T(8,128)S(1)} %slice.7.factor), channel_id=1, source_target_pairs={{0,8},{4,20},{9,1},{13,29},{18,26}} | collective-permute-start | bytes 3145736 | tf_op jit(solution)/shard_map/ppermute | solution.py:100
  14.4 5.1 %gather_mirror.3 = (bf16[512,1024]{1,0:T(8,128)(2,1)S(1)}, bf16[512,1024]{1,0:T(8,128)(2,1)S(1)}, f32[512,512]{1,0:T(8,128)S(1)}, f32[512,512]{1,0:T(8,128)}) custom-call(s32[2,16]{1,0:T(2,128)S(1)} %copy-done.2, s32[2,16]{1,0:T(2,128)S(1)} %copy-done.3, f32[2048,4096]{1,0:T(8,128)} %front.3, f32[512,512]{1,0:T(8,128)S(1)} %slice.7.factor), custom_call_target="tpu_custom_call" | custom-call | flops 1610612736 | bytes 8388608 | tf_op jit(solution)/shard_map/gather_mirror/pallas_call | solution.py:237
  19.5 1.0 copy-done.5
  20.5 1.0 copy-done.7
  21.5 4.2 %collective-permute-done.9 = f32[512,512]{1,0:T(8,128)} collective-permute-done((f32[512,512]{1,0:T(8,128)S(1)}, f32[512,512]{1,0:T(8,128)}, u32[]{:S(2)}, u32[]{:S(2)}) %collective-permute-start.9) | collective-permute-done | bytes 1048608 | tf_op jit(solution)/shard_map/ppermute | solution.py:100
  25.7 2.8 broadcast_select_fusion
  28.5 4.9 %collective-permute-start = (f32[512,512]{1,0:T(8,128)S(1)}, f32[512,512]{1,0:T(8,128)S(1)}, u32[]{:S(2)}, u32[]{:S(2)}) collective-permute-start(f32[512,512]{1,0:T(8,128)S(1)} %get-tuple-element.27.factor), channel_id=1, source_target_pairs={{0,8},{4,20},{9,1},{13,29},{18,26}} | collective-permute-start | bytes 3145736 | tf_op jit(solution)/shard_map/ppermute | solution.py:100
  33.4 4.2 %gather_mirror.2 = (bf16[512,1024]{1,0:T(8,128)(2,1)S(1)}, bf16[512,1024]{1,0:T(8,128)(2,1)S(1)}, f32[512,512]{1,0:T(8,128)S(1)}, f32[512,512]{1,0:T(8,128)S(1)}) custom-call(s32[2,16]{1,0:T(2,128)S(1)} %copy-done.2, s32[2,16]{1,0:T(2,128)S(1)} %copy-done.3, f32[2048,4096]{1,0:T(8,128)} %front.3, f32[512,512]{1,0:T(8,128)S(1)} %get-tuple-element.27.factor), custom_call_target="tpu_custom_call" | custom-call | flops 1610612736 | bytes 8388608 | tf_op jit(solution)/shard_map/gather_mirror/pallas_call | solution.py:237
  37.7 2.6 collective-permute-start.10
  40.3 2.5 add.57
  42.7 1.3 collective-permute-start.13
  44.0 7.1 %collective-permute-done = f32[512,512]{1,0:T(8,128)S(1)} collective-permute-done((f32[512,512]{1,0:T(8,128)S(1)}, f32[512,512]{1,0:T(8,128)S(1)}, u32[]{:S(2)}, u32[]{:S(2)}) %collective-permute-start) | collective-permute-done | bytes 1048608 | tf_op jit(solution)/shard_map/ppermute | solution.py:100
  51.4 2.3 collective-permute-start.1
  53.7 1.2 add.51
  54.9 1.3 collective-permute-start.4
  56.2 2.4 broadcast_select_fusion.2.rest_0_
  58.6 0.9 collective-permute-start.11
  59.7 2.7 add.58
  62.4 1.3 collective-permute-start.14
  63.7 2.1 collective-permute-done.1
  65.8 1.2 broadcast_select_fusion.3.rest_0_
  67.1 2.4 collective-permute-start.2
  69.4 6.4 %collective-permute-done.4 = f32[512,512]{1,0:T(8,128)} collective-permute-done((f32[512,512]{1,0:T(8,128)}, f32[512,512]{1,0:T(8,128)}, u32[]{:S(2)}, u32[]{:S(2)}) %collective-permute-start.4) | collective-permute-done | bytes 1048608 | tf_op jit(solution)/shard_map/ppermute | solution.py:107
  75.8 2.8 add.52
  78.6 1.3 collective-permute-start.5
  79.9 1.2 copy-done.8
  81.1 4.3 %forward.3 = (f32[512,512]{1,0:T(8,128)S(1)}, f32[512,512]{1,0:T(8,128)S(1)}) custom-call(bf16[512,1024]{1,0:T(8,128)(2,1)S(1)} %copy-done.6, bf16[512,1024]{1,0:T(8,128)(2,1)S(1)} %copy-done.8, f32[512,512]{1,0:T(8,128)S(1)} %slice.7.factor, f32[512,512]{1,0:T(8,128)} %broadcast_select_fusion.2.rest_0_, f32[512,512]{1,0:T(8,128)} %collective-permute-done.11.rest_1_), custom_call_target="tpu_custom_call" | custom-call | flops 1610612736 | bytes 8388608 | tf_op jit(solution)/shard_map/forward/pallas_call | solution.py:257
  85.4 2.1 select_add_fusion
  87.5 5.6 %collective-permute-start.15 = (f32[512,512]{1,0:T(8,128)S(1)}, f32[512,512]{1,0:T(8,128)S(1)}, u32[]{:S(2)}, u32[]{:S(2)}) collective-permute-start(f32[512,512]{1,0:T(8,128)S(1)} %select_add_fusion), channel_id=1, source_target_pairs={{0,1},{3,2},{4,5},{7,6},{8,9},{11,10},{12,13},{15,14},{16,17},{19,... | collective-permute-start | bytes 3145736 | tf_op jit(solution)/shard_map/ppermute | solution.py:114
  93.1 4.3 %forward.2 = (f32[512,512]{1,0:T(8,128)S(1)}, f32[512,512]{1,0:T(8,128)S(1)}) custom-call(bf16[512,1024]{1,0:T(8,128)(2,1)S(1)} %copy-done.10, bf16[512,1024]{1,0:T(8,128)(2,1)S(1)} %copy-done.12, f32[512,512]{1,0:T(8,128)S(1)} %get-tuple-element.27.factor, f32[512,512]{1,0:T(8,128)} %broadcast_select_fusion.3.rest_0_, f32[512,512]{1,0:T(8,128)} %collective-permute-done.2.rest_1_), custom_call_target="tpu_custom_call" | custom-call | flops 1610612736 | bytes 8388608 | tf_op jit(solution)/shard_map/forward/pallas_call | solution.py:257
  97.4 1.9 select_add_fusion.1
  99.3 1.4 collective-permute-start.6
  100.7 15.7 %collective-permute-done.15 = f32[512,512]{1,0:T(8,128)S(1)} collective-permute-done((f32[512,512]{1,0:T(8,128)S(1)}, f32[512,512]{1,0:T(8,128)S(1)}, u32[]{:S(2)}, u32[]{:S(2)}) %collective-permute-start.15) | collective-permute-done | bytes 1048608 | tf_op jit(solution)/shard_map/ppermute | solution.py:114
  117.4 14.3 %collective-permute-done.6 = f32[512,512]{1,0:T(8,128)S(1)} collective-permute-done((f32[512,512]{1,0:T(8,128)S(1)}, f32[512,512]{1,0:T(8,128)S(1)}, u32[]{:S(2)}, u32[]{:S(2)}) %collective-permute-start.6) | collective-permute-done | bytes 1048608 | tf_op jit(solution)/shard_map/ppermute | solution.py:114
  131.6 1.2 add.55
  132.8 1.7 collective-permute-start.7
  134.5 1.5 pad_maximum_fusion
  136.0 1.2 add.62
  137.2 1.4 collective-permute-start.17
  138.7 2.7 add.56
  141.4 1.3 collective-permute-start.8
  142.7 132.8 %all-reduce.2.cloned.1.call-done.cross = f32[2,512,512]{2,1,0:T(8,128)} async-done(((f32[2,512,512]{2,1,0:T(8,128)}), f32[2,512,512]{2,1,0:T(8,128)}) %all-reduce.2.cloned.1.call-update) | async-done | bytes 2097168 | tf_op jit(solution)/shard_map/psum | solution.py:283
  275.5 1.6 copy-done.1
  277.1 5.0 %diagonal.1 = f32[2,512,512]{2,1,0:T(8,128)} custom-call(f32[2,512,512]{2,1,0:T(8,128)S(1)} %copy-done.1, f32[2,512]{1,0:T(2,128)S(1)} %copy-done.4, f32[2,512,512]{2,1,0:T(8,128)S(1)} %copy-done), custom_call_target="tpu_custom_call" | custom-call | tf_op jit(solution)/shard_map/diagonal/pallas_call | solution.py:284
  282.1 1.4 broadcast_select_fusion.4.rest_1_
  283.5 1.4 broadcast_select_fusion.5.rest_0_
  285.0 6.8 %place.1 = f32[2048,1024]{1,0:T(8,128)} custom-call(s32[2,16]{1,0:T(2,128)S(1)} %copy-done.2, f32[2,512,512]{2,1,0:T(8,128)S(1)} %copy-done, f32[512,512]{1,0:T(8,128)S(1)} %broadcast_select_fusion.5.rest_0_, f32[512,512]{1,0:T(8,128)S(1)} %broadcast_select_fusion.4.rest_1_), custom_call_target="tpu_custom_call" | custom-call | tf_op jit(solution)/shard_map/place/pallas_call | solution.py:271
  (43 shorter events, 1.6 us)
Async XLA Ops:
  7.2 7.2 %copy-start.2 = (s32[2,16]{1,0:T(2,128)S(1)}, s32[2,16]{1,0:T(2,128)}, u32[]{:S(2)}) copy-start(s32[2,16]{1,0:T(2,128)} %tiles_ref.5) | copy-start | bytes 388
  7.2 7.2 %copy-start.3 = (s32[2,16]{1,0:T(2,128)S(1)}, s32[2,16]{1,0:T(2,128)}, u32[]{:S(2)}) copy-start(s32[2,16]{1,0:T(2,128)} %valid_ref.3) | copy-start | bytes 388
  7.2 268.3 %all-reduce.2.cloned.1.call-start = ((), (), s32[]{:S(2)}) async-start(), calls=%async_computation | async-start | bytes 4194304 | tf_op jit(solution)/shard_map/psum | solution.py:283
  8.5 17.2 %collective-permute-start.9 = (f32[512,512]{1,0:T(8,128)S(1)}, f32[512,512]{1,0:T(8,128)}, u32[]{:S(2)}, u32[]{:S(2)}) collective-permute-start(f32[512,512]{1,0:T(8,128)S(1)} %slice.7.factor), channel_id=1, source_target_pairs={{0,8},{4,20},{9,1},{13,29},{18,26}} | collective-permute-start | bytes 3145736 | tf_op jit(solution)/shard_map/ppermute | solution.py:100
  19.5 1.0 copy-start.5
  20.5 1.0 copy-start.7
  21.5 18.8 %collective-permute-start.12 = (f32[512,512]{1,0:T(8,128)}, f32[512,512]{1,0:T(8,128)}, u32[]{:S(2)}, u32[]{:S(2)}) collective-permute-start(f32[512,512]{1,0:T(8,128)} %get-tuple-element.23), channel_id=1, source_target_pairs={{4,0},{0,4},{12,8},{8,12},{20,16},{16,20},{28,24},{24,28},{5,1},{1... | collective-permute-start | bytes 3145736 | tf_op jit(solution)/shard_map/ppermute | solution.py:96
  28.5 22.6 %collective-permute-start = (f32[512,512]{1,0:T(8,128)S(1)}, f32[512,512]{1,0:T(8,128)S(1)}, u32[]{:S(2)}, u32[]{:S(2)}) collective-permute-start(f32[512,512]{1,0:T(8,128)S(1)} %get-tuple-element.27.factor), channel_id=1, source_target_pairs={{0,8},{4,20},{9,1},{13,29},{18,26}} | collective-permute-start | bytes 3145736 | tf_op jit(solution)/shard_map/ppermute | solution.py:100
  37.6 13.8 %copy-start.9 = (bf16[512,1024]{1,0:T(8,128)(2,1)}, bf16[512,1024]{1,0:T(8,128)(2,1)S(1)}, u32[]{:S(2)}) copy-start(bf16[512,1024]{1,0:T(8,128)(2,1)S(1)} %get-tuple-element.14.high) | copy-start | bytes 3145732
  37.6 13.8 %copy-start.11 = (bf16[512,1024]{1,0:T(8,128)(2,1)}, bf16[512,1024]{1,0:T(8,128)(2,1)S(1)}, u32[]{:S(2)}) copy-start(bf16[512,1024]{1,0:T(8,128)(2,1)S(1)} %get-tuple-element.15.low) | copy-start | bytes 3145732
  37.6 13.6 %copy-start.13 = (f32[512,1024]{1,0:T(8,128)S(1)}, f32[512,1024]{1,0:T(8,128)}, u32[]{:S(2)}) copy-start(f32[512,1024]{1,0:T(8,128)} %param.7) | copy-start | bytes 6291460
  37.6 16.1 %collective-permute-start.3 = (f32[512,512]{1,0:T(8,128)S(1)}, f32[512,512]{1,0:T(8,128)S(1)}, u32[]{:S(2)}, u32[]{:S(2)}) collective-permute-start(f32[512,512]{1,0:T(8,128)S(1)} %get-tuple-element.18), channel_id=1, source_target_pairs={{4,0},{0,4},{12,8},{8,12},{20,16},{16,20},{28,24},{24,28},{5,1},{1... | collective-permute-start | bytes 3145736 | tf_op jit(solution)/shard_map/ppermute | solution.py:96
  37.7 18.5 %collective-permute-start.10 = (f32[512,512]{1,0:T(8,128)}, f32[512,512]{1,0:T(8,128)}, u32[]{:S(2)}, u32[]{:S(2)}) collective-permute-start(f32[512,512]{1,0:T(8,128)} %get-tuple-element.26), channel_id=1, source_target_pairs={{0,16},{8,24},{4,12},{20,28},{9,25},{1,17},{29,21},{22,30}} | collective-permute-start | bytes 3145736 | tf_op jit(solution)/shard_map/ppermute | solution.py:100
  42.7 17.0 %collective-permute-start.13 = (f32[512,512]{1,0:T(8,128)}, f32[512,512]{1,0:T(8,128)}, u32[]{:S(2)}, u32[]{:S(2)}) collective-permute-start(f32[512,512]{1,0:T(8,128)} %add.57), channel_id=1, source_target_pairs={{16,0},{24,8},{12,4},{28,20},{25,9},{17,1},{21,29},{30,22}} | collective-permute-start | bytes 3145736 | tf_op jit(solution)/shard_map/ppermute | solution.py:107
  51.4 14.5 %collective-permute-start.1 = (f32[512,512]{1,0:T(8,128)S(1)}, f32[512,512]{1,0:T(8,128)}, u32[]{:S(2)}, u32[]{:S(2)}) collective-permute-start(f32[512,512]{1,0:T(8,128)S(1)} %broadcast_select_fusion.1), channel_id=1, source_target_pairs={{0,16},{8,24},{4,12},{20,28},{9,25},{1,17},{29,21},{22,30}} | collective-permute-start | bytes 3145736 | tf_op jit(solution)/shard_map/ppermute | solution.py:100
  54.9 20.9 %collective-permute-start.4 = (f32[512,512]{1,0:T(8,128)}, f32[512,512]{1,0:T(8,128)}, u32[]{:S(2)}, u32[]{:S(2)}) collective-permute-start(f32[512,512]{1,0:T(8,128)} %add.51), channel_id=1, source_target_pairs={{16,0},{24,8},{12,4},{28,20},{25,9},{17,1},{21,29},{30,22}} | collective-permute-start | bytes 3145736 | tf_op jit(solution)/shard_map/ppermute | solution.py:107
  58.6 21.3 %collective-permute-start.11 = (f32[512,512]{1,0:T(8,128)}, f32[512,512]{1,0:T(8,128)}, u32[]{:S(2)}, u32[]{:S(2)}) collective-permute-start(f32[512,512]{1,0:T(8,128)} %broadcast_select_fusion.2.rest_0_), channel_id=1, source_target_pairs={{4,0},{0,4},{12,8},{8,12},{20,16},{16,20},{28,24},{24,28},{5,1},{1... | collective-permute-start | bytes 3145736 | tf_op jit(solution)/shard_map/ppermute | solution.py:96
  62.4 23.0 %collective-permute-start.14 = (f32[512,512]{1,0:T(8,128)}, f32[512,512]{1,0:T(8,128)}, u32[]{:S(2)}, u32[]{:S(2)}) collective-permute-start(f32[512,512]{1,0:T(8,128)} %add.58), channel_id=1, source_target_pairs={{8,0},{20,4},{1,9},{29,13},{26,18}} | collective-permute-start | bytes 3145736 | tf_op jit(solution)/shard_map/ppermute | solution.py:107
  67.1 12.9 %copy-start.6 = (bf16[512,1024]{1,0:T(8,128)(2,1)S(1)}, bf16[512,1024]{1,0:T(8,128)(2,1)}, u32[]{:S(2)}) copy-start(bf16[512,1024]{1,0:T(8,128)(2,1)} %copy-done.5) | copy-start | bytes 3145732
  67.1 26.0 %collective-permute-start.2 = (f32[512,512]{1,0:T(8,128)}, f32[512,512]{1,0:T(8,128)}, u32[]{:S(2)}, u32[]{:S(2)}) collective-permute-start(f32[512,512]{1,0:T(8,128)} %broadcast_select_fusion.3.rest_0_), channel_id=1, source_target_pairs={{4,0},{0,4},{12,8},{8,12},{20,16},{16,20},{28,24},{24,28},{5,1},{1... | collective-permute-start | bytes 3145736 | tf_op jit(solution)/shard_map/ppermute | solution.py:96
  78.6 18.8 %collective-permute-start.5 = (f32[512,512]{1,0:T(8,128)}, f32[512,512]{1,0:T(8,128)}, u32[]{:S(2)}, u32[]{:S(2)}) collective-permute-start(f32[512,512]{1,0:T(8,128)} %add.52), channel_id=1, source_target_pairs={{8,0},{20,4},{1,9},{29,13},{26,18}} | collective-permute-start | bytes 3145736 | tf_op jit(solution)/shard_map/ppermute | solution.py:107
  79.9 1.2 copy-start.8
  85.4 7.7 %copy-start.10 = (bf16[512,1024]{1,0:T(8,128)(2,1)S(1)}, bf16[512,1024]{1,0:T(8,128)(2,1)}, u32[]{:S(2)}) copy-start(bf16[512,1024]{1,0:T(8,128)(2,1)} %copy-done.9) | copy-start | bytes 3145732
  85.4 7.7 %copy-start.12 = (bf16[512,1024]{1,0:T(8,128)(2,1)S(1)}, bf16[512,1024]{1,0:T(8,128)(2,1)}, u32[]{:S(2)}) copy-start(bf16[512,1024]{1,0:T(8,128)(2,1)} %copy-done.11) | copy-start | bytes 3145732
  87.5 28.9 %collective-permute-start.15 = (f32[512,512]{1,0:T(8,128)S(1)}, f32[512,512]{1,0:T(8,128)S(1)}, u32[]{:S(2)}, u32[]{:S(2)}) collective-permute-start(f32[512,512]{1,0:T(8,128)S(1)} %select_add_fusion), channel_id=1, source_target_pairs={{0,1},{3,2},{4,5},{7,6},{8,9},{11,10},{12,13},{15,14},{16,17},{19,... | collective-permute-start | bytes 3145736 | tf_op jit(solution)/shard_map/ppermute | solution.py:114
  99.3 32.3 %collective-permute-start.6 = (f32[512,512]{1,0:T(8,128)S(1)}, f32[512,512]{1,0:T(8,128)S(1)}, u32[]{:S(2)}, u32[]{:S(2)}) collective-permute-start(f32[512,512]{1,0:T(8,128)S(1)} %select_add_fusion.1), channel_id=1, source_target_pairs={{0,1},{3,2},{4,5},{7,6},{8,9},{11,10},{12,13},{15,14},{16,17},{19,... | collective-permute-start | bytes 3145736 | tf_op jit(solution)/shard_map/ppermute | solution.py:114
  116.6 19.4 %collective-permute-start.16 = (f32[512,512]{1,0:T(8,128)S(1)}, f32[512,512]{1,0:T(8,128)S(1)}, u32[]{:S(2)}, u32[]{:S(2)}) collective-permute-start(f32[512,512]{1,0:T(8,128)S(1)} %add.61), channel_id=1, source_target_pairs={{1,2},{2,1},{5,6},{6,5},{9,10},{10,9},{13,14},{14,13},{17,18},{18,... | collective-permute-start | bytes 3145736 | tf_op jit(solution)/shard_map/ppermute | solution.py:115
  132.8 5.8 %collective-permute-start.7 = (f32[512,512]{1,0:T(8,128)}, f32[512,512]{1,0:T(8,128)}, u32[]{:S(2)}, u32[]{:S(2)}) collective-permute-start(f32[512,512]{1,0:T(8,128)} %add.55), channel_id=1, source_target_pairs={{1,2},{2,1},{5,6},{6,5},{9,10},{10,9},{13,14},{14,13},{17,18},{18,... | collective-permute-start | bytes 3145736 | tf_op jit(solution)/shard_map/ppermute | solution.py:115
  137.2 138.2 %copy-start = (f32[2,512,512]{2,1,0:T(8,128)S(1)}, f32[2,512,512]{2,1,0:T(8,128)}, u32[]{:S(2)}) copy-start(f32[2,512,512]{2,1,0:T(8,128)} %unit_ref.3) | copy-start | bytes 6291460
  137.2 138.2 %copy-start.4 = (f32[2,512]{1,0:T(2,128)S(1)}, f32[2,512]{1,0:T(2,128)}, u32[]{:S(2)}) copy-start(f32[2,512]{1,0:T(2,128)} %pivot.1) | copy-start | bytes 12292
  137.2 144.8 %collective-permute-start.17 = (f32[512,512]{1,0:T(8,128)}, f32[512,512]{1,0:T(8,128)}, u32[]{:S(2)}, u32[]{:S(2)}) collective-permute-start(f32[512,512]{1,0:T(8,128)} %add.62), channel_id=1, source_target_pairs={{1,0},{2,3},{5,4},{6,7},{9,8},{10,11},{13,12},{14,15},{17,16},{18,... | collective-permute-start | bytes 3145736 | tf_op jit(solution)/shard_map/ppermute | solution.py:117
  141.4 142.1 %collective-permute-start.8 = (f32[512,512]{1,0:T(8,128)}, f32[512,512]{1,0:T(8,128)}, u32[]{:S(2)}, u32[]{:S(2)}) collective-permute-start(f32[512,512]{1,0:T(8,128)} %add.56), channel_id=1, source_target_pairs={{1,0},{2,3},{5,4},{6,7},{9,8},{10,11},{13,12},{14,15},{17,16},{18,... | collective-permute-start | bytes 3145736 | tf_op jit(solution)/shard_map/ppermute | solution.py:117
  275.5 1.6 copy-start.1
Sparse Core Ops, SparseCore 0:
  136.1 139.2 all-reduce.1

commit v2 on v1

--- a/solution.py
+++ b/solution.py
@@ -11,6 +11,7 @@
 BF16 = jnp.bfloat16
 VMEM = pltpu.MemorySpace.VMEM
 SMEM = pltpu.MemorySpace.SMEM
+SPLIT = 2
 PARAMS = pltpu.CompilerParams(vmem_limit_bytes=48 * 1024 * 1024)
 
 
@@ -88,6 +89,17 @@
             got = got | (here & (row % self.lanes == lane))
         return got
 
+    def rounds(self):
+        pairs = [[], []]
+        for turn, col, chip, plane in (
+            (0, 0, 1, 0), (1, 0, 2, 0), (0, 0, 3, 3), (0, 1, 3, 1), (1, 1, 2, 3), (0, 2, 3, 2),
+        ):
+            for lane in range(self.lanes):
+                pairs[(turn + lane) % 2].append(
+                    (self.device(col, lane, plane), self.device(chip, lane, col))
+                )
+        return pairs
+
     def swap(self, x, shift):
         pairs = []
         for row in range(self.rows):
@@ -95,17 +107,26 @@
             pairs.append((chip * self.lanes + (lane + shift) % self.lanes, row))
         return lax.ppermute(x, "row", pairs)
 
-    def spread(self, x):
+    def spread(self, x, on_diagonal):
+        if self.cols == 4:
+            first, second = (lax.ppermute(x, ("row", "col"), pairs) for pairs in self.rounds())
+            return jnp.where(on_diagonal, x, first + second), (first, second)
         for step in range(self.steps):
             got = lax.ppermute(x, ("row", "col"), self.tree(step))
             x = jnp.where(self.received(step), got, x)
-        return x
-
-    def collect(self, x):
+        return x, (x,)
+
+    def collect(self, x, on_diagonal):
+        if self.cols == 4:
+            first, second = (
+                lax.ppermute(x, ("row", "col"), [(child, parent) for parent, child in pairs])
+                for pairs in self.rounds()
+            )
+            return jnp.where(on_diagonal, x, 0.0) + first + second, (first, second)
         for step in reversed(range(self.steps)):
             pairs = [(child, parent) for parent, child in self.tree(step)]
             x = x + lax.ppermute(x, ("row", "col"), pairs)
-        return x
+        return jnp.where(on_diagonal, x, 0.0), (x,)
 
     def line_sum(self, x):
         count, half = self.cols, self.cols // 2
@@ -113,9 +134,45 @@
         for i in range(half - 1):
             x = x + lax.ppermute(x, "col", [(i, i + 1), (count - 1 - i, count - 2 - i)])
         x = x + lax.ppermute(x, "col", [(half - 1, half), (half, half - 1)])
+        got = x
         for i in range(half - 1):
             got = lax.ppermute(x, "col", [(half - 1 - i, half - 2 - i), (half + i, half + i + 1)])
-            x = jnp.where((place == half - 2 - i) | (place == half + i + 1), got, x)
+            if i < half - 2:
+                x = jnp.where((place == half - 2 - i) | (place == half + i + 1), got, x)
+        return x, got
+
+    def at_end(self):
+        place = lax.axis_index("col")
+        return (place == 0) | (place == self.cols - 1)
+
+    def bit_pairs(self, step):
+        return [
+            (self.device(chip, lane, col), self.device(chip ^ order[step], lane, col))
+            for chip in range(self.cols)
+            for lane, order in enumerate(self.orders)
+            for col in range(self.cols)
+        ]
+
+    def bit(self, step):
+        row = lax.axis_index("row")
+        chip, value = row // self.lanes, jnp.int32(0)
+        for lane, order in enumerate(self.orders):
+            value = jnp.where((row % self.lanes == lane) & ((chip & order[step]) != 0), 1, value)
+        return value
+
+    def sum_all(self, x):
+        for step in range(self.steps):
+            x = x.reshape(2, x.shape[0] // 2, x.shape[1])
+            bit = self.bit(step)
+            send = lax.dynamic_index_in_dim(x, 1 - bit, 0, keepdims=False)
+            keep = lax.dynamic_index_in_dim(x, bit, 0, keepdims=False)
+            x = keep + lax.ppermute(send, ("row", "col"), self.bit_pairs(step))
+        x, got = self.line_sum(x)
+        x = jnp.where(self.at_end(), got, x)
+        for step in reversed(range(self.steps)):
+            got = lax.ppermute(x, ("row", "col"), self.bit_pairs(step))
+            bit = self.bit(step) == 1
+            x = jnp.concatenate([jnp.where(bit, got, x), jnp.where(bit, x, got)])
         return x
 
 
@@ -165,8 +222,10 @@
 
 
 def forward_kernel(plan, high, low, factor, *rest):
-    parts, (total, cross) = rest[:plan.lanes], rest[plan.lanes:]
-    size, depth = plan.tile, plan.depth
+    lanes, size, depth = plan.lanes, plan.tile, plan.depth
+    parts, rest = rest[:lanes], rest[lanes:]
+    totals, rest = rest[:SPLIT], rest[SPLIT:]
+    cross, (total, whole) = rest[:lanes], rest[lanes:]
     right = [split(part[...]) for part in parts]
     for a in range(plan.na):
         rows = slice(a * size, (a + 1) * size)
@@ -175,52 +234,86 @@
                 (high[rows, i * depth:(i + 1) * depth], low[rows, i * depth:(i + 1) * depth]),
                 right[i],
             )
-            for i in range(plan.lanes)
+            for i in range(lanes)
         )
-    cross[...] = product(split(factor[...]), split(total[...]), contract=0)
-
-
-def place_kernel(plan, tiles_ref, unit_ref, *rest):
-    sums, (out, stack, sem) = rest[:plan.members], rest[plan.members:]
+    share = depth // SPLIT
+    for i in range(SPLIT):
+        totals[i][...] = total[i * share:(i + 1) * share, :]
+    whole[...] = product(split(factor[...]), split(total[...]), contract=0)
+    share = plan.width // lanes
+    lane = lax.rem(lax.axis_index("row"), lanes)
+    for i in range(lanes):
+        first = pl.multiple_of(lax.rem(lane + i, lanes) * share, share)
+        cross[i][...] = whole[pl.ds(first, share), :]
+
+
+def place_kernel(plan, member, tiles_ref, unit_ref, *rest):
+    sums, rest = rest[:2 * SPLIT], rest[2 * SPLIT:]
+    out, stack, zeros, sems, zero_sems = rest[member > 0:]
     size, width = plan.tile, plan.width
-    row = lax.axis_index("row")
-    for member in range(plan.members):
-        right = split(unit_inverse(unit_ref, member))
-        stack[member, plan.na] = jnp.zeros((size, width), F32)
-        for a in range(plan.na):
-            left = split(sums[member][a * size:(a + 1) * size, :])
-            stack[member, a] = -product(left, right)
-        copies = []
-        for t in range(plan.row_tiles):
-            slot = jnp.int32(plan.na)
-            for a in range(plan.na):
-                slot = jnp.where(
-                    tiles_ref[member, row * plan.na + a] == row * plan.row_tiles + t, a, slot
+    row, at_end = lax.axis_index("row"), plan.at_end()
+
+    def zero_copies(act):
+        for other in range(plan.members):
+            for t in range(plan.row_tiles):
+                taken = False
+                for a in range(plan.na):
+                    taken = taken | (
+                        tiles_ref[other, row * plan.na + a] == row * plan.row_tiles + t
+                    )
+                copy = pltpu.make_async_copy(
+                    zeros,
+                    out.at[t * size:(t + 1) * size, other * width:(other + 1) * width],
+                    zero_sems.at[other, t],
                 )
-            copy = pltpu.make_async_copy(
-                stack.at[member, slot],
-                out.at[t * size:(t + 1) * size, member * width:(member + 1) * width],
-                sem.at[member, t],
-            )
-            copy.start()
-            copies.append(copy)
-        if member == plan.members - 1:
-            last = copies
-        else:
-            for copy in copies:
-                copy.wait()
-    for copy in last:
+                pl.when(jnp.logical_not(taken))(functools.partial(act, copy))
+
+    if member == 0:
+        zeros[...] = jnp.zeros_like(zeros)
+        zero_copies(lambda copy: copy.start())
+    right = split(unit_inverse(unit_ref, member))
+    share = plan.depth // SPLIT
+    for i in range(SPLIT):
+        x = jnp.where(at_end, sums[2 * i + 1][...], sums[2 * i][...])
+        stack[i * share:(i + 1) * share, :] = -product(split(x), right)
+    copies = []
+    for a in range(plan.na):
+        t = jnp.clip(
+            tiles_ref[member, row * plan.na + a] - row * plan.row_tiles, 0, plan.row_tiles - 1
+        )
+        copy = pltpu.make_async_copy(
+            stack.at[a * size:(a + 1) * size, :],
+            out.at[
+                pl.ds(pl.multiple_of(t * size, size), size), member * width:(member + 1) * width
+            ],
+            sems.at[a],
+        )
+        copy.start()
+        copies.append(copy)
+    for copy in copies:
         copy.wait()
-
-
-def diagonal_kernel(plan, cross, pivot, unit_ref, out):
-    width = plan.width
+    if member == 0:
+        zero_copies(lambda copy: copy.wait())
+
+
+def diagonal_kernel(plan, pivot, unit_ref, *rest):
+    parts, out = rest[:plan.lanes], rest[plan.lanes]
+    width, lanes = plan.width, plan.lanes
+    share = width // lanes
+    lane = lax.rem(lax.axis_index("row"), lanes)
     row = lax.broadcasted_iota(jnp.int32, (width, width), 0)
     col = lax.broadcasted_iota(jnp.int32, (width, width), 1)
     for member in range(plan.members):
+        rows = slice(member * share, (member + 1) * share)
+        pieces = []
+        for other in range(lanes):
+            piece = parts[0][rows, :]
+            for i in range(1, lanes):
+                piece = jnp.where(lax.rem(lane + i, lanes) == other, parts[i][rows, :], piece)
+            pieces.append(piece)
+        x = jnp.concatenate(pieces)
+        x = jnp.where(row == col, pivot[member:member + 1, :], 0.0) + x + x.T
         inverse = split(unit_inverse(unit_ref, member))
-        x = cross[member]
-        x = jnp.where(row == col, pivot[member:member + 1, :], 0.0) + x + x.T
         half = product(split(x), inverse)
         out[member] = product(inverse, split(half), contract=0)
 
@@ -232,6 +325,7 @@
     on_diagonal = row // lanes == col
     flops = 6 * depth * depth * lanes * width
     sums, crosses = [], []
+    sent = returned = None
     for member in range(plan.members):
         own = factor[:, member * width:(member + 1) * width]
         high, low, *mirror = pl.pallas_call(
@@ -251,44 +345,71 @@
         back = mirror[0]
         for shift in range(1, lanes):
             back = back + plan.swap(mirror[lanes - shift], shift)
-        back = plan.collect(back)
-        held = plan.spread(own)
+        ready = own
+        if member:
+            ready, sent = lax.optimization_barrier((ready, sent))
+            back, returned = lax.optimization_barrier((back, returned))
+        back, returned = plan.collect(back, on_diagonal)
+        held, sent = plan.spread(ready, on_diagonal)
         parts = [held] + [plan.swap(held, shift) for shift in range(1, lanes)]
-        total, cross = pl.pallas_call(
+        *totals_cross, = pl.pallas_call(
             functools.partial(forward_kernel, plan),
             in_specs=vmem(3 + lanes),
-            out_specs=vmem(2),
-            out_shape=[
-                jax.ShapeDtypeStruct((depth, width), F32),
-                jax.ShapeDtypeStruct((width, width), F32),
+            out_specs=vmem(SPLIT + lanes),
+            out_shape=[jax.ShapeDtypeStruct((depth // SPLIT, width), F32)] * SPLIT
+            + [jax.ShapeDtypeStruct((width // lanes, width), F32)] * lanes,
+            scratch_shapes=[
+                pltpu.VMEM((depth, width), F32),
+                pltpu.VMEM((width, width), F32),
             ],
             compiler_params=PARAMS,
             cost_estimate=pl.CostEstimate(flops=flops, bytes_accessed=8 << 20, transcendentals=0),
             name="forward",
         )(high, low, own, *parts)
-        sums.append(plan.line_sum(total + jnp.where(on_diagonal, back, 0.0)))
-        crosses.append(cross)
-    column = pl.pallas_call(
-        functools.partial(place_kernel, plan),
-        in_specs=smem(1) + vmem(1 + plan.members),
-        out_specs=pl.BlockSpec(memory_space=pl.ANY),
-        out_shape=jax.ShapeDtypeStruct((inverse_front.shape[0], factor.shape[1]), F32),
-        scratch_shapes=[
-            pltpu.VMEM((plan.members, plan.na + 1, plan.tile, width), F32),
-            pltpu.SemaphoreType.DMA((plan.members, plan.row_tiles)),
-        ],
-        compiler_params=PARAMS,
-        name="place",
-    )(tile_list, unit_lower, *sums)
-    cross = lax.psum(jnp.stack(crosses), ("row", "col"))
+        totals, cross = totals_cross[:SPLIT], totals_cross[SPLIT:]
+        share = depth // SPLIT
+        member_sums = []
+        for i in range(SPLIT):
+            member_sums += plan.line_sum(totals[i] + back[i * share:(i + 1) * share])
+        sums.append(member_sums)
+        reduced = cross[0]
+        for shift in range(1, lanes):
+            reduced = reduced + plan.swap(cross[lanes - shift], shift)
+        crosses.append(reduced)
+    column = None
+    for member in range(plan.members):
+        column = pl.pallas_call(
+            functools.partial(place_kernel, plan, member),
+            in_specs=smem(1) + vmem(1 + 2 * SPLIT)
+            + [pl.BlockSpec(memory_space=pl.ANY)] * (member > 0),
+            out_specs=pl.BlockSpec(memory_space=pl.ANY),
+            out_shape=jax.ShapeDtypeStruct((inverse_front.shape[0], factor.shape[1]), F32),
+            scratch_shapes=[
+                pltpu.VMEM((depth, width), F32),
+                pltpu.VMEM((plan.tile, width), F32),
+                pltpu.SemaphoreType.DMA((plan.na,)),
+                pltpu.SemaphoreType.DMA((plan.members, plan.row_tiles)),
+            ],
+            input_output_aliases={2 + 2 * SPLIT: 0} if member else {},
+            compiler_params=PARAMS,
+            cost_estimate=pl.CostEstimate(
+                flops=6 * depth * width * width, bytes_accessed=8 << 20, transcendentals=0
+            ),
+            name="place",
+        )(tile_list, unit_lower, *sums[member], *([column] if member else []))
+    cross = plan.sum_all(jnp.concatenate(crosses))
+    parts = [cross] + [plan.swap(cross, shift) for shift in range(1, lanes)]
     diagonal = pl.pallas_call(
         functools.partial(diagonal_kernel, plan),
-        in_specs=vmem(3),
+        in_specs=vmem(2 + lanes),
         out_specs=vmem(1)[0],
         out_shape=jax.ShapeDtypeStruct(unit_lower.shape, F32),
         compiler_params=PARAMS,
+        cost_estimate=pl.CostEstimate(
+            flops=24 * width * width * width, bytes_accessed=8 << 20, transcendentals=0
+        ),
         name="diagonal",
-    )(cross, pivot_inverse, unit_lower)
+    )(pivot_inverse, unit_lower, *parts)
     return (column, diagonal)
 
 

time: 299 us -> 311 us (1.040)
  waiting for transfers between devices: 183 us -> 203 us
  starting transfers between devices: 36 us -> 51.9 us
  between operations: 14.4 us -> 1.25 us
  other arithmetic: 29.5 us -> 18.7 us
    psum x1 -> x0, waiting for transfers between devices: 133 us -> none  [shards(): cross = lax.psum(jnp.stack(crosses), ('row', 'col'))]
    ppermute x8 -> x12, waiting for transfers between devices: 20.1 us -> 129 us  [the longest x4 83.2 us: spread(): lax.ppermute(x, ('row', 'col'), pairs)]
    ppermute x2 -> x5, waiting for transfers between devices: 0.01 us -> 42 us  [line_sum(): lax.ppermute(x, 'col', [(half - 1 - i, half - 2 - i), (half + i, half + i...]
    ppermute x2 -> x5, starting transfers between devices: 6.91 us -> 16.5 us  [line_sum(): x = x + lax.ppermute(x, 'col', [(i, i + 1), (count - 1 - i, count - 2 - i)])]
    select_n x6 -> x5, other arithmetic: 9.58 us -> 2.55 us  [the longest x2 2.37 us: spread(): return (jnp.where(on_diagonal, x, first + second), (first, second))]
    ppermute x2 -> x5, starting transfers between devices: 2.69 us -> 6.72 us  [line_sum(): lax.ppermute(x, 'col', [(half - 1 - i, half - 2 - i), (half + i, half + i...]
    add x2 -> x5, other arithmetic: 3.92 us -> 0.36 us  [line_sum(): x = x + lax.ppermute(x, 'col', [(half - 1, half), (half, half - 1)])]
    ppermute x8 -> x12, starting transfers between devices: 20.7 us -> 23.4 us  [the longest x4 13.4 us: spread(): lax.ppermute(x, ('row', 'col'), pairs)]
  transfers between devices with their start and end apart: 19 -> 34, of which waited for: 8 -> 17; matrix products, arithmetic and copies ran while one was open for 9% -> 5% of each run, Pallas kernels for 8% -> 9%
where the time goes in v2:
time: 311 us; the launch traced here: 310 us
  waiting for transfers between devices  203 us (65%)
  starting transfers between devices  51.9 us (17%)
  Pallas kernels  31.6 us (10%)
  other arithmetic  18.7 us (6%)
  local copies, waits for them, and re-layouts  3.53 us (1%)
    ppermute x4, waiting for transfers between devices, spread(): lax.ppermute(x, ('row', 'col'), pairs)  83.2 us
    ppermute x5, waiting for transfers between devices, line_sum(): lax.ppermute(x, 'col', [(half - 1 - i, half - 2 - i), (half + i, half + i...  42 us
    ppermute x5, waiting for transfers between devices, line_sum(): x = x + lax.ppermute(x, 'col', [(i, i + 1), (count - 1 - i, count - 2 - i)])  32.3 us
    ppermute x2, waiting for transfers between devices, sum_all(): x = keep + lax.ppermute(send, ('row', 'col'), self.bit_pairs(step))  27.8 us
    ppermute x5, starting transfers between devices, line_sum(): x = x + lax.ppermute(x, 'col', [(i, i + 1), (count - 1 - i, count - 2 - i)])  16.5 us
    ppermute x4, waiting for transfers between devices, collect(): lax.ppermute(x, ('row', 'col'), [(child, parent) for parent, child in pai...  15.3 us
    ppermute x4, starting transfers between devices, spread(): lax.ppermute(x, ('row', 'col'), pairs)  13.4 us
    pallas_call x2, Pallas kernels, shards(): pl.pallas_call(functools.partial(forward_kernel, plan), in_specs=vmem(3 +...  10.2 us
  transfers between devices with their start and end apart: 34, of which 17 were waited for; matrix products, arithmetic and copies ran while one was open for 5% of the time, Pallas kernels for 9%

profile of v2, /device:TPU:0, one launch (start us, length us, event | category | flops | bytes accessed | tf_op | source)
XLA Modules:
  0.0 310.2 jit_solution(17323219534551608341)
XLA Ops:
  0.6 1.4 slice.19.factor
  2.1 5.9 %collective-permute-start.1 = (f32[512,512]{1,0:T(8,128)S(1)}, f32[512,512]{1,0:T(8,128)}, u32[]{:S(2)}, u32[]{:S(2)}) collective-permute-start(f32[512,512]{1,0:T(8,128)S(1)} %slice.19.factor), channel_id=1, source_target_pairs={{4,12},{0,16},{7,28},{13,29},{11,17},{22,30}} | collective-permute-start | bytes 3145736 | tf_op jit(solution)/shard_map/ppermute | solution.py:112
  7.9 2.3 collective-permute-start
  10.2 19.1 %collective-permute-done.1 = f32[512,512]{1,0:T(8,128)} collective-permute-done((f32[512,512]{1,0:T(8,128)S(1)}, f32[512,512]{1,0:T(8,128)}, u32[]{:S(2)}, u32[]{:S(2)}) %collective-permute-start.1) | collective-permute-done | bytes 1048608 | tf_op jit(solution)/shard_map/ppermute | solution.py:112
  29.4 44.9 %collective-permute-done = f32[512,512]{1,0:T(8,128)} collective-permute-done((f32[512,512]{1,0:T(8,128)S(1)}, f32[512,512]{1,0:T(8,128)}, u32[]{:S(2)}, u32[]{:S(2)}) %collective-permute-start) | collective-permute-done | bytes 1048608 | tf_op jit(solution)/shard_map/ppermute | solution.py:112
  74.3 2.0 add_select_fusion
  76.3 1.4 collective-permute-start.3
  77.7 3.9 %collective-permute-start.2 = (f32[512,512]{1,0:T(8,128)S(1)}, f32[512,512]{1,0:T(8,128)S(1)}, u32[]{:S(2)}, u32[]{:S(2)}) collective-permute-start(f32[512,512]{1,0:T(8,128)S(1)} %get-tuple-element.22.factor), channel_id=1, source_target_pairs={{0,8},{4,20},{3,24},{9,25},{15,21},{18,26}} | collective-permute-start | bytes 3145736 | tf_op jit(solution)/shard_map/ppermute | solution.py:112
  81.7 19.2 %collective-permute-done.3 = f32[512,512]{1,0:T(8,128)S(1)} collective-permute-done((f32[512,512]{1,0:T(8,128)S(1)}, f32[512,512]{1,0:T(8,128)S(1)}, u32[]{:S(2)}, u32[]{:S(2)}) %collective-permute-start.3) | collective-permute-done | bytes 1048608 | tf_op jit(solution)/shard_map/ppermute | solution.py:112
  101.7 4.1 %gather_mirror.3 = (bf16[512,1024]{1,0:T(8,128)(2,1)S(1)}, bf16[512,1024]{1,0:T(8,128)(2,1)S(1)}, f32[512,512]{1,0:T(8,128)S(1)}, f32[512,512]{1,0:T(8,128)S(1)}) custom-call(s32[2,16]{1,0:T(2,128)S(1)} %copy-done.5, s32[2,16]{1,0:T(2,128)S(1)} %copy-done.6, f32[2048,4096]{1,0:T(8,128)} %front.3, f32[512,512]{1,0:T(8,128)S(1)} %slice.19.factor), custom_call_target="tpu_custom_call" | custom-call | flops 1610612736 | bytes 8388608 | tf_op jit(solution)/shard_map/gather_mirror/pallas_call | solution.py:331
  106.1 5.1 %gather_mirror.2 = (bf16[512,1024]{1,0:T(8,128)(2,1)S(1)}, bf16[512,1024]{1,0:T(8,128)(2,1)S(1)}, f32[512,512]{1,0:T(8,128)S(1)}, f32[512,512]{1,0:T(8,128)}) custom-call(s32[2,16]{1,0:T(2,128)S(1)} %copy-done.5, s32[2,16]{1,0:T(2,128)S(1)} %copy-done.6, f32[2048,4096]{1,0:T(8,128)} %front.3, f32[512,512]{1,0:T(8,128)S(1)} %get-tuple-element.22.factor), custom_call_target="tpu_custom_call" | custom-call | flops 1610612736 | bytes 8388608 | tf_op jit(solution)/shard_map/gather_mirror/pallas_call | solution.py:331
  112.2 5.1 %forward.3 = (f32[256,512]{1,0:T(8,128)S(1)}, f32[256,512]{1,0:T(8,128)S(1)}, f32[256,512]{1,0:T(8,128)S(1)}, f32[256,512]{1,0:T(8,128)}) custom-call(bf16[512,1024]{1,0:T(8,128)(2,1)S(1)} %get-tuple-element.30.high, bf16[512,1024]{1,0:T(8,128)(2,1)S(1)} %get-tuple-element.31.low, f32[512,512]{1,0:T(8,128)S(1)} %slice.19.factor, f32[512,512]{1,0:T(8,128)} %copy-done.11, ...), custom_call_target="tpu_custom_call" | custom-call | flops 1610612736 | bytes 8388608 | tf_op jit(solution)/shard_map/forward/pallas_call | solution.py:355
  117.6 5.1 %forward.2 = (f32[256,512]{1,0:T(8,128)S(1)}, f32[256,512]{1,0:T(8,128)S(1)}, f32[256,512]{1,0:T(8,128)S(1)}, f32[256,512]{1,0:T(8,128)}) custom-call(bf16[512,1024]{1,0:T(8,128)(2,1)S(1)} %get-tuple-element.20.high, bf16[512,1024]{1,0:T(8,128)(2,1)S(1)} %get-tuple-element.21.low, f32[512,512]{1,0:T(8,128)S(1)} %get-tuple-element.22.factor, ...), custom_call_target="tpu_custom_call" | custom-call | flops 1610612736 | bytes 8388608 | tf_op jit(solution)/shard_map/forward/pallas_call | solution.py:355
  124.5 1.3 collective-permute-start.8
  125.7 1.5 collective-permute-start.7
  130.6 3.5 %collective-permute-start.26 = (f32[256,512]{1,0:T(8,128)S(1)}, f32[256,512]{1,0:T(8,128)S(1)}, u32[]{:S(2)}, u32[]{:S(2)}) collective-permute-start(f32[256,512]{1,0:T(8,128)S(1)} %dynamic-slice_bitcast_fusion), channel_id=1, source_target_pairs={{0,8},{1,9},{2,10},{3,11},{4,20},{5,21},{6,22},{7,23},{8,0},{9,1},... | collective-permute-start | bytes 1572872 | tf_op jit(solution)/shard_map/ppermute | solution.py:169
  134.1 2.5 add.103
  136.6 15.1 %collective-permute-done.8 = f32[512,512]{1,0:T(8,128)} collective-permute-done((f32[512,512]{1,0:T(8,128)}, f32[512,512]{1,0:T(8,128)}, u32[]{:S(2)}, u32[]{:S(2)}) %collective-permute-start.8) | collective-permute-done | bytes 1048608 | tf_op jit(solution)/shard_map/ppermute | solution.py:122
  151.9 1.3 collective-permute-start.10
  153.2 1.3 collective-permute-start.9
  154.5 2.9 collective-permute-done.26
  158.6 24.8 %collective-permute-done.27 = f32[128,512]{1,0:T(8,128)S(1)} collective-permute-done((f32[128,512]{1,0:T(8,128)S(1)}, f32[128,512]{1,0:T(8,128)S(1)}, u32[]{:S(2)}, u32[]{:S(2)}) %collective-permute-start.27) | collective-permute-done | bytes 262176 | tf_op jit(solution)/shard_map/ppermute | solution.py:169
  183.5 1.3 collective-permute-start.28
  184.9 5.3 %collective-permute-done.28 = f32[128,512]{1,0:T(8,128)S(1)} collective-permute-done((f32[128,512]{1,0:T(8,128)S(1)}, f32[128,512]{1,0:T(8,128)S(1)}, u32[]{:S(2)}, u32[]{:S(2)}) %collective-permute-start.28) | collective-permute-done | bytes 262176 | tf_op jit(solution)/shard_map/ppermute | solution.py:135
  191.0 3.6 %add_add_fusion = (f32[512,512]{1,0:T(8,128)S(1)}, f32[512,512]{1,0:T(8,128)S(1)}) fusion(f32[512,512]{1,0:T(8,128)} %collective-permute-done.8, f32[512,512]{1,0:T(8,128)} %collective-permute-done.7, f32[512,512]{1,0:T(8,128)} %add.104, pred[]{:T(512)S(6)} %eq.36, f32[512,512]{1,0:T(8,128)} %collective-permute-done.10, ...), kind=kLoop, calls=%fused_computation.2 | loop fusion | flops 1572864 | bytes 8388609 | tf_op jit(solution)/shard_map/add | solution.py:125
  194.7 1.4 collective-permute-start.30
  197.3 9.7 %collective-permute-start.14 = (f32[256,512]{1,0:T(8,128)}, f32[256,512]{1,0:T(8,128)}, u32[]{:S(2)}, u32[]{:S(2)}) collective-permute-start(f32[256,512]{1,0:T(8,128)} %get-tuple-element.44), channel_id=1, source_target_pairs={{0,1},{3,2},{4,5},{7,6},{8,9},{11,10},{12,13},{15,14},{16,17},{19,... | collective-permute-start | bytes 1572872 | tf_op jit(solution)/shard_map/ppermute | solution.py:135
  207.0 2.1 collective-permute-start.11
  209.4 2.1 collective-permute-start.21
  211.5 1.3 collective-permute-start.18
  212.9 2.7 collective-permute-done.31
  216.5 2.4 collective-permute-done.14
  218.9 1.3 add.111
  220.9 9.3 %collective-permute-done.11 = f32[256,512]{1,0:T(8,128)} collective-permute-done((f32[256,512]{1,0:T(8,128)}, f32[256,512]{1,0:T(8,128)}, u32[]{:S(2)}, u32[]{:S(2)}) %collective-permute-start.11) | collective-permute-done | bytes 524320 | tf_op jit(solution)/shard_map/ppermute | solution.py:135
  230.1 1.3 add.108
  232.1 9.1 %collective-permute-done.21 = f32[256,512]{1,0:T(8,128)} collective-permute-done((f32[256,512]{1,0:T(8,128)S(1)}, f32[256,512]{1,0:T(8,128)}, u32[]{:S(2)}, u32[]{:S(2)}) %collective-permute-start.21) | collective-permute-done | bytes 524320 | tf_op jit(solution)/shard_map/ppermute | solution.py:135
  243.1 6.2 %collective-permute-done.18 = f32[256,512]{1,0:T(8,128)S(1)} collective-permute-done((f32[256,512]{1,0:T(8,128)S(1)}, f32[256,512]{1,0:T(8,128)S(1)}, u32[]{:S(2)}, u32[]{:S(2)}) %collective-permute-start.18) | collective-permute-done | bytes 524320 | tf_op jit(solution)/shard_map/ppermute | solution.py:135
  250.4 1.4 collective-permute-start.23
  251.9 1.3 collective-permute-start.20
  253.3 1.3 collective-permute-start.16
  254.7 1.3 collective-permute-start.13
  256.0 14.4 %collective-permute-done.23.rest_3_ = f32[256,512]{1,0:T(8,128)S(1)} collective-permute-done((f32[256,512]{1,0:T(8,128)S(1)}, f32[256,512]{1,0:T(8,128)S(1)}, u32[]{:S(2)}, u32[]{:S(2)}) %collective-permute-start.23) | collective-permute-done | bytes 524320 | tf_op jit(solution)/shard_map/ppermute | solution.py:139
  270.5 11.2 %collective-permute-done.20.rest_1_ = f32[256,512]{1,0:T(8,128)S(1)} collective-permute-done((f32[256,512]{1,0:T(8,128)S(1)}, f32[256,512]{1,0:T(8,128)S(1)}, u32[]{:S(2)}, u32[]{:S(2)}) %collective-permute-start.20) | collective-permute-done | bytes 524320 | tf_op jit(solution)/shard_map/ppermute | solution.py:139
  281.7 4.3 %place.2.rest_4_ = f32[2048,1024]{1,0:T(8,128)} custom-call(s32[2,16]{1,0:T(2,128)S(1)} %copy-done.5, f32[2,512,512]{2,1,0:T(8,128)S(1)} %copy-done, f32[256,512]{1,0:T(8,128)S(1)} %add.118.rest_0_, f32[256,512]{1,0:T(8,128)S(1)} %collective-permute-done.20.rest_1_, f32[256,512]{1,0:T(8,128)S(1)} %add.121.rest_2_, f32[256,512]{1,0:T(8,128)S(1)} %collective-permute-done.23.rest_3_), custom_call_target="tpu_custom_call" | custom-call | flops 805306368 | bytes 8388608 | tf_op jit(solution)/shard_map/place/pallas_call | solution.py:381
  286.1 6.9 %collective-permute-done.16.rest_3_ = f32[256,512]{1,0:T(8,128)S(1)} collective-permute-done((f32[256,512]{1,0:T(8,128)S(1)}, f32[256,512]{1,0:T(8,128)S(1)}, u32[]{:S(2)}, u32[]{:S(2)}) %collective-permute-start.16) | collective-permute-done | bytes 524320 | tf_op jit(solution)/shard_map/ppermute | solution.py:139
  292.9 9.4 %collective-permute-done.13.rest_1_ = f32[256,512]{1,0:T(8,128)S(1)} collective-permute-done((f32[256,512]{1,0:T(8,128)S(1)}, f32[256,512]{1,0:T(8,128)S(1)}, u32[]{:S(2)}, u32[]{:S(2)}) %collective-permute-start.13) | collective-permute-done | bytes 524320 | tf_op jit(solution)/shard_map/ppermute | solution.py:139
  302.4 2.7 place.3
  305.1 5.1 %diagonal.1 = f32[2,512,512]{2,1,0:T(8,128)} custom-call(f32[2,512]{1,0:T(2,128)S(1)} %copy-done.7, f32[2,512,512]{2,1,0:T(8,128)S(1)} %copy-done, f32[512,512]{1,0:T(8,128)S(1)} %pad_maximum_fusion.1.rest_0_, f32[512,512]{1,0:T(8,128)S(1)} %collective-permute-done.33.rest_1_), custom_call_target="tpu_custom_call" | custom-call | flops 3221225472 | bytes 8388608 | tf_op jit(solution)/shard_map/diagonal/pallas_call | solution.py:402
  (85 shorter events, 16.7 us)
Async XLA Ops:
  0.6 73.7 %copy-start.8 = (f32[512,1024]{1,0:T(8,128)S(1)}, f32[512,1024]{1,0:T(8,128)}, u32[]{:S(2)}) copy-start(f32[512,1024]{1,0:T(8,128)} %param.7) | copy-start | bytes 6291460
  2.1 27.3 %collective-permute-start.1 = (f32[512,512]{1,0:T(8,128)S(1)}, f32[512,512]{1,0:T(8,128)}, u32[]{:S(2)}, u32[]{:S(2)}) collective-permute-start(f32[512,512]{1,0:T(8,128)S(1)} %slice.19.factor), channel_id=1, source_target_pairs={{4,12},{0,16},{7,28},{13,29},{11,17},{22,30}} | collective-permute-start | bytes 3145736 | tf_op jit(solution)/shard_map/ppermute | solution.py:112
  7.9 66.3 %collective-permute-start = (f32[512,512]{1,0:T(8,128)S(1)}, f32[512,512]{1,0:T(8,128)}, u32[]{:S(2)}, u32[]{:S(2)}) collective-permute-start(f32[512,512]{1,0:T(8,128)S(1)} %slice.19.factor), channel_id=1, source_target_pairs={{0,8},{4,20},{3,24},{9,25},{15,21},{18,26}} | collective-permute-start | bytes 3145736 | tf_op jit(solution)/shard_map/ppermute | solution.py:112
  76.3 25.0 %copy-start.11 = (f32[512,512]{1,0:T(8,128)}, f32[512,512]{1,0:T(8,128)S(1)}, u32[]{:S(2)}) copy-start(f32[512,512]{1,0:T(8,128)S(1)} %get-tuple-element.38.rest_0_) | copy-start | bytes 3145732
  76.3 24.6 %collective-permute-start.3 = (f32[512,512]{1,0:T(8,128)S(1)}, f32[512,512]{1,0:T(8,128)S(1)}, u32[]{:S(2)}, u32[]{:S(2)}) collective-permute-start(f32[512,512]{1,0:T(8,128)S(1)} %get-tuple-element.22.factor), channel_id=1, source_target_pairs={{4,12},{0,16},{7,28},{13,29},{11,17},{22,30}} | collective-permute-start | bytes 3145736 | tf_op jit(solution)/shard_map/ppermute | solution.py:112
  77.7 23.2 %collective-permute-start.2 = (f32[512,512]{1,0:T(8,128)S(1)}, f32[512,512]{1,0:T(8,128)S(1)}, u32[]{:S(2)}, u32[]{:S(2)}) collective-permute-start(f32[512,512]{1,0:T(8,128)S(1)} %get-tuple-element.22.factor), channel_id=1, source_target_pairs={{0,8},{4,20},{3,24},{9,25},{15,21},{18,26}} | collective-permute-start | bytes 3145736 | tf_op jit(solution)/shard_map/ppermute | solution.py:112
  81.6 20.1 %copy-start.5 = (s32[2,16]{1,0:T(2,128)S(1)}, s32[2,16]{1,0:T(2,128)}, u32[]{:S(2)}) copy-start(s32[2,16]{1,0:T(2,128)} %tiles_ref.7) | copy-start | bytes 388
  81.6 20.1 %copy-start.6 = (s32[2,16]{1,0:T(2,128)S(1)}, s32[2,16]{1,0:T(2,128)}, u32[]{:S(2)}) copy-start(s32[2,16]{1,0:T(2,128)} %valid_ref.3) | copy-start | bytes 388
  81.6 29.6 %collective-permute-start.17 = (f32[512,512]{1,0:T(8,128)S(1)}, f32[512,512]{1,0:T(8,128)S(1)}, u32[]{:S(2)}, u32[]{:S(2)}) collective-permute-start(f32[512,512]{1,0:T(8,128)S(1)} %get-tuple-element.38.rest_0_), channel_id=1, source_target_pairs={{4,0},{0,4},{12,8},{8,12},{20,16},{16,20},{28,24},{24,28},{5,1},{1... | collective-permute-start | bytes 3145736 | tf_op jit(solution)/shard_map/ppermute | solution.py:108
  101.3 4.6 %copy-start.12 = (f32[512,512]{1,0:T(8,128)}, f32[512,512]{1,0:T(8,128)S(1)}, u32[]{:S(2)}) copy-start(f32[512,512]{1,0:T(8,128)S(1)} %add_select_fusion.1.rest_0_) | copy-start | bytes 3145732
  101.3 16.3 %collective-permute-start.4 = (f32[512,512]{1,0:T(8,128)S(1)}, f32[512,512]{1,0:T(8,128)}, u32[]{:S(2)}, u32[]{:S(2)}) collective-permute-start(f32[512,512]{1,0:T(8,128)S(1)} %add_select_fusion.1.rest_0_), channel_id=1, source_target_pairs={{4,0},{0,4},{12,8},{8,12},{20,16},{16,20},{28,24},{24,28},{5,1},{1... | collective-permute-start | bytes 3145736 | tf_op jit(solution)/shard_map/ppermute | solution.py:108
  105.9 17.4 %collective-permute-start.6 = (f32[512,512]{1,0:T(8,128)S(1)}, f32[512,512]{1,0:T(8,128)S(1)}, u32[]{:S(2)}, u32[]{:S(2)}) collective-permute-start(f32[512,512]{1,0:T(8,128)S(1)} %get-tuple-element.27), channel_id=1, source_target_pairs={{4,0},{0,4},{12,8},{8,12},{20,16},{16,20},{28,24},{24,28},{5,1},{1... | collective-permute-start | bytes 3145736 | tf_op jit(solution)/shard_map/ppermute | solution.py:108
  111.2 1.0 copy-start.13
  117.3 5.5 %copy-start.1 = (f32[256,512]{1,0:T(8,128)}, f32[256,512]{1,0:T(8,128)S(1)}, u32[]{:S(2)}) copy-start(f32[256,512]{1,0:T(8,128)S(1)} %get-tuple-element.33) | copy-start | bytes 1572868
  117.3 10.0 %collective-permute-start.24 = (f32[256,512]{1,0:T(8,128)}, f32[256,512]{1,0:T(8,128)}, u32[]{:S(2)}, u32[]{:S(2)}) collective-permute-start(f32[256,512]{1,0:T(8,128)} %get-tuple-element.35), channel_id=1, source_target_pairs={{4,0},{0,4},{12,8},{8,12},{20,16},{16,20},{28,24},{24,28},{5,1},{1... | collective-permute-start | bytes 1572872 | tf_op jit(solution)/shard_map/ppermute | solution.py:108
  122.8 1.7 copy-start.3
  122.8 5.6 %collective-permute-start.25 = (f32[256,512]{1,0:T(8,128)}, f32[256,512]{1,0:T(8,128)}, u32[]{:S(2)}, u32[]{:S(2)}) collective-permute-start(f32[256,512]{1,0:T(8,128)} %get-tuple-element.37), channel_id=1, source_target_pairs={{4,0},{0,4},{12,8},{8,12},{20,16},{16,20},{28,24},{24,28},{5,1},{1... | collective-permute-start | bytes 1572872 | tf_op jit(solution)/shard_map/ppermute | solution.py:108
  123.0 11.2 %collective-permute-start.5 = (f32[512,512]{1,0:T(8,128)}, f32[512,512]{1,0:T(8,128)}, u32[]{:S(2)}, u32[]{:S(2)}) collective-permute-start(f32[512,512]{1,0:T(8,128)} %get-tuple-element.25), channel_id=1, source_target_pairs={{4,0},{0,4},{12,8},{8,12},{20,16},{16,20},{28,24},{24,28},{5,1},{1... | collective-permute-start | bytes 3145736 | tf_op jit(solution)/shard_map/ppermute | solution.py:108
  124.5 27.3 %collective-permute-start.8 = (f32[512,512]{1,0:T(8,128)}, f32[512,512]{1,0:T(8,128)}, u32[]{:S(2)}, u32[]{:S(2)}) collective-permute-start(f32[512,512]{1,0:T(8,128)} %add.104), channel_id=1, source_target_pairs={{12,4},{16,0},{28,7},{29,13},{17,11},{30,22}} | collective-permute-start | bytes 3145736 | tf_op jit(solution)/shard_map/ppermute | solution.py:122
  125.7 26.2 %collective-permute-start.7 = (f32[512,512]{1,0:T(8,128)}, f32[512,512]{1,0:T(8,128)}, u32[]{:S(2)}, u32[]{:S(2)}) collective-permute-start(f32[512,512]{1,0:T(8,128)} %add.104), channel_id=1, source_target_pairs={{8,0},{20,4},{24,3},{25,9},{21,15},{26,18}} | collective-permute-start | bytes 3145736 | tf_op jit(solution)/shard_map/ppermute | solution.py:122
  129.6 1.0 copy-start.9
  130.6 26.8 %collective-permute-start.26 = (f32[256,512]{1,0:T(8,128)S(1)}, f32[256,512]{1,0:T(8,128)S(1)}, u32[]{:S(2)}, u32[]{:S(2)}) collective-permute-start(f32[256,512]{1,0:T(8,128)S(1)} %dynamic-slice_bitcast_fusion), channel_id=1, source_target_pairs={{0,8},{1,9},{2,10},{3,11},{4,20},{5,21},{6,22},{7,23},{8,0},{9,1},... | collective-permute-start | bytes 1572872 | tf_op jit(solution)/shard_map/ppermute | solution.py:169
  134.1 23.3 %copy-start.10 = (f32[512,512]{1,0:T(8,128)S(1)}, f32[512,512]{1,0:T(8,128)}, u32[]{:S(2)}) copy-start(f32[512,512]{1,0:T(8,128)} %copy-done.9) | copy-start | bytes 3145732
  151.9 39.1 %collective-permute-start.10 = (f32[512,512]{1,0:T(8,128)}, f32[512,512]{1,0:T(8,128)}, u32[]{:S(2)}, u32[]{:S(2)}) collective-permute-start(f32[512,512]{1,0:T(8,128)} %add.103), channel_id=1, source_target_pairs={{12,4},{16,0},{28,7},{29,13},{17,11},{30,22}} | collective-permute-start | bytes 3145736 | tf_op jit(solution)/shard_map/ppermute | solution.py:122
  153.2 37.8 %collective-permute-start.9 = (f32[512,512]{1,0:T(8,128)}, f32[512,512]{1,0:T(8,128)}, u32[]{:S(2)}, u32[]{:S(2)}) collective-permute-start(f32[512,512]{1,0:T(8,128)} %add.103), channel_id=1, source_target_pairs={{8,0},{20,4},{24,3},{25,9},{21,15},{26,18}} | collective-permute-start | bytes 3145736 | tf_op jit(solution)/shard_map/ppermute | solution.py:122
  157.6 25.9 %collective-permute-start.27 = (f32[128,512]{1,0:T(8,128)S(1)}, f32[128,512]{1,0:T(8,128)S(1)}, u32[]{:S(2)}, u32[]{:S(2)}) collective-permute-start(f32[128,512]{1,0:T(8,128)S(1)} %dynamic-slice_bitcast_fusion.1), channel_id=1, source_target_pairs={{0,16},{1,17},{2,18},{3,19},{4,12},{5,13},{6,14},{7,15},{8,24},{9,... | collective-permute-start | bytes 786440 | tf_op jit(solution)/shard_map/ppermute | solution.py:169
  183.5 6.6 %collective-permute-start.28 = (f32[128,512]{1,0:T(8,128)S(1)}, f32[128,512]{1,0:T(8,128)S(1)}, u32[]{:S(2)}, u32[]{:S(2)}) collective-permute-start(f32[128,512]{1,0:T(8,128)S(1)} %bitcast_add_fusion.1), channel_id=1, source_target_pairs={{0,1},{3,2},{4,5},{7,6},{8,9},{11,10},{12,13},{15,14},{16,17},{19,... | collective-permute-start | bytes 786440 | tf_op jit(solution)/shard_map/ppermute | solution.py:135
  190.2 5.9 %copy-start.4 = (f32[256,512]{1,0:T(8,128)S(1)}, f32[256,512]{1,0:T(8,128)}, u32[]{:S(2)}) copy-start(f32[256,512]{1,0:T(8,128)} %copy-done.3) | copy-start | bytes 1572868
  190.2 4.4 %collective-permute-start.29 = (f32[128,512]{1,0:T(8,128)S(1)}, f32[128,512]{1,0:T(8,128)S(1)}, u32[]{:S(2)}, u32[]{:S(2)}) collective-permute-start(f32[128,512]{1,0:T(8,128)S(1)} %add.129), channel_id=1, source_target_pairs={{1,2},{2,1},{5,6},{6,5},{9,10},{10,9},{13,14},{14,13},{17,18},{18,... | collective-permute-start | bytes 786440 | tf_op jit(solution)/shard_map/ppermute | solution.py:136
  194.7 14.6 %copy-start.2 = (f32[256,512]{1,0:T(8,128)S(1)}, f32[256,512]{1,0:T(8,128)}, u32[]{:S(2)}) copy-start(f32[256,512]{1,0:T(8,128)} %copy-done.1) | copy-start | bytes 1572868
  194.7 14.4 %collective-permute-start.30 = (f32[128,512]{1,0:T(8,128)S(1)}, f32[128,512]{1,0:T(8,128)S(1)}, u32[]{:S(2)}, u32[]{:S(2)}) collective-permute-start(f32[128,512]{1,0:T(8,128)S(1)} %add.130), channel_id=1, source_target_pairs={{1,0},{2,3},{5,4},{6,7},{9,8},{10,11},{13,12},{14,15},{17,16},{18,... | collective-permute-start | bytes 786440 | tf_op jit(solution)/shard_map/ppermute | solution.py:139
  197.3 21.6 %collective-permute-start.14 = (f32[256,512]{1,0:T(8,128)}, f32[256,512]{1,0:T(8,128)}, u32[]{:S(2)}, u32[]{:S(2)}) collective-permute-start(f32[256,512]{1,0:T(8,128)} %get-tuple-element.44), channel_id=1, source_target_pairs={{0,1},{3,2},{4,5},{7,6},{8,9},{11,10},{12,13},{15,14},{16,17},{19,... | collective-permute-start | bytes 1572872 | tf_op jit(solution)/shard_map/ppermute | solution.py:135
  207.0 23.1 %collective-permute-start.11 = (f32[256,512]{1,0:T(8,128)}, f32[256,512]{1,0:T(8,128)}, u32[]{:S(2)}, u32[]{:S(2)}) collective-permute-start(f32[256,512]{1,0:T(8,128)} %get-tuple-element.45), channel_id=1, source_target_pairs={{0,1},{3,2},{4,5},{7,6},{8,9},{11,10},{12,13},{15,14},{16,17},{19,... | collective-permute-start | bytes 1572872 | tf_op jit(solution)/shard_map/ppermute | solution.py:135
  209.1 6.4 %collective-permute-start.31 = (f32[128,512]{1,0:T(8,128)S(1)}, f32[128,512]{1,0:T(8,128)S(1)}, u32[]{:S(2)}, u32[]{:S(2)}) collective-permute-start(f32[128,512]{1,0:T(8,128)S(1)} %broadcast_select_fusion.2), channel_id=1, source_target_pairs={{0,16},{1,17},{2,18},{3,19},{4,12},{5,13},{6,14},{7,15},{8,24},{9,... | collective-permute-start | bytes 786440 | tf_op jit(solution)/shard_map/ppermute | solution.py:173
  209.4 31.8 %collective-permute-start.21 = (f32[256,512]{1,0:T(8,128)S(1)}, f32[256,512]{1,0:T(8,128)}, u32[]{:S(2)}, u32[]{:S(2)}) collective-permute-start(f32[256,512]{1,0:T(8,128)S(1)} %get-tuple-element.42), channel_id=1, source_target_pairs={{0,1},{3,2},{4,5},{7,6},{8,9},{11,10},{12,13},{15,14},{16,17},{19,... | collective-permute-start | bytes 1572872 | tf_op jit(solution)/shard_map/ppermute | solution.py:135
  211.5 37.7 %collective-permute-start.18 = (f32[256,512]{1,0:T(8,128)S(1)}, f32[256,512]{1,0:T(8,128)S(1)}, u32[]{:S(2)}, u32[]{:S(2)}) collective-permute-start(f32[256,512]{1,0:T(8,128)S(1)} %get-tuple-element.43), channel_id=1, source_target_pairs={{0,1},{3,2},{4,5},{7,6},{8,9},{11,10},{12,13},{15,14},{16,17},{19,... | collective-permute-start | bytes 1572872 | tf_op jit(solution)/shard_map/ppermute | solution.py:135
  216.5 33.6 %collective-permute-start.32 = (f32[256,512]{1,0:T(8,128)}, f32[256,512]{1,0:T(8,128)S(1)}, u32[]{:S(2)}, u32[]{:S(2)}) collective-permute-start(f32[256,512]{1,0:T(8,128)} %pad_maximum_fusion.2), channel_id=1, source_target_pairs={{0,8},{1,9},{2,10},{3,11},{4,20},{5,21},{6,22},{7,23},{8,0},{9,1},... | collective-permute-start | bytes 1572872 | tf_op jit(solution)/shard_map/ppermute | solution.py:173
  220.2 33.1 %collective-permute-start.15 = (f32[256,512]{1,0:T(8,128)S(1)}, f32[256,512]{1,0:T(8,128)S(1)}, u32[]{:S(2)}, u32[]{:S(2)}) collective-permute-start(f32[256,512]{1,0:T(8,128)S(1)} %add.111), channel_id=1, source_target_pairs={{1,2},{2,1},{5,6},{6,5},{9,10},{10,9},{13,14},{14,13},{17,18},{18,... | collective-permute-start | bytes 1572872 | tf_op jit(solution)/shard_map/ppermute | solution.py:136
  231.4 23.2 %collective-permute-start.12 = (f32[256,512]{1,0:T(8,128)S(1)}, f32[256,512]{1,0:T(8,128)S(1)}, u32[]{:S(2)}, u32[]{:S(2)}) collective-permute-start(f32[256,512]{1,0:T(8,128)S(1)} %add.108), channel_id=1, source_target_pairs={{1,2},{2,1},{5,6},{6,5},{9,10},{10,9},{13,14},{14,13},{17,18},{18,... | collective-permute-start | bytes 1572872 | tf_op jit(solution)/shard_map/ppermute | solution.py:136
  242.4 7.9 %collective-permute-start.22 = (f32[256,512]{1,0:T(8,128)S(1)}, f32[256,512]{1,0:T(8,128)S(1)}, u32[]{:S(2)}, u32[]{:S(2)}) collective-permute-start(f32[256,512]{1,0:T(8,128)S(1)} %add.120), channel_id=1, source_target_pairs={{1,2},{2,1},{5,6},{6,5},{9,10},{10,9},{13,14},{14,13},{17,18},{18,... | collective-permute-start | bytes 1572872 | tf_op jit(solution)/shard_map/ppermute | solution.py:136
  249.3 2.5 collective-permute-start.19
  250.2 54.8 %collective-permute-start.33 = (f32[512,512]{1,0:T(8,128)S(1)}, f32[512,512]{1,0:T(8,128)S(1)}, u32[]{:S(2)}, u32[]{:S(2)}) collective-permute-start(f32[512,512]{1,0:T(8,128)S(1)} %pad_maximum_fusion.1.rest_0_), channel_id=1, source_target_pairs={{4,0},{0,4},{12,8},{8,12},{20,16},{16,20},{28,24},{24,28},{5,1},{1... | collective-permute-start | bytes 3145736 | tf_op jit(solution)/shard_map/ppermute | solution.py:108
  250.4 31.3 %copy-start = (f32[2,512,512]{2,1,0:T(8,128)S(1)}, f32[2,512,512]{2,1,0:T(8,128)}, u32[]{:S(2)}) copy-start(f32[2,512,512]{2,1,0:T(8,128)} %unit_ref.5) | copy-start | bytes 6291460
  250.4 20.1 %collective-permute-start.23 = (f32[256,512]{1,0:T(8,128)S(1)}, f32[256,512]{1,0:T(8,128)S(1)}, u32[]{:S(2)}, u32[]{:S(2)}) collective-permute-start(f32[256,512]{1,0:T(8,128)S(1)} %add.121.rest_2_), channel_id=1, source_target_pairs={{1,0},{2,3},{5,4},{6,7},{9,8},{10,11},{13,12},{14,15},{17,16},{18,... | collective-permute-start | bytes 1572872 | tf_op jit(solution)/shard_map/ppermute | solution.py:139
  251.9 29.8 %collective-permute-start.20 = (f32[256,512]{1,0:T(8,128)S(1)}, f32[256,512]{1,0:T(8,128)S(1)}, u32[]{:S(2)}, u32[]{:S(2)}) collective-permute-start(f32[256,512]{1,0:T(8,128)S(1)} %add.118.rest_0_), channel_id=1, source_target_pairs={{1,0},{2,3},{5,4},{6,7},{9,8},{10,11},{13,12},{14,15},{17,16},{18,... | collective-permute-start | bytes 1572872 | tf_op jit(solution)/shard_map/ppermute | solution.py:139
  253.3 39.6 %collective-permute-start.16 = (f32[256,512]{1,0:T(8,128)S(1)}, f32[256,512]{1,0:T(8,128)S(1)}, u32[]{:S(2)}, u32[]{:S(2)}) collective-permute-start(f32[256,512]{1,0:T(8,128)S(1)} %add.112.rest_2_), channel_id=1, source_target_pairs={{1,0},{2,3},{5,4},{6,7},{9,8},{10,11},{13,12},{14,15},{17,16},{18,... | collective-permute-start | bytes 1572872 | tf_op jit(solution)/shard_map/ppermute | solution.py:139
  254.7 47.6 %collective-permute-start.13 = (f32[256,512]{1,0:T(8,128)S(1)}, f32[256,512]{1,0:T(8,128)S(1)}, u32[]{:S(2)}, u32[]{:S(2)}) collective-permute-start(f32[256,512]{1,0:T(8,128)S(1)} %add.109.rest_0_), channel_id=1, source_target_pairs={{1,0},{2,3},{5,4},{6,7},{9,8},{10,11},{13,12},{14,15},{17,16},{18,... | collective-permute-start | bytes 1572872 | tf_op jit(solution)/shard_map/ppermute | solution.py:139
  286.0 19.0 %copy-start.7 = (f32[2,512]{1,0:T(2,128)S(1)}, f32[2,512]{1,0:T(2,128)}, u32[]{:S(2)}) copy-start(f32[2,512]{1,0:T(2,128)} %pivot.1) | copy-start | bytes 12292

commit v3 on v2

--- a/solution.py
+++ b/solution.py
@@ -90,14 +90,17 @@
         return got
 
     def rounds(self):
-        pairs = [[], []]
-        for turn, col, chip, plane in (
-            (0, 0, 1, 0), (1, 0, 2, 0), (0, 0, 3, 3), (0, 1, 3, 1), (1, 1, 2, 3), (0, 2, 3, 2),
-        ):
-            for lane in range(self.lanes):
-                pairs[(turn + lane) % 2].append(
-                    (self.device(col, lane, plane), self.device(chip, lane, col))
-                )
+        ways = (
+            (0, ((0, 1), (0, 2)), ((0, 2), (0, 1)), ((1, 3), (2, 3))),
+            (1, ((1, 3), (1, 0)), (None, (1, 3)), ((3, 2), (0, 2))),
+            (2, ((2, 3), None), (None, (2, 3)), (None, None)),
+        )
+        pairs = [[], [], []]
+        for col, *turns in ways:
+            for turn, hops in enumerate(turns):
+                for lane, hop in enumerate(hops):
+                    if hop is not None:
+                        pairs[turn].append(tuple(self.device(chip, lane, col) for chip in hop))
         return pairs
 
     def swap(self, x, shift):
@@ -107,39 +110,20 @@
             pairs.append((chip * self.lanes + (lane + shift) % self.lanes, row))
         return lax.ppermute(x, "row", pairs)
 
-    def spread(self, x, on_diagonal):
-        if self.cols == 4:
-            first, second = (lax.ppermute(x, ("row", "col"), pairs) for pairs in self.rounds())
-            return jnp.where(on_diagonal, x, first + second), (first, second)
-        for step in range(self.steps):
-            got = lax.ppermute(x, ("row", "col"), self.tree(step))
-            x = jnp.where(self.received(step), got, x)
-        return x, (x,)
-
-    def collect(self, x, on_diagonal):
-        if self.cols == 4:
-            first, second = (
-                lax.ppermute(x, ("row", "col"), [(child, parent) for parent, child in pairs])
-                for pairs in self.rounds()
-            )
-            return jnp.where(on_diagonal, x, 0.0) + first + second, (first, second)
-        for step in reversed(range(self.steps)):
-            pairs = [(child, parent) for parent, child in self.tree(step)]
-            x = x + lax.ppermute(x, ("row", "col"), pairs)
-        return jnp.where(on_diagonal, x, 0.0), (x,)
-
-    def line_sum(self, x):
+    def line_hops(self):
         count, half = self.cols, self.cols // 2
-        place = lax.axis_index("col")
-        for i in range(half - 1):
-            x = x + lax.ppermute(x, "col", [(i, i + 1), (count - 1 - i, count - 2 - i)])
-        x = x + lax.ppermute(x, "col", [(half - 1, half), (half, half - 1)])
-        got = x
-        for i in range(half - 1):
-            got = lax.ppermute(x, "col", [(half - 1 - i, half - 2 - i), (half + i, half + i + 1)])
-            if i < half - 2:
-                x = jnp.where((place == half - 2 - i) | (place == half + i + 1), got, x)
-        return x, got
+        inward = [[(i, i + 1), (count - 1 - i, count - 2 - i)] for i in range(half - 1)]
+        outward = [
+            [(half - 1 - i, half - 2 - i), (half + i, half + i + 1)] for i in range(half - 1)
+        ]
+        return inward + [[(half - 1, half), (half, half - 1)]] + outward
+
+    def line_step(self, hop, x, got):
+        half = self.cols // 2
+        if hop < half:
+            return x + got
+        place, i = lax.axis_index("col"), hop - half
+        return jnp.where((place == half - 2 - i) | (place == half + i + 1), got, x)
 
     def at_end(self):
         place = lax.axis_index("col")
@@ -160,20 +144,19 @@
             value = jnp.where((row % self.lanes == lane) & ((chip & order[step]) != 0), 1, value)
         return value
 
-    def sum_all(self, x):
-        for step in range(self.steps):
-            x = x.reshape(2, x.shape[0] // 2, x.shape[1])
-            bit = self.bit(step)
-            send = lax.dynamic_index_in_dim(x, 1 - bit, 0, keepdims=False)
-            keep = lax.dynamic_index_in_dim(x, bit, 0, keepdims=False)
-            x = keep + lax.ppermute(send, ("row", "col"), self.bit_pairs(step))
-        x, got = self.line_sum(x)
-        x = jnp.where(self.at_end(), got, x)
-        for step in reversed(range(self.steps)):
-            got = lax.ppermute(x, ("row", "col"), self.bit_pairs(step))
-            bit = self.bit(step) == 1
-            x = jnp.concatenate([jnp.where(bit, got, x), jnp.where(bit, x, got)])
-        return x
+
+class Chain:
+    def __init__(self):
+        self.last = ()
+
+    def issue(self, *requests):
+        out = []
+        for x, axis, pairs in requests:
+            if self.last:
+                x, _ = lax.optimization_barrier((x, self.last))
+            out.append(lax.ppermute(x, axis, pairs))
+        self.last = tuple(out)
+        return out
 
 
 def gather_kernel(plan, member, tiles_ref, valid_ref, front, factor, high, low, *rest):
@@ -318,16 +301,60 @@
         out[member] = product(inverse, split(half), contract=0)
 
 
+def reverse(pairs):
+    return [(receiver, sender) for sender, receiver in pairs]
+
+
+def exchange(plan, factors, mirrors):
+    row, col = lax.axis_index("row"), lax.axis_index("col")
+    on_diagonal = row // plan.lanes == col
+    both = ("row", "col")
+    plane = Chain()
+    held, back = [], []
+    if plan.cols == 4 and plan.lanes == 2:
+        a, b, c = plan.rounds()
+        first, relayed = plane.issue((factors[0], both, a)) + [None]
+        for member in range(plan.members):
+            own, mirror = factors[member], mirrors(member)
+            second, third, near, far = plane.issue(
+                (own, both, b), (first, both, c),
+                (mirror, both, reverse(b)), (mirror, both, reverse(c)),
+            )
+            held.append(jnp.where(on_diagonal, own, first + second + third))
+            last = (mirror + far, both, reverse(a))
+            if member + 1 < plan.members:
+                first, relayed = plane.issue((factors[member + 1], both, a), last)
+            else:
+                relayed, = plane.issue(last)
+            back.append(jnp.where(on_diagonal, mirror, 0.0) + near + relayed)
+        return plane, held, back
+    for member in range(plan.members):
+        x, mirror = factors[member], mirrors(member)
+        for step in range(plan.steps):
+            got, = plane.issue((x, both, plan.tree(step)))
+            x = jnp.where(plan.received(step), got, x)
+        for step in reversed(range(plan.steps)):
+            got, = plane.issue((mirror, both, reverse(plan.tree(step))))
+            mirror = mirror + got
+        held.append(x)
+        back.append(jnp.where(on_diagonal, mirror, 0.0))
+    return plane, held, back
+
+
 def shards(inverse_front, factor, unit_lower, pivot_inverse, tile_list, tile_valid):
     plan = Plan(inverse_front, factor, unit_lower, tile_list)
     width, depth, lanes = plan.width, plan.depth, plan.lanes
-    row, col = lax.axis_index("row"), lax.axis_index("col")
-    on_diagonal = row // lanes == col
     flops = 6 * depth * depth * lanes * width
-    sums, crosses = [], []
-    sent = returned = None
-    for member in range(plan.members):
-        own = factor[:, member * width:(member + 1) * width]
+    factors = [factor[:, member * width:(member + 1) * width] for member in range(plan.members)]
+    halves = {}
+
+    def lane_sum(parts):
+        out = parts[0]
+        for shift in range(1, lanes):
+            out = out + plan.swap(parts[lanes - shift], shift)
+        return out
+
+    def mirrors(member):
         high, low, *mirror = pl.pallas_call(
             functools.partial(gather_kernel, plan, member),
             in_specs=smem(2) + [pl.BlockSpec(memory_space=pl.ANY)] + vmem(1),
@@ -341,22 +368,20 @@
             compiler_params=PARAMS,
             cost_estimate=pl.CostEstimate(flops=flops, bytes_accessed=8 << 20, transcendentals=0),
             name="gather_mirror",
-        )(tile_list, tile_valid, inverse_front, own)
-        back = mirror[0]
-        for shift in range(1, lanes):
-            back = back + plan.swap(mirror[lanes - shift], shift)
-        ready = own
-        if member:
-            ready, sent = lax.optimization_barrier((ready, sent))
-            back, returned = lax.optimization_barrier((back, returned))
-        back, returned = plan.collect(back, on_diagonal)
-        held, sent = plan.spread(ready, on_diagonal)
-        parts = [held] + [plan.swap(held, shift) for shift in range(1, lanes)]
-        *totals_cross, = pl.pallas_call(
+        )(tile_list, tile_valid, inverse_front, factors[member])
+        halves[member] = (high, low)
+        return lane_sum(mirror)
+
+    plane, held, back = exchange(plan, factors, mirrors)
+    share = depth // SPLIT
+    chunks, crosses = [], []
+    for member in range(plan.members):
+        parts = [held[member]] + [plan.swap(held[member], shift) for shift in range(1, lanes)]
+        *outs, = pl.pallas_call(
             functools.partial(forward_kernel, plan),
             in_specs=vmem(3 + lanes),
             out_specs=vmem(SPLIT + lanes),
-            out_shape=[jax.ShapeDtypeStruct((depth // SPLIT, width), F32)] * SPLIT
+            out_shape=[jax.ShapeDtypeStruct((share, width), F32)] * SPLIT
             + [jax.ShapeDtypeStruct((width // lanes, width), F32)] * lanes,
             scratch_shapes=[
                 pltpu.VMEM((depth, width), F32),
@@ -365,19 +390,36 @@
             compiler_params=PARAMS,
             cost_estimate=pl.CostEstimate(flops=flops, bytes_accessed=8 << 20, transcendentals=0),
             name="forward",
-        )(high, low, own, *parts)
-        totals, cross = totals_cross[:SPLIT], totals_cross[SPLIT:]
-        share = depth // SPLIT
-        member_sums = []
+        )(*halves[member], factors[member], *parts)
         for i in range(SPLIT):
-            member_sums += plan.line_sum(totals[i] + back[i * share:(i + 1) * share])
-        sums.append(member_sums)
-        reduced = cross[0]
-        for shift in range(1, lanes):
-            reduced = reduced + plan.swap(cross[lanes - shift], shift)
-        crosses.append(reduced)
+            chunks.append(outs[i] + back[member][i * share:(i + 1) * share])
+        crosses.append(lane_sum(outs[SPLIT:]))
+
+    x = jnp.concatenate(crosses)
+    for step in range(plan.steps):
+        x = x.reshape(2, x.shape[0] // 2, x.shape[1])
+        bit = plan.bit(step)
+        send = lax.dynamic_index_in_dim(x, 1 - bit, 0, keepdims=False)
+        keep = lax.dynamic_index_in_dim(x, bit, 0, keepdims=False)
+        got, = plane.issue((send, ("row", "col"), plan.bit_pairs(step)))
+        x = keep + got
+    chunks.append(x)
+
+    line, hops = Chain(), plan.line_hops()
+    ends = [None] * len(chunks)
+    for phase in range(len(chunks) + len(hops) - 1):
+        live = [i for i in range(len(chunks)) if 0 <= phase - i < len(hops)]
+        brought = line.issue(*((chunks[i], "col", hops[phase - i]) for i in live))
+        for i, got in zip(live, brought):
+            if phase - i < len(hops) - 1 or len(hops) == 1:
+                chunks[i] = plan.line_step(phase - i, chunks[i], got)
+            ends[i] = got if len(hops) > 1 else chunks[i]
+
     column = None
     for member in range(plan.members):
+        sums = []
+        for i in range(member * SPLIT, (member + 1) * SPLIT):
+            sums += [chunks[i], ends[i]]
         column = pl.pallas_call(
             functools.partial(place_kernel, plan, member),
             in_specs=smem(1) + vmem(1 + 2 * SPLIT)
@@ -396,9 +438,14 @@
                 flops=6 * depth * width * width, bytes_accessed=8 << 20, transcendentals=0
             ),
             name="place",
-        )(tile_list, unit_lower, *sums[member], *([column] if member else []))
-    cross = plan.sum_all(jnp.concatenate(crosses))
-    parts = [cross] + [plan.swap(cross, shift) for shift in range(1, lanes)]
+        )(tile_list, unit_lower, *sums, *([column] if member else []))
+
+    x = jnp.where(plan.at_end(), ends[-1], chunks[-1])
+    for step in reversed(range(plan.steps)):
+        got, = plane.issue((x, ("row", "col"), plan.bit_pairs(step)))
+        bit = plan.bit(step) == 1
+        x = jnp.concatenate([jnp.where(bit, got, x), jnp.where(bit, x, got)])
+    parts = [x] + [plan.swap(x, shift) for shift in range(1, lanes)]
     diagonal = pl.pallas_call(
         functools.partial(diagonal_kernel, plan),
         in_specs=vmem(2 + lanes),

time: 311 us -> 246 us (0.79)
  waiting for transfers between devices: 203 us -> 102 us
  starting transfers between devices: 51.9 us -> 79.3 us
  other arithmetic: 18.7 us -> 28.8 us
    ppermute x27 -> x31, waiting for transfers between devices: 203 us -> 102 us  [issue(): out.append(lax.ppermute(x, axis, pairs))]
    ppermute x27 -> x31, starting transfers between devices: 50.2 us -> 78.4 us  [issue(): out.append(lax.ppermute(x, axis, pairs))]
    select_n x5, other arithmetic: 2.55 us -> 9.57 us  [the longest x2 5.53 us: exchange(): held.append(jnp.where(on_diagonal, own, first + second + third))]
    add x19 -> x21, other arithmetic: 15.1 us -> 18.2 us  [the longest x10 6.06 us: line_step(): return x + got]
  transfers between devices with their start and end apart: 34 -> 38, of which waited for: 17 -> 19; matrix products, arithmetic and copies ran while one was open for 5% -> 10% of each run, Pallas kernels for 9% -> 10%
where the time goes in v3:
time: 246 us; the launch traced here: 245 us
  waiting for transfers between devices  102 us (41%)
  starting transfers between devices  79.3 us (32%)
  Pallas kernels  29.2 us (12%)
  other arithmetic  28.8 us (12%)
  local copies, waits for them, and re-layouts  4.93 us (2%)
    ppermute x31, waiting for transfers between devices, issue(): out.append(lax.ppermute(x, axis, pairs))  102 us
    ppermute x31, starting transfers between devices, issue(): out.append(lax.ppermute(x, axis, pairs))  78.4 us
    pallas_call x2, Pallas kernels, shards(): pl.pallas_call(functools.partial(forward_kernel, plan), in_specs=vmem(3 +...  8.74 us
    pallas_call x2, Pallas kernels, mirrors(): pl.pallas_call(functools.partial(gather_kernel, plan, member), in_specs=s...  8.3 us
    pallas_call x2, Pallas kernels, shards(): pl.pallas_call(functools.partial(place_kernel, plan, member), in_specs=sm...  7.02 us
    add x10, other arithmetic, line_step(): return x + got  6.06 us
    select_n x2, other arithmetic, exchange(): held.append(jnp.where(on_diagonal, own, first + second + third))  5.53 us
    pallas_call x1, Pallas kernels, shards(): pl.pallas_call(functools.partial(diagonal_kernel, plan), in_specs=vmem(2...  5.12 us
  transfers between devices with their start and end apart: 38, of which 19 were waited for; matrix products, arithmetic and copies ran while one was open for 10% of the time, Pallas kernels for 10%

profile of v3, /device:TPU:0, one launch (start us, length us, event | category | flops | bytes accessed | tf_op | source)
XLA Modules:
  0.0 245.2 jit_solution(16200479471665769908)
XLA Ops:
  2.0 5.8 %collective-permute-start = (f32[512,512]{1,0:T(8,128)S(1)}, f32[512,512]{1,0:T(8,128)}, u32[]{:S(2)}, u32[]{:S(2)}) collective-permute-start(f32[512,512]{1,0:T(8,128)S(1)} %slice.19.factor), channel_id=1, source_target_pairs={{0,8},{4,20},{9,25},{13,5},{18,26}} | collective-permute-start | bytes 3145736 | tf_op jit(solution)/shard_map/ppermute | solution.py:157
  7.8 4.1 %gather_mirror.3 = (bf16[512,1024]{1,0:T(8,128)(2,1)S(1)}, bf16[512,1024]{1,0:T(8,128)(2,1)S(1)}, f32[512,512]{1,0:T(8,128)S(1)}, f32[512,512]{1,0:T(8,128)S(1)}) custom-call(s32[2,16]{1,0:T(2,128)S(1)} %copy-done.5, s32[2,16]{1,0:T(2,128)S(1)} %copy-done.6, f32[2048,4096]{1,0:T(8,128)} %front.3, f32[512,512]{1,0:T(8,128)S(1)} %slice.19.factor), custom_call_target="tpu_custom_call" | custom-call | flops 1610612736 | bytes 8388608 | tf_op jit(solution)/shard_map/gather_mirror/pallas_call | solution.py:358
  12.0 7.1 %collective-permute-done = f32[512,512]{1,0:T(8,128)} collective-permute-done((f32[512,512]{1,0:T(8,128)S(1)}, f32[512,512]{1,0:T(8,128)}, u32[]{:S(2)}, u32[]{:S(2)}) %collective-permute-start) | collective-permute-done | bytes 1048608 | tf_op jit(solution)/shard_map/ppermute | solution.py:157
  19.1 1.6 collective-permute-start.2
  20.7 2.3 collective-permute-start.1
  25.6 1.7 collective-permute-start.5
  27.2 7.1 %collective-permute-done.1 = f32[512,512]{1,0:T(8,128)} collective-permute-done((f32[512,512]{1,0:T(8,128)S(1)}, f32[512,512]{1,0:T(8,128)}, u32[]{:S(2)}, u32[]{:S(2)}) %collective-permute-start.1) | collective-permute-done | bytes 1048608 | tf_op jit(solution)/shard_map/ppermute | solution.py:157
  34.3 4.1 %add_select_fusion = (f32[512,512]{1,0:T(8,128)}, f32[512,512]{1,0:T(8,128)S(1)}) fusion(f32[512,512]{1,0:T(8,128)} %collective-permute-done.2, f32[512,512]{1,0:T(8,128)} %collective-permute-done, f32[512,512]{1,0:T(8,128)} %collective-permute-done.1, pred[]{:T(512)S(6)} %eq.36, f32[512,1024]{1,0:T(8,128)} %param.7), kind=kLoop, calls=%fused_computation.3 | loop fusion | flops 786432 | bytes 7340033 | tf_op jit(solution)/shard_map/jit(_where)/select_n | solution.py:323
  38.4 2.8 %collective-permute-done.4 = f32[512,512]{1,0:T(8,128)S(1)} collective-permute-done((f32[512,512]{1,0:T(8,128)}, f32[512,512]{1,0:T(8,128)S(1)}, u32[]{:S(2)}, u32[]{:S(2)}) %collective-permute-start.4) | collective-permute-done | bytes 1048608 | tf_op jit(solution)/shard_map/ppermute | solution.py:157
  41.2 5.4 %collective-permute-start.6 = (f32[512,512]{1,0:T(8,128)S(1)}, f32[512,512]{1,0:T(8,128)S(1)}, u32[]{:S(2)}, u32[]{:S(2)}) collective-permute-start(f32[512,512]{1,0:T(8,128)S(1)} %get-tuple-element.54.factor), channel_id=1, source_target_pairs={{0,8},{4,20},{9,25},{13,5},{18,26}} | collective-permute-start | bytes 3145736 | tf_op jit(solution)/shard_map/ppermute | solution.py:157
  46.6 1.7 add.115
  49.6 4.1 %gather_mirror.2 = (bf16[512,1024]{1,0:T(8,128)(2,1)S(1)}, bf16[512,1024]{1,0:T(8,128)(2,1)S(1)}, f32[512,512]{1,0:T(8,128)S(1)}, f32[512,512]{1,0:T(8,128)S(1)}) custom-call(s32[2,16]{1,0:T(2,128)S(1)} %copy-done.5, s32[2,16]{1,0:T(2,128)S(1)} %copy-done.6, f32[2048,4096]{1,0:T(8,128)} %front.3, f32[512,512]{1,0:T(8,128)S(1)} %get-tuple-element.54.factor), custom_call_target="tpu_custom_call" | custom-call | flops 1610612736 | bytes 8388608 | tf_op jit(solution)/shard_map/gather_mirror/pallas_call | solution.py:358
  53.9 4.9 %collective-permute-done.6 = f32[512,512]{1,0:T(8,128)S(1)} collective-permute-done((f32[512,512]{1,0:T(8,128)S(1)}, f32[512,512]{1,0:T(8,128)S(1)}, u32[]{:S(2)}, u32[]{:S(2)}) %collective-permute-start.6) | collective-permute-done | bytes 1048608 | tf_op jit(solution)/shard_map/ppermute | solution.py:157
  58.8 6.2 %collective-permute-done.7 = f32[512,512]{1,0:T(8,128)S(1)} collective-permute-done((f32[512,512]{1,0:T(8,128)S(1)}, f32[512,512]{1,0:T(8,128)S(1)}, u32[]{:S(2)}, u32[]{:S(2)}) %collective-permute-start.7) | collective-permute-done | bytes 1048608 | tf_op jit(solution)/shard_map/ppermute | solution.py:157
  66.8 1.4 collective-permute-start.8
  69.8 10.6 %collective-permute-done.8 = f32[512,512]{1,0:T(8,128)S(1)} collective-permute-done((f32[512,512]{1,0:T(8,128)S(1)}, f32[512,512]{1,0:T(8,128)S(1)}, u32[]{:S(2)}, u32[]{:S(2)}) %collective-permute-start.8) | collective-permute-done | bytes 1048608 | tf_op jit(solution)/shard_map/ppermute | solution.py:157
  80.4 4.5 %collective-permute-done.12 = f32[512,512]{1,0:T(8,128)S(1)} collective-permute-done((f32[512,512]{1,0:T(8,128)S(1)}, f32[512,512]{1,0:T(8,128)S(1)}, u32[]{:S(2)}, u32[]{:S(2)}) %collective-permute-start.12) | collective-permute-done | bytes 1048608 | tf_op jit(solution)/shard_map/ppermute | solution.py:157
  84.9 1.5 collective-permute-start.14
  86.4 1.5 add_select_fusion.1.rest_0_
  88.9 4.4 %forward.3 = (f32[256,512]{1,0:T(8,128)S(1)}, f32[256,512]{1,0:T(8,128)S(1)}, f32[256,512]{1,0:T(8,128)S(1)}, f32[256,512]{1,0:T(8,128)S(1)}) custom-call(bf16[512,1024]{1,0:T(8,128)(2,1)S(1)} %get-tuple-element.61.high, bf16[512,1024]{1,0:T(8,128)(2,1)S(1)} %copy-done.8, f32[512,512]{1,0:T(8,128)S(1)} %slice.19.factor, ...), custom_call_target="tpu_custom_call" | custom-call | flops 1610612736 | bytes 8388608 | tf_op jit(solution)/shard_map/forward/pallas_call | solution.py:380
  93.3 8.3 %collective-permute-done.14 = f32[512,512]{1,0:T(8,128)S(1)} collective-permute-done((f32[512,512]{1,0:T(8,128)S(1)}, f32[512,512]{1,0:T(8,128)S(1)}, u32[]{:S(2)}, u32[]{:S(2)}) %collective-permute-start.14) | collective-permute-done | bytes 1048608 | tf_op jit(solution)/shard_map/ppermute | solution.py:157
  101.6 3.0 %add_add_fusion = (f32[512,512]{1,0:T(8,128)S(1)}, f32[512,512]{1,0:T(8,128)}) fusion(f32[512,512]{1,0:T(8,128)S(1)} %collective-permute-done.7, f32[512,512]{1,0:T(8,128)S(1)} %copy-done.15, f32[512,512]{1,0:T(8,128)} %add.114, pred[]{:T(512)S(6)} %eq.36, f32[512,512]{1,0:T(8,128)S(1)} %collective-permute-done.14, ...), kind=kLoop, calls=%fused_computation.2 | loop fusion | flops 1572864 | bytes 8388609 | tf_op jit(solution)/shard_map/add | solution.py:329
  107.0 4.3 %forward.2 = (f32[256,512]{1,0:T(8,128)S(1)}, f32[256,512]{1,0:T(8,128)S(1)}, f32[256,512]{1,0:T(8,128)S(1)}, f32[256,512]{1,0:T(8,128)S(1)}) custom-call(bf16[512,1024]{1,0:T(8,128)(2,1)S(1)} %get-tuple-element.45.high, bf16[512,1024]{1,0:T(8,128)(2,1)S(1)} %get-tuple-element.46.low, f32[512,512]{1,0:T(8,128)S(1)} %get-tuple-element.54.factor, ...), custom_call_target="tpu_custom_call" | custom-call | flops 1610612736 | bytes 8388608 | tf_op jit(solution)/shard_map/forward/pallas_call | solution.py:380
  111.9 1.7 collective-permute-done.16
  114.4 1.4 collective-permute-start.17
  115.9 5.7 %collective-permute-start.18 = (f32[256,512]{1,0:T(8,128)}, f32[256,512]{1,0:T(8,128)}, u32[]{:S(2)}, u32[]{:S(2)}) collective-permute-start(f32[256,512]{1,0:T(8,128)} %get-tuple-element.66), channel_id=1, source_target_pairs={{0,1},{3,2},{4,5},{7,6},{8,9},{11,10},{12,13},{15,14},{16,17},{19,... | collective-permute-start | bytes 1572872 | tf_op jit(solution)/shard_map/ppermute | solution.py:157
  125.3 3.3 %collective-permute-done.18 = f32[256,512]{1,0:T(8,128)} collective-permute-done((f32[256,512]{1,0:T(8,128)}, f32[256,512]{1,0:T(8,128)}, u32[]{:S(2)}, u32[]{:S(2)}) %collective-permute-start.18) | collective-permute-done | bytes 524320 | tf_op jit(solution)/shard_map/ppermute | solution.py:157
  128.7 4.4 %collective-permute-start.19 = (f32[256,512]{1,0:T(8,128)}, f32[256,512]{1,0:T(8,128)S(1)}, u32[]{:S(2)}, u32[]{:S(2)}) collective-permute-start(f32[256,512]{1,0:T(8,128)} %get-tuple-element.67), channel_id=1, source_target_pairs={{0,1},{3,2},{4,5},{7,6},{8,9},{11,10},{12,13},{15,14},{16,17},{19,... | collective-permute-start | bytes 1572872 | tf_op jit(solution)/shard_map/ppermute | solution.py:157
  137.0 1.5 collective-permute-start.21
  139.3 2.1 collective-permute-start.29
  142.6 2.9 %collective-permute-done.20.rest_1_ = f32[256,512]{1,0:T(8,128)S(1)} collective-permute-done((f32[256,512]{1,0:T(8,128)S(1)}, f32[256,512]{1,0:T(8,128)S(1)}, u32[]{:S(2)}, u32[]{:S(2)}) %collective-permute-start.20) | collective-permute-done | bytes 524320 | tf_op jit(solution)/shard_map/ppermute | solution.py:157
  148.6 16.6 %collective-permute-start.24 = (f32[256,512]{1,0:T(8,128)}, f32[256,512]{1,0:T(8,128)S(1)}, u32[]{:S(2)}, u32[]{:S(2)}) collective-permute-start(f32[256,512]{1,0:T(8,128)} %get-tuple-element.73), channel_id=1, source_target_pairs={{0,1},{3,2},{4,5},{7,6},{8,9},{11,10},{12,13},{15,14},{16,17},{19,... | collective-permute-start | bytes 1572872 | tf_op jit(solution)/shard_map/ppermute | solution.py:157
  166.5 6.3 %collective-permute-done.24 = f32[256,512]{1,0:T(8,128)S(1)} collective-permute-done((f32[256,512]{1,0:T(8,128)}, f32[256,512]{1,0:T(8,128)S(1)}, u32[]{:S(2)}, u32[]{:S(2)}) %collective-permute-start.24) | collective-permute-done | bytes 524320 | tf_op jit(solution)/shard_map/ppermute | solution.py:157
  172.9 1.3 collective-permute-done.23.rest_3_
  176.3 4.9 %collective-permute-start.31 = (f32[128,512]{1,0:T(8,128)S(1)}, f32[128,512]{1,0:T(8,128)S(1)}, u32[]{:S(2)}, u32[]{:S(2)}) collective-permute-start(f32[128,512]{1,0:T(8,128)S(1)} %bitcast_add_fusion.1), channel_id=1, source_target_pairs={{0,1},{3,2},{4,5},{7,6},{8,9},{11,10},{12,13},{15,14},{16,17},{19,... | collective-permute-start | bytes 786440 | tf_op jit(solution)/shard_map/ppermute | solution.py:157
  181.3 3.8 %collective-permute-done.31 = f32[128,512]{1,0:T(8,128)S(1)} collective-permute-done((f32[128,512]{1,0:T(8,128)S(1)}, f32[128,512]{1,0:T(8,128)S(1)}, u32[]{:S(2)}, u32[]{:S(2)}) %collective-permute-start.31) | collective-permute-done | bytes 262176 | tf_op jit(solution)/shard_map/ppermute | solution.py:157
  185.1 3.1 %collective-permute-done.25.rest_1_ = f32[256,512]{1,0:T(8,128)S(1)} collective-permute-done((f32[256,512]{1,0:T(8,128)S(1)}, f32[256,512]{1,0:T(8,128)S(1)}, u32[]{:S(2)}, u32[]{:S(2)}) %collective-permute-start.25) | collective-permute-done | bytes 524320 | tf_op jit(solution)/shard_map/ppermute | solution.py:157
  190.2 9.0 %collective-permute-done.32.rest_3_ = f32[256,512]{1,0:T(8,128)S(1)} collective-permute-done((f32[256,512]{1,0:T(8,128)S(1)}, f32[256,512]{1,0:T(8,128)S(1)}, u32[]{:S(2)}, u32[]{:S(2)}) %collective-permute-start.32) | collective-permute-done | bytes 524320 | tf_op jit(solution)/shard_map/ppermute | solution.py:157
  200.0 1.5 collective-permute-start.34
  201.6 6.8 %collective-permute-done.34 = f32[128,512]{1,0:T(8,128)} collective-permute-done((f32[128,512]{1,0:T(8,128)S(1)}, f32[128,512]{1,0:T(8,128)}, u32[]{:S(2)}, u32[]{:S(2)}) %collective-permute-start.34) | collective-permute-done | bytes 262176 | tf_op jit(solution)/shard_map/ppermute | solution.py:157
  208.4 1.7 broadcast_select_fusion.2
  210.1 2.9 %collective-permute-start.35 = (f32[128,512]{1,0:T(8,128)}, f32[128,512]{1,0:T(8,128)}, u32[]{:S(2)}, u32[]{:S(2)}) collective-permute-start(f32[128,512]{1,0:T(8,128)} %broadcast_select_fusion.2), channel_id=1, source_target_pairs={{0,16},{1,17},{2,18},{3,19},{4,12},{5,13},{6,14},{7,15},{8,24},{9,... | collective-permute-start | bytes 786440 | tf_op jit(solution)/shard_map/ppermute | solution.py:157
  213.0 4.7 %collective-permute-done.35 = f32[128,512]{1,0:T(8,128)} collective-permute-done((f32[128,512]{1,0:T(8,128)}, f32[128,512]{1,0:T(8,128)}, u32[]{:S(2)}, u32[]{:S(2)}) %collective-permute-start.35) | collective-permute-done | bytes 262176 | tf_op jit(solution)/shard_map/ppermute | solution.py:157
  220.3 3.7 %collective-permute-start.36 = (f32[256,512]{1,0:T(8,128)}, f32[256,512]{1,0:T(8,128)}, u32[]{:S(2)}, u32[]{:S(2)}) collective-permute-start(f32[256,512]{1,0:T(8,128)} %pad_maximum_fusion.2), channel_id=1, source_target_pairs={{0,8},{1,9},{2,10},{3,11},{4,20},{5,21},{6,22},{7,23},{8,0},{9,1},... | collective-permute-start | bytes 1572872 | tf_op jit(solution)/shard_map/ppermute | solution.py:157
  224.0 7.5 %collective-permute-done.36 = f32[256,512]{1,0:T(8,128)} collective-permute-done((f32[256,512]{1,0:T(8,128)}, f32[256,512]{1,0:T(8,128)}, u32[]{:S(2)}, u32[]{:S(2)}) %collective-permute-start.36) | collective-permute-done | bytes 524320 | tf_op jit(solution)/shard_map/ppermute | solution.py:157
  233.0 4.3 %place.2.rest_4_ = f32[2048,1024]{1,0:T(8,128)} custom-call(s32[2,16]{1,0:T(2,128)S(1)} %copy-done.5, f32[2,512,512]{2,1,0:T(8,128)S(1)} %copy-done, f32[256,512]{1,0:T(8,128)S(1)} %add.131.rest_0_, f32[256,512]{1,0:T(8,128)S(1)} %collective-permute-done.20.rest_1_, f32[256,512]{1,0:T(8,128)S(1)} %add.134.rest_2_, f32[256,512]{1,0:T(8,128)S(1)} %collective-permute-done.23.rest_3_), custom_call_target="tpu_custom_call" | custom-call | flops 805306368 | bytes 8388608 | tf_op jit(solution)/shard_map/place/pallas_call | solution.py:423
  237.4 2.7 %place.3 = f32[2048,1024]{1,0:T(8,128)} custom-call(s32[2,16]{1,0:T(2,128)S(1)} %copy-done.5, f32[2,512,512]{2,1,0:T(8,128)S(1)} %copy-done, f32[256,512]{1,0:T(8,128)S(1)} %add.133.rest_0_, f32[256,512]{1,0:T(8,128)S(1)} %copy-done.2, f32[256,512]{1,0:T(8,128)S(1)} %add.137.rest_2_, f32[256,512]{1,0:T(8,128)S(1)} %copy-done.4, ...), custom_call_target="tpu_custom_call", output_to_operand_aliasing={{}: (6, {})} | custom-call | flops 805306368 | bytes 8388608 | tf_op jit(solution)/shard_map/place/pallas_call | solution.py:423
  240.1 5.1 %diagonal.1 = f32[2,512,512]{2,1,0:T(8,128)} custom-call(f32[2,512]{1,0:T(2,128)S(1)} %copy-done.9, f32[2,512,512]{2,1,0:T(8,128)S(1)} %copy-done, f32[512,512]{1,0:T(8,128)S(1)} %pad_maximum_fusion.1.rest_0_, f32[512,512]{1,0:T(8,128)S(1)} %collective-permute-done.37.rest_1_), custom_call_target="tpu_custom_call" | custom-call | flops 3221225472 | bytes 8388608 | tf_op jit(solution)/shard_map/diagonal/pallas_call | solution.py:449
  (101 shorter events, 36.7 us)
Async XLA Ops:
  0.6 7.2 %copy-start.5 = (s32[2,16]{1,0:T(2,128)S(1)}, s32[2,16]{1,0:T(2,128)}, u32[]{:S(2)}) copy-start(s32[2,16]{1,0:T(2,128)} %tiles_ref.7) | copy-start | bytes 388
  0.6 7.2 %copy-start.6 = (s32[2,16]{1,0:T(2,128)S(1)}, s32[2,16]{1,0:T(2,128)}, u32[]{:S(2)}) copy-start(s32[2,16]{1,0:T(2,128)} %valid_ref.3) | copy-start | bytes 388
  2.0 17.2 %collective-permute-start = (f32[512,512]{1,0:T(8,128)S(1)}, f32[512,512]{1,0:T(8,128)}, u32[]{:S(2)}, u32[]{:S(2)}) collective-permute-start(f32[512,512]{1,0:T(8,128)S(1)} %slice.19.factor), channel_id=1, source_target_pairs={{0,8},{4,20},{9,25},{13,5},{18,26}} | collective-permute-start | bytes 3145736 | tf_op jit(solution)/shard_map/ppermute | solution.py:157
  12.0 12.3 %copy-start.7 = (bf16[512,1024]{1,0:T(8,128)(2,1)}, bf16[512,1024]{1,0:T(8,128)(2,1)S(1)}, u32[]{:S(2)}) copy-start(bf16[512,1024]{1,0:T(8,128)(2,1)S(1)} %get-tuple-element.62.low) | copy-start | bytes 3145732
  12.0 11.1 %collective-permute-start.3 = (f32[512,512]{1,0:T(8,128)S(1)}, f32[512,512]{1,0:T(8,128)S(1)}, u32[]{:S(2)}, u32[]{:S(2)}) collective-permute-start(f32[512,512]{1,0:T(8,128)S(1)} %get-tuple-element.50), channel_id=1, source_target_pairs={{4,0},{0,4},{12,8},{8,12},{20,16},{16,20},{28,24},{24,28},{5,1},{1... | collective-permute-start | bytes 3145736 | tf_op jit(solution)/shard_map/ppermute | solution.py:111
  19.1 8.1 %collective-permute-start.2 = (f32[512,512]{1,0:T(8,128)}, f32[512,512]{1,0:T(8,128)}, u32[]{:S(2)}, u32[]{:S(2)}) collective-permute-start(f32[512,512]{1,0:T(8,128)} %collective-permute-done), channel_id=1, source_target_pairs={{8,24},{20,28},{25,17},{5,21}} | collective-permute-start | bytes 3145736 | tf_op jit(solution)/shard_map/ppermute | solution.py:157
  20.7 13.6 %collective-permute-start.1 = (f32[512,512]{1,0:T(8,128)S(1)}, f32[512,512]{1,0:T(8,128)}, u32[]{:S(2)}, u32[]{:S(2)}) collective-permute-start(f32[512,512]{1,0:T(8,128)S(1)} %slice.19.factor), channel_id=1, source_target_pairs={{0,16},{4,12},{13,29},{22,30}} | collective-permute-start | bytes 3145736 | tf_op jit(solution)/shard_map/ppermute | solution.py:157
  24.3 16.9 %collective-permute-start.4 = (f32[512,512]{1,0:T(8,128)}, f32[512,512]{1,0:T(8,128)S(1)}, u32[]{:S(2)}, u32[]{:S(2)}) collective-permute-start(f32[512,512]{1,0:T(8,128)} %add.114), channel_id=1, source_target_pairs={{16,0},{12,4},{29,13},{30,22}} | collective-permute-start | bytes 3145736 | tf_op jit(solution)/shard_map/ppermute | solution.py:157
  25.6 15.6 %collective-permute-start.5 = (f32[512,512]{1,0:T(8,128)}, f32[512,512]{1,0:T(8,128)}, u32[]{:S(2)}, u32[]{:S(2)}) collective-permute-start(f32[512,512]{1,0:T(8,128)} %add.114), channel_id=1, source_target_pairs={{24,8},{28,20},{17,25},{21,5}} | collective-permute-start | bytes 3145736 | tf_op jit(solution)/shard_map/ppermute | solution.py:157
  41.2 12.6 %copy-start.14 = (f32[512,512]{1,0:T(8,128)}, f32[512,512]{1,0:T(8,128)S(1)}, u32[]{:S(2)}) copy-start(f32[512,512]{1,0:T(8,128)S(1)} %collective-permute-done.4) | copy-start | bytes 3145732
  41.2 17.6 %collective-permute-start.6 = (f32[512,512]{1,0:T(8,128)S(1)}, f32[512,512]{1,0:T(8,128)S(1)}, u32[]{:S(2)}, u32[]{:S(2)}) collective-permute-start(f32[512,512]{1,0:T(8,128)S(1)} %get-tuple-element.54.factor), channel_id=1, source_target_pairs={{0,8},{4,20},{9,25},{13,5},{18,26}} | collective-permute-start | bytes 3145736 | tf_op jit(solution)/shard_map/ppermute | solution.py:157
  48.3 16.7 %collective-permute-start.7 = (f32[512,512]{1,0:T(8,128)S(1)}, f32[512,512]{1,0:T(8,128)S(1)}, u32[]{:S(2)}, u32[]{:S(2)}) collective-permute-start(f32[512,512]{1,0:T(8,128)S(1)} %add.115), channel_id=1, source_target_pairs={{8,0},{20,4},{25,9},{5,13},{26,18}} | collective-permute-start | bytes 3145736 | tf_op jit(solution)/shard_map/ppermute | solution.py:157
  53.8 12.0 %collective-permute-start.11 = (f32[512,512]{1,0:T(8,128)S(1)}, f32[512,512]{1,0:T(8,128)S(1)}, u32[]{:S(2)}, u32[]{:S(2)}) collective-permute-start(f32[512,512]{1,0:T(8,128)S(1)} %get-tuple-element.58), channel_id=1, source_target_pairs={{4,0},{0,4},{12,8},{8,12},{20,16},{16,20},{28,24},{24,28},{5,1},{1... | collective-permute-start | bytes 3145736 | tf_op jit(solution)/shard_map/ppermute | solution.py:111
  65.0 4.8 %collective-permute-start.9 = (f32[512,512]{1,0:T(8,128)S(1)}, f32[512,512]{1,0:T(8,128)S(1)}, u32[]{:S(2)}, u32[]{:S(2)}) collective-permute-start(f32[512,512]{1,0:T(8,128)S(1)} %collective-permute-done.6), channel_id=1, source_target_pairs={{8,24},{20,28},{25,17},{5,21}} | collective-permute-start | bytes 3145736 | tf_op jit(solution)/shard_map/ppermute | solution.py:157
  66.0 20.4 %copy-start.10 = (f32[512,1024]{1,0:T(8,128)S(1)}, f32[512,1024]{1,0:T(8,128)}, u32[]{:S(2)}) copy-start(f32[512,1024]{1,0:T(8,128)} %param.7) | copy-start | bytes 6291460
  66.0 3.6 %collective-permute-start.13 = (f32[512,512]{1,0:T(8,128)S(1)}, f32[512,512]{1,0:T(8,128)S(1)}, u32[]{:S(2)}, u32[]{:S(2)}) collective-permute-start(f32[512,512]{1,0:T(8,128)S(1)} %add.118), channel_id=1, source_target_pairs={{24,8},{28,20},{17,25},{21,5}} | collective-permute-start | bytes 3145736 | tf_op jit(solution)/shard_map/ppermute | solution.py:157
  66.8 13.6 %collective-permute-start.8 = (f32[512,512]{1,0:T(8,128)S(1)}, f32[512,512]{1,0:T(8,128)S(1)}, u32[]{:S(2)}, u32[]{:S(2)}) collective-permute-start(f32[512,512]{1,0:T(8,128)S(1)} %get-tuple-element.54.factor), channel_id=1, source_target_pairs={{0,16},{4,12},{13,29},{22,30}} | collective-permute-start | bytes 3145736 | tf_op jit(solution)/shard_map/ppermute | solution.py:157
  68.2 16.7 %collective-permute-start.12 = (f32[512,512]{1,0:T(8,128)S(1)}, f32[512,512]{1,0:T(8,128)S(1)}, u32[]{:S(2)}, u32[]{:S(2)}) collective-permute-start(f32[512,512]{1,0:T(8,128)S(1)} %add.118), channel_id=1, source_target_pairs={{16,0},{12,4},{29,13},{30,22}} | collective-permute-start | bytes 3145736 | tf_op jit(solution)/shard_map/ppermute | solution.py:157
  69.5 18.3 %collective-permute-start.15 = (f32[512,512]{1,0:T(8,128)}, f32[512,512]{1,0:T(8,128)S(1)}, u32[]{:S(2)}, u32[]{:S(2)}) collective-permute-start(f32[512,512]{1,0:T(8,128)} %get-tuple-element.88.rest_0_), channel_id=1, source_target_pairs={{4,0},{0,4},{12,8},{8,12},{20,16},{16,20},{28,24},{24,28},{5,1},{1... | collective-permute-start | bytes 3145736 | tf_op jit(solution)/shard_map/ppermute | solution.py:111
  69.8 19.0 %copy-start.8 = (bf16[512,1024]{1,0:T(8,128)(2,1)S(1)}, bf16[512,1024]{1,0:T(8,128)(2,1)}, u32[]{:S(2)}) copy-start(bf16[512,1024]{1,0:T(8,128)(2,1)} %copy-done.7) | copy-start | bytes 3145732
  84.9 16.7 %collective-permute-start.14 = (f32[512,512]{1,0:T(8,128)S(1)}, f32[512,512]{1,0:T(8,128)S(1)}, u32[]{:S(2)}, u32[]{:S(2)}) collective-permute-start(f32[512,512]{1,0:T(8,128)S(1)} %add.120), channel_id=1, source_target_pairs={{8,0},{20,4},{25,9},{5,13},{26,18}} | collective-permute-start | bytes 3145736 | tf_op jit(solution)/shard_map/ppermute | solution.py:157
  87.8 19.1 %collective-permute-start.10 = (f32[512,512]{1,0:T(8,128)}, f32[512,512]{1,0:T(8,128)}, u32[]{:S(2)}, u32[]{:S(2)}) collective-permute-start(f32[512,512]{1,0:T(8,128)} %add_select_fusion.1.rest_0_), channel_id=1, source_target_pairs={{4,0},{0,4},{12,8},{8,12},{20,16},{16,20},{28,24},{24,28},{5,1},{1... | collective-permute-start | bytes 3145736 | tf_op jit(solution)/shard_map/ppermute | solution.py:111
  88.9 12.7 %copy-start.15 = (f32[512,512]{1,0:T(8,128)S(1)}, f32[512,512]{1,0:T(8,128)}, u32[]{:S(2)}) copy-start(f32[512,512]{1,0:T(8,128)} %copy-done.14) | copy-start | bytes 3145732
  105.6 8.0 %collective-permute-start.16 = (f32[256,512]{1,0:T(8,128)S(1)}, f32[256,512]{1,0:T(8,128)S(1)}, u32[]{:S(2)}, u32[]{:S(2)}) collective-permute-start(f32[256,512]{1,0:T(8,128)S(1)} %get-tuple-element.95), channel_id=1, source_target_pairs={{0,1},{3,2},{4,5},{7,6},{8,9},{11,10},{12,13},{15,14},{16,17},{19,... | collective-permute-start | bytes 1572872 | tf_op jit(solution)/shard_map/ppermute | solution.py:157
  106.9 14.7 %collective-permute-start.27 = (f32[256,512]{1,0:T(8,128)S(1)}, f32[256,512]{1,0:T(8,128)}, u32[]{:S(2)}, u32[]{:S(2)}) collective-permute-start(f32[256,512]{1,0:T(8,128)S(1)} %get-tuple-element.77), channel_id=1, source_target_pairs={{4,0},{0,4},{12,8},{8,12},{20,16},{16,20},{28,24},{24,28},{5,1},{1... | collective-permute-start | bytes 1572872 | tf_op jit(solution)/shard_map/ppermute | solution.py:111
  111.3 12.8 %collective-permute-start.28 = (f32[256,512]{1,0:T(8,128)S(1)}, f32[256,512]{1,0:T(8,128)}, u32[]{:S(2)}, u32[]{:S(2)}) collective-permute-start(f32[256,512]{1,0:T(8,128)S(1)} %get-tuple-element.79), channel_id=1, source_target_pairs={{4,0},{0,4},{12,8},{8,12},{20,16},{16,20},{28,24},{24,28},{5,1},{1... | collective-permute-start | bytes 1572872 | tf_op jit(solution)/shard_map/ppermute | solution.py:111
  114.4 10.9 %collective-permute-start.17 = (f32[256,512]{1,0:T(8,128)}, f32[256,512]{1,0:T(8,128)}, u32[]{:S(2)}, u32[]{:S(2)}) collective-permute-start(f32[256,512]{1,0:T(8,128)} %add.128), channel_id=1, source_target_pairs={{1,2},{2,1},{5,6},{6,5},{9,10},{10,9},{13,14},{14,13},{17,18},{18,... | collective-permute-start | bytes 1572872 | tf_op jit(solution)/shard_map/ppermute | solution.py:157
  115.9 12.8 %collective-permute-start.18 = (f32[256,512]{1,0:T(8,128)}, f32[256,512]{1,0:T(8,128)}, u32[]{:S(2)}, u32[]{:S(2)}) collective-permute-start(f32[256,512]{1,0:T(8,128)} %get-tuple-element.66), channel_id=1, source_target_pairs={{0,1},{3,2},{4,5},{7,6},{8,9},{11,10},{12,13},{15,14},{16,17},{19,... | collective-permute-start | bytes 1572872 | tf_op jit(solution)/shard_map/ppermute | solution.py:157
  128.7 12.7 %collective-permute-start.19 = (f32[256,512]{1,0:T(8,128)}, f32[256,512]{1,0:T(8,128)S(1)}, u32[]{:S(2)}, u32[]{:S(2)}) collective-permute-start(f32[256,512]{1,0:T(8,128)} %get-tuple-element.67), channel_id=1, source_target_pairs={{0,1},{3,2},{4,5},{7,6},{8,9},{11,10},{12,13},{15,14},{16,17},{19,... | collective-permute-start | bytes 1572872 | tf_op jit(solution)/shard_map/ppermute | solution.py:157
  134.4 11.1 %collective-permute-start.20 = (f32[256,512]{1,0:T(8,128)S(1)}, f32[256,512]{1,0:T(8,128)S(1)}, u32[]{:S(2)}, u32[]{:S(2)}) collective-permute-start(f32[256,512]{1,0:T(8,128)S(1)} %add.131.rest_0_), channel_id=1, source_target_pairs={{1,0},{2,3},{5,4},{6,7},{9,8},{10,11},{13,12},{14,15},{17,16},{18,... | collective-permute-start | bytes 1572872 | tf_op jit(solution)/shard_map/ppermute | solution.py:157
  137.0 8.5 %collective-permute-start.21 = (f32[256,512]{1,0:T(8,128)S(1)}, f32[256,512]{1,0:T(8,128)}, u32[]{:S(2)}, u32[]{:S(2)}) collective-permute-start(f32[256,512]{1,0:T(8,128)S(1)} %add.132), channel_id=1, source_target_pairs={{1,2},{2,1},{5,6},{6,5},{9,10},{10,9},{13,14},{14,13},{17,18},{18,... | collective-permute-start | bytes 1572872 | tf_op jit(solution)/shard_map/ppermute | solution.py:157
  139.3 25.9 %collective-permute-start.29 = (f32[256,512]{1,0:T(8,128)}, f32[256,512]{1,0:T(8,128)}, u32[]{:S(2)}, u32[]{:S(2)}) collective-permute-start(f32[256,512]{1,0:T(8,128)} %dynamic-slice_bitcast_fusion), channel_id=1, source_target_pairs={{0,8},{1,9},{2,10},{3,11},{4,20},{5,21},{6,22},{7,23},{8,0},{9,1},... | collective-permute-start | bytes 1572872 | tf_op jit(solution)/shard_map/ppermute | solution.py:157
  142.6 30.2 %copy-start.13 = (f32[256,512]{1,0:T(8,128)S(1)}, f32[256,512]{1,0:T(8,128)}, u32[]{:S(2)}) copy-start(f32[256,512]{1,0:T(8,128)} %get-tuple-element.73) | copy-start | bytes 1572868
  145.4 27.4 %collective-permute-start.22 = (f32[256,512]{1,0:T(8,128)S(1)}, f32[256,512]{1,0:T(8,128)S(1)}, u32[]{:S(2)}, u32[]{:S(2)}) collective-permute-start(f32[256,512]{1,0:T(8,128)S(1)} %add.130), channel_id=1, source_target_pairs={{1,2},{2,1},{5,6},{6,5},{9,10},{10,9},{13,14},{14,13},{17,18},{18,... | collective-permute-start | bytes 1572872 | tf_op jit(solution)/shard_map/ppermute | solution.py:157
  147.3 26.9 %collective-permute-start.23 = (f32[256,512]{1,0:T(8,128)S(1)}, f32[256,512]{1,0:T(8,128)S(1)}, u32[]{:S(2)}, u32[]{:S(2)}) collective-permute-start(f32[256,512]{1,0:T(8,128)S(1)} %add.134.rest_2_), channel_id=1, source_target_pairs={{1,0},{2,3},{5,4},{6,7},{9,8},{10,11},{13,12},{14,15},{17,16},{18,... | collective-permute-start | bytes 1572872 | tf_op jit(solution)/shard_map/ppermute | solution.py:157
  148.6 24.2 %collective-permute-start.24 = (f32[256,512]{1,0:T(8,128)}, f32[256,512]{1,0:T(8,128)S(1)}, u32[]{:S(2)}, u32[]{:S(2)}) collective-permute-start(f32[256,512]{1,0:T(8,128)} %get-tuple-element.73), channel_id=1, source_target_pairs={{0,1},{3,2},{4,5},{7,6},{8,9},{11,10},{12,13},{15,14},{16,17},{19,... | collective-permute-start | bytes 1572872 | tf_op jit(solution)/shard_map/ppermute | solution.py:157
  166.4 9.9 %collective-permute-start.30 = (f32[128,512]{1,0:T(8,128)S(1)}, f32[128,512]{1,0:T(8,128)S(1)}, u32[]{:S(2)}, u32[]{:S(2)}) collective-permute-start(f32[128,512]{1,0:T(8,128)S(1)} %dynamic-slice_bitcast_fusion.1), channel_id=1, source_target_pairs={{0,16},{1,17},{2,18},{3,19},{4,12},{5,13},{6,14},{7,15},{8,24},{9,... | collective-permute-start | bytes 786440 | tf_op jit(solution)/shard_map/ppermute | solution.py:157
  174.2 7.0 %collective-permute-start.26 = (f32[256,512]{1,0:T(8,128)S(1)}, f32[256,512]{1,0:T(8,128)S(1)}, u32[]{:S(2)}, u32[]{:S(2)}) collective-permute-start(f32[256,512]{1,0:T(8,128)S(1)} %add.136), channel_id=1, source_target_pairs={{1,2},{2,1},{5,6},{6,5},{9,10},{10,9},{13,14},{14,13},{17,18},{18,... | collective-permute-start | bytes 1572872 | tf_op jit(solution)/shard_map/ppermute | solution.py:157
  175.0 13.2 %collective-permute-start.25 = (f32[256,512]{1,0:T(8,128)S(1)}, f32[256,512]{1,0:T(8,128)S(1)}, u32[]{:S(2)}, u32[]{:S(2)}) collective-permute-start(f32[256,512]{1,0:T(8,128)S(1)} %add.133.rest_0_), channel_id=1, source_target_pairs={{1,0},{2,3},{5,4},{6,7},{9,8},{10,11},{13,12},{14,15},{17,16},{18,... | collective-permute-start | bytes 1572872 | tf_op jit(solution)/shard_map/ppermute | solution.py:157
  176.3 8.7 %collective-permute-start.31 = (f32[128,512]{1,0:T(8,128)S(1)}, f32[128,512]{1,0:T(8,128)S(1)}, u32[]{:S(2)}, u32[]{:S(2)}) collective-permute-start(f32[128,512]{1,0:T(8,128)S(1)} %bitcast_add_fusion.1), channel_id=1, source_target_pairs={{0,1},{3,2},{4,5},{7,6},{8,9},{11,10},{12,13},{15,14},{16,17},{19,... | collective-permute-start | bytes 786440 | tf_op jit(solution)/shard_map/ppermute | solution.py:157
  188.2 11.1 %copy-start.1 = (f32[256,512]{1,0:T(8,128)}, f32[256,512]{1,0:T(8,128)S(1)}, u32[]{:S(2)}) copy-start(f32[256,512]{1,0:T(8,128)S(1)} %collective-permute-done.25.rest_1_) | copy-start | bytes 1572868
  188.2 11.1 %collective-permute-start.32 = (f32[256,512]{1,0:T(8,128)S(1)}, f32[256,512]{1,0:T(8,128)S(1)}, u32[]{:S(2)}, u32[]{:S(2)}) collective-permute-start(f32[256,512]{1,0:T(8,128)S(1)} %add.137.rest_2_), channel_id=1, source_target_pairs={{1,0},{2,3},{5,4},{6,7},{9,8},{10,11},{13,12},{14,15},{17,16},{18,... | collective-permute-start | bytes 1572872 | tf_op jit(solution)/shard_map/ppermute | solution.py:157
  189.5 0.7 collective-permute-start.33
  200.0 8.4 %collective-permute-start.34 = (f32[128,512]{1,0:T(8,128)S(1)}, f32[128,512]{1,0:T(8,128)}, u32[]{:S(2)}, u32[]{:S(2)}) collective-permute-start(f32[128,512]{1,0:T(8,128)S(1)} %add.146), channel_id=1, source_target_pairs={{1,0},{2,3},{5,4},{6,7},{9,8},{10,11},{13,12},{14,15},{17,16},{18,... | collective-permute-start | bytes 786440 | tf_op jit(solution)/shard_map/ppermute | solution.py:157
  210.1 7.6 %collective-permute-start.35 = (f32[128,512]{1,0:T(8,128)}, f32[128,512]{1,0:T(8,128)}, u32[]{:S(2)}, u32[]{:S(2)}) collective-permute-start(f32[128,512]{1,0:T(8,128)} %broadcast_select_fusion.2), channel_id=1, source_target_pairs={{0,16},{1,17},{2,18},{3,19},{4,12},{5,13},{6,14},{7,15},{8,24},{9,... | collective-permute-start | bytes 786440 | tf_op jit(solution)/shard_map/ppermute | solution.py:157
  220.3 11.2 %collective-permute-start.36 = (f32[256,512]{1,0:T(8,128)}, f32[256,512]{1,0:T(8,128)}, u32[]{:S(2)}, u32[]{:S(2)}) collective-permute-start(f32[256,512]{1,0:T(8,128)} %pad_maximum_fusion.2), channel_id=1, source_target_pairs={{0,8},{1,9},{2,10},{3,11},{4,20},{5,21},{6,22},{7,23},{8,0},{9,1},... | collective-permute-start | bytes 1572872 | tf_op jit(solution)/shard_map/ppermute | solution.py:157
  224.0 8.9 %copy-start = (f32[2,512,512]{2,1,0:T(8,128)S(1)}, f32[2,512,512]{2,1,0:T(8,128)}, u32[]{:S(2)}) copy-start(f32[2,512,512]{2,1,0:T(8,128)} %unit_ref.5) | copy-start | bytes 6291460
  232.9 7.2 %collective-permute-start.37 = (f32[512,512]{1,0:T(8,128)S(1)}, f32[512,512]{1,0:T(8,128)S(1)}, u32[]{:S(2)}, u32[]{:S(2)}) collective-permute-start(f32[512,512]{1,0:T(8,128)S(1)} %pad_maximum_fusion.1.rest_0_), channel_id=1, source_target_pairs={{4,0},{0,4},{12,8},{8,12},{20,16},{16,20},{28,24},{24,28},{5,1},{1... | collective-permute-start | bytes 3145736 | tf_op jit(solution)/shard_map/ppermute | solution.py:111
  (7 other events, 15.6 us)

commit v4 on v3

--- a/solution.py
+++ b/solution.py
@@ -79,30 +79,6 @@
                         )
         return pairs
 
-    def received(self, step):
-        row, col = lax.axis_index("row"), lax.axis_index("col")
-        offset = (row // self.lanes) ^ col
-        got = False
-        for lane, order in enumerate(self.orders):
-            later = sum(order[step + 1:])
-            here = ((offset & order[step]) != 0) & ((offset & later) == 0)
-            got = got | (here & (row % self.lanes == lane))
-        return got
-
-    def rounds(self):
-        ways = (
-            (0, ((0, 1), (0, 2)), ((0, 2), (0, 1)), ((1, 3), (2, 3))),
-            (1, ((1, 3), (1, 0)), (None, (1, 3)), ((3, 2), (0, 2))),
-            (2, ((2, 3), None), (None, (2, 3)), (None, None)),
-        )
-        pairs = [[], [], []]
-        for col, *turns in ways:
-            for turn, hops in enumerate(turns):
-                for lane, hop in enumerate(hops):
-                    if hop is not None:
-                        pairs[turn].append(tuple(self.device(chip, lane, col) for chip in hop))
-        return pairs
-
     def swap(self, x, shift):
         pairs = []
         for row in range(self.rows):
@@ -125,6 +101,9 @@
         place, i = lax.axis_index("col"), hop - half
         return jnp.where((place == half - 2 - i) | (place == half + i + 1), got, x)
 
+    def on_diagonal(self):
+        return lax.axis_index("row") // self.lanes == lax.axis_index("col")
+
     def at_end(self):
         place = lax.axis_index("col")
         return (place == 0) | (place == self.cols - 1)
@@ -149,11 +128,11 @@
     def __init__(self):
         self.last = ()
 
-    def issue(self, *requests):
+    def issue(self, *requests, after=()):
         out = []
         for x, axis, pairs in requests:
-            if self.last:
-                x, _ = lax.optimization_barrier((x, self.last))
+            if self.last or after:
+                x, _ = lax.optimization_barrier((x, self.last + tuple(after)))
             out.append(lax.ppermute(x, axis, pairs))
         self.last = tuple(out)
         return out
@@ -204,7 +183,7 @@
         mirror[b // na][first:first + size, :] = product(left, right, contract=0)
 
 
-def forward_kernel(plan, high, low, factor, *rest):
+def forward_kernel(plan, high, low, factor, mirror, *rest):
     lanes, size, depth = plan.lanes, plan.tile, plan.depth
     parts, rest = rest[:lanes], rest[lanes:]
     totals, rest = rest[:SPLIT], rest[SPLIT:]
@@ -220,8 +199,10 @@
             for i in range(lanes)
         )
     share = depth // SPLIT
+    on_diagonal = plan.on_diagonal()
     for i in range(SPLIT):
-        totals[i][...] = total[i * share:(i + 1) * share, :]
+        rows = slice(i * share, (i + 1) * share)
+        totals[i][...] = total[rows, :] + jnp.where(on_diagonal, mirror[rows, :], 0.0)
     whole[...] = product(split(factor[...]), split(total[...]), contract=0)
     share = plan.width // lanes
     lane = lax.rem(lax.axis_index("row"), lanes)
@@ -305,48 +286,13 @@
     return [(receiver, sender) for sender, receiver in pairs]
 
 
-def exchange(plan, factors, mirrors):
-    row, col = lax.axis_index("row"), lax.axis_index("col")
-    on_diagonal = row // plan.lanes == col
-    both = ("row", "col")
-    plane = Chain()
-    held, back = [], []
-    if plan.cols == 4 and plan.lanes == 2:
-        a, b, c = plan.rounds()
-        first, relayed = plane.issue((factors[0], both, a)) + [None]
-        for member in range(plan.members):
-            own, mirror = factors[member], mirrors(member)
-            second, third, near, far = plane.issue(
-                (own, both, b), (first, both, c),
-                (mirror, both, reverse(b)), (mirror, both, reverse(c)),
-            )
-            held.append(jnp.where(on_diagonal, own, first + second + third))
-            last = (mirror + far, both, reverse(a))
-            if member + 1 < plan.members:
-                first, relayed = plane.issue((factors[member + 1], both, a), last)
-            else:
-                relayed, = plane.issue(last)
-            back.append(jnp.where(on_diagonal, mirror, 0.0) + near + relayed)
-        return plane, held, back
-    for member in range(plan.members):
-        x, mirror = factors[member], mirrors(member)
-        for step in range(plan.steps):
-            got, = plane.issue((x, both, plan.tree(step)))
-            x = jnp.where(plan.received(step), got, x)
-        for step in reversed(range(plan.steps)):
-            got, = plane.issue((mirror, both, reverse(plan.tree(step))))
-            mirror = mirror + got
-        held.append(x)
-        back.append(jnp.where(on_diagonal, mirror, 0.0))
-    return plane, held, back
-
-
 def shards(inverse_front, factor, unit_lower, pivot_inverse, tile_list, tile_valid):
     plan = Plan(inverse_front, factor, unit_lower, tile_list)
-    width, depth, lanes = plan.width, plan.depth, plan.lanes
+    width, depth, lanes, members, steps = plan.width, plan.depth, plan.lanes, plan.members, plan.steps
+    both = ("row", "col")
+    share = depth // SPLIT
     flops = 6 * depth * depth * lanes * width
-    factors = [factor[:, member * width:(member + 1) * width] for member in range(plan.members)]
-    halves = {}
+    factors = [factor[:, member * width:(member + 1) * width] for member in range(members)]
 
     def lane_sum(parts):
         out = parts[0]
@@ -354,8 +300,8 @@
             out = out + plan.swap(parts[lanes - shift], shift)
         return out
 
-    def mirrors(member):
-        high, low, *mirror = pl.pallas_call(
+    def gather(member):
+        return pl.pallas_call(
             functools.partial(gather_kernel, plan, member),
             in_specs=smem(2) + [pl.BlockSpec(memory_space=pl.ANY)] + vmem(1),
             out_specs=vmem(2 + lanes),
@@ -369,17 +315,12 @@
             cost_estimate=pl.CostEstimate(flops=flops, bytes_accessed=8 << 20, transcendentals=0),
             name="gather_mirror",
         )(tile_list, tile_valid, inverse_front, factors[member])
-        halves[member] = (high, low)
-        return lane_sum(mirror)
-
-    plane, held, back = exchange(plan, factors, mirrors)
-    share = depth // SPLIT
-    chunks, crosses = [], []
-    for member in range(plan.members):
-        parts = [held[member]] + [plan.swap(held[member], shift) for shift in range(1, lanes)]
-        *outs, = pl.pallas_call(
+
+    def forward(high, low, own, mirror, held):
+        parts = [held] + [plan.swap(held, shift) for shift in range(1, lanes)]
+        outs = pl.pallas_call(
             functools.partial(forward_kernel, plan),
-            in_specs=vmem(3 + lanes),
+            in_specs=vmem(4 + lanes),
             out_specs=vmem(SPLIT + lanes),
             out_shape=[jax.ShapeDtypeStruct((share, width), F32)] * SPLIT
             + [jax.ShapeDtypeStruct((width // lanes, width), F32)] * lanes,
@@ -390,37 +331,83 @@
             compiler_params=PARAMS,
             cost_estimate=pl.CostEstimate(flops=flops, bytes_accessed=8 << 20, transcendentals=0),
             name="forward",
-        )(*halves[member], factors[member], *parts)
-        for i in range(SPLIT):
-            chunks.append(outs[i] + back[member][i * share:(i + 1) * share])
-        crosses.append(lane_sum(outs[SPLIT:]))
-
-    x = jnp.concatenate(crosses)
-    for step in range(plan.steps):
+        )(high, low, own, mirror, *parts)
+        return outs[:SPLIT], outs[SPLIT:]
+
+    line, hops = Chain(), plan.line_hops()
+    chunks, ends, phase_now = [], [], [0]
+
+    def line_phase(after=(), beside=()):
+        phase = phase_now[0]
+        live = [i for i in range(len(chunks)) if 0 <= phase - i < len(hops)]
+        brought = line.issue(
+            *((chunks[i], "col", hops[phase - i]) for i in live), after=after
+        )
+        brought, beside = lax.optimization_barrier((brought, beside))
+        line.last = tuple(brought)
+        ends.extend([None] * (len(chunks) - len(ends)))
+        for i, got in zip(live, brought):
+            if phase - i < len(hops) - 1 or len(hops) == 1:
+                chunks[i] = plan.line_step(phase - i, chunks[i], got)
+            ends[i] = got if len(hops) > 1 else chunks[i]
+        phase_now[0] += 1
+        return beside
+
+    plane = Chain()
+    count = members * steps
+    tiles, held, mirror, crosses = {}, {}, {}, []
+    after = ()
+    for phase in range(count + 1):
+        requests = []
+        if phase < count:
+            out, step = divmod(phase, steps)
+            x = factors[out] if step == 0 else held[out]
+            requests.append((x, both, plan.tree(step)))
+        if phase:
+            back, turn = divmod(phase - 1, steps)
+            requests.append((mirror[back], both, reverse(plan.tree(steps - 1 - turn))))
+        brought = plane.issue(*requests, after=after)
+        if chunks:
+            brought = line_phase(beside=brought)
+            plane.last = tuple(brought)
+        after = ()
+        if phase % steps == 0 and phase < count:
+            high, low, *parts = gather(out) if out == 0 else tiles[out]
+            tiles[out] = (high, low)
+            mirror[out] = lane_sum(parts)
+        if phase % steps == 1 % steps and phase < count and out + 1 < members:
+            tiles[out + 1] = gather(out + 1)
+            after = (tiles[out + 1][0],)
+        if phase < count:
+            got = brought[0]
+            held[out] = jnp.where(plan.on_diagonal(), x, got) if step == 0 else x + got
+        if phase:
+            if turn < steps - 1:
+                mirror[back] = mirror[back] + brought[-1]
+            else:
+                sums, cross = forward(*tiles[back], factors[back], mirror[back], held[back])
+                new = [
+                    part + brought[-1][i * share:(i + 1) * share] for i, part in enumerate(sums)
+                ]
+                chunks += new
+                after = tuple(new)
+                crosses.append(cross)
+
+    x = jnp.concatenate([lane_sum(cross) for cross in crosses])
+    for step in range(steps):
         x = x.reshape(2, x.shape[0] // 2, x.shape[1])
         bit = plan.bit(step)
         send = lax.dynamic_index_in_dim(x, 1 - bit, 0, keepdims=False)
         keep = lax.dynamic_index_in_dim(x, bit, 0, keepdims=False)
-        got, = plane.issue((send, ("row", "col"), plan.bit_pairs(step)))
+        got, = plane.issue((send, both, plan.bit_pairs(step)))
         x = keep + got
     chunks.append(x)
 
-    line, hops = Chain(), plan.line_hops()
-    ends = [None] * len(chunks)
-    for phase in range(len(chunks) + len(hops) - 1):
-        live = [i for i in range(len(chunks)) if 0 <= phase - i < len(hops)]
-        brought = line.issue(*((chunks[i], "col", hops[phase - i]) for i in live))
-        for i, got in zip(live, brought):
-            if phase - i < len(hops) - 1 or len(hops) == 1:
-                chunks[i] = plan.line_step(phase - i, chunks[i], got)
-            ends[i] = got if len(hops) > 1 else chunks[i]
-
-    column = None
-    for member in range(plan.members):
+    def place(member, column):
         sums = []
         for i in range(member * SPLIT, (member + 1) * SPLIT):
             sums += [chunks[i], ends[i]]
-        column = pl.pallas_call(
+        return pl.pallas_call(
             functools.partial(place_kernel, plan, member),
             in_specs=smem(1) + vmem(1 + 2 * SPLIT)
             + [pl.BlockSpec(memory_space=pl.ANY)] * (member > 0),
@@ -430,7 +417,7 @@
                 pltpu.VMEM((depth, width), F32),
                 pltpu.VMEM((plan.tile, width), F32),
                 pltpu.SemaphoreType.DMA((plan.na,)),
-                pltpu.SemaphoreType.DMA((plan.members, plan.row_tiles)),
+                pltpu.SemaphoreType.DMA((members, plan.row_tiles)),
             ],
             input_output_aliases={2 + 2 * SPLIT: 0} if member else {},
             compiler_params=PARAMS,
@@ -440,9 +427,22 @@
             name="place",
         )(tile_list, unit_lower, *sums, *([column] if member else []))
 
+    column, placed, after = None, 0, ()
+    while phase_now[0] < len(chunks) + len(hops) - 1:
+        line_phase(after)
+        after = ()
+        if phase_now[0] > (placed + 1) * SPLIT + len(hops) - 1 and placed < members - 1:
+            column = place(placed, column)
+            placed += 1
+            after = (column,)
+    for member in range(placed, members):
+        column = place(member, column)
+
     x = jnp.where(plan.at_end(), ends[-1], chunks[-1])
-    for step in reversed(range(plan.steps)):
-        got, = plane.issue((x, ("row", "col"), plan.bit_pairs(step)))
+    for step in reversed(range(steps)):
+        got, = plane.issue(
+            (x, both, plan.bit_pairs(step)), after=(column,) if step < steps - 1 else ()
+        )
         bit = plan.bit(step) == 1
         x = jnp.concatenate([jnp.where(bit, got, x), jnp.where(bit, x, got)])
     parts = [x] + [plan.swap(x, shift) for shift in range(1, lanes)]

time: 246 us -> 213 us (0.87)
  starting transfers between devices: 79.3 us -> 57.1 us
  waiting for transfers between devices: 102 us -> 91.3 us
  other arithmetic: 28.8 us -> 22.3 us
  local copies, waits for them, and re-layouts: 4.93 us -> 8.07 us
    ppermute x31 -> x27, starting transfers between devices: 78.4 us -> 56.1 us  [issue(): out.append(lax.ppermute(x, axis, pairs))]
    ppermute x31 -> x27, waiting for transfers between devices: 102 us -> 88.7 us  [issue(): out.append(lax.ppermute(x, axis, pairs))]
    select_n x2, other arithmetic: 5.53 us -> 2.08 us  [shards(): held[out] = jnp.where(plan.on_diagonal(), x, got) if step == 0 else x + got]
    unnamed x34 -> x44, local copies, waits for them, and re-layouts: 2.76 us -> 5.88 us
    ppermute x7, waiting for transfers between devices: 0.02 us -> 2.66 us  [swap(): return lax.ppermute(x, 'row', pairs)]
    add x5 -> x6, other arithmetic: 7.12 us -> 5.25 us  [the longest x2 3.4 us: shards(): part + brought[-1][i * share:(i + 1) * share]]
  transfers between devices with their start and end apart: 38 -> 34, of which waited for: 19 -> 18; matrix products, arithmetic and copies ran while one was open for 10% -> 9% of each run, Pallas kernels for 10% -> 13%
where the time goes in v4:
time: 213 us; the launch traced here: 212 us
  waiting for transfers between devices  91.3 us (43%)
  starting transfers between devices  57.1 us (27%)
  Pallas kernels  31.6 us (15%)
  other arithmetic  22.3 us (10%)
  local copies, waits for them, and re-layouts  8.07 us (4%)
    ppermute x27, waiting for transfers between devices, issue(): out.append(lax.ppermute(x, axis, pairs))  88.7 us
    ppermute x27, starting transfers between devices, issue(): out.append(lax.ppermute(x, axis, pairs))  56.1 us
    pallas_call x2, Pallas kernels, forward(): pl.pallas_call(functools.partial(forward_kernel, plan), in_specs=vmem(4 +...  10.2 us
    pallas_call x2, Pallas kernels, gather(): pl.pallas_call(functools.partial(gather_kernel, plan, member), in_specs=s...  9.27 us
    pallas_call x2, Pallas kernels, place(): pl.pallas_call(functools.partial(place_kernel, plan, member), in_specs=sm...  7.01 us
    add x10, other arithmetic, line_step(): return x + got  6.06 us
    unnamed x44, local copies, waits for them, and re-layouts  5.88 us
    pallas_call x1, Pallas kernels, shards(): pl.pallas_call(functools.partial(diagonal_kernel, plan), in_specs=vmem(2...  5.11 us
  transfers between devices with their start and end apart: 34, of which 18 were waited for; matrix products, arithmetic and copies ran while one was open for 9% of the time, Pallas kernels for 13%

profile of v4, /device:TPU:0, one launch (start us, length us, event | category | flops | bytes accessed | tf_op | source)
XLA Modules:
  0.0 211.7 jit_solution(17708292510774202173)
XLA Ops:
  0.6 1.3 slice.19.factor
  2.0 5.9 %collective-permute-start.2 = (f32[512,512]{1,0:T(8,128)S(1)}, f32[512,512]{1,0:T(8,128)}, u32[]{:S(2)}, u32[]{:S(2)}) collective-permute-start(f32[512,512]{1,0:T(8,128)S(1)} %slice.19.factor), channel_id=1, source_target_pairs={{0,8},{4,20},{9,1},{13,29},{18,26}} | collective-permute-start | bytes 3145736 | tf_op jit(solution)/shard_map/ppermute | solution.py:136
  7.8 5.1 %gather_mirror.3 = (bf16[512,1024]{1,0:T(8,128)(2,1)S(1)}, bf16[512,1024]{1,0:T(8,128)(2,1)S(1)}, f32[512,512]{1,0:T(8,128)S(1)}, f32[512,512]{1,0:T(8,128)}) custom-call(s32[2,16]{1,0:T(2,128)S(1)} %copy-done.11, s32[2,16]{1,0:T(2,128)S(1)} %copy-done.12, f32[2048,4096]{1,0:T(8,128)} %front.3, f32[512,512]{1,0:T(8,128)S(1)} %slice.19.factor), custom_call_target="tpu_custom_call" | custom-call | flops 1610612736 | bytes 8388608 | tf_op jit(solution)/shard_map/gather_mirror/pallas_call | solution.py:304
  13.9 5.2 %collective-permute-done.2 = f32[512,512]{1,0:T(8,128)} collective-permute-done((f32[512,512]{1,0:T(8,128)S(1)}, f32[512,512]{1,0:T(8,128)}, u32[]{:S(2)}, u32[]{:S(2)}) %collective-permute-start.2) | collective-permute-done | bytes 1048608 | tf_op jit(solution)/shard_map/ppermute | solution.py:136
  19.1 1.9 broadcast_select_fusion.1
  21.0 1.4 collective-permute-start.4
  22.4 1.4 add.97
  23.7 1.3 collective-permute-start.3
  25.0 4.2 %gather_mirror.2 = (bf16[512,1024]{1,0:T(8,128)(2,1)S(1)}, bf16[512,1024]{1,0:T(8,128)(2,1)S(1)}, f32[512,512]{1,0:T(8,128)S(1)}, f32[512,512]{1,0:T(8,128)S(1)}) custom-call(s32[2,16]{1,0:T(2,128)S(1)} %copy-done.11, s32[2,16]{1,0:T(2,128)S(1)} %copy-done.12, f32[2048,4096]{1,0:T(8,128)} %front.3, f32[512,512]{1,0:T(8,128)S(1)} %get-tuple-element.72.factor), custom_call_target="tpu_custom_call" | custom-call | flops 1610612736 | bytes 8388608 | tf_op jit(solution)/shard_map/gather_mirror/pallas_call | solution.py:304
  29.3 5.3 %collective-permute-done.4 = f32[512,512]{1,0:T(8,128)S(1)} collective-permute-done((f32[512,512]{1,0:T(8,128)S(1)}, f32[512,512]{1,0:T(8,128)S(1)}, u32[]{:S(2)}, u32[]{:S(2)}) %collective-permute-start.4) | collective-permute-done | bytes 1048608 | tf_op jit(solution)/shard_map/ppermute | solution.py:136
  34.9 5.6 %collective-permute-done.3 = f32[512,512]{1,0:T(8,128)S(1)} collective-permute-done((f32[512,512]{1,0:T(8,128)S(1)}, f32[512,512]{1,0:T(8,128)S(1)}, u32[]{:S(2)}, u32[]{:S(2)}) %collective-permute-start.3) | collective-permute-done | bytes 1048608 | tf_op jit(solution)/shard_map/ppermute | solution.py:136
  40.7 1.4 collective-permute-start.6
  42.1 4.9 %collective-permute-start.8 = (f32[512,512]{1,0:T(8,128)S(1)}, f32[512,512]{1,0:T(8,128)S(1)}, u32[]{:S(2)}, u32[]{:S(2)}) collective-permute-start(f32[512,512]{1,0:T(8,128)S(1)} %get-tuple-element.72.factor), channel_id=1, source_target_pairs={{0,8},{4,20},{9,1},{13,29},{18,26}} | collective-permute-start | bytes 3145736 | tf_op jit(solution)/shard_map/ppermute | solution.py:136
  48.3 5.5 %forward.2 = (f32[256,512]{1,0:T(8,128)S(1)}, f32[256,512]{1,0:T(8,128)S(1)}, f32[256,512]{1,0:T(8,128)S(1)}, f32[256,512]{1,0:T(8,128)}) custom-call(bf16[512,1024]{1,0:T(8,128)(2,1)S(1)} %get-tuple-element.64.high, bf16[512,1024]{1,0:T(8,128)(2,1)S(1)} %copy-done.2, f32[512,512]{1,0:T(8,128)S(1)} %slice.19.factor, f32[512,512]{1,0:T(8,128)} %copy-done.17, ...), custom_call_target="tpu_custom_call" | custom-call | flops 1610612736 | bytes 8388608 | tf_op jit(solution)/shard_map/forward/pallas_call | solution.py:321
  53.8 4.0 %collective-permute-done.6 = f32[512,512]{1,0:T(8,128)S(1)} collective-permute-done((f32[512,512]{1,0:T(8,128)S(1)}, f32[512,512]{1,0:T(8,128)S(1)}, u32[]{:S(2)}, u32[]{:S(2)}) %collective-permute-start.6) | collective-permute-done | bytes 1048608 | tf_op jit(solution)/shard_map/ppermute | solution.py:136
  58.8 1.8 collective-permute-done.8
  60.8 1.4 collective-permute-start.9
  62.2 1.3 collective-permute-start.10
  63.5 3.2 %collective-permute-start.7 = (f32[256,512]{1,0:T(8,128)S(1)}, f32[256,512]{1,0:T(8,128)S(1)}, u32[]{:S(2)}, u32[]{:S(2)}) collective-permute-start(f32[256,512]{1,0:T(8,128)S(1)} %get-tuple-element.125), channel_id=1, source_target_pairs={{0,1},{3,2},{4,5},{7,6},{8,9},{11,10},{12,13},{15,14},{16,17},{19,... | collective-permute-start | bytes 1572872 | tf_op jit(solution)/shard_map/ppermute | solution.py:136
  66.7 6.6 %collective-permute-done.7 = f32[256,512]{1,0:T(8,128)S(1)} collective-permute-done((f32[256,512]{1,0:T(8,128)S(1)}, f32[256,512]{1,0:T(8,128)S(1)}, u32[]{:S(2)}, u32[]{:S(2)}) %collective-permute-start.7) | collective-permute-done | bytes 524320 | tf_op jit(solution)/shard_map/ppermute | solution.py:136
  74.4 4.5 %collective-permute-done.10 = f32[512,512]{1,0:T(8,128)S(1)} collective-permute-done((f32[512,512]{1,0:T(8,128)S(1)}, f32[512,512]{1,0:T(8,128)S(1)}, u32[]{:S(2)}, u32[]{:S(2)}) %collective-permute-start.10) | collective-permute-done | bytes 1048608 | tf_op jit(solution)/shard_map/ppermute | solution.py:136
  82.3 4.7 %collective-permute-start.13 = (f32[256,512]{1,0:T(8,128)}, f32[256,512]{1,0:T(8,128)}, u32[]{:S(2)}, u32[]{:S(2)}) collective-permute-start(f32[256,512]{1,0:T(8,128)} %get-tuple-element.81), channel_id=1, source_target_pairs={{0,1},{3,2},{4,5},{7,6},{8,9},{11,10},{12,13},{15,14},{16,17},{19,... | collective-permute-start | bytes 1572872 | tf_op jit(solution)/shard_map/ppermute | solution.py:136
  86.9 1.5 collective-permute-start.12
  89.4 4.7 %forward.3 = (f32[256,512]{1,0:T(8,128)S(1)}, f32[256,512]{1,0:T(8,128)S(1)}, f32[256,512]{1,0:T(8,128)S(1)}, f32[256,512]{1,0:T(8,128)S(1)}) custom-call(bf16[512,1024]{1,0:T(8,128)(2,1)S(1)} %get-tuple-element.60.high, bf16[512,1024]{1,0:T(8,128)(2,1)S(1)} %get-tuple-element.61.low, f32[512,512]{1,0:T(8,128)S(1)} %get-tuple-element.72.factor, ...), custom_call_target="tpu_custom_call" | custom-call | flops 1610612736 | bytes 8388608 | tf_op jit(solution)/shard_map/forward/pallas_call | solution.py:321
  95.6 2.7 %collective-permute-done.13 = f32[256,512]{1,0:T(8,128)} collective-permute-done((f32[256,512]{1,0:T(8,128)}, f32[256,512]{1,0:T(8,128)}, u32[]{:S(2)}, u32[]{:S(2)}) %collective-permute-start.13) | collective-permute-done | bytes 524320 | tf_op jit(solution)/shard_map/ppermute | solution.py:136
  99.5 2.1 add.107
  102.8 1.5 collective-permute-start.16
  104.3 2.4 %slice_add_fusion.2 = (f32[256,512]{1,0:T(8,128)}, f32[256,512]{1,0:T(8,128)}) fusion(f32[256,512]{1,0:T(8,128)S(1)} %get-tuple-element.94, f32[512,512]{1,0:T(8,128)} %collective-permute-done.14, f32[256,512]{1,0:T(8,128)S(1)} %get-tuple-element.78), kind=kLoop, calls=%fused_computation.7 | loop fusion | flops 262144 | bytes 3145728 | tf_op jit(solution)/shard_map/add | solution.py:390
  106.7 6.3 %collective-permute-start.17 = (f32[256,512]{1,0:T(8,128)}, f32[256,512]{1,0:T(8,128)S(1)}, u32[]{:S(2)}, u32[]{:S(2)}) collective-permute-start(f32[256,512]{1,0:T(8,128)} %get-tuple-element.88), channel_id=1, source_target_pairs={{0,1},{3,2},{4,5},{7,6},{8,9},{11,10},{12,13},{15,14},{16,17},{19,... | collective-permute-start | bytes 1572872 | tf_op jit(solution)/shard_map/ppermute | solution.py:136
  115.1 3.1 %collective-permute-done.15.rest_1_ = f32[256,512]{1,0:T(8,128)S(1)} collective-permute-done((f32[256,512]{1,0:T(8,128)S(1)}, f32[256,512]{1,0:T(8,128)S(1)}, u32[]{:S(2)}, u32[]{:S(2)}) %collective-permute-start.15) | collective-permute-done | bytes 524320 | tf_op jit(solution)/shard_map/ppermute | solution.py:136
  118.2 6.1 %collective-permute-done.17 = f32[256,512]{1,0:T(8,128)S(1)} collective-permute-done((f32[256,512]{1,0:T(8,128)}, f32[256,512]{1,0:T(8,128)S(1)}, u32[]{:S(2)}, u32[]{:S(2)}) %collective-permute-start.17) | collective-permute-done | bytes 524320 | tf_op jit(solution)/shard_map/ppermute | solution.py:136
  125.4 1.3 add.109.rest_2_
  126.7 4.4 %collective-permute-start.20 = (f32[256,512]{1,0:T(8,128)S(1)}, f32[256,512]{1,0:T(8,128)S(1)}, u32[]{:S(2)}, u32[]{:S(2)}) collective-permute-start(f32[256,512]{1,0:T(8,128)S(1)} %copy-done.18), channel_id=1, source_target_pairs={{0,1},{3,2},{4,5},{7,6},{8,9},{11,10},{12,13},{15,14},{16,17},{19,... | collective-permute-start | bytes 1572872 | tf_op jit(solution)/shard_map/ppermute | solution.py:136
  131.9 1.3 collective-permute-start.18
  134.5 6.7 %collective-permute-done.20 = f32[256,512]{1,0:T(8,128)S(1)} collective-permute-done((f32[256,512]{1,0:T(8,128)S(1)}, f32[256,512]{1,0:T(8,128)S(1)}, u32[]{:S(2)}, u32[]{:S(2)}) %collective-permute-start.20) | collective-permute-done | bytes 524320 | tf_op jit(solution)/shard_map/ppermute | solution.py:136
  141.2 4.8 %collective-permute-done.18.rest_3_ = f32[256,512]{1,0:T(8,128)S(1)} collective-permute-done((f32[256,512]{1,0:T(8,128)S(1)}, f32[256,512]{1,0:T(8,128)S(1)}, u32[]{:S(2)}, u32[]{:S(2)}) %collective-permute-start.18) | collective-permute-done | bytes 524320 | tf_op jit(solution)/shard_map/ppermute | solution.py:136
  146.2 1.3 collective-permute-start.21
  148.3 7.1 %collective-permute-start.27 = (f32[128,512]{1,0:T(8,128)S(1)}, f32[128,512]{1,0:T(8,128)S(1)}, u32[]{:S(2)}, u32[]{:S(2)}) collective-permute-start(f32[128,512]{1,0:T(8,128)S(1)} %bitcast_add_fusion.1), channel_id=1, source_target_pairs={{0,1},{3,2},{4,5},{7,6},{8,9},{11,10},{12,13},{15,14},{16,17},{19,... | collective-permute-start | bytes 786440 | tf_op jit(solution)/shard_map/ppermute | solution.py:136
  155.4 4.3 %place.2.rest_4_ = f32[2048,1024]{1,0:T(8,128)} custom-call(s32[2,16]{1,0:T(2,128)S(1)} %copy-done.11, f32[2,512,512]{2,1,0:T(8,128)S(1)} %copy-done, f32[256,512]{1,0:T(8,128)S(1)} %add.106.rest_0_, f32[256,512]{1,0:T(8,128)S(1)} %copy-done.6, f32[256,512]{1,0:T(8,128)S(1)} %add.109.rest_2_, f32[256,512]{1,0:T(8,128)S(1)} %collective-permute-done.18.rest_3_), custom_call_target="tpu_custom_call" | custom-call | flops 805306368 | bytes 8388608 | tf_op jit(solution)/shard_map/place/pallas_call | solution.py:410
  159.9 1.3 collective-permute-start.28
  161.9 11.1 %collective-permute-done.28.rest_3_ = f32[256,512]{1,0:T(8,128)S(1)} collective-permute-done((f32[256,512]{1,0:T(8,128)S(1)}, f32[256,512]{1,0:T(8,128)S(1)}, u32[]{:S(2)}, u32[]{:S(2)}) %collective-permute-start.28) | collective-permute-done | bytes 524320 | tf_op jit(solution)/shard_map/ppermute | solution.py:136
  175.1 7.1 %collective-permute-done.30 = f32[128,512]{1,0:T(8,128)} collective-permute-done((f32[128,512]{1,0:T(8,128)S(1)}, f32[128,512]{1,0:T(8,128)}, u32[]{:S(2)}, u32[]{:S(2)}) %collective-permute-start.30) | collective-permute-done | bytes 262176 | tf_op jit(solution)/shard_map/ppermute | solution.py:136
  182.2 1.7 broadcast_select_fusion.4
  186.0 2.7 %place.3 = f32[2048,1024]{1,0:T(8,128)} custom-call(s32[2,16]{1,0:T(2,128)S(1)} %copy-done.11, f32[2,512,512]{2,1,0:T(8,128)S(1)} %copy-done, f32[256,512]{1,0:T(8,128)S(1)} %add.111.rest_0_, f32[256,512]{1,0:T(8,128)S(1)} %copy-done.8, f32[256,512]{1,0:T(8,128)S(1)} %add.120.rest_2_, f32[256,512]{1,0:T(8,128)S(1)} %copy-done.10, ...), custom_call_target="tpu_custom_call", output_to_operand_aliasing={{}: (6, {})} | custom-call | flops 805306368 | bytes 8388608 | tf_op jit(solution)/shard_map/place/pallas_call | solution.py:410
  188.7 3.8 %collective-permute-done.31 = f32[128,512]{1,0:T(8,128)S(1)} collective-permute-done((f32[128,512]{1,0:T(8,128)}, f32[128,512]{1,0:T(8,128)S(1)}, u32[]{:S(2)}, u32[]{:S(2)}) %collective-permute-start.31) | collective-permute-done | bytes 262176 | tf_op jit(solution)/shard_map/ppermute | solution.py:136
  194.3 9.4 %collective-permute-done.32 = f32[256,512]{1,0:T(8,128)S(1)} collective-permute-done((f32[256,512]{1,0:T(8,128)}, f32[256,512]{1,0:T(8,128)S(1)}, u32[]{:S(2)}, u32[]{:S(2)}) %collective-permute-start.32) | collective-permute-done | bytes 524320 | tf_op jit(solution)/shard_map/ppermute | solution.py:136
  203.9 2.6 %collective-permute-done.33.rest_1_ = f32[512,512]{1,0:T(8,128)S(1)} collective-permute-done((f32[512,512]{1,0:T(8,128)S(1)}, f32[512,512]{1,0:T(8,128)S(1)}, u32[]{:S(2)}, u32[]{:S(2)}) %collective-permute-start.33) | collective-permute-done | bytes 1048608 | tf_op jit(solution)/shard_map/ppermute | solution.py:87
  206.6 5.1 %diagonal.1 = f32[2,512,512]{2,1,0:T(8,128)} custom-call(f32[2,512]{1,0:T(2,128)S(1)} %copy-done.13, f32[2,512,512]{2,1,0:T(8,128)S(1)} %copy-done, f32[512,512]{1,0:T(8,128)S(1)} %pad_maximum_fusion.1.rest_0_, f32[512,512]{1,0:T(8,128)S(1)} %collective-permute-done.33.rest_1_), custom_call_target="tpu_custom_call" | custom-call | flops 3221225472 | bytes 8388608 | tf_op jit(solution)/shard_map/diagonal/pallas_call | solution.py:449
  (104 shorter events, 26.5 us)
Async XLA Ops:
  0.6 7.2 %copy-start.11 = (s32[2,16]{1,0:T(2,128)S(1)}, s32[2,16]{1,0:T(2,128)}, u32[]{:S(2)}) copy-start(s32[2,16]{1,0:T(2,128)} %tiles_ref.7) | copy-start | bytes 388
  0.6 7.2 %copy-start.12 = (s32[2,16]{1,0:T(2,128)S(1)}, s32[2,16]{1,0:T(2,128)}, u32[]{:S(2)}) copy-start(s32[2,16]{1,0:T(2,128)} %valid_ref.3) | copy-start | bytes 388
  2.0 17.2 %collective-permute-start.2 = (f32[512,512]{1,0:T(8,128)S(1)}, f32[512,512]{1,0:T(8,128)}, u32[]{:S(2)}, u32[]{:S(2)}) collective-permute-start(f32[512,512]{1,0:T(8,128)S(1)} %slice.19.factor), channel_id=1, source_target_pairs={{0,8},{4,20},{9,1},{13,29},{18,26}} | collective-permute-start | bytes 3145736 | tf_op jit(solution)/shard_map/ppermute | solution.py:136
  13.9 8.4 %collective-permute-start.1 = (f32[512,512]{1,0:T(8,128)}, f32[512,512]{1,0:T(8,128)}, u32[]{:S(2)}, u32[]{:S(2)}) collective-permute-start(f32[512,512]{1,0:T(8,128)} %get-tuple-element.67), channel_id=1, source_target_pairs={{4,0},{0,4},{12,8},{8,12},{20,16},{16,20},{28,24},{24,28},{5,1},{1... | collective-permute-start | bytes 3145736 | tf_op jit(solution)/shard_map/ppermute | solution.py:87
  21.0 13.6 %collective-permute-start.4 = (f32[512,512]{1,0:T(8,128)S(1)}, f32[512,512]{1,0:T(8,128)S(1)}, u32[]{:S(2)}, u32[]{:S(2)}) collective-permute-start(f32[512,512]{1,0:T(8,128)S(1)} %get-tuple-element.69), channel_id=1, source_target_pairs={{0,16},{8,24},{4,12},{20,28},{9,25},{1,17},{29,21},{22,30}} | collective-permute-start | bytes 3145736 | tf_op jit(solution)/shard_map/ppermute | solution.py:136
  23.7 16.7 %collective-permute-start.3 = (f32[512,512]{1,0:T(8,128)S(1)}, f32[512,512]{1,0:T(8,128)S(1)}, u32[]{:S(2)}, u32[]{:S(2)}) collective-permute-start(f32[512,512]{1,0:T(8,128)S(1)} %add.97), channel_id=1, source_target_pairs={{16,0},{24,8},{12,4},{28,20},{25,9},{17,1},{21,29},{30,22}} | collective-permute-start | bytes 3145736 | tf_op jit(solution)/shard_map/ppermute | solution.py:136
  29.2 17.8 %collective-permute-start = (f32[512,512]{1,0:T(8,128)S(1)}, f32[512,512]{1,0:T(8,128)S(1)}, u32[]{:S(2)}, u32[]{:S(2)}) collective-permute-start(f32[512,512]{1,0:T(8,128)S(1)} %get-tuple-element.63), channel_id=1, source_target_pairs={{4,0},{0,4},{12,8},{8,12},{20,16},{16,20},{28,24},{24,28},{5,1},{1... | collective-permute-start | bytes 3145736 | tf_op jit(solution)/shard_map/ppermute | solution.py:87
  34.8 12.5 %copy-start.16 = (f32[512,512]{1,0:T(8,128)}, f32[512,512]{1,0:T(8,128)S(1)}, u32[]{:S(2)}) copy-start(f32[512,512]{1,0:T(8,128)S(1)} %add.99.rest_0_) | copy-start | bytes 3145732
  34.8 12.5 %collective-permute-start.5 = (f32[512,512]{1,0:T(8,128)S(1)}, f32[512,512]{1,0:T(8,128)S(1)}, u32[]{:S(2)}, u32[]{:S(2)}) collective-permute-start(f32[512,512]{1,0:T(8,128)S(1)} %add.99.rest_0_), channel_id=1, source_target_pairs={{4,0},{0,4},{12,8},{8,12},{20,16},{16,20},{28,24},{24,28},{5,1},{1... | collective-permute-start | bytes 3145736 | tf_op jit(solution)/shard_map/ppermute | solution.py:87
  40.7 6.7 %copy-start.17 = (f32[512,512]{1,0:T(8,128)}, f32[512,512]{1,0:T(8,128)S(1)}, u32[]{:S(2)}) copy-start(f32[512,512]{1,0:T(8,128)S(1)} %add.98.mirror) | copy-start | bytes 3145732
  40.7 7.6 %copy-start.2 = (bf16[512,1024]{1,0:T(8,128)(2,1)S(1)}, bf16[512,1024]{1,0:T(8,128)(2,1)}, u32[]{:S(2)}) copy-start(bf16[512,1024]{1,0:T(8,128)(2,1)} %copy-done.1) | copy-start | bytes 3145732
  40.7 17.1 %collective-permute-start.6 = (f32[512,512]{1,0:T(8,128)S(1)}, f32[512,512]{1,0:T(8,128)S(1)}, u32[]{:S(2)}, u32[]{:S(2)}) collective-permute-start(f32[512,512]{1,0:T(8,128)S(1)} %add.98.mirror), channel_id=1, source_target_pairs={{8,0},{20,4},{1,9},{29,13},{26,18}} | collective-permute-start | bytes 3145736 | tf_op jit(solution)/shard_map/ppermute | solution.py:136
  42.1 18.5 %collective-permute-start.8 = (f32[512,512]{1,0:T(8,128)S(1)}, f32[512,512]{1,0:T(8,128)S(1)}, u32[]{:S(2)}, u32[]{:S(2)}) collective-permute-start(f32[512,512]{1,0:T(8,128)S(1)} %get-tuple-element.72.factor), channel_id=1, source_target_pairs={{0,8},{4,20},{9,1},{13,29},{18,26}} | collective-permute-start | bytes 3145736 | tf_op jit(solution)/shard_map/ppermute | solution.py:136
  53.8 7.0 %copy-start.3 = (f32[256,512]{1,0:T(8,128)}, f32[256,512]{1,0:T(8,128)S(1)}, u32[]{:S(2)}) copy-start(f32[256,512]{1,0:T(8,128)S(1)} %get-tuple-element.101) | copy-start | bytes 1572868
  53.8 6.8 %copy-start.14 = (f32[512,1024]{1,0:T(8,128)S(1)}, f32[512,1024]{1,0:T(8,128)}, u32[]{:S(2)}) copy-start(f32[512,1024]{1,0:T(8,128)} %param.7) | copy-start | bytes 6291460
  60.8 13.6 %collective-permute-start.9 = (f32[512,512]{1,0:T(8,128)S(1)}, f32[512,512]{1,0:T(8,128)S(1)}, u32[]{:S(2)}, u32[]{:S(2)}) collective-permute-start(f32[512,512]{1,0:T(8,128)S(1)} %broadcast_select_fusion), channel_id=1, source_target_pairs={{0,16},{8,24},{4,12},{20,28},{9,25},{1,17},{29,21},{22,30}} | collective-permute-start | bytes 3145736 | tf_op jit(solution)/shard_map/ppermute | solution.py:136
  62.2 16.7 %collective-permute-start.10 = (f32[512,512]{1,0:T(8,128)S(1)}, f32[512,512]{1,0:T(8,128)S(1)}, u32[]{:S(2)}, u32[]{:S(2)}) collective-permute-start(f32[512,512]{1,0:T(8,128)S(1)} %add.96), channel_id=1, source_target_pairs={{16,0},{24,8},{12,4},{28,20},{25,9},{17,1},{21,29},{30,22}} | collective-permute-start | bytes 3145736 | tf_op jit(solution)/shard_map/ppermute | solution.py:136
  63.5 9.9 %collective-permute-start.7 = (f32[256,512]{1,0:T(8,128)S(1)}, f32[256,512]{1,0:T(8,128)S(1)}, u32[]{:S(2)}, u32[]{:S(2)}) collective-permute-start(f32[256,512]{1,0:T(8,128)S(1)} %get-tuple-element.125), channel_id=1, source_target_pairs={{0,1},{3,2},{4,5},{7,6},{8,9},{11,10},{12,13},{15,14},{16,17},{19,... | collective-permute-start | bytes 1572872 | tf_op jit(solution)/shard_map/ppermute | solution.py:136
  79.1 9.3 %collective-permute-start.11 = (f32[512,512]{1,0:T(8,128)S(1)}, f32[512,512]{1,0:T(8,128)S(1)}, u32[]{:S(2)}, u32[]{:S(2)}) collective-permute-start(f32[512,512]{1,0:T(8,128)S(1)} %add.103.rest_0_), channel_id=1, source_target_pairs={{4,0},{0,4},{12,8},{8,12},{20,16},{16,20},{28,24},{24,28},{5,1},{1... | collective-permute-start | bytes 3145736 | tf_op jit(solution)/shard_map/ppermute | solution.py:87
  80.4 17.9 %collective-permute-start.14 = (f32[512,512]{1,0:T(8,128)}, f32[512,512]{1,0:T(8,128)}, u32[]{:S(2)}, u32[]{:S(2)}) collective-permute-start(f32[512,512]{1,0:T(8,128)} %add.102.mirror), channel_id=1, source_target_pairs={{8,0},{20,4},{1,9},{29,13},{26,18}} | collective-permute-start | bytes 3145736 | tf_op jit(solution)/shard_map/ppermute | solution.py:136
  81.7 12.8 %collective-permute-start.23 = (f32[256,512]{1,0:T(8,128)}, f32[256,512]{1,0:T(8,128)}, u32[]{:S(2)}, u32[]{:S(2)}) collective-permute-start(f32[256,512]{1,0:T(8,128)} %get-tuple-element.102), channel_id=1, source_target_pairs={{4,0},{0,4},{12,8},{8,12},{20,16},{16,20},{28,24},{24,28},{5,1},{1... | collective-permute-start | bytes 1572872 | tf_op jit(solution)/shard_map/ppermute | solution.py:87
  82.3 16.0 %collective-permute-start.13 = (f32[256,512]{1,0:T(8,128)}, f32[256,512]{1,0:T(8,128)}, u32[]{:S(2)}, u32[]{:S(2)}) collective-permute-start(f32[256,512]{1,0:T(8,128)} %get-tuple-element.81), channel_id=1, source_target_pairs={{0,1},{3,2},{4,5},{7,6},{8,9},{11,10},{12,13},{15,14},{16,17},{19,... | collective-permute-start | bytes 1572872 | tf_op jit(solution)/shard_map/ppermute | solution.py:136
  86.9 11.4 %collective-permute-start.12 = (f32[256,512]{1,0:T(8,128)S(1)}, f32[256,512]{1,0:T(8,128)}, u32[]{:S(2)}, u32[]{:S(2)}) collective-permute-start(f32[256,512]{1,0:T(8,128)S(1)} %add.104), channel_id=1, source_target_pairs={{1,2},{2,1},{5,6},{6,5},{9,10},{10,9},{13,14},{14,13},{17,18},{18,... | collective-permute-start | bytes 1572872 | tf_op jit(solution)/shard_map/ppermute | solution.py:136
  94.1 18.9 %collective-permute-start.24 = (f32[256,512]{1,0:T(8,128)S(1)}, f32[256,512]{1,0:T(8,128)}, u32[]{:S(2)}, u32[]{:S(2)}) collective-permute-start(f32[256,512]{1,0:T(8,128)S(1)} %get-tuple-element.104), channel_id=1, source_target_pairs={{4,0},{0,4},{12,8},{8,12},{20,16},{16,20},{28,24},{24,28},{5,1},{1... | collective-permute-start | bytes 1572872 | tf_op jit(solution)/shard_map/ppermute | solution.py:87
  101.6 16.6 %collective-permute-start.15 = (f32[256,512]{1,0:T(8,128)S(1)}, f32[256,512]{1,0:T(8,128)S(1)}, u32[]{:S(2)}, u32[]{:S(2)}) collective-permute-start(f32[256,512]{1,0:T(8,128)S(1)} %add.106.rest_0_), channel_id=1, source_target_pairs={{1,0},{2,3},{5,4},{6,7},{9,8},{10,11},{13,12},{14,15},{17,16},{18,... | collective-permute-start | bytes 1572872 | tf_op jit(solution)/shard_map/ppermute | solution.py:136
  102.8 15.4 %collective-permute-start.16 = (f32[256,512]{1,0:T(8,128)}, f32[256,512]{1,0:T(8,128)}, u32[]{:S(2)}, u32[]{:S(2)}) collective-permute-start(f32[256,512]{1,0:T(8,128)} %add.107), channel_id=1, source_target_pairs={{1,2},{2,1},{5,6},{6,5},{9,10},{10,9},{13,14},{14,13},{17,18},{18,... | collective-permute-start | bytes 1572872 | tf_op jit(solution)/shard_map/ppermute | solution.py:136
  106.7 17.6 %collective-permute-start.17 = (f32[256,512]{1,0:T(8,128)}, f32[256,512]{1,0:T(8,128)S(1)}, u32[]{:S(2)}, u32[]{:S(2)}) collective-permute-start(f32[256,512]{1,0:T(8,128)} %get-tuple-element.88), channel_id=1, source_target_pairs={{0,1},{3,2},{4,5},{7,6},{8,9},{11,10},{12,13},{15,14},{16,17},{19,... | collective-permute-start | bytes 1572872 | tf_op jit(solution)/shard_map/ppermute | solution.py:136
  114.2 12.5 %copy-start.18 = (f32[256,512]{1,0:T(8,128)S(1)}, f32[256,512]{1,0:T(8,128)}, u32[]{:S(2)}) copy-start(f32[256,512]{1,0:T(8,128)} %get-tuple-element.95) | copy-start | bytes 1572868
  115.1 18.1 %collective-permute-start.25 = (f32[256,512]{1,0:T(8,128)}, f32[256,512]{1,0:T(8,128)}, u32[]{:S(2)}, u32[]{:S(2)}) collective-permute-start(f32[256,512]{1,0:T(8,128)} %dynamic-slice_bitcast_fusion), channel_id=1, source_target_pairs={{0,8},{1,9},{2,10},{3,11},{4,20},{5,21},{6,22},{7,23},{8,0},{9,1},... | collective-permute-start | bytes 1572872 | tf_op jit(solution)/shard_map/ppermute | solution.py:136
  118.2 16.1 %copy-start.5 = (f32[256,512]{1,0:T(8,128)}, f32[256,512]{1,0:T(8,128)S(1)}, u32[]{:S(2)}) copy-start(f32[256,512]{1,0:T(8,128)S(1)} %collective-permute-done.15.rest_1_) | copy-start | bytes 1572868
  126.7 19.5 %copy-start.19 = (f32[256,512]{1,0:T(8,128)S(1)}, f32[256,512]{1,0:T(8,128)}, u32[]{:S(2)}) copy-start(f32[256,512]{1,0:T(8,128)} %get-tuple-element.95) | copy-start | bytes 1572868
  126.7 14.5 %collective-permute-start.20 = (f32[256,512]{1,0:T(8,128)S(1)}, f32[256,512]{1,0:T(8,128)S(1)}, u32[]{:S(2)}, u32[]{:S(2)}) collective-permute-start(f32[256,512]{1,0:T(8,128)S(1)} %copy-done.18), channel_id=1, source_target_pairs={{0,1},{3,2},{4,5},{7,6},{8,9},{11,10},{12,13},{15,14},{16,17},{19,... | collective-permute-start | bytes 1572872 | tf_op jit(solution)/shard_map/ppermute | solution.py:136
  131.2 10.0 %collective-permute-start.19 = (f32[256,512]{1,0:T(8,128)S(1)}, f32[256,512]{1,0:T(8,128)S(1)}, u32[]{:S(2)}, u32[]{:S(2)}) collective-permute-start(f32[256,512]{1,0:T(8,128)S(1)} %add.108), channel_id=1, source_target_pairs={{1,2},{2,1},{5,6},{6,5},{9,10},{10,9},{13,14},{14,13},{17,18},{18,... | collective-permute-start | bytes 1572872 | tf_op jit(solution)/shard_map/ppermute | solution.py:136
  131.9 14.2 %collective-permute-start.18 = (f32[256,512]{1,0:T(8,128)S(1)}, f32[256,512]{1,0:T(8,128)S(1)}, u32[]{:S(2)}, u32[]{:S(2)}) collective-permute-start(f32[256,512]{1,0:T(8,128)S(1)} %add.109.rest_2_), channel_id=1, source_target_pairs={{1,0},{2,3},{5,4},{6,7},{9,8},{10,11},{13,12},{14,15},{17,16},{18,... | collective-permute-start | bytes 1572872 | tf_op jit(solution)/shard_map/ppermute | solution.py:136
  134.4 21.0 %copy-start = (f32[2,512,512]{2,1,0:T(8,128)S(1)}, f32[2,512,512]{2,1,0:T(8,128)}, u32[]{:S(2)}) copy-start(f32[2,512,512]{2,1,0:T(8,128)} %unit_ref.5) | copy-start | bytes 6291460
  134.4 21.0 %copy-start.6 = (f32[256,512]{1,0:T(8,128)S(1)}, f32[256,512]{1,0:T(8,128)}, u32[]{:S(2)}) copy-start(f32[256,512]{1,0:T(8,128)} %copy-done.5) | copy-start | bytes 1572868
  134.4 13.8 %collective-permute-start.26 = (f32[128,512]{1,0:T(8,128)S(1)}, f32[128,512]{1,0:T(8,128)S(1)}, u32[]{:S(2)}, u32[]{:S(2)}) collective-permute-start(f32[128,512]{1,0:T(8,128)S(1)} %dynamic-slice_bitcast_fusion.1), channel_id=1, source_target_pairs={{0,16},{1,17},{2,18},{3,19},{4,12},{5,13},{6,14},{7,15},{8,24},{9,... | collective-permute-start | bytes 786440 | tf_op jit(solution)/shard_map/ppermute | solution.py:136
  146.2 13.5 %collective-permute-start.21 = (f32[256,512]{1,0:T(8,128)S(1)}, f32[256,512]{1,0:T(8,128)S(1)}, u32[]{:S(2)}, u32[]{:S(2)}) collective-permute-start(f32[256,512]{1,0:T(8,128)S(1)} %add.111.rest_0_), channel_id=1, source_target_pairs={{1,0},{2,3},{5,4},{6,7},{9,8},{10,11},{13,12},{14,15},{17,16},{18,... | collective-permute-start | bytes 1572872 | tf_op jit(solution)/shard_map/ppermute | solution.py:136
  147.5 12.3 %collective-permute-start.22 = (f32[256,512]{1,0:T(8,128)S(1)}, f32[256,512]{1,0:T(8,128)S(1)}, u32[]{:S(2)}, u32[]{:S(2)}) collective-permute-start(f32[256,512]{1,0:T(8,128)S(1)} %add.112), channel_id=1, source_target_pairs={{1,2},{2,1},{5,6},{6,5},{9,10},{10,9},{13,14},{14,13},{17,18},{18,... | collective-permute-start | bytes 1572872 | tf_op jit(solution)/shard_map/ppermute | solution.py:136
  148.3 11.5 %collective-permute-start.27 = (f32[128,512]{1,0:T(8,128)S(1)}, f32[128,512]{1,0:T(8,128)S(1)}, u32[]{:S(2)}, u32[]{:S(2)}) collective-permute-start(f32[128,512]{1,0:T(8,128)S(1)} %bitcast_add_fusion.1), channel_id=1, source_target_pairs={{0,1},{3,2},{4,5},{7,6},{8,9},{11,10},{12,13},{15,14},{16,17},{19,... | collective-permute-start | bytes 786440 | tf_op jit(solution)/shard_map/ppermute | solution.py:136
  159.8 13.2 %copy-start.7 = (f32[256,512]{1,0:T(8,128)}, f32[256,512]{1,0:T(8,128)S(1)}, u32[]{:S(2)}) copy-start(f32[256,512]{1,0:T(8,128)S(1)} %collective-permute-done.21.rest_1_) | copy-start | bytes 1572868
  159.9 13.1 %collective-permute-start.28 = (f32[256,512]{1,0:T(8,128)S(1)}, f32[256,512]{1,0:T(8,128)S(1)}, u32[]{:S(2)}, u32[]{:S(2)}) collective-permute-start(f32[256,512]{1,0:T(8,128)S(1)} %add.120.rest_2_), channel_id=1, source_target_pairs={{1,0},{2,3},{5,4},{6,7},{9,8},{10,11},{13,12},{14,15},{17,16},{18,... | collective-permute-start | bytes 1572872 | tf_op jit(solution)/shard_map/ppermute | solution.py:136
  161.2 0.7 collective-permute-start.29
  173.8 8.4 %collective-permute-start.30 = (f32[128,512]{1,0:T(8,128)S(1)}, f32[128,512]{1,0:T(8,128)}, u32[]{:S(2)}, u32[]{:S(2)}) collective-permute-start(f32[128,512]{1,0:T(8,128)S(1)} %add.122), channel_id=1, source_target_pairs={{1,0},{2,3},{5,4},{6,7},{9,8},{10,11},{13,12},{14,15},{17,16},{18,... | collective-permute-start | bytes 786440 | tf_op jit(solution)/shard_map/ppermute | solution.py:136
  183.9 8.5 %collective-permute-start.31 = (f32[128,512]{1,0:T(8,128)}, f32[128,512]{1,0:T(8,128)S(1)}, u32[]{:S(2)}, u32[]{:S(2)}) collective-permute-start(f32[128,512]{1,0:T(8,128)} %broadcast_select_fusion.4), channel_id=1, source_target_pairs={{0,16},{1,17},{2,18},{3,19},{4,12},{5,13},{6,14},{7,15},{8,24},{9,... | collective-permute-start | bytes 786440 | tf_op jit(solution)/shard_map/ppermute | solution.py:136
  194.3 9.4 %collective-permute-start.32 = (f32[256,512]{1,0:T(8,128)}, f32[256,512]{1,0:T(8,128)S(1)}, u32[]{:S(2)}, u32[]{:S(2)}) collective-permute-start(f32[256,512]{1,0:T(8,128)} %pad_maximum_fusion.2), channel_id=1, source_target_pairs={{0,8},{1,9},{2,10},{3,11},{4,20},{5,21},{6,22},{7,23},{8,0},{9,1},... | collective-permute-start | bytes 1572872 | tf_op jit(solution)/shard_map/ppermute | solution.py:136
  194.3 12.3 %copy-start.13 = (f32[2,512]{1,0:T(2,128)S(1)}, f32[2,512]{1,0:T(2,128)}, u32[]{:S(2)}) copy-start(f32[2,512]{1,0:T(2,128)} %pivot.1) | copy-start | bytes 12292
  203.8 2.7 %collective-permute-start.33 = (f32[512,512]{1,0:T(8,128)S(1)}, f32[512,512]{1,0:T(8,128)S(1)}, u32[]{:S(2)}, u32[]{:S(2)}) collective-permute-start(f32[512,512]{1,0:T(8,128)S(1)} %pad_maximum_fusion.1.rest_0_), channel_id=1, source_target_pairs={{4,0},{0,4},{12,8},{8,12},{20,16},{16,20},{28,24},{24,28},{5,1},{1... | collective-permute-start | bytes 3145736 | tf_op jit(solution)/shard_map/ppermute | solution.py:87
  (8 other events, 14.1 us)

commit v5 on v4

--- a/solution.py
+++ b/solution.py
@@ -115,6 +115,25 @@
             for lane, order in enumerate(self.orders)
             for col in range(self.cols)
         ]
+
+    def offset_pairs(self, offset):
+        pairs = []
+        for lane, order in enumerate(self.orders):
+            flip = sum(
+                bit for step, bit in enumerate(order) if offset >> (self.steps - 1 - step) & 1
+            )
+            for chip in range(self.cols):
+                for col in range(self.cols):
+                    pairs.append(
+                        (self.device(chip, lane, col), self.device(chip ^ flip, lane, col))
+                    )
+        return pairs
+
+    def place_of(self, lane):
+        chip, place = lax.axis_index("row") // self.lanes, jnp.int32(0)
+        for step, bit in enumerate(self.orders[lane]):
+            place = jnp.where((chip & bit) != 0, place + (1 << (self.steps - 1 - step)), place)
+        return place
 
     def bit(self, step):
         row = lax.axis_index("row")
@@ -183,9 +202,10 @@
         mirror[b // na][first:first + size, :] = product(left, right, contract=0)
 
 
-def forward_kernel(plan, high, low, factor, mirror, *rest):
+def forward_kernel(plan, member, high, low, factor, mirror, *rest):
     lanes, size, depth = plan.lanes, plan.tile, plan.depth
     parts, rest = rest[:lanes], rest[lanes:]
+    earlier, rest = rest[:lanes * bool(member)], rest[lanes * bool(member):]
     totals, rest = rest[:SPLIT], rest[SPLIT:]
     cross, (total, whole) = rest[:lanes], rest[lanes:]
     right = [split(part[...]) for part in parts]
@@ -208,7 +228,9 @@
     lane = lax.rem(lax.axis_index("row"), lanes)
     for i in range(lanes):
         first = pl.multiple_of(lax.rem(lane + i, lanes) * share, share)
-        cross[i][...] = whole[pl.ds(first, share), :]
+        cross[i][member * share:, :] = whole[pl.ds(first, share), :]
+        if member:
+            cross[i][:member * share, :] = earlier[i][...]
 
 
 def place_kernel(plan, member, tiles_ref, unit_ref, *rest):
@@ -261,21 +283,27 @@
 
 
 def diagonal_kernel(plan, pivot, unit_ref, *rest):
-    parts, out = rest[:plan.lanes], rest[plan.lanes]
-    width, lanes = plan.width, plan.lanes
+    parts, (out, cross) = rest[:plan.lanes], rest[plan.lanes:]
+    width, lanes, members = plan.width, plan.lanes, plan.members
+    lane = lax.rem(lax.axis_index("row"), lanes)
+    count = 1 << plan.steps
+    size = members * width // (lanes * count)
+    for other in range(lanes):
+        mine = plan.place_of(other)
+        for place in range(count):
+            first = pl.multiple_of((mine ^ place) * size, size)
+            piece = parts[0][pl.ds(first, size), :]
+            for i in range(1, lanes):
+                piece = jnp.where(
+                    lax.rem(lane + i, lanes) == other, parts[i][pl.ds(first, size), :], piece
+                )
+            cross[other, place * size:(place + 1) * size, :] = piece
     share = width // lanes
-    lane = lax.rem(lax.axis_index("row"), lanes)
     row = lax.broadcasted_iota(jnp.int32, (width, width), 0)
     col = lax.broadcasted_iota(jnp.int32, (width, width), 1)
-    for member in range(plan.members):
+    for member in range(members):
         rows = slice(member * share, (member + 1) * share)
-        pieces = []
-        for other in range(lanes):
-            piece = parts[0][rows, :]
-            for i in range(1, lanes):
-                piece = jnp.where(lax.rem(lane + i, lanes) == other, parts[i][rows, :], piece)
-            pieces.append(piece)
-        x = jnp.concatenate(pieces)
+        x = jnp.concatenate([cross[other, rows, :] for other in range(lanes)])
         x = jnp.where(row == col, pivot[member:member + 1, :], 0.0) + x + x.T
         inverse = split(unit_inverse(unit_ref, member))
         half = product(split(x), inverse)
@@ -316,14 +344,14 @@
             name="gather_mirror",
         )(tile_list, tile_valid, inverse_front, factors[member])
 
-    def forward(high, low, own, mirror, held):
+    def forward(member, high, low, mirror, held, earlier):
         parts = [held] + [plan.swap(held, shift) for shift in range(1, lanes)]
         outs = pl.pallas_call(
-            functools.partial(forward_kernel, plan),
-            in_specs=vmem(4 + lanes),
+            functools.partial(forward_kernel, plan, member),
+            in_specs=vmem(4 + lanes + len(earlier)),
             out_specs=vmem(SPLIT + lanes),
             out_shape=[jax.ShapeDtypeStruct((share, width), F32)] * SPLIT
-            + [jax.ShapeDtypeStruct((width // lanes, width), F32)] * lanes,
+            + [jax.ShapeDtypeStruct(((member + 1) * width // lanes, width), F32)] * lanes,
             scratch_shapes=[
                 pltpu.VMEM((depth, width), F32),
                 pltpu.VMEM((width, width), F32),
@@ -331,45 +359,46 @@
             compiler_params=PARAMS,
             cost_estimate=pl.CostEstimate(flops=flops, bytes_accessed=8 << 20, transcendentals=0),
             name="forward",
-        )(high, low, own, mirror, *parts)
-        return outs[:SPLIT], outs[SPLIT:]
-
-    line, hops = Chain(), plan.line_hops()
-    chunks, ends, phase_now = [], [], [0]
-
-    def line_phase(after=(), beside=()):
-        phase = phase_now[0]
-        live = [i for i in range(len(chunks)) if 0 <= phase - i < len(hops)]
-        brought = line.issue(
-            *((chunks[i], "col", hops[phase - i]) for i in live), after=after
-        )
-        brought, beside = lax.optimization_barrier((brought, beside))
-        line.last = tuple(brought)
-        ends.extend([None] * (len(chunks) - len(ends)))
-        for i, got in zip(live, brought):
-            if phase - i < len(hops) - 1 or len(hops) == 1:
-                chunks[i] = plan.line_step(phase - i, chunks[i], got)
-            ends[i] = got if len(hops) > 1 else chunks[i]
-        phase_now[0] += 1
-        return beside
-
-    plane = Chain()
+        )(high, low, factors[member], mirror, *parts, *earlier)
+        return outs[:SPLIT], outs[SPLIT:], parts[-1]
+
+    hops = plan.line_hops()
+
+    def enter(x, after=()):
+        if after:
+            x, _ = lax.optimization_barrier((x, tuple(after)))
+        return lax.ppermute(x, "col", hops[0])
+
+    def run(x, got, before_last=()):
+        for hop in range(1, len(hops)):
+            x = plan.line_step(hop - 1, x, got)
+            sent = x
+            if hop == len(hops) - 1 and before_last:
+                sent, _ = lax.optimization_barrier((x, tuple(before_last)))
+            got = lax.ppermute(sent, "col", hops[hop])
+        if len(hops) == 1:
+            got = x = x + got
+        return x, got
+
+    spread, collect = Chain(), Chain()
     count = members * steps
-    tiles, held, mirror, crosses = {}, {}, {}, []
-    after = ()
+    tiles, held, mirror, chunks, entered = {}, {}, {}, [], {}
+    after, cross, last_swap = (), [], None
     for phase in range(count + 1):
-        requests = []
         if phase < count:
             out, step = divmod(phase, steps)
             x = factors[out] if step == 0 else held[out]
-            requests.append((x, both, plan.tree(step)))
+            got_out, = spread.issue((x, both, plan.tree(step)), after=after)
         if phase:
             back, turn = divmod(phase - 1, steps)
-            requests.append((mirror[back], both, reverse(plan.tree(steps - 1 - turn))))
-        brought = plane.issue(*requests, after=after)
-        if chunks:
-            brought = line_phase(beside=brought)
-            plane.last = tuple(brought)
+            got_back, = collect.issue(
+                (mirror[back], both, reverse(plan.tree(steps - 1 - turn))), after=after
+            )
+        if chunks and 0 not in entered:
+            entered[0] = enter(chunks[0])
+            entered[0], got_out, got_back = lax.optimization_barrier(
+                (entered[0], got_out, got_back)
+            )
         after = ()
         if phase % steps == 0 and phase < count:
             high, low, *parts = gather(out) if out == 0 else tiles[out]
@@ -379,29 +408,27 @@
             tiles[out + 1] = gather(out + 1)
             after = (tiles[out + 1][0],)
         if phase < count:
-            got = brought[0]
-            held[out] = jnp.where(plan.on_diagonal(), x, got) if step == 0 else x + got
+            held[out] = jnp.where(plan.on_diagonal(), x, got_out) if step == 0 else x + got_out
         if phase:
             if turn < steps - 1:
-                mirror[back] = mirror[back] + brought[-1]
+                mirror[back] = mirror[back] + got_back
             else:
-                sums, cross = forward(*tiles[back], factors[back], mirror[back], held[back])
-                new = [
-                    part + brought[-1][i * share:(i + 1) * share] for i, part in enumerate(sums)
+                sums, cross, last_swap = forward(
+                    back, *tiles[back], mirror[back], held[back], cross
+                )
+                chunks += [
+                    part + got_back[i * share:(i + 1) * share] for i, part in enumerate(sums)
                 ]
-                chunks += new
-                after = tuple(new)
-                crosses.append(cross)
-
-    x = jnp.concatenate([lane_sum(cross) for cross in crosses])
+                after = tuple(chunks[-SPLIT:])
+
+    x, _ = lax.optimization_barrier((lane_sum(cross), tuple(chunks[-SPLIT:])))
     for step in range(steps):
         x = x.reshape(2, x.shape[0] // 2, x.shape[1])
         bit = plan.bit(step)
         send = lax.dynamic_index_in_dim(x, 1 - bit, 0, keepdims=False)
         keep = lax.dynamic_index_in_dim(x, bit, 0, keepdims=False)
-        got, = plane.issue((send, both, plan.bit_pairs(step)))
-        x = keep + got
-    chunks.append(x)
+        x = keep + lax.ppermute(send, both, plan.bit_pairs(step))
+    update = x
 
     def place(member, column):
         sums = []
@@ -427,30 +454,34 @@
             name="place",
         )(tile_list, unit_lower, *sums, *([column] if member else []))
 
-    column, placed, after = None, 0, ()
-    while phase_now[0] < len(chunks) + len(hops) - 1:
-        line_phase(after)
-        after = ()
-        if phase_now[0] > (placed + 1) * SPLIT + len(hops) - 1 and placed < members - 1:
-            column = place(placed, column)
-            placed += 1
-            after = (column,)
-    for member in range(placed, members):
-        column = place(member, column)
-
-    x = jnp.where(plan.at_end(), ends[-1], chunks[-1])
-    for step in reversed(range(steps)):
-        got, = plane.issue(
-            (x, both, plan.bit_pairs(step)), after=(column,) if step < steps - 1 else ()
-        )
-        bit = plan.bit(step) == 1
-        x = jnp.concatenate([jnp.where(bit, got, x), jnp.where(bit, x, got)])
+    ends, column = {}, None
+    for i in range(len(chunks)):
+        if i + 1 < len(chunks):
+            if i + 1 < SPLIT:
+                wait = (last_swap, entered[i])
+            elif (i + 1) % SPLIT and i >= SPLIT:
+                wait = (ends[i - SPLIT],)
+            else:
+                wait = ()
+            entered[i + 1] = enter(chunks[i + 1], wait)
+            wait = (entered[i + 1],)
+        else:
+            wait = () if column is None else (column,)
+        chunks[i], ends[i] = run(chunks[i], entered[i], wait)
+        if i % SPLIT == SPLIT - 1:
+            column = place(i // SPLIT, column)
+
+    x, got = run(update, enter(update))
+    x = jnp.where(plan.at_end(), got, x)
+    pieces = [x] + [lax.ppermute(x, both, plan.offset_pairs(r)) for r in range(1, 1 << steps)]
+    x, _ = lax.optimization_barrier((jnp.concatenate(pieces), column))
     parts = [x] + [plan.swap(x, shift) for shift in range(1, lanes)]
     diagonal = pl.pallas_call(
         functools.partial(diagonal_kernel, plan),
         in_specs=vmem(2 + lanes),
         out_specs=vmem(1)[0],
         out_shape=jax.ShapeDtypeStruct(unit_lower.shape, F32),
+        scratch_shapes=[pltpu.VMEM((lanes, members * width // lanes, width), F32)],
         compiler_params=PARAMS,
         cost_estimate=pl.CostEstimate(
             flops=24 * width * width * width, bytes_accessed=8 << 20, transcendentals=0

time: 213 us -> 198 us (0.930)
  starting transfers between devices: 57.1 us -> 47.4 us
  other arithmetic: 22.3 us -> 15.7 us
  waiting for transfers between devices: 91.3 us -> 95.4 us
  local copies, waits for them, and re-layouts: 8.07 us -> 5.2 us
    ppermute x0 -> x20, waiting for transfers between devices: none -> 63.7 us  [the longest x10 35.5 us: run(): got = lax.ppermute(sent, 'col', hops[hop])]
    ppermute x27 -> x8, waiting for transfers between devices: 88.7 us -> 29.1 us  [issue(): out.append(lax.ppermute(x, axis, pairs))]
    ppermute x27 -> x8, starting transfers between devices: 56.1 us -> 19 us  [issue(): out.append(lax.ppermute(x, axis, pairs))]
    ppermute x0 -> x20, starting transfers between devices: none -> 27.7 us  [the longest x5 14 us: enter(): return lax.ppermute(x, 'col', hops[0])]
    add x10, other arithmetic: 6.06 us -> 2.99 us  [line_step(): return x + got]
    unnamed x44 -> x42, local copies, waits for them, and re-layouts: 5.88 us -> 3.01 us
    select_n x5 -> x3, other arithmetic: 4.91 us -> 3.08 us  [the longest x2 2.08 us: shards(): jnp.where(plan.on_diagonal(), x, got_out)]
  transfers between devices with their start and end apart: 34 -> 34, of which waited for: 18 -> 19; matrix products, arithmetic and copies ran while one was open for 9% -> 8% of each run, Pallas kernels for 13% -> 14%
where the time goes in v5:
time: 198 us; the launch traced here: 197 us
  waiting for transfers between devices  95.4 us (48%)
  starting transfers between devices  47.4 us (24%)
  Pallas kernels  32.1 us (16%)
  other arithmetic  15.7 us (8%)
  local copies, waits for them, and re-layouts  5.2 us (3%)
    ppermute x10, waiting for transfers between devices, run(): got = lax.ppermute(sent, 'col', hops[hop])  35.5 us
    ppermute x8, waiting for transfers between devices, issue(): out.append(lax.ppermute(x, axis, pairs))  29.1 us
    ppermute x5, waiting for transfers between devices, enter(): return lax.ppermute(x, 'col', hops[0])  25.6 us
    ppermute x8, starting transfers between devices, issue(): out.append(lax.ppermute(x, axis, pairs))  19 us
    ppermute x5, starting transfers between devices, enter(): return lax.ppermute(x, 'col', hops[0])  14 us
    ppermute x10, starting transfers between devices, run(): got = lax.ppermute(sent, 'col', hops[hop])  10 us
    pallas_call x2, Pallas kernels, forward(): pl.pallas_call(functools.partial(forward_kernel, plan, member), in_specs=...  9.98 us
    pallas_call x2, Pallas kernels, gather(): pl.pallas_call(functools.partial(gather_kernel, plan, member), in_specs=s...  9.27 us
  transfers between devices with their start and end apart: 34, of which 19 were waited for; matrix products, arithmetic and copies ran while one was open for 8% of the time, Pallas kernels for 14%

profile of v5, /device:TPU:0, one launch (start us, length us, event | category | flops | bytes accessed | tf_op | source)
XLA Modules:
  0.0 197.2 jit_solution(15930370597437646629)
XLA Ops:
  0.6 1.3 slice.19.factor
  2.0 5.8 %collective-permute-start.3 = (f32[512,512]{1,0:T(8,128)S(1)}, f32[512,512]{1,0:T(8,128)}, u32[]{:S(2)}, u32[]{:S(2)}) collective-permute-start(f32[512,512]{1,0:T(8,128)S(1)} %slice.19.factor), channel_id=1, source_target_pairs={{0,8},{4,20},{9,1},{13,29},{18,26}} | collective-permute-start | bytes 3145736 | tf_op jit(solution)/shard_map/ppermute | solution.py:155
  7.8 5.1 %gather_mirror.3 = (bf16[512,1024]{1,0:T(8,128)(2,1)S(1)}, bf16[512,1024]{1,0:T(8,128)(2,1)S(1)}, f32[512,512]{1,0:T(8,128)S(1)}, f32[512,512]{1,0:T(8,128)}) custom-call(s32[2,16]{1,0:T(2,128)S(1)} %copy-done.7, s32[2,16]{1,0:T(2,128)S(1)} %copy-done.8, f32[2048,4096]{1,0:T(8,128)} %front.3, f32[512,512]{1,0:T(8,128)S(1)} %slice.19.factor), custom_call_target="tpu_custom_call" | custom-call | flops 1610612736 | bytes 8388608 | tf_op jit(solution)/shard_map/gather_mirror/pallas_call | solution.py:332
  14.0 5.1 %collective-permute-done.3 = f32[512,512]{1,0:T(8,128)} collective-permute-done((f32[512,512]{1,0:T(8,128)S(1)}, f32[512,512]{1,0:T(8,128)}, u32[]{:S(2)}, u32[]{:S(2)}) %collective-permute-start.3) | collective-permute-done | bytes 1048608 | tf_op jit(solution)/shard_map/ppermute | solution.py:155
  19.1 1.9 broadcast_select_fusion.1
  21.0 1.4 collective-permute-start.4
  22.4 1.4 add.90
  23.8 1.3 collective-permute-start.2
  25.1 4.1 %gather_mirror.2 = (bf16[512,1024]{1,0:T(8,128)(2,1)S(1)}, bf16[512,1024]{1,0:T(8,128)(2,1)S(1)}, f32[512,512]{1,0:T(8,128)S(1)}, f32[512,512]{1,0:T(8,128)S(1)}) custom-call(s32[2,16]{1,0:T(2,128)S(1)} %copy-done.7, s32[2,16]{1,0:T(2,128)S(1)} %copy-done.8, f32[2048,4096]{1,0:T(8,128)} %front.3, f32[512,512]{1,0:T(8,128)S(1)} %get-tuple-element.46.factor), custom_call_target="tpu_custom_call" | custom-call | flops 1610612736 | bytes 8388608 | tf_op jit(solution)/shard_map/gather_mirror/pallas_call | solution.py:332
  29.3 5.3 %collective-permute-done.4 = f32[512,512]{1,0:T(8,128)S(1)} collective-permute-done((f32[512,512]{1,0:T(8,128)S(1)}, f32[512,512]{1,0:T(8,128)S(1)}, u32[]{:S(2)}, u32[]{:S(2)}) %collective-permute-start.4) | collective-permute-done | bytes 1048608 | tf_op jit(solution)/shard_map/ppermute | solution.py:155
  34.9 5.6 %collective-permute-done.2 = f32[512,512]{1,0:T(8,128)S(1)} collective-permute-done((f32[512,512]{1,0:T(8,128)S(1)}, f32[512,512]{1,0:T(8,128)S(1)}, u32[]{:S(2)}, u32[]{:S(2)}) %collective-permute-start.2) | collective-permute-done | bytes 1048608 | tf_op jit(solution)/shard_map/ppermute | solution.py:155
  40.7 1.4 collective-permute-start.6
  42.1 4.9 %collective-permute-start.8 = (f32[512,512]{1,0:T(8,128)S(1)}, f32[512,512]{1,0:T(8,128)S(1)}, u32[]{:S(2)}, u32[]{:S(2)}) collective-permute-start(f32[512,512]{1,0:T(8,128)S(1)} %get-tuple-element.46.factor), channel_id=1, source_target_pairs={{0,8},{4,20},{9,1},{13,29},{18,26}} | collective-permute-start | bytes 3145736 | tf_op jit(solution)/shard_map/ppermute | solution.py:155
  48.3 4.7 %forward.2 = (f32[256,512]{1,0:T(8,128)S(1)}, f32[256,512]{1,0:T(8,128)S(1)}, f32[256,512]{1,0:T(8,128)S(1)}, f32[256,512]{1,0:T(8,128)S(1)}) custom-call(bf16[512,1024]{1,0:T(8,128)(2,1)S(1)} %get-tuple-element.39.high, bf16[512,1024]{1,0:T(8,128)(2,1)S(1)} %copy-done.4, f32[512,512]{1,0:T(8,128)S(1)} %slice.19.factor, f32[512,512]{1,0:T(8,128)} %copy-done.13, ...), custom_call_target="tpu_custom_call" | custom-call | flops 1610612736 | bytes 8388608 | tf_op jit(solution)/shard_map/forward/pallas_call | solution.py:349
  53.0 4.8 %collective-permute-done.6 = f32[512,512]{1,0:T(8,128)S(1)} collective-permute-done((f32[512,512]{1,0:T(8,128)S(1)}, f32[512,512]{1,0:T(8,128)S(1)}, u32[]{:S(2)}, u32[]{:S(2)}) %collective-permute-start.6) | collective-permute-done | bytes 1048608 | tf_op jit(solution)/shard_map/ppermute | solution.py:155
  58.8 1.8 collective-permute-done.8
  60.8 1.4 collective-permute-start.9
  62.2 1.3 collective-permute-start.10
  63.5 3.2 %collective-permute-start.7 = (f32[256,512]{1,0:T(8,128)S(1)}, f32[256,512]{1,0:T(8,128)S(1)}, u32[]{:S(2)}, u32[]{:S(2)}) collective-permute-start(f32[256,512]{1,0:T(8,128)S(1)} %get-tuple-element.73), channel_id=1, source_target_pairs={{0,1},{3,2},{4,5},{7,6},{8,9},{11,10},{12,13},{15,14},{16,17},{19,... | collective-permute-start | bytes 1572872 | tf_op jit(solution)/shard_map/ppermute | solution.py:370
  66.7 6.6 %collective-permute-done.7 = f32[256,512]{1,0:T(8,128)S(1)} collective-permute-done((f32[256,512]{1,0:T(8,128)S(1)}, f32[256,512]{1,0:T(8,128)S(1)}, u32[]{:S(2)}, u32[]{:S(2)}) %collective-permute-start.7) | collective-permute-done | bytes 524320 | tf_op jit(solution)/shard_map/ppermute | solution.py:370
  74.4 4.5 %collective-permute-done.10 = f32[512,512]{1,0:T(8,128)S(1)} collective-permute-done((f32[512,512]{1,0:T(8,128)S(1)}, f32[512,512]{1,0:T(8,128)S(1)}, u32[]{:S(2)}, u32[]{:S(2)}) %collective-permute-start.10) | collective-permute-done | bytes 1048608 | tf_op jit(solution)/shard_map/ppermute | solution.py:155
  80.4 1.5 collective-permute-start.12
  82.9 5.3 %forward.3 = (f32[256,512]{1,0:T(8,128)S(1)}, f32[256,512]{1,0:T(8,128)S(1)}, f32[512,512]{1,0:T(8,128)S(1)}, f32[512,512]{1,0:T(8,128)S(1)}) custom-call(bf16[512,1024]{1,0:T(8,128)(2,1)S(1)} %get-tuple-element.35.high, bf16[512,1024]{1,0:T(8,128)(2,1)} %copy-done.2, f32[512,512]{1,0:T(8,128)} %copy-done, f32[512,512]{1,0:T(8,128)} %add.95.mirror, ...), custom_call_target="tpu_custom_call" | custom-call | flops 1610612736 | bytes 8388608 | tf_op jit(solution)/shard_map/forward/pallas_call | solution.py:349
  90.7 5.8 %collective-permute-start.16 = (f32[256,512]{1,0:T(8,128)}, f32[256,512]{1,0:T(8,128)}, u32[]{:S(2)}, u32[]{:S(2)}) collective-permute-start(f32[256,512]{1,0:T(8,128)} %get-tuple-element.58), channel_id=1, source_target_pairs={{0,1},{3,2},{4,5},{7,6},{8,9},{11,10},{12,13},{15,14},{16,17},{19,... | collective-permute-start | bytes 1572872 | tf_op jit(solution)/shard_map/ppermute | solution.py:370
  97.4 2.4 %slice_add_fusion = (f32[256,512]{1,0:T(8,128)}, f32[256,512]{1,0:T(8,128)}) fusion(f32[256,512]{1,0:T(8,128)S(1)} %get-tuple-element.56, f32[512,512]{1,0:T(8,128)} %collective-permute-done.12, f32[256,512]{1,0:T(8,128)S(1)} %get-tuple-element.54), kind=kLoop, calls=%fused_computation.1 | loop fusion | flops 262144 | bytes 3145728 | tf_op jit(solution)/shard_map/add | solution.py:420
  99.9 1.5 add.107
  102.3 5.5 %collective-permute-done.16 = f32[256,512]{1,0:T(8,128)} collective-permute-done((f32[256,512]{1,0:T(8,128)}, f32[256,512]{1,0:T(8,128)}, u32[]{:S(2)}, u32[]{:S(2)}) %collective-permute-start.16) | collective-permute-done | bytes 524320 | tf_op jit(solution)/shard_map/ppermute | solution.py:370
  109.1 2.5 %collective-permute-done.25 = f32[256,512]{1,0:T(8,128)} collective-permute-done((f32[256,512]{1,0:T(8,128)}, f32[256,512]{1,0:T(8,128)}, u32[]{:S(2)}, u32[]{:S(2)}) %collective-permute-start.25) | collective-permute-done | bytes 524320 | tf_op jit(solution)/shard_map/ppermute | solution.py:430
  113.0 2.2 %collective-permute-start.13 = (f32[256,512]{1,0:T(8,128)S(1)}, f32[256,512]{1,0:T(8,128)S(1)}, u32[]{:S(2)}, u32[]{:S(2)}) collective-permute-start(f32[256,512]{1,0:T(8,128)S(1)} %copy-done.17), channel_id=1, source_target_pairs={{0,1},{3,2},{4,5},{7,6},{8,9},{11,10},{12,13},{15,14},{16,17},{19,... | collective-permute-start | bytes 1572872 | tf_op jit(solution)/shard_map/ppermute | solution.py:370
  117.1 6.3 %collective-permute-done.17.rest_1_ = f32[256,512]{1,0:T(8,128)S(1)} collective-permute-done((f32[256,512]{1,0:T(8,128)S(1)}, f32[256,512]{1,0:T(8,128)S(1)}, u32[]{:S(2)}, u32[]{:S(2)}) %collective-permute-start.17) | collective-permute-done | bytes 524320 | tf_op jit(solution)/shard_map/ppermute | solution.py:378
  123.3 1.5 collective-permute-start.18
  124.9 1.3 collective-permute-start.27
  126.2 1.4 collective-permute-done.13
  128.4 1.4 collective-permute-start.22
  129.9 8.9 %collective-permute-done.18 = f32[256,512]{1,0:T(8,128)S(1)} collective-permute-done((f32[256,512]{1,0:T(8,128)S(1)}, f32[256,512]{1,0:T(8,128)S(1)}, u32[]{:S(2)}, u32[]{:S(2)}) %collective-permute-start.18) | collective-permute-done | bytes 524320 | tf_op jit(solution)/shard_map/ppermute | solution.py:370
  139.6 3.2 %collective-permute-done.27 = f32[128,512]{1,0:T(8,128)S(1)} collective-permute-done((f32[128,512]{1,0:T(8,128)S(1)}, f32[128,512]{1,0:T(8,128)S(1)}, u32[]{:S(2)}, u32[]{:S(2)}) %collective-permute-start.27) | collective-permute-done | bytes 262176 | tf_op jit(solution)/shard_map/ppermute | solution.py:370
  143.5 1.3 collective-permute-start.29
  144.9 1.3 collective-permute-start.19
  146.3 4.3 %place.2.rest_4_ = f32[2048,1024]{1,0:T(8,128)} custom-call(s32[2,16]{1,0:T(2,128)S(1)} %copy-done.7, f32[2,512,512]{2,1,0:T(8,128)S(1)} %copy-done.1, f32[256,512]{1,0:T(8,128)S(1)} %add.102.rest_0_, f32[256,512]{1,0:T(8,128)S(1)} %copy-done.6, f32[256,512]{1,0:T(8,128)S(1)} %add.106.rest_2_, f32[256,512]{1,0:T(8,128)S(1)} %collective-permute-done.22.rest_3_), custom_call_target="tpu_custom_call" | custom-call | flops 805306368 | bytes 8388608 | tf_op jit(solution)/shard_map/place/pallas_call | solution.py:437
  150.7 1.3 collective-permute-start.23
  152.0 16.2 %collective-permute-done.29 = f32[128,512]{1,0:T(8,128)} collective-permute-done((f32[128,512]{1,0:T(8,128)S(1)}, f32[128,512]{1,0:T(8,128)}, u32[]{:S(2)}, u32[]{:S(2)}) %collective-permute-start.29) | collective-permute-done | bytes 262176 | tf_op jit(solution)/shard_map/ppermute | solution.py:378
  169.5 1.7 collective-permute-start.31
  171.2 1.6 collective-permute-start.30
  172.7 6.7 %collective-permute-done.19.rest_1_ = f32[256,512]{1,0:T(8,128)} collective-permute-done((f32[256,512]{1,0:T(8,128)S(1)}, f32[256,512]{1,0:T(8,128)}, u32[]{:S(2)}, u32[]{:S(2)}) %collective-permute-start.19) | collective-permute-done | bytes 524320 | tf_op jit(solution)/shard_map/ppermute | solution.py:378
  179.4 6.4 %collective-permute-done.23.rest_3_ = f32[256,512]{1,0:T(8,128)} collective-permute-done((f32[256,512]{1,0:T(8,128)S(1)}, f32[256,512]{1,0:T(8,128)}, u32[]{:S(2)}, u32[]{:S(2)}) %collective-permute-start.23) | collective-permute-done | bytes 524320 | tf_op jit(solution)/shard_map/ppermute | solution.py:378
  185.8 3.4 %place.3 = f32[2048,1024]{1,0:T(8,128)} custom-call(s32[2,16]{1,0:T(2,128)S(1)} %copy-done.7, f32[2,512,512]{2,1,0:T(8,128)S(1)} %copy-done.1, f32[256,512]{1,0:T(8,128)S(1)} %add.99.rest_0_, f32[256,512]{1,0:T(8,128)} %collective-permute-done.19.rest_1_, f32[256,512]{1,0:T(8,128)S(1)} %add.104.rest_2_, ...), custom_call_target="tpu_custom_call", output_to_operand_aliasing={{}: (6, {})} | custom-call | flops 805306368 | bytes 8388608 | tf_op jit(solution)/shard_map/place/pallas_call | solution.py:437
  189.4 2.6 %collective-permute-done.33.rest_1_ = f32[512,512]{1,0:T(8,128)S(1)} collective-permute-done((f32[512,512]{1,0:T(8,128)S(1)}, f32[512,512]{1,0:T(8,128)S(1)}, u32[]{:S(2)}, u32[]{:S(2)}) %collective-permute-start.33) | collective-permute-done | bytes 1048608 | tf_op jit(solution)/shard_map/ppermute | solution.py:87
  192.1 5.1 %diagonal.1 = f32[2,512,512]{2,1,0:T(8,128)} custom-call(f32[2,512]{1,0:T(2,128)S(1)} %copy-done.9, f32[2,512,512]{2,1,0:T(8,128)S(1)} %copy-done.1, f32[512,512]{1,0:T(8,128)S(1)} %pad_maximum_fusion.rest_0_, f32[512,512]{1,0:T(8,128)S(1)} %collective-permute-done.33.rest_1_), custom_call_target="tpu_custom_call" | custom-call | flops 3221225472 | bytes 8388608 | tf_op jit(solution)/shard_map/diagonal/pallas_call | solution.py:479
  (97 shorter events, 20.4 us)
Async XLA Ops:
  0.6 7.2 %copy-start.7 = (s32[2,16]{1,0:T(2,128)S(1)}, s32[2,16]{1,0:T(2,128)}, u32[]{:S(2)}) copy-start(s32[2,16]{1,0:T(2,128)} %tiles_ref.7) | copy-start | bytes 388
  0.6 7.2 %copy-start.8 = (s32[2,16]{1,0:T(2,128)S(1)}, s32[2,16]{1,0:T(2,128)}, u32[]{:S(2)}) copy-start(s32[2,16]{1,0:T(2,128)} %valid_ref.3) | copy-start | bytes 388
  2.0 17.2 %collective-permute-start.3 = (f32[512,512]{1,0:T(8,128)S(1)}, f32[512,512]{1,0:T(8,128)}, u32[]{:S(2)}, u32[]{:S(2)}) collective-permute-start(f32[512,512]{1,0:T(8,128)S(1)} %slice.19.factor), channel_id=1, source_target_pairs={{0,8},{4,20},{9,1},{13,29},{18,26}} | collective-permute-start | bytes 3145736 | tf_op jit(solution)/shard_map/ppermute | solution.py:155
  14.0 8.4 %collective-permute-start.1 = (f32[512,512]{1,0:T(8,128)}, f32[512,512]{1,0:T(8,128)}, u32[]{:S(2)}, u32[]{:S(2)}) collective-permute-start(f32[512,512]{1,0:T(8,128)} %get-tuple-element.42), channel_id=1, source_target_pairs={{4,0},{0,4},{12,8},{8,12},{20,16},{16,20},{28,24},{24,28},{5,1},{1... | collective-permute-start | bytes 3145736 | tf_op jit(solution)/shard_map/ppermute | solution.py:87
  21.0 21.1 %copy-start = (f32[512,512]{1,0:T(8,128)}, f32[512,512]{1,0:T(8,128)S(1)}, u32[]{:S(2)}) copy-start(f32[512,512]{1,0:T(8,128)S(1)} %get-tuple-element.46.factor) | copy-start | bytes 3145732
  21.0 13.6 %collective-permute-start.4 = (f32[512,512]{1,0:T(8,128)S(1)}, f32[512,512]{1,0:T(8,128)S(1)}, u32[]{:S(2)}, u32[]{:S(2)}) collective-permute-start(f32[512,512]{1,0:T(8,128)S(1)} %get-tuple-element.43), channel_id=1, source_target_pairs={{0,16},{8,24},{4,12},{20,28},{9,25},{1,17},{29,21},{22,30}} | collective-permute-start | bytes 3145736 | tf_op jit(solution)/shard_map/ppermute | solution.py:155
  23.8 16.7 %collective-permute-start.2 = (f32[512,512]{1,0:T(8,128)S(1)}, f32[512,512]{1,0:T(8,128)S(1)}, u32[]{:S(2)}, u32[]{:S(2)}) collective-permute-start(f32[512,512]{1,0:T(8,128)S(1)} %add.90), channel_id=1, source_target_pairs={{16,0},{24,8},{12,4},{28,20},{25,9},{17,1},{21,29},{30,22}} | collective-permute-start | bytes 3145736 | tf_op jit(solution)/shard_map/ppermute | solution.py:155
  29.2 11.4 %copy-start.2 = (bf16[512,1024]{1,0:T(8,128)(2,1)}, bf16[512,1024]{1,0:T(8,128)(2,1)S(1)}, u32[]{:S(2)}) copy-start(bf16[512,1024]{1,0:T(8,128)(2,1)S(1)} %get-tuple-element.36.low) | copy-start | bytes 3145732
  29.2 17.9 %collective-permute-start = (f32[512,512]{1,0:T(8,128)S(1)}, f32[512,512]{1,0:T(8,128)S(1)}, u32[]{:S(2)}, u32[]{:S(2)}) collective-permute-start(f32[512,512]{1,0:T(8,128)S(1)} %get-tuple-element.38), channel_id=1, source_target_pairs={{4,0},{0,4},{12,8},{8,12},{20,16},{16,20},{28,24},{24,28},{5,1},{1... | collective-permute-start | bytes 3145736 | tf_op jit(solution)/shard_map/ppermute | solution.py:87
  34.8 12.5 %copy-start.12 = (f32[512,512]{1,0:T(8,128)}, f32[512,512]{1,0:T(8,128)S(1)}, u32[]{:S(2)}) copy-start(f32[512,512]{1,0:T(8,128)S(1)} %add.92.rest_0_) | copy-start | bytes 3145732
  34.8 12.5 %collective-permute-start.5 = (f32[512,512]{1,0:T(8,128)S(1)}, f32[512,512]{1,0:T(8,128)S(1)}, u32[]{:S(2)}, u32[]{:S(2)}) collective-permute-start(f32[512,512]{1,0:T(8,128)S(1)} %add.92.rest_0_), channel_id=1, source_target_pairs={{4,0},{0,4},{12,8},{8,12},{20,16},{16,20},{28,24},{24,28},{5,1},{1... | collective-permute-start | bytes 3145736 | tf_op jit(solution)/shard_map/ppermute | solution.py:87
  40.7 6.7 %copy-start.13 = (f32[512,512]{1,0:T(8,128)}, f32[512,512]{1,0:T(8,128)S(1)}, u32[]{:S(2)}) copy-start(f32[512,512]{1,0:T(8,128)S(1)} %add.91.mirror) | copy-start | bytes 3145732
  40.7 7.6 %copy-start.4 = (bf16[512,1024]{1,0:T(8,128)(2,1)S(1)}, bf16[512,1024]{1,0:T(8,128)(2,1)}, u32[]{:S(2)}) copy-start(bf16[512,1024]{1,0:T(8,128)(2,1)} %copy-done.3) | copy-start | bytes 3145732
  40.7 17.1 %collective-permute-start.6 = (f32[512,512]{1,0:T(8,128)S(1)}, f32[512,512]{1,0:T(8,128)S(1)}, u32[]{:S(2)}, u32[]{:S(2)}) collective-permute-start(f32[512,512]{1,0:T(8,128)S(1)} %add.91.mirror), channel_id=1, source_target_pairs={{8,0},{20,4},{1,9},{29,13},{26,18}} | collective-permute-start | bytes 3145736 | tf_op jit(solution)/shard_map/ppermute | solution.py:155
  42.1 18.5 %collective-permute-start.8 = (f32[512,512]{1,0:T(8,128)S(1)}, f32[512,512]{1,0:T(8,128)S(1)}, u32[]{:S(2)}, u32[]{:S(2)}) collective-permute-start(f32[512,512]{1,0:T(8,128)S(1)} %get-tuple-element.46.factor), channel_id=1, source_target_pairs={{0,8},{4,20},{9,1},{13,29},{18,26}} | collective-permute-start | bytes 3145736 | tf_op jit(solution)/shard_map/ppermute | solution.py:155
  53.0 7.6 %copy-start.10 = (f32[512,1024]{1,0:T(8,128)S(1)}, f32[512,1024]{1,0:T(8,128)}, u32[]{:S(2)}) copy-start(f32[512,1024]{1,0:T(8,128)} %param.7) | copy-start | bytes 6291460
  58.8 20.3 %copy-start.16 = (f32[256,512]{1,0:T(8,128)}, f32[256,512]{1,0:T(8,128)S(1)}, u32[]{:S(2)}) copy-start(f32[256,512]{1,0:T(8,128)S(1)} %get-tuple-element.73) | copy-start | bytes 1572868
  60.8 13.6 %collective-permute-start.9 = (f32[512,512]{1,0:T(8,128)S(1)}, f32[512,512]{1,0:T(8,128)S(1)}, u32[]{:S(2)}, u32[]{:S(2)}) collective-permute-start(f32[512,512]{1,0:T(8,128)S(1)} %broadcast_select_fusion), channel_id=1, source_target_pairs={{0,16},{8,24},{4,12},{20,28},{9,25},{1,17},{29,21},{22,30}} | collective-permute-start | bytes 3145736 | tf_op jit(solution)/shard_map/ppermute | solution.py:155
  62.2 16.7 %collective-permute-start.10 = (f32[512,512]{1,0:T(8,128)S(1)}, f32[512,512]{1,0:T(8,128)S(1)}, u32[]{:S(2)}, u32[]{:S(2)}) collective-permute-start(f32[512,512]{1,0:T(8,128)S(1)} %add.89), channel_id=1, source_target_pairs={{16,0},{24,8},{12,4},{28,20},{25,9},{17,1},{21,29},{30,22}} | collective-permute-start | bytes 3145736 | tf_op jit(solution)/shard_map/ppermute | solution.py:155
  63.5 9.9 %collective-permute-start.7 = (f32[256,512]{1,0:T(8,128)S(1)}, f32[256,512]{1,0:T(8,128)S(1)}, u32[]{:S(2)}, u32[]{:S(2)}) collective-permute-start(f32[256,512]{1,0:T(8,128)S(1)} %get-tuple-element.73), channel_id=1, source_target_pairs={{0,1},{3,2},{4,5},{7,6},{8,9},{11,10},{12,13},{15,14},{16,17},{19,... | collective-permute-start | bytes 1572872 | tf_op jit(solution)/shard_map/ppermute | solution.py:370
  79.1 2.8 %collective-permute-start.11 = (f32[512,512]{1,0:T(8,128)S(1)}, f32[512,512]{1,0:T(8,128)S(1)}, u32[]{:S(2)}, u32[]{:S(2)}) collective-permute-start(f32[512,512]{1,0:T(8,128)S(1)} %add.96.rest_0_), channel_id=1, source_target_pairs={{4,0},{0,4},{12,8},{8,12},{20,16},{16,20},{28,24},{24,28},{5,1},{1... | collective-permute-start | bytes 3145736 | tf_op jit(solution)/shard_map/ppermute | solution.py:87
  80.4 17.0 %collective-permute-start.12 = (f32[512,512]{1,0:T(8,128)}, f32[512,512]{1,0:T(8,128)}, u32[]{:S(2)}, u32[]{:S(2)}) collective-permute-start(f32[512,512]{1,0:T(8,128)} %add.95.mirror), channel_id=1, source_target_pairs={{8,0},{20,4},{1,9},{29,13},{26,18}} | collective-permute-start | bytes 3145736 | tf_op jit(solution)/shard_map/ppermute | solution.py:155
  88.2 11.6 %collective-permute-start.24 = (f32[512,512]{1,0:T(8,128)S(1)}, f32[512,512]{1,0:T(8,128)}, u32[]{:S(2)}, u32[]{:S(2)}) collective-permute-start(f32[512,512]{1,0:T(8,128)S(1)} %get-tuple-element.65), channel_id=1, source_target_pairs={{4,0},{0,4},{12,8},{8,12},{20,16},{16,20},{28,24},{24,28},{5,1},{1... | collective-permute-start | bytes 3145736 | tf_op jit(solution)/shard_map/ppermute | solution.py:87
  90.0 12.2 %collective-permute-start.15 = (f32[256,512]{1,0:T(8,128)S(1)}, f32[256,512]{1,0:T(8,128)S(1)}, u32[]{:S(2)}, u32[]{:S(2)}) collective-permute-start(f32[256,512]{1,0:T(8,128)S(1)} %add.101), channel_id=1, source_target_pairs={{1,2},{2,1},{5,6},{6,5},{9,10},{10,9},{13,14},{14,13},{17,18},{18,... | collective-permute-start | bytes 1572872 | tf_op jit(solution)/shard_map/ppermute | solution.py:378
  90.7 17.1 %collective-permute-start.16 = (f32[256,512]{1,0:T(8,128)}, f32[256,512]{1,0:T(8,128)}, u32[]{:S(2)}, u32[]{:S(2)}) collective-permute-start(f32[256,512]{1,0:T(8,128)} %get-tuple-element.58), channel_id=1, source_target_pairs={{0,1},{3,2},{4,5},{7,6},{8,9},{11,10},{12,13},{15,14},{16,17},{19,... | collective-permute-start | bytes 1572872 | tf_op jit(solution)/shard_map/ppermute | solution.py:370
  102.2 13.0 %copy-start.14 = (f32[256,512]{1,0:T(8,128)S(1)}, f32[256,512]{1,0:T(8,128)}, u32[]{:S(2)}) copy-start(f32[256,512]{1,0:T(8,128)} %get-tuple-element.58) | copy-start | bytes 1572868
  102.2 9.5 %collective-permute-start.25 = (f32[256,512]{1,0:T(8,128)}, f32[256,512]{1,0:T(8,128)}, u32[]{:S(2)}, u32[]{:S(2)}) collective-permute-start(f32[256,512]{1,0:T(8,128)} %dynamic-slice_bitcast_fusion), channel_id=1, source_target_pairs={{0,8},{1,9},{2,10},{3,11},{4,20},{5,21},{6,22},{7,23},{8,0},{9,1},... | collective-permute-start | bytes 1572872 | tf_op jit(solution)/shard_map/ppermute | solution.py:430
  102.3 21.1 %copy-start.15 = (f32[256,512]{1,0:T(8,128)S(1)}, f32[256,512]{1,0:T(8,128)}, u32[]{:S(2)}) copy-start(f32[256,512]{1,0:T(8,128)} %get-tuple-element.60) | copy-start | bytes 1572868
  107.8 15.5 %collective-permute-start.17 = (f32[256,512]{1,0:T(8,128)S(1)}, f32[256,512]{1,0:T(8,128)S(1)}, u32[]{:S(2)}, u32[]{:S(2)}) collective-permute-start(f32[256,512]{1,0:T(8,128)S(1)} %add.102.rest_0_), channel_id=1, source_target_pairs={{1,0},{2,3},{5,4},{6,7},{9,8},{10,11},{13,12},{14,15},{17,16},{18,... | collective-permute-start | bytes 1572872 | tf_op jit(solution)/shard_map/ppermute | solution.py:378
  112.9 11.9 %collective-permute-start.26 = (f32[128,512]{1,0:T(8,128)S(1)}, f32[128,512]{1,0:T(8,128)S(1)}, u32[]{:S(2)}, u32[]{:S(2)}) collective-permute-start(f32[128,512]{1,0:T(8,128)S(1)} %dynamic-slice_bitcast_fusion.1), channel_id=1, source_target_pairs={{0,16},{1,17},{2,18},{3,19},{4,12},{5,13},{6,14},{7,15},{8,24},{9,... | collective-permute-start | bytes 786440 | tf_op jit(solution)/shard_map/ppermute | solution.py:430
  113.0 14.6 %collective-permute-start.13 = (f32[256,512]{1,0:T(8,128)S(1)}, f32[256,512]{1,0:T(8,128)S(1)}, u32[]{:S(2)}, u32[]{:S(2)}) collective-permute-start(f32[256,512]{1,0:T(8,128)S(1)} %copy-done.17), channel_id=1, source_target_pairs={{0,1},{3,2},{4,5},{7,6},{8,9},{11,10},{12,13},{15,14},{16,17},{19,... | collective-permute-start | bytes 1572872 | tf_op jit(solution)/shard_map/ppermute | solution.py:370
  116.4 12.0 %collective-permute-start.21 = (f32[256,512]{1,0:T(8,128)S(1)}, f32[256,512]{1,0:T(8,128)S(1)}, u32[]{:S(2)}, u32[]{:S(2)}) collective-permute-start(f32[256,512]{1,0:T(8,128)S(1)} %add.105), channel_id=1, source_target_pairs={{1,2},{2,1},{5,6},{6,5},{9,10},{10,9},{13,14},{14,13},{17,18},{18,... | collective-permute-start | bytes 1572872 | tf_op jit(solution)/shard_map/ppermute | solution.py:378
  123.3 5.0 %copy-start.5 = (f32[256,512]{1,0:T(8,128)}, f32[256,512]{1,0:T(8,128)S(1)}, u32[]{:S(2)}) copy-start(f32[256,512]{1,0:T(8,128)S(1)} %collective-permute-done.17.rest_1_) | copy-start | bytes 1572868
  123.3 15.4 %collective-permute-start.18 = (f32[256,512]{1,0:T(8,128)S(1)}, f32[256,512]{1,0:T(8,128)S(1)}, u32[]{:S(2)}, u32[]{:S(2)}) collective-permute-start(f32[256,512]{1,0:T(8,128)S(1)} %copy-done.15), channel_id=1, source_target_pairs={{0,1},{3,2},{4,5},{7,6},{8,9},{11,10},{12,13},{15,14},{16,17},{19,... | collective-permute-start | bytes 1572872 | tf_op jit(solution)/shard_map/ppermute | solution.py:370
  124.9 17.9 %collective-permute-start.27 = (f32[128,512]{1,0:T(8,128)S(1)}, f32[128,512]{1,0:T(8,128)S(1)}, u32[]{:S(2)}, u32[]{:S(2)}) collective-permute-start(f32[128,512]{1,0:T(8,128)S(1)} %bitcast_add_fusion.1), channel_id=1, source_target_pairs={{0,1},{3,2},{4,5},{7,6},{8,9},{11,10},{12,13},{15,14},{16,17},{19,... | collective-permute-start | bytes 786440 | tf_op jit(solution)/shard_map/ppermute | solution.py:370
  127.6 17.2 %collective-permute-start.14 = (f32[256,512]{1,0:T(8,128)S(1)}, f32[256,512]{1,0:T(8,128)S(1)}, u32[]{:S(2)}, u32[]{:S(2)}) collective-permute-start(f32[256,512]{1,0:T(8,128)S(1)} %add.98), channel_id=1, source_target_pairs={{1,2},{2,1},{5,6},{6,5},{9,10},{10,9},{13,14},{14,13},{17,18},{18,... | collective-permute-start | bytes 1572872 | tf_op jit(solution)/shard_map/ppermute | solution.py:378
  128.4 17.8 %copy-start.1 = (f32[2,512,512]{2,1,0:T(8,128)S(1)}, f32[2,512,512]{2,1,0:T(8,128)}, u32[]{:S(2)}) copy-start(f32[2,512,512]{2,1,0:T(8,128)} %unit_ref.5) | copy-start | bytes 6291460
  128.4 17.8 %copy-start.6 = (f32[256,512]{1,0:T(8,128)S(1)}, f32[256,512]{1,0:T(8,128)}, u32[]{:S(2)}) copy-start(f32[256,512]{1,0:T(8,128)} %copy-done.5) | copy-start | bytes 1572868
  128.4 17.8 %collective-permute-start.22 = (f32[256,512]{1,0:T(8,128)S(1)}, f32[256,512]{1,0:T(8,128)S(1)}, u32[]{:S(2)}, u32[]{:S(2)}) collective-permute-start(f32[256,512]{1,0:T(8,128)S(1)} %add.106.rest_2_), channel_id=1, source_target_pairs={{1,0},{2,3},{5,4},{6,7},{9,8},{10,11},{13,12},{14,15},{17,16},{18,... | collective-permute-start | bytes 1572872 | tf_op jit(solution)/shard_map/ppermute | solution.py:378
  138.8 11.8 %collective-permute-start.20 = (f32[256,512]{1,0:T(8,128)S(1)}, f32[256,512]{1,0:T(8,128)S(1)}, u32[]{:S(2)}, u32[]{:S(2)}) collective-permute-start(f32[256,512]{1,0:T(8,128)S(1)} %add.103), channel_id=1, source_target_pairs={{1,2},{2,1},{5,6},{6,5},{9,10},{10,9},{13,14},{14,13},{17,18},{18,... | collective-permute-start | bytes 1572872 | tf_op jit(solution)/shard_map/ppermute | solution.py:378
  142.8 0.7 collective-permute-start.28
  143.5 24.6 %collective-permute-start.29 = (f32[128,512]{1,0:T(8,128)S(1)}, f32[128,512]{1,0:T(8,128)}, u32[]{:S(2)}, u32[]{:S(2)}) collective-permute-start(f32[128,512]{1,0:T(8,128)S(1)} %add.114), channel_id=1, source_target_pairs={{1,0},{2,3},{5,4},{6,7},{9,8},{10,11},{13,12},{14,15},{17,16},{18,... | collective-permute-start | bytes 786440 | tf_op jit(solution)/shard_map/ppermute | solution.py:378
  144.9 34.5 %collective-permute-start.19 = (f32[256,512]{1,0:T(8,128)S(1)}, f32[256,512]{1,0:T(8,128)}, u32[]{:S(2)}, u32[]{:S(2)}) collective-permute-start(f32[256,512]{1,0:T(8,128)S(1)} %add.99.rest_0_), channel_id=1, source_target_pairs={{1,0},{2,3},{5,4},{6,7},{9,8},{10,11},{13,12},{14,15},{17,16},{18,... | collective-permute-start | bytes 1572872 | tf_op jit(solution)/shard_map/ppermute | solution.py:378
  150.7 35.1 %collective-permute-start.23 = (f32[256,512]{1,0:T(8,128)S(1)}, f32[256,512]{1,0:T(8,128)}, u32[]{:S(2)}, u32[]{:S(2)}) collective-permute-start(f32[256,512]{1,0:T(8,128)S(1)} %add.104.rest_2_), channel_id=1, source_target_pairs={{1,0},{2,3},{5,4},{6,7},{9,8},{10,11},{13,12},{14,15},{17,16},{18,... | collective-permute-start | bytes 1572872 | tf_op jit(solution)/shard_map/ppermute | solution.py:378
  169.2 20.1 %collective-permute-start.32 = (f32[128,512]{1,0:T(8,128)S(1)}, f32[128,512]{1,0:T(8,128)S(1)}, u32[]{:S(2)}, u32[]{:S(2)}) collective-permute-start(f32[128,512]{1,0:T(8,128)S(1)} %broadcast_select_fusion.2), channel_id=1, source_target_pairs={{0,24},{1,25},{2,26},{3,27},{8,16},{9,17},{10,18},{11,19},{16,8},{... | collective-permute-start | bytes 786440 | tf_op jit(solution)/shard_map/ppermute | solution.py:476
  169.5 19.7 %collective-permute-start.31 = (f32[128,512]{1,0:T(8,128)S(1)}, f32[128,512]{1,0:T(8,128)S(1)}, u32[]{:S(2)}, u32[]{:S(2)}) collective-permute-start(f32[128,512]{1,0:T(8,128)S(1)} %broadcast_select_fusion.2), channel_id=1, source_target_pairs={{0,8},{1,9},{2,10},{3,11},{8,0},{9,1},{10,2},{11,3},{16,24},{17,25... | collective-permute-start | bytes 786440 | tf_op jit(solution)/shard_map/ppermute | solution.py:476
  171.2 18.1 %collective-permute-start.30 = (f32[128,512]{1,0:T(8,128)S(1)}, f32[128,512]{1,0:T(8,128)S(1)}, u32[]{:S(2)}, u32[]{:S(2)}) collective-permute-start(f32[128,512]{1,0:T(8,128)S(1)} %broadcast_select_fusion.2), channel_id=1, source_target_pairs={{0,16},{1,17},{2,18},{3,19},{8,24},{9,25},{10,26},{11,27},{16,0},{... | collective-permute-start | bytes 786440 | tf_op jit(solution)/shard_map/ppermute | solution.py:476
  189.3 2.7 %collective-permute-start.33 = (f32[512,512]{1,0:T(8,128)S(1)}, f32[512,512]{1,0:T(8,128)S(1)}, u32[]{:S(2)}, u32[]{:S(2)}) collective-permute-start(f32[512,512]{1,0:T(8,128)S(1)} %pad_maximum_fusion.rest_0_), channel_id=1, source_target_pairs={{4,0},{0,4},{12,8},{8,12},{20,16},{16,20},{28,24},{24,28},{5,1},{1... | collective-permute-start | bytes 3145736 | tf_op jit(solution)/shard_map/ppermute | solution.py:87
  (7 other events, 13.6 us)

commit v6 on v5

--- a/solution.py
+++ b/solution.py
@@ -11,7 +11,7 @@
 BF16 = jnp.bfloat16
 VMEM = pltpu.MemorySpace.VMEM
 SMEM = pltpu.MemorySpace.SMEM
-SPLIT = 2
+SMALL = pl.CostEstimate(flops=1 << 20, bytes_accessed=1 << 16, transcendentals=0)
 PARAMS = pltpu.CompilerParams(vmem_limit_bytes=48 * 1024 * 1024)
 
 
@@ -58,6 +58,7 @@
             bits[lane % len(bits):] + bits[:lane % len(bits)] for lane in range(self.lanes)
         ]
         self.steps = len(bits)
+        self.splits = [1] + [2] * (self.members - 1)
 
     def device(self, chip, lane, col):
         return (chip * self.lanes + lane) * self.cols + col
@@ -206,7 +207,8 @@
     lanes, size, depth = plan.lanes, plan.tile, plan.depth
     parts, rest = rest[:lanes], rest[lanes:]
     earlier, rest = rest[:lanes * bool(member)], rest[lanes * bool(member):]
-    totals, rest = rest[:SPLIT], rest[SPLIT:]
+    splits = plan.splits[member]
+    totals, rest = rest[:splits], rest[splits:]
     cross, (total, whole) = rest[:lanes], rest[lanes:]
     right = [split(part[...]) for part in parts]
     for a in range(plan.na):
@@ -218,9 +220,9 @@
             )
             for i in range(lanes)
         )
-    share = depth // SPLIT
+    share = depth // splits
     on_diagonal = plan.on_diagonal()
-    for i in range(SPLIT):
+    for i in range(splits):
         rows = slice(i * share, (i + 1) * share)
         totals[i][...] = total[rows, :] + jnp.where(on_diagonal, mirror[rows, :], 0.0)
     whole[...] = product(split(factor[...]), split(total[...]), contract=0)
@@ -234,7 +236,8 @@
 
 
 def place_kernel(plan, member, tiles_ref, unit_ref, *rest):
-    sums, rest = rest[:2 * SPLIT], rest[2 * SPLIT:]
+    splits = plan.splits[member]
+    sums, rest = rest[:2 * splits], rest[2 * splits:]
     out, stack, zeros, sems, zero_sems = rest[member > 0:]
     size, width = plan.tile, plan.width
     row, at_end = lax.axis_index("row"), plan.at_end()
@@ -258,8 +261,8 @@
         zeros[...] = jnp.zeros_like(zeros)
         zero_copies(lambda copy: copy.start())
     right = split(unit_inverse(unit_ref, member))
-    share = plan.depth // SPLIT
-    for i in range(SPLIT):
+    share = plan.depth // splits
+    for i in range(splits):
         x = jnp.where(at_end, sums[2 * i + 1][...], sums[2 * i][...])
         stack[i * share:(i + 1) * share, :] = -product(split(x), right)
     copies = []
@@ -318,8 +321,6 @@
     plan = Plan(inverse_front, factor, unit_lower, tile_list)
     width, depth, lanes, members, steps = plan.width, plan.depth, plan.lanes, plan.members, plan.steps
     both = ("row", "col")
-    share = depth // SPLIT
-    flops = 6 * depth * depth * lanes * width
     factors = [factor[:, member * width:(member + 1) * width] for member in range(members)]
 
     def lane_sum(parts):
@@ -340,27 +341,28 @@
                 pltpu.SemaphoreType.DMA((plan.na, plan.nb)),
             ],
             compiler_params=PARAMS,
-            cost_estimate=pl.CostEstimate(flops=flops, bytes_accessed=8 << 20, transcendentals=0),
+            cost_estimate=SMALL,
             name="gather_mirror",
         )(tile_list, tile_valid, inverse_front, factors[member])
 
     def forward(member, high, low, mirror, held, earlier):
         parts = [held] + [plan.swap(held, shift) for shift in range(1, lanes)]
+        splits = plan.splits[member]
         outs = pl.pallas_call(
             functools.partial(forward_kernel, plan, member),
             in_specs=vmem(4 + lanes + len(earlier)),
-            out_specs=vmem(SPLIT + lanes),
-            out_shape=[jax.ShapeDtypeStruct((share, width), F32)] * SPLIT
+            out_specs=vmem(splits + lanes),
+            out_shape=[jax.ShapeDtypeStruct((depth // splits, width), F32)] * splits
             + [jax.ShapeDtypeStruct(((member + 1) * width // lanes, width), F32)] * lanes,
             scratch_shapes=[
                 pltpu.VMEM((depth, width), F32),
                 pltpu.VMEM((width, width), F32),
             ],
             compiler_params=PARAMS,
-            cost_estimate=pl.CostEstimate(flops=flops, bytes_accessed=8 << 20, transcendentals=0),
+            cost_estimate=SMALL,
             name="forward",
         )(high, low, factors[member], mirror, *parts, *earlier)
-        return outs[:SPLIT], outs[SPLIT:], parts[-1]
+        return outs[:splits], outs[splits:]
 
     hops = plan.line_hops()
 
@@ -369,21 +371,26 @@
             x, _ = lax.optimization_barrier((x, tuple(after)))
         return lax.ppermute(x, "col", hops[0])
 
-    def run(x, got, before_last=()):
+    def run(x, got, ties=(), second=None):
+        sent, brought = [], []
         for hop in range(1, len(hops)):
             x = plan.line_step(hop - 1, x, got)
-            sent = x
-            if hop == len(hops) - 1 and before_last:
-                sent, _ = lax.optimization_barrier((x, tuple(before_last)))
-            got = lax.ppermute(sent, "col", hops[hop])
+            sent.append(x)
+            tie = ties[hop - 1] if hop <= len(ties) else ()
+            y = lax.optimization_barrier((x, tuple(tie)))[0] if tie else x
+            if hop == 1 and second is not None:
+                got = second
+            else:
+                got = lax.ppermute(y, "col", hops[hop])
+            brought.append(got)
         if len(hops) == 1:
             got = x = x + got
-        return x, got
+        return x, got, sent, brought
 
     spread, collect = Chain(), Chain()
     count = members * steps
     tiles, held, mirror, chunks, entered = {}, {}, {}, [], {}
-    after, cross, last_swap = (), [], None
+    after, cross, second = (), [], None
     for phase in range(count + 1):
         if phase < count:
             out, step = divmod(phase, steps)
@@ -399,6 +406,9 @@
             entered[0], got_out, got_back = lax.optimization_barrier(
                 (entered[0], got_out, got_back)
             )
+        if phase == count and chunks and len(hops) > 1:
+            second = lax.ppermute(plan.line_step(0, chunks[0], entered[0]), "col", hops[1])
+            second, got_back = lax.optimization_barrier((second, got_back))
         after = ()
         if phase % steps == 0 and phase < count:
             high, low, *parts = gather(out) if out == 0 else tiles[out]
@@ -413,15 +423,19 @@
             if turn < steps - 1:
                 mirror[back] = mirror[back] + got_back
             else:
-                sums, cross, last_swap = forward(
-                    back, *tiles[back], mirror[back], held[back], cross
+                x = mirror[back]
+                if chunks:
+                    x, _ = lax.optimization_barrier(
+                        (x, plan.line_step(0, chunks[0], entered[0]))
+                    )
+                sums, cross = forward(back, *tiles[back], x, held[back], cross)
+                share = sums[0].shape[0]
+                after = tuple(
+                    part + got_back[i * share:(i + 1) * share] for i, part in enumerate(sums)
                 )
-                chunks += [
-                    part + got_back[i * share:(i + 1) * share] for i, part in enumerate(sums)
-                ]
-                after = tuple(chunks[-SPLIT:])
-
-    x, _ = lax.optimization_barrier((lane_sum(cross), tuple(chunks[-SPLIT:])))
+                chunks += after
+
+    x = lane_sum(cross)
     for step in range(steps):
         x = x.reshape(2, x.shape[0] // 2, x.shape[1])
         bit = plan.bit(step)
@@ -431,12 +445,13 @@
     update = x
 
     def place(member, column):
-        sums = []
-        for i in range(member * SPLIT, (member + 1) * SPLIT):
+        sums, splits = [], plan.splits[member]
+        first = sum(plan.splits[:member])
+        for i in range(first, first + splits):
             sums += [chunks[i], ends[i]]
         return pl.pallas_call(
             functools.partial(place_kernel, plan, member),
-            in_specs=smem(1) + vmem(1 + 2 * SPLIT)
+            in_specs=smem(1) + vmem(1 + 2 * splits)
             + [pl.BlockSpec(memory_space=pl.ANY)] * (member > 0),
             out_specs=pl.BlockSpec(memory_space=pl.ANY),
             out_shape=jax.ShapeDtypeStruct((inverse_front.shape[0], factor.shape[1]), F32),
@@ -446,32 +461,29 @@
                 pltpu.SemaphoreType.DMA((plan.na,)),
                 pltpu.SemaphoreType.DMA((members, plan.row_tiles)),
             ],
-            input_output_aliases={2 + 2 * SPLIT: 0} if member else {},
+            input_output_aliases={2 + 2 * splits: 0} if member else {},
             compiler_params=PARAMS,
-            cost_estimate=pl.CostEstimate(
-                flops=6 * depth * width * width, bytes_accessed=8 << 20, transcendentals=0
-            ),
+            cost_estimate=SMALL,
             name="place",
         )(tile_list, unit_lower, *sums, *([column] if member else []))
 
-    ends, column = {}, None
-    for i in range(len(chunks)):
-        if i + 1 < len(chunks):
-            if i + 1 < SPLIT:
-                wait = (last_swap, entered[i])
-            elif (i + 1) % SPLIT and i >= SPLIT:
-                wait = (ends[i - SPLIT],)
-            else:
-                wait = ()
-            entered[i + 1] = enter(chunks[i + 1], wait)
-            wait = (entered[i + 1],)
-        else:
-            wait = () if column is None else (column,)
-        chunks[i], ends[i] = run(chunks[i], entered[i], wait)
-        if i % SPLIT == SPLIT - 1:
-            column = place(i // SPLIT, column)
-
-    x, got = run(update, enter(update))
+    ends, sent, column, last = {}, {}, None, len(chunks) - 1
+    middle = len(hops) - 1
+    for i in range(1, last + 1):
+        entered[i] = enter(chunks[i], (entered[i - 1],) if i > 1 else ())
+    for i in range(last + 1):
+        ties = [()] * (middle - 1) + [(ends[0],)] if i == 1 and middle else ()
+        chunks[i], ends[i], sent[i], _ = run(
+            chunks[i], entered[i], ties, second if i == 0 else None
+        )
+    ties = [tuple(sent[max(last - 1, 0)][-1:]), tuple(sent[last][-1:])][:middle]
+    update, got, _, _ = run(update, enter(update), ties)
+    for member in range(members):
+        column = place(member, column)
+        if member == 0:
+            got, _ = lax.optimization_barrier((got, column))
+
+    x = update
     x = jnp.where(plan.at_end(), got, x)
     pieces = [x] + [lax.ppermute(x, both, plan.offset_pairs(r)) for r in range(1, 1 << steps)]
     x, _ = lax.optimization_barrier((jnp.concatenate(pieces), column))
@@ -483,9 +495,7 @@
         out_shape=jax.ShapeDtypeStruct(unit_lower.shape, F32),
         scratch_shapes=[pltpu.VMEM((lanes, members * width // lanes, width), F32)],
         compiler_params=PARAMS,
-        cost_estimate=pl.CostEstimate(
-            flops=24 * width * width * width, bytes_accessed=8 << 20, transcendentals=0
-        ),
+        cost_estimate=SMALL,
         name="diagonal",
     )(pivot_inverse, unit_lower, *parts)
     return (column, diagonal)

time: 198 us -> 216 us (1.091)
  starting transfers between devices: 47.4 us -> 59.3 us
  other arithmetic: 15.7 us -> 18 us
    ppermute x5 -> x4, starting transfers between devices: 14 us -> 23.6 us  [enter(): return lax.ppermute(x, 'col', hops[0])]
    add x10 -> x8, other arithmetic: 2.99 us -> 7.13 us  [line_step(): return x + got]
    ppermute x2, starting transfers between devices: 0.07 us -> 3.49 us  [shards(): x = keep + lax.ppermute(send, both, plan.bit_pairs(step))]
    unnamed x42 -> x36, local copies, waits for them, and re-layouts: 3.01 us -> 5.19 us
    ppermute x10 -> x8, starting transfers between devices: 10 us -> 8.99 us  [the longest x7 7.35 us: run(): got = lax.ppermute(y, 'col', hops[hop])]
    ppermute x10 -> x8, waiting for transfers between devices: 35.5 us -> 36.5 us  [the longest x7 36.5 us: run(): got = lax.ppermute(y, 'col', hops[hop])]
    ppermute x5 -> x4, waiting for transfers between devices: 25.6 us -> 26.5 us  [enter(): return lax.ppermute(x, 'col', hops[0])]
  transfers between devices with their start and end apart: 34 -> 31, of which waited for: 19 -> 14; matrix products, arithmetic and copies ran while one was open for 8% -> 8% of each run, Pallas kernels for 14% -> 13%
where the time goes in v6:
time: 216 us; the launch traced here: 215 us
  waiting for transfers between devices  97.4 us (45%)
  starting transfers between devices  59.3 us (27%)
  Pallas kernels  32.1 us (15%)
  other arithmetic  18 us (8%)
  local copies, waits for them, and re-layouts  6.57 us (3%)
    ppermute x7, waiting for transfers between devices, run(): got = lax.ppermute(y, 'col', hops[hop])  36.5 us
    ppermute x8, waiting for transfers between devices, issue(): out.append(lax.ppermute(x, axis, pairs))  30.3 us
    ppermute x4, waiting for transfers between devices, enter(): return lax.ppermute(x, 'col', hops[0])  26.5 us
    ppermute x4, starting transfers between devices, enter(): return lax.ppermute(x, 'col', hops[0])  23.6 us
    ppermute x8, starting transfers between devices, issue(): out.append(lax.ppermute(x, axis, pairs))  18.9 us
    pallas_call x2, Pallas kernels, forward(): pl.pallas_call(functools.partial(forward_kernel, plan, member), in_specs=...  9.98 us
    pallas_call x2, Pallas kernels, gather(): pl.pallas_call(functools.partial(gather_kernel, plan, member), in_specs=s...  9.26 us
    pallas_call x2, Pallas kernels, place(): pl.pallas_call(functools.partial(place_kernel, plan, member), in_specs=sm...  7.79 us
  transfers between devices with their start and end apart: 31, of which 14 were waited for; matrix products, arithmetic and copies ran while one was open for 8% of the time, Pallas kernels for 13%

profile of v6, /device:TPU:0, one launch (start us, length us, event | category | flops | bytes accessed | tf_op | source)
XLA Modules:
  0.0 214.6 jit_solution(10563296660786732626)
XLA Ops:
  0.6 1.3 slice.13.factor
  2.0 5.8 %collective-permute-start.3 = (f32[512,512]{1,0:T(8,128)S(1)}, f32[512,512]{1,0:T(8,128)}, u32[]{:S(2)}, u32[]{:S(2)}) collective-permute-start(f32[512,512]{1,0:T(8,128)S(1)} %slice.13.factor), channel_id=1, source_target_pairs={{0,8},{4,20},{9,1},{13,29},{18,26}} | collective-permute-start | bytes 3145736 | tf_op jit(solution)/shard_map/ppermute | solution.py:156
  7.8 5.1 %gather_mirror.3 = (bf16[512,1024]{1,0:T(8,128)(2,1)S(1)}, bf16[512,1024]{1,0:T(8,128)(2,1)S(1)}, f32[512,512]{1,0:T(8,128)S(1)}, f32[512,512]{1,0:T(8,128)}) custom-call(s32[2,16]{1,0:T(2,128)S(1)} %copy-done.7, s32[2,16]{1,0:T(2,128)S(1)} %copy-done.8, f32[2048,4096]{1,0:T(8,128)} %front.3, f32[512,512]{1,0:T(8,128)S(1)} %slice.13.factor), custom_call_target="tpu_custom_call" | custom-call | flops 1048576 | bytes 65536 | tf_op jit(solution)/shard_map/gather_mirror/pallas_call | solution.py:333
  13.9 5.2 %collective-permute-done.3 = f32[512,512]{1,0:T(8,128)} collective-permute-done((f32[512,512]{1,0:T(8,128)S(1)}, f32[512,512]{1,0:T(8,128)}, u32[]{:S(2)}, u32[]{:S(2)}) %collective-permute-start.3) | collective-permute-done | bytes 1048608 | tf_op jit(solution)/shard_map/ppermute | solution.py:156
  19.1 1.9 broadcast_select_fusion.1
  21.0 1.4 collective-permute-start.4
  22.4 1.4 add.83
  23.8 1.3 collective-permute-start.2
  25.1 4.1 %gather_mirror.2 = (bf16[512,1024]{1,0:T(8,128)(2,1)S(1)}, bf16[512,1024]{1,0:T(8,128)(2,1)S(1)}, f32[512,512]{1,0:T(8,128)S(1)}, f32[512,512]{1,0:T(8,128)S(1)}) custom-call(s32[2,16]{1,0:T(2,128)S(1)} %copy-done.7, s32[2,16]{1,0:T(2,128)S(1)} %copy-done.8, f32[2048,4096]{1,0:T(8,128)} %front.3, f32[512,512]{1,0:T(8,128)S(1)} %get-tuple-element.46.factor), custom_call_target="tpu_custom_call" | custom-call | flops 1048576 | bytes 65536 | tf_op jit(solution)/shard_map/gather_mirror/pallas_call | solution.py:333
  29.3 5.3 %collective-permute-done.4 = f32[512,512]{1,0:T(8,128)S(1)} collective-permute-done((f32[512,512]{1,0:T(8,128)S(1)}, f32[512,512]{1,0:T(8,128)S(1)}, u32[]{:S(2)}, u32[]{:S(2)}) %collective-permute-start.4) | collective-permute-done | bytes 1048608 | tf_op jit(solution)/shard_map/ppermute | solution.py:156
  34.9 5.6 %collective-permute-done.2 = f32[512,512]{1,0:T(8,128)S(1)} collective-permute-done((f32[512,512]{1,0:T(8,128)S(1)}, f32[512,512]{1,0:T(8,128)S(1)}, u32[]{:S(2)}, u32[]{:S(2)}) %collective-permute-start.2) | collective-permute-done | bytes 1048608 | tf_op jit(solution)/shard_map/ppermute | solution.py:156
  40.7 1.4 collective-permute-start.6
  42.1 4.9 %collective-permute-start.8 = (f32[512,512]{1,0:T(8,128)S(1)}, f32[512,512]{1,0:T(8,128)S(1)}, u32[]{:S(2)}, u32[]{:S(2)}) collective-permute-start(f32[512,512]{1,0:T(8,128)S(1)} %get-tuple-element.46.factor), channel_id=1, source_target_pairs={{0,8},{4,20},{9,1},{13,29},{18,26}} | collective-permute-start | bytes 3145736 | tf_op jit(solution)/shard_map/ppermute | solution.py:156
  48.3 4.7 %forward.2 = (f32[512,512]{1,0:T(8,128)S(1)}, f32[256,512]{1,0:T(8,128)S(1)}, f32[256,512]{1,0:T(8,128)S(1)}) custom-call(bf16[512,1024]{1,0:T(8,128)(2,1)S(1)} %get-tuple-element.39.high, bf16[512,1024]{1,0:T(8,128)(2,1)S(1)} %copy-done.6, f32[512,512]{1,0:T(8,128)S(1)} %slice.13.factor, f32[512,512]{1,0:T(8,128)} %copy-done.13, f32[512,512]{1,0:T(8,128)} %copy-done.12, ...), custom_call_target="tpu_custom_call" | custom-call | flops 1048576 | bytes 65536 | tf_op jit(solution)/shard_map/forward/pallas_call | solution.py:351
  53.0 4.8 %collective-permute-done.6 = f32[512,512]{1,0:T(8,128)S(1)} collective-permute-done((f32[512,512]{1,0:T(8,128)S(1)}, f32[512,512]{1,0:T(8,128)S(1)}, u32[]{:S(2)}, u32[]{:S(2)}) %collective-permute-start.6) | collective-permute-done | bytes 1048608 | tf_op jit(solution)/shard_map/ppermute | solution.py:156
  58.0 1.6 collective-permute-start.7
  59.8 1.4 collective-permute-start.9
  61.2 1.3 collective-permute-start.10
  62.5 16.7 %collective-permute-done.7 = f32[512,512]{1,0:T(8,128)S(1)} collective-permute-done((f32[512,512]{1,0:T(8,128)S(1)}, f32[512,512]{1,0:T(8,128)S(1)}, u32[]{:S(2)}, u32[]{:S(2)}) %collective-permute-start.7) | collective-permute-done | bytes 1048608 | tf_op jit(solution)/shard_map/ppermute | solution.py:372
  79.5 1.3 add.87.mirror
  82.0 1.6 collective-permute-start.12
  83.6 1.5 collective-permute-start.13
  86.1 5.3 %forward.3 = (f32[256,512]{1,0:T(8,128)S(1)}, f32[256,512]{1,0:T(8,128)S(1)}, f32[512,512]{1,0:T(8,128)S(1)}, f32[512,512]{1,0:T(8,128)S(1)}) custom-call(bf16[512,1024]{1,0:T(8,128)(2,1)S(1)} %get-tuple-element.35.high, bf16[512,1024]{1,0:T(8,128)(2,1)} %copy-done.2, f32[512,512]{1,0:T(8,128)} %copy-done.1, f32[512,512]{1,0:T(8,128)} %add.87.mirror, ...), custom_call_target="tpu_custom_call" | custom-call | flops 1048576 | bytes 65536 | tf_op jit(solution)/shard_map/forward/pallas_call | solution.py:351
  91.9 9.4 %collective-permute-done.13 = f32[512,512]{1,0:T(8,128)} collective-permute-done((f32[512,512]{1,0:T(8,128)}, f32[512,512]{1,0:T(8,128)}, u32[]{:S(2)}, u32[]{:S(2)}) %collective-permute-start.13) | collective-permute-done | bytes 1048608 | tf_op jit(solution)/shard_map/ppermute | solution.py:156
  101.3 2.4 %slice_add_fusion = (f32[256,512]{1,0:T(8,128)}, f32[256,512]{1,0:T(8,128)}) fusion(f32[256,512]{1,0:T(8,128)S(1)} %get-tuple-element.60, f32[512,512]{1,0:T(8,128)} %collective-permute-done.13, f32[256,512]{1,0:T(8,128)S(1)} %get-tuple-element.55), kind=kLoop, calls=%fused_computation.3 | loop fusion | flops 262144 | bytes 3145728 | tf_op jit(solution)/shard_map/add | solution.py:434
  103.7 12.8 %collective-permute-start.14 = (f32[256,512]{1,0:T(8,128)}, f32[256,512]{1,0:T(8,128)S(1)}, u32[]{:S(2)}, u32[]{:S(2)}) collective-permute-start(f32[256,512]{1,0:T(8,128)} %get-tuple-element.71), channel_id=1, source_target_pairs={{0,1},{3,2},{4,5},{7,6},{8,9},{11,10},{12,13},{15,14},{16,17},{19,... | collective-permute-start | bytes 1572872 | tf_op jit(solution)/shard_map/ppermute | solution.py:372
  116.5 1.5 add.97
  118.0 3.4 %collective-permute-start.22 = (f32[256,512]{1,0:T(8,128)S(1)}, f32[256,512]{1,0:T(8,128)S(1)}, u32[]{:S(2)}, u32[]{:S(2)}) collective-permute-start(f32[256,512]{1,0:T(8,128)S(1)} %dynamic-slice_bitcast_fusion), channel_id=1, source_target_pairs={{0,8},{1,9},{2,10},{3,11},{4,20},{5,21},{6,22},{7,23},{8,0},{9,1},... | collective-permute-start | bytes 1572872 | tf_op jit(solution)/shard_map/ppermute | solution.py:444
  121.4 6.3 %collective-permute-done.14 = f32[256,512]{1,0:T(8,128)S(1)} collective-permute-done((f32[256,512]{1,0:T(8,128)}, f32[256,512]{1,0:T(8,128)S(1)}, u32[]{:S(2)}, u32[]{:S(2)}) %collective-permute-start.14) | collective-permute-done | bytes 524320 | tf_op jit(solution)/shard_map/ppermute | solution.py:372
  127.7 4.3 %collective-permute-start.18 = (f32[256,512]{1,0:T(8,128)}, f32[256,512]{1,0:T(8,128)S(1)}, u32[]{:S(2)}, u32[]{:S(2)}) collective-permute-start(f32[256,512]{1,0:T(8,128)} %get-tuple-element.61), channel_id=1, source_target_pairs={{0,1},{3,2},{4,5},{7,6},{8,9},{11,10},{12,13},{15,14},{16,17},{19,... | collective-permute-start | bytes 1572872 | tf_op jit(solution)/shard_map/ppermute | solution.py:372
  132.3 1.8 add.93.rest_0_
  134.1 1.3 collective-permute-start.16
  137.2 1.4 collective-permute-done.23
  138.7 4.9 %collective-permute-start.24 = (f32[128,512]{1,0:T(8,128)S(1)}, f32[128,512]{1,0:T(8,128)S(1)}, u32[]{:S(2)}, u32[]{:S(2)}) collective-permute-start(f32[128,512]{1,0:T(8,128)S(1)} %bitcast_add_fusion.1), channel_id=1, source_target_pairs={{0,1},{3,2},{4,5},{7,6},{8,9},{11,10},{12,13},{15,14},{16,17},{19,... | collective-permute-start | bytes 786440 | tf_op jit(solution)/shard_map/ppermute | solution.py:372
  146.5 3.6 %collective-permute-done.24 = f32[128,512]{1,0:T(8,128)S(1)} collective-permute-done((f32[128,512]{1,0:T(8,128)S(1)}, f32[128,512]{1,0:T(8,128)S(1)}, u32[]{:S(2)}, u32[]{:S(2)}) %collective-permute-start.24) | collective-permute-done | bytes 262176 | tf_op jit(solution)/shard_map/ppermute | solution.py:372
  151.7 1.3 collective-permute-start.26
  153.0 8.5 %collective-permute-done.16.rest_1_ = f32[512,512]{1,0:T(8,128)S(1)} collective-permute-done((f32[512,512]{1,0:T(8,128)S(1)}, f32[512,512]{1,0:T(8,128)S(1)}, u32[]{:S(2)}, u32[]{:S(2)}) %collective-permute-start.16) | collective-permute-done | bytes 1048608 | tf_op jit(solution)/shard_map/ppermute | solution.py:384
  162.5 1.3 collective-permute-start.17
  163.8 1.3 collective-permute-start.20
  165.1 1.2 copy-done.4
  166.3 4.1 %place.2.rest_4_ = f32[2048,1024]{1,0:T(8,128)} custom-call(s32[2,16]{1,0:T(2,128)S(1)} %copy-done.7, f32[2,512,512]{2,1,0:T(8,128)S(1)} %copy-done, f32[512,512]{1,0:T(8,128)S(1)} %add.93.rest_0_, f32[512,512]{1,0:T(8,128)S(1)} %copy-done.4), custom_call_target="tpu_custom_call" | custom-call | flops 1048576 | bytes 65536 | tf_op jit(solution)/shard_map/place/pallas_call | solution.py:452
  170.5 10.6 %collective-permute-done.26 = f32[128,512]{1,0:T(8,128)} collective-permute-done((f32[128,512]{1,0:T(8,128)S(1)}, f32[128,512]{1,0:T(8,128)}, u32[]{:S(2)}, u32[]{:S(2)}) %collective-permute-start.26) | collective-permute-done | bytes 262176 | tf_op jit(solution)/shard_map/ppermute | solution.py:384
  183.1 2.5 %collective-permute-start.27 = (f32[128,512]{1,0:T(8,128)S(1)}, f32[128,512]{1,0:T(8,128)S(1)}, u32[]{:S(2)}, u32[]{:S(2)}) collective-permute-start(f32[128,512]{1,0:T(8,128)S(1)} %broadcast_select_fusion.2), channel_id=1, source_target_pairs={{0,16},{1,17},{2,18},{3,19},{8,24},{9,25},{10,26},{11,27},{16,0},{... | collective-permute-start | bytes 786440 | tf_op jit(solution)/shard_map/ppermute | solution.py:488
  185.6 6.7 %collective-permute-done.17.rest_1_ = f32[256,512]{1,0:T(8,128)} collective-permute-done((f32[256,512]{1,0:T(8,128)}, f32[256,512]{1,0:T(8,128)}, u32[]{:S(2)}, u32[]{:S(2)}) %collective-permute-start.17) | collective-permute-done | bytes 524320 | tf_op jit(solution)/shard_map/ppermute | solution.py:384
  192.3 10.7 %collective-permute-done.20.rest_3_ = f32[256,512]{1,0:T(8,128)} collective-permute-done((f32[256,512]{1,0:T(8,128)}, f32[256,512]{1,0:T(8,128)}, u32[]{:S(2)}, u32[]{:S(2)}) %collective-permute-start.20) | collective-permute-done | bytes 524320 | tf_op jit(solution)/shard_map/ppermute | solution.py:384
  203.0 3.7 %place.3 = f32[2048,1024]{1,0:T(8,128)} custom-call(s32[2,16]{1,0:T(2,128)S(1)} %copy-done.7, f32[2,512,512]{2,1,0:T(8,128)S(1)} %copy-done, f32[256,512]{1,0:T(8,128)} %add.92.rest_0_, f32[256,512]{1,0:T(8,128)} %collective-permute-done.17.rest_1_, f32[256,512]{1,0:T(8,128)} %add.96.rest_2_, ...), custom_call_target="tpu_custom_call", output_to_operand_aliasing={{}: (6, {})} | custom-call | flops 1048576 | bytes 65536 | tf_op jit(solution)/shard_map/place/pallas_call | solution.py:452
  206.9 2.6 %collective-permute-done.30.rest_1_ = f32[512,512]{1,0:T(8,128)S(1)} collective-permute-done((f32[512,512]{1,0:T(8,128)S(1)}, f32[512,512]{1,0:T(8,128)S(1)}, u32[]{:S(2)}, u32[]{:S(2)}) %collective-permute-start.30) | collective-permute-done | bytes 1048608 | tf_op jit(solution)/shard_map/ppermute | solution.py:88
  209.5 5.1 %diagonal.1 = f32[2,512,512]{2,1,0:T(8,128)} custom-call(f32[2,512]{1,0:T(2,128)S(1)} %copy-done.9, f32[2,512,512]{2,1,0:T(8,128)S(1)} %copy-done, f32[512,512]{1,0:T(8,128)S(1)} %pad_maximum_fusion.rest_0_, f32[512,512]{1,0:T(8,128)S(1)} %collective-permute-done.30.rest_1_), custom_call_target="tpu_custom_call" | custom-call | flops 1048576 | bytes 65536 | tf_op jit(solution)/shard_map/diagonal/pallas_call | solution.py:491
  (83 shorter events, 15.9 us)
Async XLA Ops:
  0.6 7.2 %copy-start.7 = (s32[2,16]{1,0:T(2,128)S(1)}, s32[2,16]{1,0:T(2,128)}, u32[]{:S(2)}) copy-start(s32[2,16]{1,0:T(2,128)} %tiles_ref.7) | copy-start | bytes 388
  0.6 7.1 %copy-start.8 = (s32[2,16]{1,0:T(2,128)S(1)}, s32[2,16]{1,0:T(2,128)}, u32[]{:S(2)}) copy-start(s32[2,16]{1,0:T(2,128)} %valid_ref.3) | copy-start | bytes 388
  2.0 17.2 %collective-permute-start.3 = (f32[512,512]{1,0:T(8,128)S(1)}, f32[512,512]{1,0:T(8,128)}, u32[]{:S(2)}, u32[]{:S(2)}) collective-permute-start(f32[512,512]{1,0:T(8,128)S(1)} %slice.13.factor), channel_id=1, source_target_pairs={{0,8},{4,20},{9,1},{13,29},{18,26}} | collective-permute-start | bytes 3145736 | tf_op jit(solution)/shard_map/ppermute | solution.py:156
  12.9 1.0 copy-start.5
  13.9 8.5 %collective-permute-start.1 = (f32[512,512]{1,0:T(8,128)}, f32[512,512]{1,0:T(8,128)}, u32[]{:S(2)}, u32[]{:S(2)}) collective-permute-start(f32[512,512]{1,0:T(8,128)} %get-tuple-element.42), channel_id=1, source_target_pairs={{4,0},{0,4},{12,8},{8,12},{20,16},{16,20},{28,24},{24,28},{5,1},{1... | collective-permute-start | bytes 3145736 | tf_op jit(solution)/shard_map/ppermute | solution.py:88
  21.0 21.1 %copy-start.1 = (f32[512,512]{1,0:T(8,128)}, f32[512,512]{1,0:T(8,128)S(1)}, u32[]{:S(2)}) copy-start(f32[512,512]{1,0:T(8,128)S(1)} %get-tuple-element.46.factor) | copy-start | bytes 3145732
  21.0 13.6 %collective-permute-start.4 = (f32[512,512]{1,0:T(8,128)S(1)}, f32[512,512]{1,0:T(8,128)S(1)}, u32[]{:S(2)}, u32[]{:S(2)}) collective-permute-start(f32[512,512]{1,0:T(8,128)S(1)} %get-tuple-element.43), channel_id=1, source_target_pairs={{0,16},{8,24},{4,12},{20,28},{9,25},{1,17},{29,21},{22,30}} | collective-permute-start | bytes 3145736 | tf_op jit(solution)/shard_map/ppermute | solution.py:156
  23.8 16.7 %collective-permute-start.2 = (f32[512,512]{1,0:T(8,128)S(1)}, f32[512,512]{1,0:T(8,128)S(1)}, u32[]{:S(2)}, u32[]{:S(2)}) collective-permute-start(f32[512,512]{1,0:T(8,128)S(1)} %add.83), channel_id=1, source_target_pairs={{16,0},{24,8},{12,4},{28,20},{25,9},{17,1},{21,29},{30,22}} | collective-permute-start | bytes 3145736 | tf_op jit(solution)/shard_map/ppermute | solution.py:156
  29.2 11.5 %copy-start.2 = (bf16[512,1024]{1,0:T(8,128)(2,1)}, bf16[512,1024]{1,0:T(8,128)(2,1)S(1)}, u32[]{:S(2)}) copy-start(bf16[512,1024]{1,0:T(8,128)(2,1)S(1)} %get-tuple-element.36.low) | copy-start | bytes 3145732
  29.2 17.9 %collective-permute-start = (f32[512,512]{1,0:T(8,128)S(1)}, f32[512,512]{1,0:T(8,128)S(1)}, u32[]{:S(2)}, u32[]{:S(2)}) collective-permute-start(f32[512,512]{1,0:T(8,128)S(1)} %get-tuple-element.38), channel_id=1, source_target_pairs={{4,0},{0,4},{12,8},{8,12},{20,16},{16,20},{28,24},{24,28},{5,1},{1... | collective-permute-start | bytes 3145736 | tf_op jit(solution)/shard_map/ppermute | solution.py:88
  34.8 12.5 %copy-start.12 = (f32[512,512]{1,0:T(8,128)}, f32[512,512]{1,0:T(8,128)S(1)}, u32[]{:S(2)}) copy-start(f32[512,512]{1,0:T(8,128)S(1)} %add.85.rest_0_) | copy-start | bytes 3145732
  34.8 12.5 %collective-permute-start.5 = (f32[512,512]{1,0:T(8,128)S(1)}, f32[512,512]{1,0:T(8,128)S(1)}, u32[]{:S(2)}, u32[]{:S(2)}) collective-permute-start(f32[512,512]{1,0:T(8,128)S(1)} %add.85.rest_0_), channel_id=1, source_target_pairs={{4,0},{0,4},{12,8},{8,12},{20,16},{16,20},{28,24},{24,28},{5,1},{1... | collective-permute-start | bytes 3145736 | tf_op jit(solution)/shard_map/ppermute | solution.py:88
  40.7 6.7 %copy-start.13 = (f32[512,512]{1,0:T(8,128)}, f32[512,512]{1,0:T(8,128)S(1)}, u32[]{:S(2)}) copy-start(f32[512,512]{1,0:T(8,128)S(1)} %add.84.mirror) | copy-start | bytes 3145732
  40.7 7.6 %copy-start.6 = (bf16[512,1024]{1,0:T(8,128)(2,1)S(1)}, bf16[512,1024]{1,0:T(8,128)(2,1)}, u32[]{:S(2)}) copy-start(bf16[512,1024]{1,0:T(8,128)(2,1)} %copy-done.5) | copy-start | bytes 3145732
  40.7 17.1 %collective-permute-start.6 = (f32[512,512]{1,0:T(8,128)S(1)}, f32[512,512]{1,0:T(8,128)S(1)}, u32[]{:S(2)}, u32[]{:S(2)}) collective-permute-start(f32[512,512]{1,0:T(8,128)S(1)} %add.84.mirror), channel_id=1, source_target_pairs={{8,0},{20,4},{1,9},{29,13},{26,18}} | collective-permute-start | bytes 3145736 | tf_op jit(solution)/shard_map/ppermute | solution.py:156
  42.1 17.5 %collective-permute-start.8 = (f32[512,512]{1,0:T(8,128)S(1)}, f32[512,512]{1,0:T(8,128)S(1)}, u32[]{:S(2)}, u32[]{:S(2)}) collective-permute-start(f32[512,512]{1,0:T(8,128)S(1)} %get-tuple-element.46.factor), channel_id=1, source_target_pairs={{0,8},{4,20},{9,1},{13,29},{18,26}} | collective-permute-start | bytes 3145736 | tf_op jit(solution)/shard_map/ppermute | solution.py:156
  47.3 1.0 copy-start.15
  53.0 6.6 %copy-start.10 = (f32[512,1024]{1,0:T(8,128)S(1)}, f32[512,1024]{1,0:T(8,128)}, u32[]{:S(2)}) copy-start(f32[512,1024]{1,0:T(8,128)} %param.7) | copy-start | bytes 6291460
  58.0 21.2 %collective-permute-start.7 = (f32[512,512]{1,0:T(8,128)S(1)}, f32[512,512]{1,0:T(8,128)S(1)}, u32[]{:S(2)}, u32[]{:S(2)}) collective-permute-start(f32[512,512]{1,0:T(8,128)S(1)} %add.86), channel_id=1, source_target_pairs={{0,1},{3,2},{4,5},{7,6},{8,9},{11,10},{12,13},{15,14},{16,17},{19,... | collective-permute-start | bytes 3145736 | tf_op jit(solution)/shard_map/ppermute | solution.py:372
  59.8 19.3 %collective-permute-start.9 = (f32[512,512]{1,0:T(8,128)S(1)}, f32[512,512]{1,0:T(8,128)S(1)}, u32[]{:S(2)}, u32[]{:S(2)}) collective-permute-start(f32[512,512]{1,0:T(8,128)S(1)} %broadcast_select_fusion), channel_id=1, source_target_pairs={{0,16},{8,24},{4,12},{20,28},{9,25},{1,17},{29,21},{22,30}} | collective-permute-start | bytes 3145736 | tf_op jit(solution)/shard_map/ppermute | solution.py:156
  61.2 18.0 %collective-permute-start.10 = (f32[512,512]{1,0:T(8,128)S(1)}, f32[512,512]{1,0:T(8,128)S(1)}, u32[]{:S(2)}, u32[]{:S(2)}) collective-permute-start(f32[512,512]{1,0:T(8,128)S(1)} %add.82), channel_id=1, source_target_pairs={{16,0},{24,8},{12,4},{28,20},{25,9},{17,1},{21,29},{30,22}} | collective-permute-start | bytes 3145736 | tf_op jit(solution)/shard_map/ppermute | solution.py:156
  79.4 2.6 %copy-start.11 = (f32[512,512]{1,0:T(8,128)}, f32[512,512]{1,0:T(8,128)S(1)}, u32[]{:S(2)}) copy-start(f32[512,512]{1,0:T(8,128)S(1)} %add.89.rest_0_) | copy-start | bytes 3145732
  79.4 5.7 %collective-permute-start.11 = (f32[512,512]{1,0:T(8,128)S(1)}, f32[512,512]{1,0:T(8,128)S(1)}, u32[]{:S(2)}, u32[]{:S(2)}) collective-permute-start(f32[512,512]{1,0:T(8,128)S(1)} %add.89.rest_0_), channel_id=1, source_target_pairs={{4,0},{0,4},{12,8},{8,12},{20,16},{16,20},{28,24},{24,28},{5,1},{1... | collective-permute-start | bytes 3145736 | tf_op jit(solution)/shard_map/ppermute | solution.py:88
  82.0 9.9 %collective-permute-start.12 = (f32[512,512]{1,0:T(8,128)}, f32[512,512]{1,0:T(8,128)}, u32[]{:S(2)}, u32[]{:S(2)}) collective-permute-start(f32[512,512]{1,0:T(8,128)} %add.88), channel_id=1, source_target_pairs={{1,2},{2,1},{5,6},{6,5},{9,10},{10,9},{13,14},{14,13},{17,18},{18,... | collective-permute-start | bytes 3145736 | tf_op jit(solution)/shard_map/ppermute | solution.py:410
  83.6 17.7 %collective-permute-start.13 = (f32[512,512]{1,0:T(8,128)}, f32[512,512]{1,0:T(8,128)}, u32[]{:S(2)}, u32[]{:S(2)}) collective-permute-start(f32[512,512]{1,0:T(8,128)} %add.87.mirror), channel_id=1, source_target_pairs={{8,0},{20,4},{1,9},{29,13},{26,18}} | collective-permute-start | bytes 3145736 | tf_op jit(solution)/shard_map/ppermute | solution.py:156
  85.1 1.0 copy-start.14
  91.4 25.1 %collective-permute-start.21 = (f32[512,512]{1,0:T(8,128)S(1)}, f32[512,512]{1,0:T(8,128)}, u32[]{:S(2)}, u32[]{:S(2)}) collective-permute-start(f32[512,512]{1,0:T(8,128)S(1)} %get-tuple-element.63), channel_id=1, source_target_pairs={{4,0},{0,4},{12,8},{8,12},{20,16},{16,20},{28,24},{24,28},{5,1},{1... | collective-permute-start | bytes 3145736 | tf_op jit(solution)/shard_map/ppermute | solution.py:88
  103.7 24.0 %collective-permute-start.14 = (f32[256,512]{1,0:T(8,128)}, f32[256,512]{1,0:T(8,128)S(1)}, u32[]{:S(2)}, u32[]{:S(2)}) collective-permute-start(f32[256,512]{1,0:T(8,128)} %get-tuple-element.71), channel_id=1, source_target_pairs={{0,1},{3,2},{4,5},{7,6},{8,9},{11,10},{12,13},{15,14},{16,17},{19,... | collective-permute-start | bytes 1572872 | tf_op jit(solution)/shard_map/ppermute | solution.py:372
  118.0 14.0 %collective-permute-start.22 = (f32[256,512]{1,0:T(8,128)S(1)}, f32[256,512]{1,0:T(8,128)S(1)}, u32[]{:S(2)}, u32[]{:S(2)}) collective-permute-start(f32[256,512]{1,0:T(8,128)S(1)} %dynamic-slice_bitcast_fusion), channel_id=1, source_target_pairs={{0,8},{1,9},{2,10},{3,11},{4,20},{5,21},{6,22},{7,23},{8,0},{9,1},... | collective-permute-start | bytes 1572872 | tf_op jit(solution)/shard_map/ppermute | solution.py:444
  127.7 4.5 %copy-start.16 = (f32[256,512]{1,0:T(8,128)}, f32[256,512]{1,0:T(8,128)S(1)}, u32[]{:S(2)}) copy-start(f32[256,512]{1,0:T(8,128)S(1)} %collective-permute-done.14) | copy-start | bytes 1572868
  127.7 15.9 %collective-permute-start.18 = (f32[256,512]{1,0:T(8,128)}, f32[256,512]{1,0:T(8,128)S(1)}, u32[]{:S(2)}, u32[]{:S(2)}) collective-permute-start(f32[256,512]{1,0:T(8,128)} %get-tuple-element.61), channel_id=1, source_target_pairs={{0,1},{3,2},{4,5},{7,6},{8,9},{11,10},{12,13},{15,14},{16,17},{19,... | collective-permute-start | bytes 1572872 | tf_op jit(solution)/shard_map/ppermute | solution.py:372
  132.2 6.4 %collective-permute-start.23 = (f32[128,512]{1,0:T(8,128)S(1)}, f32[128,512]{1,0:T(8,128)S(1)}, u32[]{:S(2)}, u32[]{:S(2)}) collective-permute-start(f32[128,512]{1,0:T(8,128)S(1)} %dynamic-slice_bitcast_fusion.1), channel_id=1, source_target_pairs={{0,16},{1,17},{2,18},{3,19},{4,12},{5,13},{6,14},{7,15},{8,24},{9,... | collective-permute-start | bytes 786440 | tf_op jit(solution)/shard_map/ppermute | solution.py:444
  132.3 3.1 %copy-start.17 = (f32[256,512]{1,0:T(8,128)S(1)}, f32[256,512]{1,0:T(8,128)}, u32[]{:S(2)}) copy-start(f32[256,512]{1,0:T(8,128)} %copy-done.16) | copy-start | bytes 1572868
  134.1 27.5 %collective-permute-start.16 = (f32[512,512]{1,0:T(8,128)S(1)}, f32[512,512]{1,0:T(8,128)S(1)}, u32[]{:S(2)}, u32[]{:S(2)}) collective-permute-start(f32[512,512]{1,0:T(8,128)S(1)} %add.93.rest_0_), channel_id=1, source_target_pairs={{1,0},{2,3},{5,4},{6,7},{9,8},{10,11},{13,12},{14,15},{17,16},{18,... | collective-permute-start | bytes 3145736 | tf_op jit(solution)/shard_map/ppermute | solution.py:384
  136.5 9.1 %collective-permute-start.15 = (f32[256,512]{1,0:T(8,128)S(1)}, f32[256,512]{1,0:T(8,128)S(1)}, u32[]{:S(2)}, u32[]{:S(2)}) collective-permute-start(f32[256,512]{1,0:T(8,128)S(1)} %add.91), channel_id=1, source_target_pairs={{1,2},{2,1},{5,6},{6,5},{9,10},{10,9},{13,14},{14,13},{17,18},{18,... | collective-permute-start | bytes 1572872 | tf_op jit(solution)/shard_map/ppermute | solution.py:384
  138.7 11.4 %collective-permute-start.24 = (f32[128,512]{1,0:T(8,128)S(1)}, f32[128,512]{1,0:T(8,128)S(1)}, u32[]{:S(2)}, u32[]{:S(2)}) collective-permute-start(f32[128,512]{1,0:T(8,128)S(1)} %bitcast_add_fusion.1), channel_id=1, source_target_pairs={{0,1},{3,2},{4,5},{7,6},{8,9},{11,10},{12,13},{15,14},{16,17},{19,... | collective-permute-start | bytes 786440 | tf_op jit(solution)/shard_map/ppermute | solution.py:372
  144.8 20.3 %copy-start = (f32[2,512,512]{2,1,0:T(8,128)S(1)}, f32[2,512,512]{2,1,0:T(8,128)}, u32[]{:S(2)}) copy-start(f32[2,512,512]{2,1,0:T(8,128)} %unit_ref.5) | copy-start | bytes 6291460
  144.8 6.0 %collective-permute-start.19 = (f32[256,512]{1,0:T(8,128)S(1)}, f32[256,512]{1,0:T(8,128)S(1)}, u32[]{:S(2)}, u32[]{:S(2)}) collective-permute-start(f32[256,512]{1,0:T(8,128)S(1)} %add.95), channel_id=1, source_target_pairs={{1,2},{2,1},{5,6},{6,5},{9,10},{10,9},{13,14},{14,13},{17,18},{18,... | collective-permute-start | bytes 1572872 | tf_op jit(solution)/shard_map/ppermute | solution.py:384
  150.1 1.6 collective-permute-start.25
  151.7 29.3 %collective-permute-start.26 = (f32[128,512]{1,0:T(8,128)S(1)}, f32[128,512]{1,0:T(8,128)}, u32[]{:S(2)}, u32[]{:S(2)}) collective-permute-start(f32[128,512]{1,0:T(8,128)S(1)} %add.104), channel_id=1, source_target_pairs={{1,0},{2,3},{5,4},{6,7},{9,8},{10,11},{13,12},{14,15},{17,16},{18,... | collective-permute-start | bytes 786440 | tf_op jit(solution)/shard_map/ppermute | solution.py:384
  162.5 29.8 %collective-permute-start.17 = (f32[256,512]{1,0:T(8,128)}, f32[256,512]{1,0:T(8,128)}, u32[]{:S(2)}, u32[]{:S(2)}) collective-permute-start(f32[256,512]{1,0:T(8,128)} %add.92.rest_0_), channel_id=1, source_target_pairs={{1,0},{2,3},{5,4},{6,7},{9,8},{10,11},{13,12},{14,15},{17,16},{18,... | collective-permute-start | bytes 1572872 | tf_op jit(solution)/shard_map/ppermute | solution.py:384
  163.8 39.2 %collective-permute-start.20 = (f32[256,512]{1,0:T(8,128)}, f32[256,512]{1,0:T(8,128)}, u32[]{:S(2)}, u32[]{:S(2)}) collective-permute-start(f32[256,512]{1,0:T(8,128)} %add.96.rest_2_), channel_id=1, source_target_pairs={{1,0},{2,3},{5,4},{6,7},{9,8},{10,11},{13,12},{14,15},{17,16},{18,... | collective-permute-start | bytes 1572872 | tf_op jit(solution)/shard_map/ppermute | solution.py:384
  165.1 1.2 copy-start.4
  182.0 24.6 %collective-permute-start.29 = (f32[128,512]{1,0:T(8,128)S(1)}, f32[128,512]{1,0:T(8,128)S(1)}, u32[]{:S(2)}, u32[]{:S(2)}) collective-permute-start(f32[128,512]{1,0:T(8,128)S(1)} %broadcast_select_fusion.2), channel_id=1, source_target_pairs={{0,24},{1,25},{2,26},{3,27},{8,16},{9,17},{10,18},{11,19},{16,8},{... | collective-permute-start | bytes 786440 | tf_op jit(solution)/shard_map/ppermute | solution.py:488
  182.1 24.6 %collective-permute-start.28 = (f32[128,512]{1,0:T(8,128)S(1)}, f32[128,512]{1,0:T(8,128)S(1)}, u32[]{:S(2)}, u32[]{:S(2)}) collective-permute-start(f32[128,512]{1,0:T(8,128)S(1)} %broadcast_select_fusion.2), channel_id=1, source_target_pairs={{0,8},{1,9},{2,10},{3,11},{8,0},{9,1},{10,2},{11,3},{16,24},{17,25... | collective-permute-start | bytes 786440 | tf_op jit(solution)/shard_map/ppermute | solution.py:488
  183.1 23.6 %collective-permute-start.27 = (f32[128,512]{1,0:T(8,128)S(1)}, f32[128,512]{1,0:T(8,128)S(1)}, u32[]{:S(2)}, u32[]{:S(2)}) collective-permute-start(f32[128,512]{1,0:T(8,128)S(1)} %broadcast_select_fusion.2), channel_id=1, source_target_pairs={{0,16},{1,17},{2,18},{3,19},{8,24},{9,25},{10,26},{11,27},{16,0},{... | collective-permute-start | bytes 786440 | tf_op jit(solution)/shard_map/ppermute | solution.py:488
  206.7 2.9 %copy-start.9 = (f32[2,512]{1,0:T(2,128)S(1)}, f32[2,512]{1,0:T(2,128)}, u32[]{:S(2)}) copy-start(f32[2,512]{1,0:T(2,128)} %pivot.1) | copy-start | bytes 12292
  206.8 2.7 %collective-permute-start.30 = (f32[512,512]{1,0:T(8,128)S(1)}, f32[512,512]{1,0:T(8,128)S(1)}, u32[]{:S(2)}, u32[]{:S(2)}) collective-permute-start(f32[512,512]{1,0:T(8,128)S(1)} %pad_maximum_fusion.rest_0_), channel_id=1, source_target_pairs={{4,0},{0,4},{12,8},{8,12},{20,16},{16,20},{28,24},{24,28},{5,1},{1... | collective-permute-start | bytes 3145736 | tf_op jit(solution)/shard_map/ppermute | solution.py:88
  (1 other events, 1.0 us)

commit v7 on v6

--- a/solution.py
+++ b/solution.py
@@ -11,7 +11,7 @@
 BF16 = jnp.bfloat16
 VMEM = pltpu.MemorySpace.VMEM
 SMEM = pltpu.MemorySpace.SMEM
-SMALL = pl.CostEstimate(flops=1 << 20, bytes_accessed=1 << 16, transcendentals=0)
+COST = pl.CostEstimate(flops=1600 << 20, bytes_accessed=8 << 20, transcendentals=0)
 PARAMS = pltpu.CompilerParams(vmem_limit_bytes=48 * 1024 * 1024)
 
 
@@ -58,7 +58,7 @@
             bits[lane % len(bits):] + bits[:lane % len(bits)] for lane in range(self.lanes)
         ]
         self.steps = len(bits)
-        self.splits = [1] + [2] * (self.members - 1)
+        self.splits = [2] * self.members
 
     def device(self, chip, lane, col):
         return (chip * self.lanes + lane) * self.cols + col
@@ -341,7 +341,7 @@
                 pltpu.SemaphoreType.DMA((plan.na, plan.nb)),
             ],
             compiler_params=PARAMS,
-            cost_estimate=SMALL,
+            cost_estimate=COST,
             name="gather_mirror",
         )(tile_list, tile_valid, inverse_front, factors[member])
 
@@ -359,10 +359,10 @@
                 pltpu.VMEM((width, width), F32),
             ],
             compiler_params=PARAMS,
-            cost_estimate=SMALL,
+            cost_estimate=COST,
             name="forward",
         )(high, low, factors[member], mirror, *parts, *earlier)
-        return outs[:splits], outs[splits:]
+        return outs[:splits], outs[splits:], parts[-1]
 
     hops = plan.line_hops()
 
@@ -371,26 +371,22 @@
             x, _ = lax.optimization_barrier((x, tuple(after)))
         return lax.ppermute(x, "col", hops[0])
 
-    def run(x, got, ties=(), second=None):
-        sent, brought = [], []
+    def run(x, got, ties=()):
+        sent = []
         for hop in range(1, len(hops)):
             x = plan.line_step(hop - 1, x, got)
             sent.append(x)
             tie = ties[hop - 1] if hop <= len(ties) else ()
             y = lax.optimization_barrier((x, tuple(tie)))[0] if tie else x
-            if hop == 1 and second is not None:
-                got = second
-            else:
-                got = lax.ppermute(y, "col", hops[hop])
-            brought.append(got)
+            got = lax.ppermute(y, "col", hops[hop])
         if len(hops) == 1:
             got = x = x + got
-        return x, got, sent, brought
+        return x, got, sent
 
     spread, collect = Chain(), Chain()
     count = members * steps
     tiles, held, mirror, chunks, entered = {}, {}, {}, [], {}
-    after, cross, second = (), [], None
+    after, cross, last_swap = (), [], ()
     for phase in range(count + 1):
         if phase < count:
             out, step = divmod(phase, steps)
@@ -406,9 +402,6 @@
             entered[0], got_out, got_back = lax.optimization_barrier(
                 (entered[0], got_out, got_back)
             )
-        if phase == count and chunks and len(hops) > 1:
-            second = lax.ppermute(plan.line_step(0, chunks[0], entered[0]), "col", hops[1])
-            second, got_back = lax.optimization_barrier((second, got_back))
         after = ()
         if phase % steps == 0 and phase < count:
             high, low, *parts = gather(out) if out == 0 else tiles[out]
@@ -423,19 +416,14 @@
             if turn < steps - 1:
                 mirror[back] = mirror[back] + got_back
             else:
-                x = mirror[back]
-                if chunks:
-                    x, _ = lax.optimization_barrier(
-                        (x, plan.line_step(0, chunks[0], entered[0]))
-                    )
-                sums, cross = forward(back, *tiles[back], x, held[back], cross)
+                sums, cross, last_swap = forward(back, *tiles[back], mirror[back], held[back], cross)
                 share = sums[0].shape[0]
                 after = tuple(
                     part + got_back[i * share:(i + 1) * share] for i, part in enumerate(sums)
                 )
                 chunks += after
 
-    x = lane_sum(cross)
+    x, _ = lax.optimization_barrier((lane_sum(cross), after))
     for step in range(steps):
         x = x.reshape(2, x.shape[0] // 2, x.shape[1])
         bit = plan.bit(step)
@@ -463,21 +451,23 @@
             ],
             input_output_aliases={2 + 2 * splits: 0} if member else {},
             compiler_params=PARAMS,
-            cost_estimate=SMALL,
+            cost_estimate=COST,
             name="place",
         )(tile_list, unit_lower, *sums, *([column] if member else []))
 
     ends, sent, column, last = {}, {}, None, len(chunks) - 1
     middle = len(hops) - 1
-    for i in range(1, last + 1):
-        entered[i] = enter(chunks[i], (entered[i - 1],) if i > 1 else ())
     for i in range(last + 1):
-        ties = [()] * (middle - 1) + [(ends[0],)] if i == 1 and middle else ()
-        chunks[i], ends[i], sent[i], _ = run(
-            chunks[i], entered[i], ties, second if i == 0 else None
-        )
-    ties = [tuple(sent[max(last - 1, 0)][-1:]), tuple(sent[last][-1:])][:middle]
-    update, got, _, _ = run(update, enter(update), ties)
+        if i < last:
+            if i + 1 == last and last > 2:
+                wait = (ends[i - 2],)
+            else:
+                wait = (entered[i], last_swap) if i == 0 else ()
+            entered[i + 1] = enter(chunks[i + 1], wait)
+        ties = [()] * (middle - 1) + [(entered[i + 1],)] if i < last and middle else ()
+        chunks[i], ends[i], sent[i] = run(chunks[i], entered[i], ties)
+    ahead = sent[max(last - 1, 0)]
+    update, got, _ = run(update, enter(update), [(x,) for x in ahead])
     for member in range(members):
         column = place(member, column)
         if member == 0:
@@ -495,7 +485,7 @@
         out_shape=jax.ShapeDtypeStruct(unit_lower.shape, F32),
         scratch_shapes=[pltpu.VMEM((lanes, members * width // lanes, width), F32)],
         compiler_params=PARAMS,
-        cost_estimate=SMALL,
+        cost_estimate=COST,
         name="diagonal",
     )(pivot_inverse, unit_lower, *parts)
     return (column, diagonal)

time: 216 us -> 208 us (0.963)
  starting transfers between devices: 59.3 us -> 52.1 us
    ppermute x7 -> x10, waiting for transfers between devices: 36.5 us -> 45.8 us  [run(): got = lax.ppermute(y, 'col', hops[hop])]
    ppermute x8, waiting for transfers between devices: 30.3 us -> 24.2 us  [issue(): out.append(lax.ppermute(x, axis, pairs))]
    ppermute x4 -> x5, starting transfers between devices: 23.6 us -> 18.7 us  [enter(): return lax.ppermute(x, 'col', hops[0])]
    ppermute x2, starting transfers between devices: 3.49 us -> 0.07 us  [shards(): x = keep + lax.ppermute(send, both, plan.bit_pairs(step))]
    ppermute x7 -> x10, starting transfers between devices: 7.35 us -> 10 us  [run(): got = lax.ppermute(y, 'col', hops[hop])]
    ppermute x4 -> x5, waiting for transfers between devices: 26.5 us -> 23.9 us  [enter(): return lax.ppermute(x, 'col', hops[0])]
    add x8 -> x10, other arithmetic: 7.13 us -> 4.59 us  [line_step(): return x + got]
    unnamed x36 -> x42, local copies, waits for them, and re-layouts: 5.19 us -> 4.84 us
  transfers between devices with their start and end apart: 31 -> 34, of which waited for: 14 -> 16; matrix products, arithmetic and copies ran while one was open for 8% -> 8% of each run, Pallas kernels for 13% -> 13%
where the time goes in v7:
time: 208 us; the launch traced here: 207 us
  waiting for transfers between devices  96.6 us (46%)
  starting transfers between devices  52.1 us (25%)
  Pallas kernels  33 us (16%)
  other arithmetic  17.3 us (8%)
  local copies, waits for them, and re-layouts  7.02 us (3%)
    ppermute x10, waiting for transfers between devices, run(): got = lax.ppermute(y, 'col', hops[hop])  45.8 us
    ppermute x8, waiting for transfers between devices, issue(): out.append(lax.ppermute(x, axis, pairs))  24.2 us
    ppermute x5, waiting for transfers between devices, enter(): return lax.ppermute(x, 'col', hops[0])  23.9 us
    ppermute x8, starting transfers between devices, issue(): out.append(lax.ppermute(x, axis, pairs))  18.9 us
    ppermute x5, starting transfers between devices, enter(): return lax.ppermute(x, 'col', hops[0])  18.7 us
    pallas_call x2, Pallas kernels, forward(): pl.pallas_call(functools.partial(forward_kernel, plan, member), in_specs=...  10.1 us
    ppermute x10, starting transfers between devices, run(): got = lax.ppermute(y, 'col', hops[hop])  10 us
    pallas_call x2, Pallas kernels, gather(): pl.pallas_call(functools.partial(gather_kernel, plan, member), in_specs=s...  9.28 us
  transfers between devices with their start and end apart: 34, of which 16 were waited for; matrix products, arithmetic and copies ran while one was open for 8% of the time, Pallas kernels for 13%

profile of v7, /device:TPU:0, one launch (start us, length us, event | category | flops | bytes accessed | tf_op | source)
XLA Modules:
  0.0 207.3 jit_solution(13548994153046339159)
XLA Ops:
  0.6 1.3 slice.19.factor
  2.0 5.8 %collective-permute-start.3 = (f32[512,512]{1,0:T(8,128)S(1)}, f32[512,512]{1,0:T(8,128)}, u32[]{:S(2)}, u32[]{:S(2)}) collective-permute-start(f32[512,512]{1,0:T(8,128)S(1)} %slice.19.factor), channel_id=1, source_target_pairs={{0,8},{4,20},{9,1},{13,29},{18,26}} | collective-permute-start | bytes 3145736 | tf_op jit(solution)/shard_map/ppermute | solution.py:156
  7.8 5.1 %gather_mirror.3 = (bf16[512,1024]{1,0:T(8,128)(2,1)S(1)}, bf16[512,1024]{1,0:T(8,128)(2,1)S(1)}, f32[512,512]{1,0:T(8,128)S(1)}, f32[512,512]{1,0:T(8,128)}) custom-call(s32[2,16]{1,0:T(2,128)S(1)} %copy-done.7, s32[2,16]{1,0:T(2,128)S(1)} %copy-done.8, f32[2048,4096]{1,0:T(8,128)} %front.3, f32[512,512]{1,0:T(8,128)S(1)} %slice.19.factor), custom_call_target="tpu_custom_call" | custom-call | flops 1677721600 | bytes 8388608 | tf_op jit(solution)/shard_map/gather_mirror/pallas_call | solution.py:333
  14.0 5.1 %collective-permute-done.3 = f32[512,512]{1,0:T(8,128)} collective-permute-done((f32[512,512]{1,0:T(8,128)S(1)}, f32[512,512]{1,0:T(8,128)}, u32[]{:S(2)}, u32[]{:S(2)}) %collective-permute-start.3) | collective-permute-done | bytes 1048608 | tf_op jit(solution)/shard_map/ppermute | solution.py:156
  19.1 1.9 broadcast_select_fusion.1
  21.0 1.4 collective-permute-start.4
  22.4 1.4 add.90
  23.8 1.3 collective-permute-start.2
  25.1 4.2 %gather_mirror.2 = (bf16[512,1024]{1,0:T(8,128)(2,1)S(1)}, bf16[512,1024]{1,0:T(8,128)(2,1)S(1)}, f32[512,512]{1,0:T(8,128)S(1)}, f32[512,512]{1,0:T(8,128)S(1)}) custom-call(s32[2,16]{1,0:T(2,128)S(1)} %copy-done.7, s32[2,16]{1,0:T(2,128)S(1)} %copy-done.8, f32[2048,4096]{1,0:T(8,128)} %front.3, f32[512,512]{1,0:T(8,128)S(1)} %get-tuple-element.48.factor), custom_call_target="tpu_custom_call" | custom-call | flops 1677721600 | bytes 8388608 | tf_op jit(solution)/shard_map/gather_mirror/pallas_call | solution.py:333
  29.3 5.3 %collective-permute-done.4 = f32[512,512]{1,0:T(8,128)S(1)} collective-permute-done((f32[512,512]{1,0:T(8,128)S(1)}, f32[512,512]{1,0:T(8,128)S(1)}, u32[]{:S(2)}, u32[]{:S(2)}) %collective-permute-start.4) | collective-permute-done | bytes 1048608 | tf_op jit(solution)/shard_map/ppermute | solution.py:156
  34.9 4.9 %collective-permute-start.8 = (f32[512,512]{1,0:T(8,128)S(1)}, f32[512,512]{1,0:T(8,128)S(1)}, u32[]{:S(2)}, u32[]{:S(2)}) collective-permute-start(f32[512,512]{1,0:T(8,128)S(1)} %get-tuple-element.48.factor), channel_id=1, source_target_pairs={{0,8},{4,20},{9,1},{13,29},{18,26}} | collective-permute-start | bytes 3145736 | tf_op jit(solution)/shard_map/ppermute | solution.py:156
  40.7 1.4 collective-permute-start.6
  43.4 4.8 %forward.2 = (f32[256,512]{1,0:T(8,128)S(1)}, f32[256,512]{1,0:T(8,128)S(1)}, f32[256,512]{1,0:T(8,128)S(1)}, f32[256,512]{1,0:T(8,128)S(1)}) custom-call(bf16[512,1024]{1,0:T(8,128)(2,1)S(1)} %get-tuple-element.41.high, bf16[512,1024]{1,0:T(8,128)(2,1)S(1)} %copy-done.4, f32[512,512]{1,0:T(8,128)S(1)} %slice.19.factor, f32[512,512]{1,0:T(8,128)} %copy-done.13, ...), custom_call_target="tpu_custom_call" | custom-call | flops 1677721600 | bytes 8388608 | tf_op jit(solution)/shard_map/forward/pallas_call | solution.py:351
  48.2 3.8 %collective-permute-done.8 = f32[512,512]{1,0:T(8,128)S(1)} collective-permute-done((f32[512,512]{1,0:T(8,128)S(1)}, f32[512,512]{1,0:T(8,128)S(1)}, u32[]{:S(2)}, u32[]{:S(2)}) %collective-permute-start.8) | collective-permute-done | bytes 1048608 | tf_op jit(solution)/shard_map/ppermute | solution.py:156
  52.2 5.5 %collective-permute-done.6 = f32[512,512]{1,0:T(8,128)S(1)} collective-permute-done((f32[512,512]{1,0:T(8,128)S(1)}, f32[512,512]{1,0:T(8,128)S(1)}, u32[]{:S(2)}, u32[]{:S(2)}) %collective-permute-start.6) | collective-permute-done | bytes 1048608 | tf_op jit(solution)/shard_map/ppermute | solution.py:156
  58.8 1.3 collective-permute-start.9
  60.1 1.3 collective-permute-start.10
  61.4 1.6 collective-permute-start.7
  63.0 9.3 %collective-permute-done.7 = f32[256,512]{1,0:T(8,128)S(1)} collective-permute-done((f32[256,512]{1,0:T(8,128)S(1)}, f32[256,512]{1,0:T(8,128)S(1)}, u32[]{:S(2)}, u32[]{:S(2)}) %collective-permute-start.7) | collective-permute-done | bytes 524320 | tf_op jit(solution)/shard_map/ppermute | solution.py:372
  73.2 3.7 %collective-permute-done.10 = f32[512,512]{1,0:T(8,128)S(1)} collective-permute-done((f32[512,512]{1,0:T(8,128)S(1)}, f32[512,512]{1,0:T(8,128)S(1)}, u32[]{:S(2)}, u32[]{:S(2)}) %collective-permute-start.10) | collective-permute-done | bytes 1048608 | tf_op jit(solution)/shard_map/ppermute | solution.py:156
  77.1 1.3 add.95.mirror
  78.4 1.5 collective-permute-start.12
  80.9 5.3 %forward.3 = (f32[256,512]{1,0:T(8,128)S(1)}, f32[256,512]{1,0:T(8,128)S(1)}, f32[512,512]{1,0:T(8,128)S(1)}, f32[512,512]{1,0:T(8,128)S(1)}) custom-call(bf16[512,1024]{1,0:T(8,128)(2,1)S(1)} %get-tuple-element.37.high, bf16[512,1024]{1,0:T(8,128)(2,1)} %copy-done.2, f32[512,512]{1,0:T(8,128)} %copy-done.1, f32[512,512]{1,0:T(8,128)} %add.95.mirror, ...), custom_call_target="tpu_custom_call" | custom-call | flops 1677721600 | bytes 8388608 | tf_op jit(solution)/shard_map/forward/pallas_call | solution.py:351
  86.7 1.3 add.101
  88.7 7.0 %collective-permute-start.16 = (f32[256,512]{1,0:T(8,128)}, f32[256,512]{1,0:T(8,128)}, u32[]{:S(2)}, u32[]{:S(2)}) collective-permute-start(f32[256,512]{1,0:T(8,128)} %get-tuple-element.60), channel_id=1, source_target_pairs={{0,1},{3,2},{4,5},{7,6},{8,9},{11,10},{12,13},{15,14},{16,17},{19,... | collective-permute-start | bytes 1572872 | tf_op jit(solution)/shard_map/ppermute | solution.py:372
  95.7 2.4 %slice_add_fusion = (f32[256,512]{1,0:T(8,128)}, f32[256,512]{1,0:T(8,128)}) fusion(f32[256,512]{1,0:T(8,128)S(1)} %get-tuple-element.58, f32[512,512]{1,0:T(8,128)} %collective-permute-done.12, f32[256,512]{1,0:T(8,128)S(1)} %get-tuple-element.56), kind=kLoop, calls=%fused_computation.1 | loop fusion | flops 262144 | bytes 3145728 | tf_op jit(solution)/shard_map/add | solution.py:422
  98.1 1.5 add.107
  100.6 6.5 %collective-permute-done.16 = f32[256,512]{1,0:T(8,128)} collective-permute-done((f32[256,512]{1,0:T(8,128)}, f32[256,512]{1,0:T(8,128)}, u32[]{:S(2)}, u32[]{:S(2)}) %collective-permute-start.16) | collective-permute-done | bytes 524320 | tf_op jit(solution)/shard_map/ppermute | solution.py:372
  107.1 1.3 collective-permute-start.17
  108.4 4.7 %collective-permute-start.13 = (f32[256,512]{1,0:T(8,128)}, f32[256,512]{1,0:T(8,128)S(1)}, u32[]{:S(2)}, u32[]{:S(2)}) collective-permute-start(f32[256,512]{1,0:T(8,128)} %get-tuple-element.75), channel_id=1, source_target_pairs={{0,1},{3,2},{4,5},{7,6},{8,9},{11,10},{12,13},{15,14},{16,17},{19,... | collective-permute-start | bytes 1572872 | tf_op jit(solution)/shard_map/ppermute | solution.py:372
  114.4 8.2 %collective-permute-done.17.rest_1_ = f32[256,512]{1,0:T(8,128)S(1)} collective-permute-done((f32[256,512]{1,0:T(8,128)S(1)}, f32[256,512]{1,0:T(8,128)S(1)}, u32[]{:S(2)}, u32[]{:S(2)}) %collective-permute-start.17) | collective-permute-done | bytes 524320 | tf_op jit(solution)/shard_map/ppermute | solution.py:381
  122.6 1.5 collective-permute-start.18
  126.0 3.9 %collective-permute-start.27 = (f32[128,512]{1,0:T(8,128)S(1)}, f32[128,512]{1,0:T(8,128)S(1)}, u32[]{:S(2)}, u32[]{:S(2)}) collective-permute-start(f32[128,512]{1,0:T(8,128)S(1)} %bitcast_add_fusion.1), channel_id=1, source_target_pairs={{0,1},{3,2},{4,5},{7,6},{8,9},{11,10},{12,13},{15,14},{16,17},{19,... | collective-permute-start | bytes 786440 | tf_op jit(solution)/shard_map/ppermute | solution.py:372
  130.7 5.7 %collective-permute-done.18 = f32[256,512]{1,0:T(8,128)S(1)} collective-permute-done((f32[256,512]{1,0:T(8,128)S(1)}, f32[256,512]{1,0:T(8,128)S(1)}, u32[]{:S(2)}, u32[]{:S(2)}) %collective-permute-start.18) | collective-permute-done | bytes 524320 | tf_op jit(solution)/shard_map/ppermute | solution.py:372
  137.3 1.3 collective-permute-start.23
  138.6 2.4 %collective-permute-done.27 = f32[128,512]{1,0:T(8,128)S(1)} collective-permute-done((f32[128,512]{1,0:T(8,128)S(1)}, f32[128,512]{1,0:T(8,128)S(1)}, u32[]{:S(2)}, u32[]{:S(2)}) %collective-permute-start.27) | collective-permute-done | bytes 262176 | tf_op jit(solution)/shard_map/ppermute | solution.py:372
  142.8 1.3 collective-permute-start.29
  144.1 1.3 collective-permute-start.19
  146.3 1.3 collective-permute-start.21
  147.6 5.8 %collective-permute-done.23.rest_3_ = f32[256,512]{1,0:T(8,128)} collective-permute-done((f32[256,512]{1,0:T(8,128)S(1)}, f32[256,512]{1,0:T(8,128)}, u32[]{:S(2)}, u32[]{:S(2)}) %collective-permute-start.23) | collective-permute-done | bytes 524320 | tf_op jit(solution)/shard_map/ppermute | solution.py:381
  154.5 4.8 %place.2.rest_4_ = f32[2048,1024]{1,0:T(8,128)} custom-call(s32[2,16]{1,0:T(2,128)S(1)} %copy-done.7, f32[2,512,512]{2,1,0:T(8,128)S(1)} %copy-done, f32[256,512]{1,0:T(8,128)S(1)} %add.102.rest_0_, f32[256,512]{1,0:T(8,128)S(1)} %copy-done.6, f32[256,512]{1,0:T(8,128)S(1)} %add.106.rest_2_, f32[256,512]{1,0:T(8,128)} %collective-permute-done.23.rest_3_), custom_call_target="tpu_custom_call" | custom-call | flops 1677721600 | bytes 8388608 | tf_op jit(solution)/shard_map/place/pallas_call | solution.py:440
  159.3 16.7 %collective-permute-done.29 = f32[128,512]{1,0:T(8,128)} collective-permute-done((f32[128,512]{1,0:T(8,128)S(1)}, f32[128,512]{1,0:T(8,128)}, u32[]{:S(2)}, u32[]{:S(2)}) %collective-permute-start.29) | collective-permute-done | bytes 262176 | tf_op jit(solution)/shard_map/ppermute | solution.py:381
  177.2 3.3 %collective-permute-start.30 = (f32[128,512]{1,0:T(8,128)S(1)}, f32[128,512]{1,0:T(8,128)S(1)}, u32[]{:S(2)}, u32[]{:S(2)}) collective-permute-start(f32[128,512]{1,0:T(8,128)S(1)} %broadcast_select_fusion.2), channel_id=1, source_target_pairs={{0,16},{1,17},{2,18},{3,19},{8,24},{9,25},{10,26},{11,27},{16,0},{... | collective-permute-start | bytes 786440 | tf_op jit(solution)/shard_map/ppermute | solution.py:478
  180.5 6.7 %collective-permute-done.19.rest_1_ = f32[256,512]{1,0:T(8,128)} collective-permute-done((f32[256,512]{1,0:T(8,128)}, f32[256,512]{1,0:T(8,128)}, u32[]{:S(2)}, u32[]{:S(2)}) %collective-permute-start.19) | collective-permute-done | bytes 524320 | tf_op jit(solution)/shard_map/ppermute | solution.py:381
  187.2 8.5 %collective-permute-done.21.rest_3_ = f32[256,512]{1,0:T(8,128)} collective-permute-done((f32[256,512]{1,0:T(8,128)}, f32[256,512]{1,0:T(8,128)}, u32[]{:S(2)}, u32[]{:S(2)}) %collective-permute-start.21) | collective-permute-done | bytes 524320 | tf_op jit(solution)/shard_map/ppermute | solution.py:381
  195.7 3.7 %place.3 = f32[2048,1024]{1,0:T(8,128)} custom-call(s32[2,16]{1,0:T(2,128)S(1)} %copy-done.7, f32[2,512,512]{2,1,0:T(8,128)S(1)} %copy-done, f32[256,512]{1,0:T(8,128)} %add.99.rest_0_, f32[256,512]{1,0:T(8,128)} %collective-permute-done.19.rest_1_, f32[256,512]{1,0:T(8,128)} %add.104.rest_2_, ...), custom_call_target="tpu_custom_call", output_to_operand_aliasing={{}: (6, {})} | custom-call | flops 1677721600 | bytes 8388608 | tf_op jit(solution)/shard_map/place/pallas_call | solution.py:440
  199.5 2.6 %collective-permute-done.33.rest_1_ = f32[512,512]{1,0:T(8,128)S(1)} collective-permute-done((f32[512,512]{1,0:T(8,128)S(1)}, f32[512,512]{1,0:T(8,128)S(1)}, u32[]{:S(2)}, u32[]{:S(2)}) %collective-permute-start.33) | collective-permute-done | bytes 1048608 | tf_op jit(solution)/shard_map/ppermute | solution.py:88
  202.2 5.1 %diagonal.1 = f32[2,512,512]{2,1,0:T(8,128)} custom-call(f32[2,512]{1,0:T(2,128)S(1)} %copy-done.9, f32[2,512,512]{2,1,0:T(8,128)S(1)} %copy-done, f32[512,512]{1,0:T(8,128)S(1)} %pad_maximum_fusion.rest_0_, f32[512,512]{1,0:T(8,128)S(1)} %collective-permute-done.33.rest_1_), custom_call_target="tpu_custom_call" | custom-call | flops 1677721600 | bytes 8388608 | tf_op jit(solution)/shard_map/diagonal/pallas_call | solution.py:481
  (97 shorter events, 18.8 us)
Async XLA Ops:
  0.6 7.2 %copy-start.7 = (s32[2,16]{1,0:T(2,128)S(1)}, s32[2,16]{1,0:T(2,128)}, u32[]{:S(2)}) copy-start(s32[2,16]{1,0:T(2,128)} %tiles_ref.7) | copy-start | bytes 388
  0.6 7.2 %copy-start.8 = (s32[2,16]{1,0:T(2,128)S(1)}, s32[2,16]{1,0:T(2,128)}, u32[]{:S(2)}) copy-start(s32[2,16]{1,0:T(2,128)} %valid_ref.3) | copy-start | bytes 388
  2.0 17.2 %collective-permute-start.3 = (f32[512,512]{1,0:T(8,128)S(1)}, f32[512,512]{1,0:T(8,128)}, u32[]{:S(2)}, u32[]{:S(2)}) collective-permute-start(f32[512,512]{1,0:T(8,128)S(1)} %slice.19.factor), channel_id=1, source_target_pairs={{0,8},{4,20},{9,1},{13,29},{18,26}} | collective-permute-start | bytes 3145736 | tf_op jit(solution)/shard_map/ppermute | solution.py:156
  14.0 8.4 %collective-permute-start.1 = (f32[512,512]{1,0:T(8,128)}, f32[512,512]{1,0:T(8,128)}, u32[]{:S(2)}, u32[]{:S(2)}) collective-permute-start(f32[512,512]{1,0:T(8,128)} %get-tuple-element.44), channel_id=1, source_target_pairs={{4,0},{0,4},{12,8},{8,12},{20,16},{16,20},{28,24},{24,28},{5,1},{1... | collective-permute-start | bytes 3145736 | tf_op jit(solution)/shard_map/ppermute | solution.py:88
  21.0 13.9 %copy-start.1 = (f32[512,512]{1,0:T(8,128)}, f32[512,512]{1,0:T(8,128)S(1)}, u32[]{:S(2)}) copy-start(f32[512,512]{1,0:T(8,128)S(1)} %get-tuple-element.48.factor) | copy-start | bytes 3145732
  21.0 13.6 %collective-permute-start.4 = (f32[512,512]{1,0:T(8,128)S(1)}, f32[512,512]{1,0:T(8,128)S(1)}, u32[]{:S(2)}, u32[]{:S(2)}) collective-permute-start(f32[512,512]{1,0:T(8,128)S(1)} %get-tuple-element.45), channel_id=1, source_target_pairs={{0,16},{8,24},{4,12},{20,28},{9,25},{1,17},{29,21},{22,30}} | collective-permute-start | bytes 3145736 | tf_op jit(solution)/shard_map/ppermute | solution.py:156
  23.8 16.7 %collective-permute-start.2 = (f32[512,512]{1,0:T(8,128)S(1)}, f32[512,512]{1,0:T(8,128)S(1)}, u32[]{:S(2)}, u32[]{:S(2)}) collective-permute-start(f32[512,512]{1,0:T(8,128)S(1)} %add.90), channel_id=1, source_target_pairs={{16,0},{24,8},{12,4},{28,20},{25,9},{17,1},{21,29},{30,22}} | collective-permute-start | bytes 3145736 | tf_op jit(solution)/shard_map/ppermute | solution.py:156
  29.2 11.4 %copy-start.2 = (bf16[512,1024]{1,0:T(8,128)(2,1)}, bf16[512,1024]{1,0:T(8,128)(2,1)S(1)}, u32[]{:S(2)}) copy-start(bf16[512,1024]{1,0:T(8,128)(2,1)S(1)} %get-tuple-element.38.low) | copy-start | bytes 3145732
  29.2 12.9 %collective-permute-start = (f32[512,512]{1,0:T(8,128)S(1)}, f32[512,512]{1,0:T(8,128)S(1)}, u32[]{:S(2)}, u32[]{:S(2)}) collective-permute-start(f32[512,512]{1,0:T(8,128)S(1)} %get-tuple-element.40), channel_id=1, source_target_pairs={{4,0},{0,4},{12,8},{8,12},{20,16},{16,20},{28,24},{24,28},{5,1},{1... | collective-permute-start | bytes 3145736 | tf_op jit(solution)/shard_map/ppermute | solution.py:88
  34.8 7.5 %copy-start.12 = (f32[512,512]{1,0:T(8,128)}, f32[512,512]{1,0:T(8,128)S(1)}, u32[]{:S(2)}) copy-start(f32[512,512]{1,0:T(8,128)S(1)} %add.92.rest_0_) | copy-start | bytes 3145732
  34.8 7.5 %collective-permute-start.5 = (f32[512,512]{1,0:T(8,128)S(1)}, f32[512,512]{1,0:T(8,128)S(1)}, u32[]{:S(2)}, u32[]{:S(2)}) collective-permute-start(f32[512,512]{1,0:T(8,128)S(1)} %add.92.rest_0_), channel_id=1, source_target_pairs={{4,0},{0,4},{12,8},{8,12},{20,16},{16,20},{28,24},{24,28},{5,1},{1... | collective-permute-start | bytes 3145736 | tf_op jit(solution)/shard_map/ppermute | solution.py:88
  34.9 17.1 %collective-permute-start.8 = (f32[512,512]{1,0:T(8,128)S(1)}, f32[512,512]{1,0:T(8,128)S(1)}, u32[]{:S(2)}, u32[]{:S(2)}) collective-permute-start(f32[512,512]{1,0:T(8,128)S(1)} %get-tuple-element.48.factor), channel_id=1, source_target_pairs={{0,8},{4,20},{9,1},{13,29},{18,26}} | collective-permute-start | bytes 3145736 | tf_op jit(solution)/shard_map/ppermute | solution.py:156
  40.7 17.1 %collective-permute-start.6 = (f32[512,512]{1,0:T(8,128)S(1)}, f32[512,512]{1,0:T(8,128)S(1)}, u32[]{:S(2)}, u32[]{:S(2)}) collective-permute-start(f32[512,512]{1,0:T(8,128)S(1)} %add.91.mirror), channel_id=1, source_target_pairs={{8,0},{20,4},{1,9},{29,13},{26,18}} | collective-permute-start | bytes 3145736 | tf_op jit(solution)/shard_map/ppermute | solution.py:156
  43.4 8.7 %copy-start.10 = (f32[512,1024]{1,0:T(8,128)S(1)}, f32[512,1024]{1,0:T(8,128)}, u32[]{:S(2)}) copy-start(f32[512,1024]{1,0:T(8,128)} %param.7) | copy-start | bytes 6291460
  58.8 13.6 %copy-start.17 = (f32[256,512]{1,0:T(8,128)}, f32[256,512]{1,0:T(8,128)S(1)}, u32[]{:S(2)}) copy-start(f32[256,512]{1,0:T(8,128)S(1)} %get-tuple-element.77) | copy-start | bytes 1572868
  58.8 13.6 %collective-permute-start.9 = (f32[512,512]{1,0:T(8,128)S(1)}, f32[512,512]{1,0:T(8,128)S(1)}, u32[]{:S(2)}, u32[]{:S(2)}) collective-permute-start(f32[512,512]{1,0:T(8,128)S(1)} %broadcast_select_fusion), channel_id=1, source_target_pairs={{0,16},{8,24},{4,12},{20,28},{9,25},{1,17},{29,21},{22,30}} | collective-permute-start | bytes 3145736 | tf_op jit(solution)/shard_map/ppermute | solution.py:156
  60.1 16.7 %collective-permute-start.10 = (f32[512,512]{1,0:T(8,128)S(1)}, f32[512,512]{1,0:T(8,128)S(1)}, u32[]{:S(2)}, u32[]{:S(2)}) collective-permute-start(f32[512,512]{1,0:T(8,128)S(1)} %add.89), channel_id=1, source_target_pairs={{16,0},{24,8},{12,4},{28,20},{25,9},{17,1},{21,29},{30,22}} | collective-permute-start | bytes 3145736 | tf_op jit(solution)/shard_map/ppermute | solution.py:156
  61.4 10.9 %collective-permute-start.7 = (f32[256,512]{1,0:T(8,128)S(1)}, f32[256,512]{1,0:T(8,128)S(1)}, u32[]{:S(2)}, u32[]{:S(2)}) collective-permute-start(f32[256,512]{1,0:T(8,128)S(1)} %get-tuple-element.77), channel_id=1, source_target_pairs={{0,1},{3,2},{4,5},{7,6},{8,9},{11,10},{12,13},{15,14},{16,17},{19,... | collective-permute-start | bytes 1572872 | tf_op jit(solution)/shard_map/ppermute | solution.py:372
  77.1 2.9 %copy-start.11 = (f32[512,512]{1,0:T(8,128)}, f32[512,512]{1,0:T(8,128)S(1)}, u32[]{:S(2)}) copy-start(f32[512,512]{1,0:T(8,128)S(1)} %add.96.rest_0_) | copy-start | bytes 3145732
  77.1 2.8 %collective-permute-start.11 = (f32[512,512]{1,0:T(8,128)S(1)}, f32[512,512]{1,0:T(8,128)S(1)}, u32[]{:S(2)}, u32[]{:S(2)}) collective-permute-start(f32[512,512]{1,0:T(8,128)S(1)} %add.96.rest_0_), channel_id=1, source_target_pairs={{4,0},{0,4},{12,8},{8,12},{20,16},{16,20},{28,24},{24,28},{5,1},{1... | collective-permute-start | bytes 3145736 | tf_op jit(solution)/shard_map/ppermute | solution.py:88
  78.4 17.3 %collective-permute-start.12 = (f32[512,512]{1,0:T(8,128)}, f32[512,512]{1,0:T(8,128)}, u32[]{:S(2)}, u32[]{:S(2)}) collective-permute-start(f32[512,512]{1,0:T(8,128)} %add.95.mirror), channel_id=1, source_target_pairs={{8,0},{20,4},{1,9},{29,13},{26,18}} | collective-permute-start | bytes 3145736 | tf_op jit(solution)/shard_map/ppermute | solution.py:156
  86.2 12.0 %collective-permute-start.24 = (f32[512,512]{1,0:T(8,128)S(1)}, f32[512,512]{1,0:T(8,128)}, u32[]{:S(2)}, u32[]{:S(2)}) collective-permute-start(f32[512,512]{1,0:T(8,128)S(1)} %get-tuple-element.66), channel_id=1, source_target_pairs={{4,0},{0,4},{12,8},{8,12},{20,16},{16,20},{28,24},{24,28},{5,1},{1... | collective-permute-start | bytes 3145736 | tf_op jit(solution)/shard_map/ppermute | solution.py:88
  88.0 12.5 %collective-permute-start.15 = (f32[256,512]{1,0:T(8,128)S(1)}, f32[256,512]{1,0:T(8,128)S(1)}, u32[]{:S(2)}, u32[]{:S(2)}) collective-permute-start(f32[256,512]{1,0:T(8,128)S(1)} %add.101), channel_id=1, source_target_pairs={{1,2},{2,1},{5,6},{6,5},{9,10},{10,9},{13,14},{14,13},{17,18},{18,... | collective-permute-start | bytes 1572872 | tf_op jit(solution)/shard_map/ppermute | solution.py:381
  88.7 18.4 %collective-permute-start.16 = (f32[256,512]{1,0:T(8,128)}, f32[256,512]{1,0:T(8,128)}, u32[]{:S(2)}, u32[]{:S(2)}) collective-permute-start(f32[256,512]{1,0:T(8,128)} %get-tuple-element.60), channel_id=1, source_target_pairs={{0,1},{3,2},{4,5},{7,6},{8,9},{11,10},{12,13},{15,14},{16,17},{19,... | collective-permute-start | bytes 1572872 | tf_op jit(solution)/shard_map/ppermute | solution.py:372
  100.5 22.1 %copy-start.15 = (f32[256,512]{1,0:T(8,128)S(1)}, f32[256,512]{1,0:T(8,128)}, u32[]{:S(2)}) copy-start(f32[256,512]{1,0:T(8,128)} %get-tuple-element.62) | copy-start | bytes 1572868
  100.5 23.6 %copy-start.14 = (f32[256,512]{1,0:T(8,128)S(1)}, f32[256,512]{1,0:T(8,128)}, u32[]{:S(2)}) copy-start(f32[256,512]{1,0:T(8,128)} %get-tuple-element.60) | copy-start | bytes 1572868
  100.5 12.7 %collective-permute-start.25 = (f32[256,512]{1,0:T(8,128)}, f32[256,512]{1,0:T(8,128)}, u32[]{:S(2)}, u32[]{:S(2)}) collective-permute-start(f32[256,512]{1,0:T(8,128)} %dynamic-slice_bitcast_fusion), channel_id=1, source_target_pairs={{0,8},{1,9},{2,10},{3,11},{4,20},{5,21},{6,22},{7,23},{8,0},{9,1},... | collective-permute-start | bytes 1572872 | tf_op jit(solution)/shard_map/ppermute | solution.py:432
  107.1 15.5 %collective-permute-start.17 = (f32[256,512]{1,0:T(8,128)S(1)}, f32[256,512]{1,0:T(8,128)S(1)}, u32[]{:S(2)}, u32[]{:S(2)}) collective-permute-start(f32[256,512]{1,0:T(8,128)S(1)} %add.102.rest_0_), channel_id=1, source_target_pairs={{1,0},{2,3},{5,4},{6,7},{9,8},{10,11},{13,12},{14,15},{17,16},{18,... | collective-permute-start | bytes 1572872 | tf_op jit(solution)/shard_map/ppermute | solution.py:381
  108.4 21.5 %copy-start.16 = (f32[256,512]{1,0:T(8,128)S(1)}, f32[256,512]{1,0:T(8,128)}, u32[]{:S(2)}) copy-start(f32[256,512]{1,0:T(8,128)} %get-tuple-element.75) | copy-start | bytes 1572868
  108.4 21.5 %collective-permute-start.13 = (f32[256,512]{1,0:T(8,128)}, f32[256,512]{1,0:T(8,128)S(1)}, u32[]{:S(2)}, u32[]{:S(2)}) collective-permute-start(f32[256,512]{1,0:T(8,128)} %get-tuple-element.75), channel_id=1, source_target_pairs={{0,1},{3,2},{4,5},{7,6},{8,9},{11,10},{12,13},{15,14},{16,17},{19,... | collective-permute-start | bytes 1572872 | tf_op jit(solution)/shard_map/ppermute | solution.py:372
  114.3 11.6 %collective-permute-start.26 = (f32[128,512]{1,0:T(8,128)S(1)}, f32[128,512]{1,0:T(8,128)S(1)}, u32[]{:S(2)}, u32[]{:S(2)}) collective-permute-start(f32[128,512]{1,0:T(8,128)S(1)} %dynamic-slice_bitcast_fusion.1), channel_id=1, source_target_pairs={{0,16},{1,17},{2,18},{3,19},{4,12},{5,13},{6,14},{7,15},{8,24},{9,... | collective-permute-start | bytes 786440 | tf_op jit(solution)/shard_map/ppermute | solution.py:432
  122.6 13.9 %copy-start.5 = (f32[256,512]{1,0:T(8,128)}, f32[256,512]{1,0:T(8,128)S(1)}, u32[]{:S(2)}) copy-start(f32[256,512]{1,0:T(8,128)S(1)} %collective-permute-done.17.rest_1_) | copy-start | bytes 1572868
  122.6 13.8 %collective-permute-start.18 = (f32[256,512]{1,0:T(8,128)S(1)}, f32[256,512]{1,0:T(8,128)S(1)}, u32[]{:S(2)}, u32[]{:S(2)}) collective-permute-start(f32[256,512]{1,0:T(8,128)S(1)} %copy-done.15), channel_id=1, source_target_pairs={{0,1},{3,2},{4,5},{7,6},{8,9},{11,10},{12,13},{15,14},{16,17},{19,... | collective-permute-start | bytes 1572872 | tf_op jit(solution)/shard_map/ppermute | solution.py:372
  125.2 12.0 %collective-permute-start.22 = (f32[256,512]{1,0:T(8,128)S(1)}, f32[256,512]{1,0:T(8,128)S(1)}, u32[]{:S(2)}, u32[]{:S(2)}) collective-permute-start(f32[256,512]{1,0:T(8,128)S(1)} %add.105), channel_id=1, source_target_pairs={{1,2},{2,1},{5,6},{6,5},{9,10},{10,9},{13,14},{14,13},{17,18},{18,... | collective-permute-start | bytes 1572872 | tf_op jit(solution)/shard_map/ppermute | solution.py:381
  126.0 15.0 %collective-permute-start.27 = (f32[128,512]{1,0:T(8,128)S(1)}, f32[128,512]{1,0:T(8,128)S(1)}, u32[]{:S(2)}, u32[]{:S(2)}) collective-permute-start(f32[128,512]{1,0:T(8,128)S(1)} %bitcast_add_fusion.1), channel_id=1, source_target_pairs={{0,1},{3,2},{4,5},{7,6},{8,9},{11,10},{12,13},{15,14},{16,17},{19,... | collective-permute-start | bytes 786440 | tf_op jit(solution)/shard_map/ppermute | solution.py:372
  130.0 11.9 %collective-permute-start.14 = (f32[256,512]{1,0:T(8,128)S(1)}, f32[256,512]{1,0:T(8,128)S(1)}, u32[]{:S(2)}, u32[]{:S(2)}) collective-permute-start(f32[256,512]{1,0:T(8,128)S(1)} %add.98), channel_id=1, source_target_pairs={{1,2},{2,1},{5,6},{6,5},{9,10},{10,9},{13,14},{14,13},{17,18},{18,... | collective-permute-start | bytes 1572872 | tf_op jit(solution)/shard_map/ppermute | solution.py:381
  136.5 8.9 %collective-permute-start.20 = (f32[256,512]{1,0:T(8,128)S(1)}, f32[256,512]{1,0:T(8,128)S(1)}, u32[]{:S(2)}, u32[]{:S(2)}) collective-permute-start(f32[256,512]{1,0:T(8,128)S(1)} %add.103), channel_id=1, source_target_pairs={{1,2},{2,1},{5,6},{6,5},{9,10},{10,9},{13,14},{14,13},{17,18},{18,... | collective-permute-start | bytes 1572872 | tf_op jit(solution)/shard_map/ppermute | solution.py:381
  137.3 16.1 %collective-permute-start.23 = (f32[256,512]{1,0:T(8,128)S(1)}, f32[256,512]{1,0:T(8,128)}, u32[]{:S(2)}, u32[]{:S(2)}) collective-permute-start(f32[256,512]{1,0:T(8,128)S(1)} %add.106.rest_2_), channel_id=1, source_target_pairs={{1,0},{2,3},{5,4},{6,7},{9,8},{10,11},{13,12},{14,15},{17,16},{18,... | collective-permute-start | bytes 1572872 | tf_op jit(solution)/shard_map/ppermute | solution.py:381
  141.0 12.4 %copy-start = (f32[2,512,512]{2,1,0:T(8,128)S(1)}, f32[2,512,512]{2,1,0:T(8,128)}, u32[]{:S(2)}) copy-start(f32[2,512,512]{2,1,0:T(8,128)} %unit_ref.5) | copy-start | bytes 6291460
  141.1 1.7 collective-permute-start.28
  142.8 33.2 %collective-permute-start.29 = (f32[128,512]{1,0:T(8,128)S(1)}, f32[128,512]{1,0:T(8,128)}, u32[]{:S(2)}, u32[]{:S(2)}) collective-permute-start(f32[128,512]{1,0:T(8,128)S(1)} %add.114), channel_id=1, source_target_pairs={{1,0},{2,3},{5,4},{6,7},{9,8},{10,11},{13,12},{14,15},{17,16},{18,... | collective-permute-start | bytes 786440 | tf_op jit(solution)/shard_map/ppermute | solution.py:381
  144.1 43.1 %collective-permute-start.19 = (f32[256,512]{1,0:T(8,128)}, f32[256,512]{1,0:T(8,128)}, u32[]{:S(2)}, u32[]{:S(2)}) collective-permute-start(f32[256,512]{1,0:T(8,128)} %add.99.rest_0_), channel_id=1, source_target_pairs={{1,0},{2,3},{5,4},{6,7},{9,8},{10,11},{13,12},{14,15},{17,16},{18,... | collective-permute-start | bytes 1572872 | tf_op jit(solution)/shard_map/ppermute | solution.py:381
  146.3 49.4 %collective-permute-start.21 = (f32[256,512]{1,0:T(8,128)}, f32[256,512]{1,0:T(8,128)}, u32[]{:S(2)}, u32[]{:S(2)}) collective-permute-start(f32[256,512]{1,0:T(8,128)} %add.104.rest_2_), channel_id=1, source_target_pairs={{1,0},{2,3},{5,4},{6,7},{9,8},{10,11},{13,12},{14,15},{17,16},{18,... | collective-permute-start | bytes 1572872 | tf_op jit(solution)/shard_map/ppermute | solution.py:381
  177.0 22.4 %collective-permute-start.32 = (f32[128,512]{1,0:T(8,128)S(1)}, f32[128,512]{1,0:T(8,128)S(1)}, u32[]{:S(2)}, u32[]{:S(2)}) collective-permute-start(f32[128,512]{1,0:T(8,128)S(1)} %broadcast_select_fusion.2), channel_id=1, source_target_pairs={{0,24},{1,25},{2,26},{3,27},{8,16},{9,17},{10,18},{11,19},{16,8},{... | collective-permute-start | bytes 786440 | tf_op jit(solution)/shard_map/ppermute | solution.py:478
  177.2 22.2 %collective-permute-start.31 = (f32[128,512]{1,0:T(8,128)S(1)}, f32[128,512]{1,0:T(8,128)S(1)}, u32[]{:S(2)}, u32[]{:S(2)}) collective-permute-start(f32[128,512]{1,0:T(8,128)S(1)} %broadcast_select_fusion.2), channel_id=1, source_target_pairs={{0,8},{1,9},{2,10},{3,11},{8,0},{9,1},{10,2},{11,3},{16,24},{17,25... | collective-permute-start | bytes 786440 | tf_op jit(solution)/shard_map/ppermute | solution.py:478
  177.2 22.2 %collective-permute-start.30 = (f32[128,512]{1,0:T(8,128)S(1)}, f32[128,512]{1,0:T(8,128)S(1)}, u32[]{:S(2)}, u32[]{:S(2)}) collective-permute-start(f32[128,512]{1,0:T(8,128)S(1)} %broadcast_select_fusion.2), channel_id=1, source_target_pairs={{0,16},{1,17},{2,18},{3,19},{8,24},{9,25},{10,26},{11,27},{16,0},{... | collective-permute-start | bytes 786440 | tf_op jit(solution)/shard_map/ppermute | solution.py:478
  199.3 2.9 %copy-start.9 = (f32[2,512]{1,0:T(2,128)S(1)}, f32[2,512]{1,0:T(2,128)}, u32[]{:S(2)}) copy-start(f32[2,512]{1,0:T(2,128)} %pivot.1) | copy-start | bytes 12292
  199.5 2.7 %collective-permute-start.33 = (f32[512,512]{1,0:T(8,128)S(1)}, f32[512,512]{1,0:T(8,128)S(1)}, u32[]{:S(2)}, u32[]{:S(2)}) collective-permute-start(f32[512,512]{1,0:T(8,128)S(1)} %pad_maximum_fusion.rest_0_), channel_id=1, source_target_pairs={{4,0},{0,4},{12,8},{8,12},{20,16},{16,20},{28,24},{24,28},{5,1},{1... | collective-permute-start | bytes 3145736 | tf_op jit(solution)/shard_map/ppermute | solution.py:88
  (7 other events, 10.1 us)

commit v8 on v7

--- a/solution.py
+++ b/solution.py
@@ -372,16 +372,17 @@
         return lax.ppermute(x, "col", hops[0])
 
     def run(x, got, ties=()):
-        sent = []
+        sent, brought = [], [got]
         for hop in range(1, len(hops)):
             x = plan.line_step(hop - 1, x, got)
             sent.append(x)
             tie = ties[hop - 1] if hop <= len(ties) else ()
             y = lax.optimization_barrier((x, tuple(tie)))[0] if tie else x
             got = lax.ppermute(y, "col", hops[hop])
+            brought.append(got)
         if len(hops) == 1:
             got = x = x + got
-        return x, got, sent
+        return x, got, sent, brought
 
     spread, collect = Chain(), Chain()
     count = members * steps
@@ -455,19 +456,23 @@
             name="place",
         )(tile_list, unit_lower, *sums, *([column] if member else []))
 
-    ends, sent, column, last = {}, {}, None, len(chunks) - 1
-    middle = len(hops) - 1
+    ends, sent, brought, column = {}, {}, {}, None
+    last, middle = len(chunks) - 1, len(hops) - 1
     for i in range(last + 1):
-        if i < last:
-            if i + 1 == last and last > 2:
-                wait = (ends[i - 2],)
-            else:
-                wait = (entered[i], last_swap) if i == 0 else ()
-            entered[i + 1] = enter(chunks[i + 1], wait)
-        ties = [()] * (middle - 1) + [(entered[i + 1],)] if i < last and middle else ()
-        chunks[i], ends[i], sent[i] = run(chunks[i], entered[i], ties)
-    ahead = sent[max(last - 1, 0)]
-    update, got, _ = run(update, enter(update), [(x,) for x in ahead])
+        if i > 2:
+            entered[i] = enter(chunks[i], (brought[i - 2][min(1, middle)],))
+        if i == 1 and last > 1:
+            entered[2] = enter(chunks[2])
+        ties = [()] * middle
+        if i < 2 and i < last and middle:
+            if i == 0:
+                entered[1] = enter(chunks[1], (entered[0], last_swap))
+            ties[-1] = (entered[i + 1],)
+        elif i > 1 and middle:
+            ties = [(brought[i - 2][hop + 1],) for hop in range(1, middle)]
+            ties.append((brought[i - 1][-1],))
+        chunks[i], ends[i], sent[i], brought[i] = run(chunks[i], entered[i], ties)
+    update, got, _, _ = run(update, enter(update), [(x,) for x in sent[last]])
     for member in range(members):
         column = place(member, column)
         if member == 0:

time: 208 us -> 193 us (0.928)
  waiting for transfers between devices: 96.6 us -> 67.8 us
  starting transfers between devices: 52.1 us -> 59.6 us
  local copies, waits for them, and re-layouts: 7.02 us -> 10.4 us
  other arithmetic: 17.3 us -> 19.9 us
    ppermute x10, waiting for transfers between devices: 45.8 us -> 21.4 us  [run(): got = lax.ppermute(y, 'col', hops[hop])]
    ppermute x5, starting transfers between devices: 18.7 us -> 25.6 us  [enter(): return lax.ppermute(x, 'col', hops[0])]
    ppermute x5, waiting for transfers between devices: 23.9 us -> 18.6 us  [enter(): return lax.ppermute(x, 'col', hops[0])]
    unnamed x42 -> x48, local copies, waits for them, and re-layouts: 4.84 us -> 8.26 us
    add x10, other arithmetic: 4.59 us -> 7.24 us  [line_step(): return x + got]
  transfers between devices with their start and end apart: 34 -> 34, of which waited for: 16 -> 16; matrix products, arithmetic and copies ran while one was open for 8% -> 10% of each run, Pallas kernels for 13% -> 14%
where the time goes in v8:
time: 193 us; the launch traced here: 191 us
  waiting for transfers between devices  67.8 us (35%)
  starting transfers between devices  59.6 us (31%)
  Pallas kernels  32.2 us (17%)
  other arithmetic  19.9 us (10%)
  local copies, waits for them, and re-layouts  10.4 us (5%)
    ppermute x5, starting transfers between devices, enter(): return lax.ppermute(x, 'col', hops[0])  25.6 us
    ppermute x8, waiting for transfers between devices, issue(): out.append(lax.ppermute(x, axis, pairs))  25.1 us
    ppermute x10, waiting for transfers between devices, run(): got = lax.ppermute(y, 'col', hops[hop])  21.4 us
    ppermute x8, starting transfers between devices, issue(): out.append(lax.ppermute(x, axis, pairs))  18.9 us
    ppermute x5, waiting for transfers between devices, enter(): return lax.ppermute(x, 'col', hops[0])  18.6 us
    ppermute x10, starting transfers between devices, run(): got = lax.ppermute(y, 'col', hops[hop])  10.7 us
    pallas_call x2, Pallas kernels, forward(): pl.pallas_call(functools.partial(forward_kernel, plan, member), in_specs=...  10.1 us
    pallas_call x2, Pallas kernels, gather(): pl.pallas_call(functools.partial(gather_kernel, plan, member), in_specs=s...  9.27 us
  transfers between devices with their start and end apart: 34, of which 16 were waited for; matrix products, arithmetic and copies ran while one was open for 10% of the time, Pallas kernels for 14%

profile of v8, /device:TPU:0, one launch (start us, length us, event | category | flops | bytes accessed | tf_op | source)
XLA Modules:
  0.0 191.2 jit_solution(2265889099399017125)
XLA Ops:
  0.6 1.3 slice.19.factor
  2.0 5.8 %collective-permute-start.3 = (f32[512,512]{1,0:T(8,128)S(1)}, f32[512,512]{1,0:T(8,128)}, u32[]{:S(2)}, u32[]{:S(2)}) collective-permute-start(f32[512,512]{1,0:T(8,128)S(1)} %slice.19.factor), channel_id=1, source_target_pairs={{0,8},{4,20},{9,1},{13,29},{18,26}} | collective-permute-start | bytes 3145736 | tf_op jit(solution)/shard_map/ppermute | solution.py:156
  7.8 5.1 %gather_mirror.3 = (bf16[512,1024]{1,0:T(8,128)(2,1)S(1)}, bf16[512,1024]{1,0:T(8,128)(2,1)S(1)}, f32[512,512]{1,0:T(8,128)S(1)}, f32[512,512]{1,0:T(8,128)}) custom-call(s32[2,16]{1,0:T(2,128)S(1)} %copy-done.13, s32[2,16]{1,0:T(2,128)S(1)} %copy-done.14, f32[2048,4096]{1,0:T(8,128)} %front.3, f32[512,512]{1,0:T(8,128)S(1)} %slice.19.factor), custom_call_target="tpu_custom_call" | custom-call | flops 1677721600 | bytes 8388608 | tf_op jit(solution)/shard_map/gather_mirror/pallas_call | solution.py:333
  14.0 5.1 %collective-permute-done.3 = f32[512,512]{1,0:T(8,128)} collective-permute-done((f32[512,512]{1,0:T(8,128)S(1)}, f32[512,512]{1,0:T(8,128)}, u32[]{:S(2)}, u32[]{:S(2)}) %collective-permute-start.3) | collective-permute-done | bytes 1048608 | tf_op jit(solution)/shard_map/ppermute | solution.py:156
  19.1 1.9 broadcast_select_fusion.1
  21.0 1.4 collective-permute-start.4
  22.4 1.4 add.90
  23.8 1.3 collective-permute-start.2
  25.1 4.2 %gather_mirror.2 = (bf16[512,1024]{1,0:T(8,128)(2,1)S(1)}, bf16[512,1024]{1,0:T(8,128)(2,1)S(1)}, f32[512,512]{1,0:T(8,128)S(1)}, f32[512,512]{1,0:T(8,128)S(1)}) custom-call(s32[2,16]{1,0:T(2,128)S(1)} %copy-done.13, s32[2,16]{1,0:T(2,128)S(1)} %copy-done.14, f32[2048,4096]{1,0:T(8,128)} %front.3, f32[512,512]{1,0:T(8,128)S(1)} %get-tuple-element.51.factor), custom_call_target="tpu_custom_call" | custom-call | flops 1677721600 | bytes 8388608 | tf_op jit(solution)/shard_map/gather_mirror/pallas_call | solution.py:333
  29.3 5.3 %collective-permute-done.4 = f32[512,512]{1,0:T(8,128)S(1)} collective-permute-done((f32[512,512]{1,0:T(8,128)S(1)}, f32[512,512]{1,0:T(8,128)S(1)}, u32[]{:S(2)}, u32[]{:S(2)}) %collective-permute-start.4) | collective-permute-done | bytes 1048608 | tf_op jit(solution)/shard_map/ppermute | solution.py:156
  34.9 4.9 %collective-permute-start.8 = (f32[512,512]{1,0:T(8,128)S(1)}, f32[512,512]{1,0:T(8,128)S(1)}, u32[]{:S(2)}, u32[]{:S(2)}) collective-permute-start(f32[512,512]{1,0:T(8,128)S(1)} %get-tuple-element.51.factor), channel_id=1, source_target_pairs={{0,8},{4,20},{9,1},{13,29},{18,26}} | collective-permute-start | bytes 3145736 | tf_op jit(solution)/shard_map/ppermute | solution.py:156
  40.7 1.4 collective-permute-start.6
  43.4 4.8 %forward.2 = (f32[256,512]{1,0:T(8,128)S(1)}, f32[256,512]{1,0:T(8,128)S(1)}, f32[256,512]{1,0:T(8,128)S(1)}, f32[256,512]{1,0:T(8,128)S(1)}) custom-call(bf16[512,1024]{1,0:T(8,128)(2,1)S(1)} %get-tuple-element.44.high, bf16[512,1024]{1,0:T(8,128)(2,1)S(1)} %copy-done.6, f32[512,512]{1,0:T(8,128)S(1)} %slice.19.factor, f32[512,512]{1,0:T(8,128)} %copy-done.19, ...), custom_call_target="tpu_custom_call" | custom-call | flops 1677721600 | bytes 8388608 | tf_op jit(solution)/shard_map/forward/pallas_call | solution.py:351
  48.2 3.8 %collective-permute-done.8 = f32[512,512]{1,0:T(8,128)S(1)} collective-permute-done((f32[512,512]{1,0:T(8,128)S(1)}, f32[512,512]{1,0:T(8,128)S(1)}, u32[]{:S(2)}, u32[]{:S(2)}) %collective-permute-start.8) | collective-permute-done | bytes 1048608 | tf_op jit(solution)/shard_map/ppermute | solution.py:156
  52.2 5.5 %collective-permute-done.6 = f32[512,512]{1,0:T(8,128)S(1)} collective-permute-done((f32[512,512]{1,0:T(8,128)S(1)}, f32[512,512]{1,0:T(8,128)S(1)}, u32[]{:S(2)}, u32[]{:S(2)}) %collective-permute-start.6) | collective-permute-done | bytes 1048608 | tf_op jit(solution)/shard_map/ppermute | solution.py:156
  58.8 1.3 collective-permute-start.9
  60.1 1.3 collective-permute-start.10
  61.4 1.6 collective-permute-start.7
  63.0 9.3 %collective-permute-done.7 = f32[256,512]{1,0:T(8,128)S(1)} collective-permute-done((f32[256,512]{1,0:T(8,128)S(1)}, f32[256,512]{1,0:T(8,128)S(1)}, u32[]{:S(2)}, u32[]{:S(2)}) %collective-permute-start.7) | collective-permute-done | bytes 524320 | tf_op jit(solution)/shard_map/ppermute | solution.py:372
  73.2 3.7 %collective-permute-done.10 = f32[512,512]{1,0:T(8,128)S(1)} collective-permute-done((f32[512,512]{1,0:T(8,128)S(1)}, f32[512,512]{1,0:T(8,128)S(1)}, u32[]{:S(2)}, u32[]{:S(2)}) %collective-permute-start.10) | collective-permute-done | bytes 1048608 | tf_op jit(solution)/shard_map/ppermute | solution.py:156
  78.4 1.5 collective-permute-start.12
  80.8 5.3 %forward.3 = (f32[256,512]{1,0:T(8,128)S(1)}, f32[256,512]{1,0:T(8,128)S(1)}, f32[512,512]{1,0:T(8,128)S(1)}, f32[512,512]{1,0:T(8,128)S(1)}) custom-call(bf16[512,1024]{1,0:T(8,128)(2,1)S(1)} %get-tuple-element.40.high, bf16[512,1024]{1,0:T(8,128)(2,1)} %copy-done.4, f32[512,512]{1,0:T(8,128)} %copy-done.1, f32[512,512]{1,0:T(8,128)} %add.95.mirror, ...), custom_call_target="tpu_custom_call" | custom-call | flops 1677721600 | bytes 8388608 | tf_op jit(solution)/shard_map/forward/pallas_call | solution.py:351
  86.7 5.8 %collective-permute-start.15 = (f32[256,512]{1,0:T(8,128)}, f32[256,512]{1,0:T(8,128)}, u32[]{:S(2)}, u32[]{:S(2)}) collective-permute-start(f32[256,512]{1,0:T(8,128)} %get-tuple-element.62), channel_id=1, source_target_pairs={{0,1},{3,2},{4,5},{7,6},{8,9},{11,10},{12,13},{15,14},{16,17},{19,... | collective-permute-start | bytes 1572872 | tf_op jit(solution)/shard_map/ppermute | solution.py:372
  92.5 1.3 add.99
  95.4 2.4 %slice_add_fusion = (f32[256,512]{1,0:T(8,128)}, f32[256,512]{1,0:T(8,128)}) fusion(f32[256,512]{1,0:T(8,128)S(1)} %get-tuple-element.67, f32[512,512]{1,0:T(8,128)} %collective-permute-done.12, f32[256,512]{1,0:T(8,128)S(1)} %get-tuple-element.59), kind=kLoop, calls=%fused_computation.1 | loop fusion | flops 262144 | bytes 3145728 | tf_op jit(solution)/shard_map/add | solution.py:423
  97.8 2.3 %collective-permute-start.13 = (f32[256,512]{1,0:T(8,128)}, f32[256,512]{1,0:T(8,128)}, u32[]{:S(2)}, u32[]{:S(2)}) collective-permute-start(f32[256,512]{1,0:T(8,128)} %get-tuple-element.81), channel_id=1, source_target_pairs={{0,1},{3,2},{4,5},{7,6},{8,9},{11,10},{12,13},{15,14},{16,17},{19,... | collective-permute-start | bytes 1572872 | tf_op jit(solution)/shard_map/ppermute | solution.py:372
  100.1 4.1 %collective-permute-done.15 = f32[256,512]{1,0:T(8,128)} collective-permute-done((f32[256,512]{1,0:T(8,128)}, f32[256,512]{1,0:T(8,128)}, u32[]{:S(2)}, u32[]{:S(2)}) %collective-permute-start.15) | collective-permute-done | bytes 524320 | tf_op jit(solution)/shard_map/ppermute | solution.py:372
  105.5 1.5 collective-permute-start.18
  107.0 1.5 add.107
  109.4 1.3 collective-permute-start.16
  110.7 14.3 %collective-permute-start.21 = (f32[256,512]{1,0:T(8,128)}, f32[256,512]{1,0:T(8,128)S(1)}, u32[]{:S(2)}, u32[]{:S(2)}) collective-permute-start(f32[256,512]{1,0:T(8,128)} %get-tuple-element.68), channel_id=1, source_target_pairs={{0,1},{3,2},{4,5},{7,6},{8,9},{11,10},{12,13},{15,14},{16,17},{19,... | collective-permute-start | bytes 1572872 | tf_op jit(solution)/shard_map/ppermute | solution.py:372
  126.2 1.3 collective-permute-start.19
  128.8 1.3 add.98
  130.8 4.2 %collective-permute-done.21 = f32[256,512]{1,0:T(8,128)S(1)} collective-permute-done((f32[256,512]{1,0:T(8,128)}, f32[256,512]{1,0:T(8,128)S(1)}, u32[]{:S(2)}, u32[]{:S(2)}) %collective-permute-start.21) | collective-permute-done | bytes 524320 | tf_op jit(solution)/shard_map/ppermute | solution.py:372
  136.2 3.9 %collective-permute-done.19.rest_3_ = f32[256,512]{1,0:T(8,128)S(1)} collective-permute-done((f32[256,512]{1,0:T(8,128)S(1)}, f32[256,512]{1,0:T(8,128)S(1)}, u32[]{:S(2)}, u32[]{:S(2)}) %collective-permute-start.19) | collective-permute-done | bytes 524320 | tf_op jit(solution)/shard_map/ppermute | solution.py:381
  140.9 1.6 collective-permute-start.27
  143.3 1.3 collective-permute-start.20
  148.0 1.3 collective-permute-start.29
  149.3 8.2 %collective-permute-done.20.rest_1_ = f32[256,512]{1,0:T(8,128)S(1)} collective-permute-done((f32[256,512]{1,0:T(8,128)S(1)}, f32[256,512]{1,0:T(8,128)S(1)}, u32[]{:S(2)}, u32[]{:S(2)}) %collective-permute-start.20) | collective-permute-done | bytes 524320 | tf_op jit(solution)/shard_map/ppermute | solution.py:381
  158.4 1.3 collective-permute-start.23
  161.8 4.3 %place.2.rest_4_ = f32[2048,1024]{1,0:T(8,128)} custom-call(s32[2,16]{1,0:T(2,128)S(1)} %copy-done.13, f32[2,512,512]{2,1,0:T(8,128)S(1)} %copy-done, f32[256,512]{1,0:T(8,128)S(1)} %add.100.rest_0_, f32[256,512]{1,0:T(8,128)S(1)} %copy-done.8, f32[256,512]{1,0:T(8,128)S(1)} %add.103.rest_2_, f32[256,512]{1,0:T(8,128)S(1)} %copy-done.10), custom_call_target="tpu_custom_call" | custom-call | flops 1677721600 | bytes 8388608 | tf_op jit(solution)/shard_map/place/pallas_call | solution.py:441
  166.1 5.7 %collective-permute-done.29 = f32[128,512]{1,0:T(8,128)} collective-permute-done((f32[128,512]{1,0:T(8,128)S(1)}, f32[128,512]{1,0:T(8,128)}, u32[]{:S(2)}, u32[]{:S(2)}) %collective-permute-start.29) | collective-permute-done | bytes 262176 | tf_op jit(solution)/shard_map/ppermute | solution.py:381
  172.8 1.8 collective-permute-start.31
  174.6 1.7 collective-permute-start.30
  176.3 3.6 %collective-permute-done.23.rest_3_ = f32[256,512]{1,0:T(8,128)} collective-permute-done((f32[256,512]{1,0:T(8,128)}, f32[256,512]{1,0:T(8,128)}, u32[]{:S(2)}, u32[]{:S(2)}) %collective-permute-start.23) | collective-permute-done | bytes 524320 | tf_op jit(solution)/shard_map/ppermute | solution.py:381
  179.9 3.3 %place.3 = f32[2048,1024]{1,0:T(8,128)} custom-call(s32[2,16]{1,0:T(2,128)S(1)} %copy-done.13, f32[2,512,512]{2,1,0:T(8,128)S(1)} %copy-done, f32[256,512]{1,0:T(8,128)S(1)} %copy-done.3, f32[256,512]{1,0:T(8,128)S(1)} %copy-done.12, f32[256,512]{1,0:T(8,128)} %add.106.rest_2_, ...), custom_call_target="tpu_custom_call", output_to_operand_aliasing={{}: (6, {})} | custom-call | flops 1677721600 | bytes 8388608 | tf_op jit(solution)/shard_map/place/pallas_call | solution.py:441
  183.4 2.6 %collective-permute-done.33.rest_1_ = f32[512,512]{1,0:T(8,128)S(1)} collective-permute-done((f32[512,512]{1,0:T(8,128)S(1)}, f32[512,512]{1,0:T(8,128)S(1)}, u32[]{:S(2)}, u32[]{:S(2)}) %collective-permute-start.33) | collective-permute-done | bytes 1048608 | tf_op jit(solution)/shard_map/ppermute | solution.py:88
  186.1 5.1 %diagonal.1 = f32[2,512,512]{2,1,0:T(8,128)} custom-call(f32[2,512]{1,0:T(2,128)S(1)} %copy-done.15, f32[2,512,512]{2,1,0:T(8,128)S(1)} %copy-done, f32[512,512]{1,0:T(8,128)S(1)} %pad_maximum_fusion.rest_0_, f32[512,512]{1,0:T(8,128)S(1)} %collective-permute-done.33.rest_1_), custom_call_target="tpu_custom_call" | custom-call | flops 1677721600 | bytes 8388608 | tf_op jit(solution)/shard_map/diagonal/pallas_call | solution.py:486
  (103 shorter events, 25.7 us)
Async XLA Ops:
  0.6 7.2 %copy-start.13 = (s32[2,16]{1,0:T(2,128)S(1)}, s32[2,16]{1,0:T(2,128)}, u32[]{:S(2)}) copy-start(s32[2,16]{1,0:T(2,128)} %tiles_ref.7) | copy-start | bytes 388
  0.6 7.2 %copy-start.14 = (s32[2,16]{1,0:T(2,128)S(1)}, s32[2,16]{1,0:T(2,128)}, u32[]{:S(2)}) copy-start(s32[2,16]{1,0:T(2,128)} %valid_ref.3) | copy-start | bytes 388
  2.0 17.2 %collective-permute-start.3 = (f32[512,512]{1,0:T(8,128)S(1)}, f32[512,512]{1,0:T(8,128)}, u32[]{:S(2)}, u32[]{:S(2)}) collective-permute-start(f32[512,512]{1,0:T(8,128)S(1)} %slice.19.factor), channel_id=1, source_target_pairs={{0,8},{4,20},{9,1},{13,29},{18,26}} | collective-permute-start | bytes 3145736 | tf_op jit(solution)/shard_map/ppermute | solution.py:156
  14.0 8.4 %collective-permute-start.1 = (f32[512,512]{1,0:T(8,128)}, f32[512,512]{1,0:T(8,128)}, u32[]{:S(2)}, u32[]{:S(2)}) collective-permute-start(f32[512,512]{1,0:T(8,128)} %get-tuple-element.47), channel_id=1, source_target_pairs={{4,0},{0,4},{12,8},{8,12},{20,16},{16,20},{28,24},{24,28},{5,1},{1... | collective-permute-start | bytes 3145736 | tf_op jit(solution)/shard_map/ppermute | solution.py:88
  21.0 13.9 %copy-start.1 = (f32[512,512]{1,0:T(8,128)}, f32[512,512]{1,0:T(8,128)S(1)}, u32[]{:S(2)}) copy-start(f32[512,512]{1,0:T(8,128)S(1)} %get-tuple-element.51.factor) | copy-start | bytes 3145732
  21.0 13.6 %collective-permute-start.4 = (f32[512,512]{1,0:T(8,128)S(1)}, f32[512,512]{1,0:T(8,128)S(1)}, u32[]{:S(2)}, u32[]{:S(2)}) collective-permute-start(f32[512,512]{1,0:T(8,128)S(1)} %get-tuple-element.48), channel_id=1, source_target_pairs={{0,16},{8,24},{4,12},{20,28},{9,25},{1,17},{29,21},{22,30}} | collective-permute-start | bytes 3145736 | tf_op jit(solution)/shard_map/ppermute | solution.py:156
  23.8 16.7 %collective-permute-start.2 = (f32[512,512]{1,0:T(8,128)S(1)}, f32[512,512]{1,0:T(8,128)S(1)}, u32[]{:S(2)}, u32[]{:S(2)}) collective-permute-start(f32[512,512]{1,0:T(8,128)S(1)} %add.90), channel_id=1, source_target_pairs={{16,0},{24,8},{12,4},{28,20},{25,9},{17,1},{21,29},{30,22}} | collective-permute-start | bytes 3145736 | tf_op jit(solution)/shard_map/ppermute | solution.py:156
  29.2 11.4 %copy-start.4 = (bf16[512,1024]{1,0:T(8,128)(2,1)}, bf16[512,1024]{1,0:T(8,128)(2,1)S(1)}, u32[]{:S(2)}) copy-start(bf16[512,1024]{1,0:T(8,128)(2,1)S(1)} %get-tuple-element.41.low) | copy-start | bytes 3145732
  29.2 12.9 %collective-permute-start = (f32[512,512]{1,0:T(8,128)S(1)}, f32[512,512]{1,0:T(8,128)S(1)}, u32[]{:S(2)}, u32[]{:S(2)}) collective-permute-start(f32[512,512]{1,0:T(8,128)S(1)} %get-tuple-element.43), channel_id=1, source_target_pairs={{4,0},{0,4},{12,8},{8,12},{20,16},{16,20},{28,24},{24,28},{5,1},{1... | collective-permute-start | bytes 3145736 | tf_op jit(solution)/shard_map/ppermute | solution.py:88
  34.8 7.5 %copy-start.18 = (f32[512,512]{1,0:T(8,128)}, f32[512,512]{1,0:T(8,128)S(1)}, u32[]{:S(2)}) copy-start(f32[512,512]{1,0:T(8,128)S(1)} %add.92.rest_0_) | copy-start | bytes 3145732
  34.8 7.5 %collective-permute-start.5 = (f32[512,512]{1,0:T(8,128)S(1)}, f32[512,512]{1,0:T(8,128)S(1)}, u32[]{:S(2)}, u32[]{:S(2)}) collective-permute-start(f32[512,512]{1,0:T(8,128)S(1)} %add.92.rest_0_), channel_id=1, source_target_pairs={{4,0},{0,4},{12,8},{8,12},{20,16},{16,20},{28,24},{24,28},{5,1},{1... | collective-permute-start | bytes 3145736 | tf_op jit(solution)/shard_map/ppermute | solution.py:88
  34.9 17.1 %collective-permute-start.8 = (f32[512,512]{1,0:T(8,128)S(1)}, f32[512,512]{1,0:T(8,128)S(1)}, u32[]{:S(2)}, u32[]{:S(2)}) collective-permute-start(f32[512,512]{1,0:T(8,128)S(1)} %get-tuple-element.51.factor), channel_id=1, source_target_pairs={{0,8},{4,20},{9,1},{13,29},{18,26}} | collective-permute-start | bytes 3145736 | tf_op jit(solution)/shard_map/ppermute | solution.py:156
  40.7 2.7 %copy-start.19 = (f32[512,512]{1,0:T(8,128)}, f32[512,512]{1,0:T(8,128)S(1)}, u32[]{:S(2)}) copy-start(f32[512,512]{1,0:T(8,128)S(1)} %add.91.mirror) | copy-start | bytes 3145732
  40.7 17.1 %collective-permute-start.6 = (f32[512,512]{1,0:T(8,128)S(1)}, f32[512,512]{1,0:T(8,128)S(1)}, u32[]{:S(2)}, u32[]{:S(2)}) collective-permute-start(f32[512,512]{1,0:T(8,128)S(1)} %add.91.mirror), channel_id=1, source_target_pairs={{8,0},{20,4},{1,9},{29,13},{26,18}} | collective-permute-start | bytes 3145736 | tf_op jit(solution)/shard_map/ppermute | solution.py:156
  43.4 8.7 %copy-start.16 = (f32[512,1024]{1,0:T(8,128)S(1)}, f32[512,1024]{1,0:T(8,128)}, u32[]{:S(2)}) copy-start(f32[512,1024]{1,0:T(8,128)} %param.7) | copy-start | bytes 6291460
  58.8 13.6 %copy-start.20 = (f32[256,512]{1,0:T(8,128)}, f32[256,512]{1,0:T(8,128)S(1)}, u32[]{:S(2)}) copy-start(f32[256,512]{1,0:T(8,128)S(1)} %get-tuple-element.83) | copy-start | bytes 1572868
  58.8 13.6 %collective-permute-start.9 = (f32[512,512]{1,0:T(8,128)S(1)}, f32[512,512]{1,0:T(8,128)S(1)}, u32[]{:S(2)}, u32[]{:S(2)}) collective-permute-start(f32[512,512]{1,0:T(8,128)S(1)} %broadcast_select_fusion), channel_id=1, source_target_pairs={{0,16},{8,24},{4,12},{20,28},{9,25},{1,17},{29,21},{22,30}} | collective-permute-start | bytes 3145736 | tf_op jit(solution)/shard_map/ppermute | solution.py:156
  60.1 16.7 %collective-permute-start.10 = (f32[512,512]{1,0:T(8,128)S(1)}, f32[512,512]{1,0:T(8,128)S(1)}, u32[]{:S(2)}, u32[]{:S(2)}) collective-permute-start(f32[512,512]{1,0:T(8,128)S(1)} %add.89), channel_id=1, source_target_pairs={{16,0},{24,8},{12,4},{28,20},{25,9},{17,1},{21,29},{30,22}} | collective-permute-start | bytes 3145736 | tf_op jit(solution)/shard_map/ppermute | solution.py:156
  61.4 10.9 %collective-permute-start.7 = (f32[256,512]{1,0:T(8,128)S(1)}, f32[256,512]{1,0:T(8,128)S(1)}, u32[]{:S(2)}, u32[]{:S(2)}) collective-permute-start(f32[256,512]{1,0:T(8,128)S(1)} %get-tuple-element.83), channel_id=1, source_target_pairs={{0,1},{3,2},{4,5},{7,6},{8,9},{11,10},{12,13},{15,14},{16,17},{19,... | collective-permute-start | bytes 1572872 | tf_op jit(solution)/shard_map/ppermute | solution.py:372
  77.0 2.8 %copy-start.17 = (f32[512,512]{1,0:T(8,128)}, f32[512,512]{1,0:T(8,128)S(1)}, u32[]{:S(2)}) copy-start(f32[512,512]{1,0:T(8,128)S(1)} %add.96.rest_0_) | copy-start | bytes 3145732
  77.1 2.8 %collective-permute-start.11 = (f32[512,512]{1,0:T(8,128)S(1)}, f32[512,512]{1,0:T(8,128)S(1)}, u32[]{:S(2)}, u32[]{:S(2)}) collective-permute-start(f32[512,512]{1,0:T(8,128)S(1)} %add.96.rest_0_), channel_id=1, source_target_pairs={{4,0},{0,4},{12,8},{8,12},{20,16},{16,20},{28,24},{24,28},{5,1},{1... | collective-permute-start | bytes 3145736 | tf_op jit(solution)/shard_map/ppermute | solution.py:88
  78.4 17.0 %collective-permute-start.12 = (f32[512,512]{1,0:T(8,128)}, f32[512,512]{1,0:T(8,128)}, u32[]{:S(2)}, u32[]{:S(2)}) collective-permute-start(f32[512,512]{1,0:T(8,128)} %add.95.mirror), channel_id=1, source_target_pairs={{8,0},{20,4},{1,9},{29,13},{26,18}} | collective-permute-start | bytes 3145736 | tf_op jit(solution)/shard_map/ppermute | solution.py:156
  86.2 20.8 %collective-permute-start.24 = (f32[512,512]{1,0:T(8,128)S(1)}, f32[512,512]{1,0:T(8,128)}, u32[]{:S(2)}, u32[]{:S(2)}) collective-permute-start(f32[512,512]{1,0:T(8,128)S(1)} %get-tuple-element.72), channel_id=1, source_target_pairs={{4,0},{0,4},{12,8},{8,12},{20,16},{16,20},{28,24},{24,28},{5,1},{1... | collective-permute-start | bytes 3145736 | tf_op jit(solution)/shard_map/ppermute | solution.py:88
  86.7 17.5 %collective-permute-start.15 = (f32[256,512]{1,0:T(8,128)}, f32[256,512]{1,0:T(8,128)}, u32[]{:S(2)}, u32[]{:S(2)}) collective-permute-start(f32[256,512]{1,0:T(8,128)} %get-tuple-element.62), channel_id=1, source_target_pairs={{0,1},{3,2},{4,5},{7,6},{8,9},{11,10},{12,13},{15,14},{16,17},{19,... | collective-permute-start | bytes 1572872 | tf_op jit(solution)/shard_map/ppermute | solution.py:372
  93.8 15.6 %collective-permute-start.14 = (f32[256,512]{1,0:T(8,128)S(1)}, f32[256,512]{1,0:T(8,128)S(1)}, u32[]{:S(2)}, u32[]{:S(2)}) collective-permute-start(f32[256,512]{1,0:T(8,128)S(1)} %add.99), channel_id=1, source_target_pairs={{1,2},{2,1},{5,6},{6,5},{9,10},{10,9},{13,14},{14,13},{17,18},{18,... | collective-permute-start | bytes 1572872 | tf_op jit(solution)/shard_map/ppermute | solution.py:381
  97.8 28.4 %collective-permute-start.13 = (f32[256,512]{1,0:T(8,128)}, f32[256,512]{1,0:T(8,128)}, u32[]{:S(2)}, u32[]{:S(2)}) collective-permute-start(f32[256,512]{1,0:T(8,128)} %get-tuple-element.81), channel_id=1, source_target_pairs={{0,1},{3,2},{4,5},{7,6},{8,9},{11,10},{12,13},{15,14},{16,17},{19,... | collective-permute-start | bytes 1572872 | tf_op jit(solution)/shard_map/ppermute | solution.py:372
  105.5 5.2 %collective-permute-start.18 = (f32[256,512]{1,0:T(8,128)S(1)}, f32[256,512]{1,0:T(8,128)}, u32[]{:S(2)}, u32[]{:S(2)}) collective-permute-start(f32[256,512]{1,0:T(8,128)S(1)} %add.102), channel_id=1, source_target_pairs={{1,2},{2,1},{5,6},{6,5},{9,10},{10,9},{13,14},{14,13},{17,18},{18,... | collective-permute-start | bytes 1572872 | tf_op jit(solution)/shard_map/ppermute | solution.py:381
  109.3 18.2 %collective-permute-start.25 = (f32[256,512]{1,0:T(8,128)}, f32[256,512]{1,0:T(8,128)}, u32[]{:S(2)}, u32[]{:S(2)}) collective-permute-start(f32[256,512]{1,0:T(8,128)} %dynamic-slice_bitcast_fusion), channel_id=1, source_target_pairs={{0,8},{1,9},{2,10},{3,11},{4,20},{5,21},{6,22},{7,23},{8,0},{9,1},... | collective-permute-start | bytes 1572872 | tf_op jit(solution)/shard_map/ppermute | solution.py:433
  109.4 20.7 %collective-permute-start.16 = (f32[256,512]{1,0:T(8,128)S(1)}, f32[256,512]{1,0:T(8,128)S(1)}, u32[]{:S(2)}, u32[]{:S(2)}) collective-permute-start(f32[256,512]{1,0:T(8,128)S(1)} %add.100.rest_0_), channel_id=1, source_target_pairs={{1,0},{2,3},{5,4},{6,7},{9,8},{10,11},{13,12},{14,15},{17,16},{18,... | collective-permute-start | bytes 1572872 | tf_op jit(solution)/shard_map/ppermute | solution.py:381
  110.7 24.3 %collective-permute-start.21 = (f32[256,512]{1,0:T(8,128)}, f32[256,512]{1,0:T(8,128)S(1)}, u32[]{:S(2)}, u32[]{:S(2)}) collective-permute-start(f32[256,512]{1,0:T(8,128)} %get-tuple-element.68), channel_id=1, source_target_pairs={{0,1},{3,2},{4,5},{7,6},{8,9},{11,10},{12,13},{15,14},{16,17},{19,... | collective-permute-start | bytes 1572872 | tf_op jit(solution)/shard_map/ppermute | solution.py:372
  126.2 13.8 %collective-permute-start.19 = (f32[256,512]{1,0:T(8,128)S(1)}, f32[256,512]{1,0:T(8,128)S(1)}, u32[]{:S(2)}, u32[]{:S(2)}) collective-permute-start(f32[256,512]{1,0:T(8,128)S(1)} %add.103.rest_2_), channel_id=1, source_target_pairs={{1,0},{2,3},{5,4},{6,7},{9,8},{10,11},{13,12},{14,15},{17,16},{18,... | collective-permute-start | bytes 1572872 | tf_op jit(solution)/shard_map/ppermute | solution.py:381
  128.7 12.1 %collective-permute-start.26 = (f32[128,512]{1,0:T(8,128)S(1)}, f32[128,512]{1,0:T(8,128)S(1)}, u32[]{:S(2)}, u32[]{:S(2)}) collective-permute-start(f32[128,512]{1,0:T(8,128)S(1)} %dynamic-slice_bitcast_fusion.1), channel_id=1, source_target_pairs={{0,16},{1,17},{2,18},{3,19},{4,12},{5,13},{6,14},{7,15},{8,24},{9,... | collective-permute-start | bytes 786440 | tf_op jit(solution)/shard_map/ppermute | solution.py:433
  130.1 10.7 %copy-start.7 = (f32[256,512]{1,0:T(8,128)}, f32[256,512]{1,0:T(8,128)S(1)}, u32[]{:S(2)}) copy-start(f32[256,512]{1,0:T(8,128)S(1)} %collective-permute-done.16.rest_1_) | copy-start | bytes 1572868
  130.1 13.1 %collective-permute-start.17 = (f32[256,512]{1,0:T(8,128)S(1)}, f32[256,512]{1,0:T(8,128)S(1)}, u32[]{:S(2)}, u32[]{:S(2)}) collective-permute-start(f32[256,512]{1,0:T(8,128)S(1)} %add.98), channel_id=1, source_target_pairs={{1,2},{2,1},{5,6},{6,5},{9,10},{10,9},{13,14},{14,13},{17,18},{18,... | collective-permute-start | bytes 1572872 | tf_op jit(solution)/shard_map/ppermute | solution.py:381
  140.9 18.8 %copy-start = (f32[2,512,512]{2,1,0:T(8,128)S(1)}, f32[2,512,512]{2,1,0:T(8,128)}, u32[]{:S(2)}) copy-start(f32[2,512,512]{2,1,0:T(8,128)} %unit_ref.5) | copy-start | bytes 6291460
  140.9 5.5 %collective-permute-start.27 = (f32[128,512]{1,0:T(8,128)S(1)}, f32[128,512]{1,0:T(8,128)S(1)}, u32[]{:S(2)}, u32[]{:S(2)}) collective-permute-start(f32[128,512]{1,0:T(8,128)S(1)} %bitcast_add_fusion.1), channel_id=1, source_target_pairs={{0,1},{3,2},{4,5},{7,6},{8,9},{11,10},{12,13},{15,14},{16,17},{19,... | collective-permute-start | bytes 786440 | tf_op jit(solution)/shard_map/ppermute | solution.py:372
  142.5 4.6 %collective-permute-start.22 = (f32[256,512]{1,0:T(8,128)S(1)}, f32[256,512]{1,0:T(8,128)S(1)}, u32[]{:S(2)}, u32[]{:S(2)}) collective-permute-start(f32[256,512]{1,0:T(8,128)S(1)} %add.105), channel_id=1, source_target_pairs={{1,2},{2,1},{5,6},{6,5},{9,10},{10,9},{13,14},{14,13},{17,18},{18,... | collective-permute-start | bytes 1572872 | tf_op jit(solution)/shard_map/ppermute | solution.py:381
  143.3 14.3 %collective-permute-start.20 = (f32[256,512]{1,0:T(8,128)S(1)}, f32[256,512]{1,0:T(8,128)S(1)}, u32[]{:S(2)}, u32[]{:S(2)}) collective-permute-start(f32[256,512]{1,0:T(8,128)S(1)} %add.101.rest_0_), channel_id=1, source_target_pairs={{1,0},{2,3},{5,4},{6,7},{9,8},{10,11},{13,12},{14,15},{17,16},{18,... | collective-permute-start | bytes 1572872 | tf_op jit(solution)/shard_map/ppermute | solution.py:381
  146.4 1.6 collective-permute-start.28
  148.0 23.7 %collective-permute-start.29 = (f32[128,512]{1,0:T(8,128)S(1)}, f32[128,512]{1,0:T(8,128)}, u32[]{:S(2)}, u32[]{:S(2)}) collective-permute-start(f32[128,512]{1,0:T(8,128)S(1)} %add.114), channel_id=1, source_target_pairs={{1,0},{2,3},{5,4},{6,7},{9,8},{10,11},{13,12},{14,15},{17,16},{18,... | collective-permute-start | bytes 786440 | tf_op jit(solution)/shard_map/ppermute | solution.py:381
  158.4 21.5 %collective-permute-start.23 = (f32[256,512]{1,0:T(8,128)}, f32[256,512]{1,0:T(8,128)}, u32[]{:S(2)}, u32[]{:S(2)}) collective-permute-start(f32[256,512]{1,0:T(8,128)} %add.106.rest_2_), channel_id=1, source_target_pairs={{1,0},{2,3},{5,4},{6,7},{9,8},{10,11},{13,12},{14,15},{17,16},{18,... | collective-permute-start | bytes 1572872 | tf_op jit(solution)/shard_map/ppermute | solution.py:381
  161.8 18.1 %copy-start.3 = (f32[256,512]{1,0:T(8,128)S(1)}, f32[256,512]{1,0:T(8,128)}, u32[]{:S(2)}) copy-start(f32[256,512]{1,0:T(8,128)} %copy-done.2) | copy-start | bytes 1572868
  161.8 18.1 %copy-start.12 = (f32[256,512]{1,0:T(8,128)S(1)}, f32[256,512]{1,0:T(8,128)}, u32[]{:S(2)}) copy-start(f32[256,512]{1,0:T(8,128)} %copy-done.11) | copy-start | bytes 1572868
  172.7 10.5 %collective-permute-start.32 = (f32[128,512]{1,0:T(8,128)S(1)}, f32[128,512]{1,0:T(8,128)S(1)}, u32[]{:S(2)}, u32[]{:S(2)}) collective-permute-start(f32[128,512]{1,0:T(8,128)S(1)} %broadcast_select_fusion.2), channel_id=1, source_target_pairs={{0,24},{1,25},{2,26},{3,27},{8,16},{9,17},{10,18},{11,19},{16,8},{... | collective-permute-start | bytes 786440 | tf_op jit(solution)/shard_map/ppermute | solution.py:483
  172.8 10.4 %collective-permute-start.31 = (f32[128,512]{1,0:T(8,128)S(1)}, f32[128,512]{1,0:T(8,128)S(1)}, u32[]{:S(2)}, u32[]{:S(2)}) collective-permute-start(f32[128,512]{1,0:T(8,128)S(1)} %broadcast_select_fusion.2), channel_id=1, source_target_pairs={{0,8},{1,9},{2,10},{3,11},{8,0},{9,1},{10,2},{11,3},{16,24},{17,25... | collective-permute-start | bytes 786440 | tf_op jit(solution)/shard_map/ppermute | solution.py:483
  174.6 8.7 %collective-permute-start.30 = (f32[128,512]{1,0:T(8,128)S(1)}, f32[128,512]{1,0:T(8,128)S(1)}, u32[]{:S(2)}, u32[]{:S(2)}) collective-permute-start(f32[128,512]{1,0:T(8,128)S(1)} %broadcast_select_fusion.2), channel_id=1, source_target_pairs={{0,16},{1,17},{2,18},{3,19},{8,24},{9,25},{10,26},{11,27},{16,0},{... | collective-permute-start | bytes 786440 | tf_op jit(solution)/shard_map/ppermute | solution.py:483
  183.2 2.9 %copy-start.15 = (f32[2,512]{1,0:T(2,128)S(1)}, f32[2,512]{1,0:T(2,128)}, u32[]{:S(2)}) copy-start(f32[2,512]{1,0:T(2,128)} %pivot.1) | copy-start | bytes 12292
  183.4 2.7 %collective-permute-start.33 = (f32[512,512]{1,0:T(8,128)S(1)}, f32[512,512]{1,0:T(8,128)S(1)}, u32[]{:S(2)}, u32[]{:S(2)}) collective-permute-start(f32[512,512]{1,0:T(8,128)S(1)} %pad_maximum_fusion.rest_0_), channel_id=1, source_target_pairs={{4,0},{0,4},{12,8},{8,12},{20,16},{16,20},{28,24},{24,28},{5,1},{1... | collective-permute-start | bytes 3145736 | tf_op jit(solution)/shard_map/ppermute | solution.py:88
  (10 other events, 10.9 us)

commit v9 on v8

--- a/solution.py
+++ b/solution.py
@@ -362,7 +362,7 @@
             cost_estimate=COST,
             name="forward",
         )(high, low, factors[member], mirror, *parts, *earlier)
-        return outs[:splits], outs[splits:], parts[-1]
+        return outs[:splits], outs[splits:]
 
     hops = plan.line_hops()
 
@@ -371,14 +371,17 @@
             x, _ = lax.optimization_barrier((x, tuple(after)))
         return lax.ppermute(x, "col", hops[0])
 
-    def run(x, got, ties=()):
+    def run(x, got, ties=(), second=None):
         sent, brought = [], [got]
         for hop in range(1, len(hops)):
             x = plan.line_step(hop - 1, x, got)
             sent.append(x)
             tie = ties[hop - 1] if hop <= len(ties) else ()
             y = lax.optimization_barrier((x, tuple(tie)))[0] if tie else x
-            got = lax.ppermute(y, "col", hops[hop])
+            if hop == 1 and second is not None:
+                got = second
+            else:
+                got = lax.ppermute(y, "col", hops[hop])
             brought.append(got)
         if len(hops) == 1:
             got = x = x + got
@@ -387,7 +390,7 @@
     spread, collect = Chain(), Chain()
     count = members * steps
     tiles, held, mirror, chunks, entered = {}, {}, {}, [], {}
-    after, cross, last_swap = (), [], ()
+    after, cross, second = (), [], None
     for phase in range(count + 1):
         if phase < count:
             out, step = divmod(phase, steps)
@@ -400,9 +403,13 @@
             )
         if chunks and 0 not in entered:
             entered[0] = enter(chunks[0])
-            entered[0], got_out, got_back = lax.optimization_barrier(
-                (entered[0], got_out, got_back)
-            )
+            entered[0], got_out = lax.optimization_barrier((entered[0], got_out))
+            if len(hops) > 1 and len(chunks) > 1:
+                second = lax.ppermute(plan.line_step(0, chunks[0], entered[0]), "col", hops[1])
+                entered[1] = enter(chunks[1], (entered[0],))
+                second, entered[1], got_back = lax.optimization_barrier(
+                    (second, entered[1], got_back)
+                )
         after = ()
         if phase % steps == 0 and phase < count:
             high, low, *parts = gather(out) if out == 0 else tiles[out]
@@ -417,7 +424,7 @@
             if turn < steps - 1:
                 mirror[back] = mirror[back] + got_back
             else:
-                sums, cross, last_swap = forward(back, *tiles[back], mirror[back], held[back], cross)
+                sums, cross = forward(back, *tiles[back], mirror[back], held[back], cross)
                 share = sums[0].shape[0]
                 after = tuple(
                     part + got_back[i * share:(i + 1) * share] for i, part in enumerate(sums)
@@ -465,13 +472,15 @@
             entered[2] = enter(chunks[2])
         ties = [()] * middle
         if i < 2 and i < last and middle:
-            if i == 0:
-                entered[1] = enter(chunks[1], (entered[0], last_swap))
+            if 1 not in entered:
+                entered[1] = enter(chunks[1], (entered[0],))
             ties[-1] = (entered[i + 1],)
         elif i > 1 and middle:
             ties = [(brought[i - 2][hop + 1],) for hop in range(1, middle)]
             ties.append((brought[i - 1][-1],))
-        chunks[i], ends[i], sent[i], brought[i] = run(chunks[i], entered[i], ties)
+        chunks[i], ends[i], sent[i], brought[i] = run(
+            chunks[i], entered[i], ties, second if i == 0 else None
+        )
     update, got, _, _ = run(update, enter(update), [(x,) for x in sent[last]])
     for member in range(members):
         column = place(member, column)

time: 193 us -> 203 us (1.052)
  waiting for transfers between devices: 67.8 us -> 84.1 us
  starting transfers between devices: 59.6 us -> 54.5 us
    ppermute x5, starting transfers between devices: 25.6 us -> 18.5 us  [enter(): return lax.ppermute(x, 'col', hops[0])]
    ppermute x8, waiting for transfers between devices: 25.1 us -> 29.9 us  [issue(): out.append(lax.ppermute(x, axis, pairs))]
    ppermute x10 -> x9, waiting for transfers between devices: 21.4 us -> 25.7 us  [run(): got = lax.ppermute(y, 'col', hops[hop])]
    ppermute x5, waiting for transfers between devices: 18.6 us -> 22.9 us  [enter(): return lax.ppermute(x, 'col', hops[0])]
    ppermute x3, waiting for transfers between devices: 0.01 us -> 2.9 us  [shards(): lax.ppermute(x, both, plan.offset_pairs(r))]
    ppermute x2, starting transfers between devices: 0.07 us -> 2.55 us  [shards(): x = keep + lax.ppermute(send, both, plan.bit_pairs(step))]
    unnamed x48 -> x56, local copies, waits for them, and re-layouts: 8.26 us -> 9.25 us
    ppermute x10 -> x9, starting transfers between devices: 10.7 us -> 9.97 us  [run(): got = lax.ppermute(y, 'col', hops[hop])]
  transfers between devices with their start and end apart: 34 -> 34, of which waited for: 16 -> 18; matrix products, arithmetic and copies ran while one was open for 10% -> 9% of each run, Pallas kernels for 14% -> 13%
where the time goes in v9:
time: 203 us; the launch traced here: 201 us
  waiting for transfers between devices  84.1 us (41%)
  starting transfers between devices  54.5 us (27%)
  Pallas kernels  32.2 us (16%)
  other arithmetic  17.9 us (9%)
  local copies, waits for them, and re-layouts  11.4 us (6%)
    ppermute x8, waiting for transfers between devices, issue(): out.append(lax.ppermute(x, axis, pairs))  29.9 us
    ppermute x9, waiting for transfers between devices, run(): got = lax.ppermute(y, 'col', hops[hop])  25.7 us
    ppermute x5, waiting for transfers between devices, enter(): return lax.ppermute(x, 'col', hops[0])  22.9 us
    ppermute x8, starting transfers between devices, issue(): out.append(lax.ppermute(x, axis, pairs))  18.9 us
    ppermute x5, starting transfers between devices, enter(): return lax.ppermute(x, 'col', hops[0])  18.5 us
    pallas_call x2, Pallas kernels, forward(): pl.pallas_call(functools.partial(forward_kernel, plan, member), in_specs=...  10.1 us
    ppermute x9, starting transfers between devices, run(): got = lax.ppermute(y, 'col', hops[hop])  9.97 us
    pallas_call x2, Pallas kernels, gather(): pl.pallas_call(functools.partial(gather_kernel, plan, member), in_specs=s...  9.28 us
  transfers between devices with their start and end apart: 34, of which 18 were waited for; matrix products, arithmetic and copies ran while one was open for 9% of the time, Pallas kernels for 13%

profile of v9, /device:TPU:0, one launch (start us, length us, event | category | flops | bytes accessed | tf_op | source)
XLA Modules:
  0.0 201.4 jit_solution(14915341337453503238)
XLA Ops:
  0.6 1.3 slice.19.factor
  2.0 5.8 %collective-permute-start.3 = (f32[512,512]{1,0:T(8,128)S(1)}, f32[512,512]{1,0:T(8,128)}, u32[]{:S(2)}, u32[]{:S(2)}) collective-permute-start(f32[512,512]{1,0:T(8,128)S(1)} %slice.19.factor), channel_id=1, source_target_pairs={{0,8},{4,20},{9,1},{13,29},{18,26}} | collective-permute-start | bytes 3145736 | tf_op jit(solution)/shard_map/ppermute | solution.py:156
  7.8 5.1 %gather_mirror.3 = (bf16[512,1024]{1,0:T(8,128)(2,1)S(1)}, bf16[512,1024]{1,0:T(8,128)(2,1)S(1)}, f32[512,512]{1,0:T(8,128)S(1)}, f32[512,512]{1,0:T(8,128)}) custom-call(s32[2,16]{1,0:T(2,128)S(1)} %copy-done.13, s32[2,16]{1,0:T(2,128)S(1)} %copy-done.14, f32[2048,4096]{1,0:T(8,128)} %front.3, f32[512,512]{1,0:T(8,128)S(1)} %slice.19.factor), custom_call_target="tpu_custom_call" | custom-call | flops 1677721600 | bytes 8388608 | tf_op jit(solution)/shard_map/gather_mirror/pallas_call | solution.py:333
  13.9 5.2 %collective-permute-done.3 = f32[512,512]{1,0:T(8,128)} collective-permute-done((f32[512,512]{1,0:T(8,128)S(1)}, f32[512,512]{1,0:T(8,128)}, u32[]{:S(2)}, u32[]{:S(2)}) %collective-permute-start.3) | collective-permute-done | bytes 1048608 | tf_op jit(solution)/shard_map/ppermute | solution.py:156
  19.1 1.9 broadcast_select_fusion.1
  21.0 1.4 collective-permute-start.4
  22.4 1.4 add.91
  23.8 1.3 collective-permute-start.2
  25.1 9.5 %collective-permute-done.4 = f32[512,512]{1,0:T(8,128)S(1)} collective-permute-done((f32[512,512]{1,0:T(8,128)S(1)}, f32[512,512]{1,0:T(8,128)S(1)}, u32[]{:S(2)}, u32[]{:S(2)}) %collective-permute-start.4) | collective-permute-done | bytes 1048608 | tf_op jit(solution)/shard_map/ppermute | solution.py:156
  34.9 4.2 %gather_mirror.2 = (bf16[512,1024]{1,0:T(8,128)(2,1)S(1)}, bf16[512,1024]{1,0:T(8,128)(2,1)S(1)}, f32[512,512]{1,0:T(8,128)S(1)}, f32[512,512]{1,0:T(8,128)S(1)}) custom-call(s32[2,16]{1,0:T(2,128)S(1)} %copy-done.13, s32[2,16]{1,0:T(2,128)S(1)} %copy-done.14, f32[2048,4096]{1,0:T(8,128)} %front.3, f32[512,512]{1,0:T(8,128)S(1)} %get-tuple-element.53.factor), custom_call_target="tpu_custom_call" | custom-call | flops 1677721600 | bytes 8388608 | tf_op jit(solution)/shard_map/gather_mirror/pallas_call | solution.py:333
  40.1 5.0 %collective-permute-start.8 = (f32[512,512]{1,0:T(8,128)S(1)}, f32[512,512]{1,0:T(8,128)S(1)}, u32[]{:S(2)}, u32[]{:S(2)}) collective-permute-start(f32[512,512]{1,0:T(8,128)S(1)} %get-tuple-element.53.factor), channel_id=1, source_target_pairs={{0,8},{4,20},{9,1},{13,29},{18,26}} | collective-permute-start | bytes 3145736 | tf_op jit(solution)/shard_map/ppermute | solution.py:156
  45.3 1.3 collective-permute-start.6
  47.7 4.8 %forward.2 = (f32[256,512]{1,0:T(8,128)S(1)}, f32[256,512]{1,0:T(8,128)S(1)}, f32[256,512]{1,0:T(8,128)S(1)}, f32[256,512]{1,0:T(8,128)S(1)}) custom-call(bf16[512,1024]{1,0:T(8,128)(2,1)S(1)} %get-tuple-element.46.high, bf16[512,1024]{1,0:T(8,128)(2,1)S(1)} %copy-done.6, f32[512,512]{1,0:T(8,128)S(1)} %slice.19.factor, f32[512,512]{1,0:T(8,128)} %copy-done.19, ...), custom_call_target="tpu_custom_call" | custom-call | flops 1677721600 | bytes 8388608 | tf_op jit(solution)/shard_map/forward/pallas_call | solution.py:351
  52.5 4.8 %collective-permute-done.8 = f32[512,512]{1,0:T(8,128)S(1)} collective-permute-done((f32[512,512]{1,0:T(8,128)S(1)}, f32[512,512]{1,0:T(8,128)S(1)}, u32[]{:S(2)}, u32[]{:S(2)}) %collective-permute-start.8) | collective-permute-done | bytes 1048608 | tf_op jit(solution)/shard_map/ppermute | solution.py:156
  57.5 4.5 %collective-permute-done.6 = f32[512,512]{1,0:T(8,128)S(1)} collective-permute-done((f32[512,512]{1,0:T(8,128)S(1)}, f32[512,512]{1,0:T(8,128)S(1)}, u32[]{:S(2)}, u32[]{:S(2)}) %collective-permute-start.6) | collective-permute-done | bytes 1048608 | tf_op jit(solution)/shard_map/ppermute | solution.py:156
  62.2 1.4 collective-permute-start.9
  63.6 1.6 collective-permute-start.7
  65.4 1.3 collective-permute-start.12
  66.7 8.7 %collective-permute-done.7 = f32[256,512]{1,0:T(8,128)S(1)} collective-permute-done((f32[256,512]{1,0:T(8,128)S(1)}, f32[256,512]{1,0:T(8,128)S(1)}, u32[]{:S(2)}, u32[]{:S(2)}) %collective-permute-start.7) | collective-permute-done | bytes 524320 | tf_op jit(solution)/shard_map/ppermute | solution.py:372
  76.9 6.0 %collective-permute-start.11 = (f32[256,512]{1,0:T(8,128)S(1)}, f32[256,512]{1,0:T(8,128)}, u32[]{:S(2)}, u32[]{:S(2)}) collective-permute-start(f32[256,512]{1,0:T(8,128)S(1)} %get-tuple-element.57), channel_id=1, source_target_pairs={{0,1},{3,2},{4,5},{7,6},{8,9},{11,10},{12,13},{15,14},{16,17},{19,... | collective-permute-start | bytes 1572872 | tf_op jit(solution)/shard_map/ppermute | solution.py:372
  83.7 10.2 %collective-permute-done.11 = f32[256,512]{1,0:T(8,128)} collective-permute-done((f32[256,512]{1,0:T(8,128)S(1)}, f32[256,512]{1,0:T(8,128)}, u32[]{:S(2)}, u32[]{:S(2)}) %collective-permute-start.11) | collective-permute-done | bytes 524320 | tf_op jit(solution)/shard_map/ppermute | solution.py:372
  95.2 1.5 collective-permute-start.14
  97.6 5.3 %forward.3 = (f32[256,512]{1,0:T(8,128)S(1)}, f32[256,512]{1,0:T(8,128)S(1)}, f32[512,512]{1,0:T(8,128)S(1)}, f32[512,512]{1,0:T(8,128)S(1)}) custom-call(bf16[512,1024]{1,0:T(8,128)(2,1)S(1)} %get-tuple-element.42.high, bf16[512,1024]{1,0:T(8,128)(2,1)} %copy-done.4, f32[512,512]{1,0:T(8,128)} %copy-done.1, f32[512,512]{1,0:T(8,128)} %add.97.mirror, ...), custom_call_target="tpu_custom_call" | custom-call | flops 1677721600 | bytes 8388608 | tf_op jit(solution)/shard_map/forward/pallas_call | solution.py:351
  103.1 2.1 %add.103 = f32[256,512]{1,0:T(8,128)} add(f32[256,512]{1,0:T(8,128)} %copy-done.22, f32[256,512]{1,0:T(8,128)} %collective-permute-done.11) | non-fusion elementwise | flops 131072 | bytes 1572864 | tf_op jit(solution)/shard_map/add | solution.py:101
  105.2 1.5 collective-permute-start.18
  106.6 5.5 %collective-permute-done.14 = f32[512,512]{1,0:T(8,128)} collective-permute-done((f32[512,512]{1,0:T(8,128)}, f32[512,512]{1,0:T(8,128)}, u32[]{:S(2)}, u32[]{:S(2)}) %collective-permute-start.14) | collective-permute-done | bytes 1048608 | tf_op jit(solution)/shard_map/ppermute | solution.py:156
  112.2 2.4 %slice_add_fusion = (f32[256,512]{1,0:T(8,128)}, f32[256,512]{1,0:T(8,128)}) fusion(f32[256,512]{1,0:T(8,128)S(1)} %get-tuple-element.71, f32[512,512]{1,0:T(8,128)} %collective-permute-done.14, f32[256,512]{1,0:T(8,128)S(1)} %get-tuple-element.63), kind=kLoop, calls=%fused_computation.1 | loop fusion | flops 262144 | bytes 3145728 | tf_op jit(solution)/shard_map/add | solution.py:430
  114.6 4.7 %collective-permute-start.15 = (f32[256,512]{1,0:T(8,128)}, f32[256,512]{1,0:T(8,128)}, u32[]{:S(2)}, u32[]{:S(2)}) collective-permute-start(f32[256,512]{1,0:T(8,128)} %get-tuple-element.85), channel_id=1, source_target_pairs={{0,1},{3,2},{4,5},{7,6},{8,9},{11,10},{12,13},{15,14},{16,17},{19,... | collective-permute-start | bytes 1572872 | tf_op jit(solution)/shard_map/ppermute | solution.py:372
  119.2 1.6 add.108
  121.7 2.5 %collective-permute-start.25 = (f32[256,512]{1,0:T(8,128)}, f32[256,512]{1,0:T(8,128)}, u32[]{:S(2)}, u32[]{:S(2)}) collective-permute-start(f32[256,512]{1,0:T(8,128)} %dynamic-slice_bitcast_fusion), channel_id=1, source_target_pairs={{0,8},{1,9},{2,10},{3,11},{4,20},{5,21},{6,22},{7,23},{8,0},{9,1},... | collective-permute-start | bytes 1572872 | tf_op jit(solution)/shard_map/ppermute | solution.py:440
  124.2 1.3 collective-permute-start.16
  126.8 4.6 %collective-permute-start.21 = (f32[256,512]{1,0:T(8,128)S(1)}, f32[256,512]{1,0:T(8,128)S(1)}, u32[]{:S(2)}, u32[]{:S(2)}) collective-permute-start(f32[256,512]{1,0:T(8,128)S(1)} %copy-done.23), channel_id=1, source_target_pairs={{0,1},{3,2},{4,5},{7,6},{8,9},{11,10},{12,13},{15,14},{16,17},{19,... | collective-permute-start | bytes 1572872 | tf_op jit(solution)/shard_map/ppermute | solution.py:372
  131.5 1.3 collective-permute-start.19
  135.3 2.9 %collective-permute-done.16.rest_1_ = f32[256,512]{1,0:T(8,128)S(1)} collective-permute-done((f32[256,512]{1,0:T(8,128)S(1)}, f32[256,512]{1,0:T(8,128)S(1)}, u32[]{:S(2)}, u32[]{:S(2)}) %collective-permute-start.16) | collective-permute-done | bytes 524320 | tf_op jit(solution)/shard_map/ppermute | solution.py:384
  139.0 2.7 %collective-permute-done.21 = f32[256,512]{1,0:T(8,128)S(1)} collective-permute-done((f32[256,512]{1,0:T(8,128)S(1)}, f32[256,512]{1,0:T(8,128)S(1)}, u32[]{:S(2)}, u32[]{:S(2)}) %collective-permute-start.21) | collective-permute-done | bytes 524320 | tf_op jit(solution)/shard_map/ppermute | solution.py:372
  141.8 5.9 %collective-permute-done.19.rest_3_ = f32[256,512]{1,0:T(8,128)S(1)} collective-permute-done((f32[256,512]{1,0:T(8,128)S(1)}, f32[256,512]{1,0:T(8,128)S(1)}, u32[]{:S(2)}, u32[]{:S(2)}) %collective-permute-start.19) | collective-permute-done | bytes 524320 | tf_op jit(solution)/shard_map/ppermute | solution.py:384
  148.6 1.6 collective-permute-start.27
  151.0 1.3 collective-permute-start.20
  156.0 1.3 collective-permute-start.29
  157.3 8.1 %collective-permute-done.20.rest_1_ = f32[256,512]{1,0:T(8,128)S(1)} collective-permute-done((f32[256,512]{1,0:T(8,128)S(1)}, f32[256,512]{1,0:T(8,128)S(1)}, u32[]{:S(2)}, u32[]{:S(2)}) %collective-permute-start.20) | collective-permute-done | bytes 524320 | tf_op jit(solution)/shard_map/ppermute | solution.py:384
  169.6 4.3 %place.2.rest_4_ = f32[2048,1024]{1,0:T(8,128)} custom-call(s32[2,16]{1,0:T(2,128)S(1)} %copy-done.13, f32[2,512,512]{2,1,0:T(8,128)S(1)} %copy-done, f32[256,512]{1,0:T(8,128)S(1)} %add.101.rest_0_, f32[256,512]{1,0:T(8,128)S(1)} %copy-done.8, f32[256,512]{1,0:T(8,128)S(1)} %add.104.rest_2_, f32[256,512]{1,0:T(8,128)S(1)} %copy-done.10), custom_call_target="tpu_custom_call" | custom-call | flops 1677721600 | bytes 8388608 | tf_op jit(solution)/shard_map/place/pallas_call | solution.py:448
  174.0 4.6 %collective-permute-done.29 = f32[128,512]{1,0:T(8,128)} collective-permute-done((f32[128,512]{1,0:T(8,128)S(1)}, f32[128,512]{1,0:T(8,128)}, u32[]{:S(2)}, u32[]{:S(2)}) %collective-permute-start.29) | collective-permute-done | bytes 262176 | tf_op jit(solution)/shard_map/ppermute | solution.py:384
  179.6 2.7 %collective-permute-start.32 = (f32[128,512]{1,0:T(8,128)S(1)}, f32[128,512]{1,0:T(8,128)S(1)}, u32[]{:S(2)}, u32[]{:S(2)}) collective-permute-start(f32[128,512]{1,0:T(8,128)S(1)} %broadcast_select_fusion.2), channel_id=1, source_target_pairs={{0,24},{1,25},{2,26},{3,27},{8,16},{9,17},{10,18},{11,19},{16,8},{... | collective-permute-start | bytes 786440 | tf_op jit(solution)/shard_map/ppermute | solution.py:492
  183.1 4.1 %collective-permute-done.23.rest_3_ = f32[256,512]{1,0:T(8,128)} collective-permute-done((f32[256,512]{1,0:T(8,128)}, f32[256,512]{1,0:T(8,128)}, u32[]{:S(2)}, u32[]{:S(2)}) %collective-permute-start.23) | collective-permute-done | bytes 524320 | tf_op jit(solution)/shard_map/ppermute | solution.py:384
  187.2 3.3 %place.3 = f32[2048,1024]{1,0:T(8,128)} custom-call(s32[2,16]{1,0:T(2,128)S(1)} %copy-done.13, f32[2,512,512]{2,1,0:T(8,128)S(1)} %copy-done, f32[256,512]{1,0:T(8,128)S(1)} %copy-done.3, f32[256,512]{1,0:T(8,128)S(1)} %copy-done.12, f32[256,512]{1,0:T(8,128)} %add.107.rest_2_, ...), custom_call_target="tpu_custom_call", output_to_operand_aliasing={{}: (6, {})} | custom-call | flops 1677721600 | bytes 8388608 | tf_op jit(solution)/shard_map/place/pallas_call | solution.py:448
  190.6 2.2 %collective-permute-done.31 = f32[128,512]{1,0:T(8,128)S(1)} collective-permute-done((f32[128,512]{1,0:T(8,128)S(1)}, f32[128,512]{1,0:T(8,128)S(1)}, u32[]{:S(2)}, u32[]{:S(2)}) %collective-permute-start.31) | collective-permute-done | bytes 262176 | tf_op jit(solution)/shard_map/ppermute | solution.py:492
  193.6 2.6 %collective-permute-done.33.rest_1_ = f32[512,512]{1,0:T(8,128)S(1)} collective-permute-done((f32[512,512]{1,0:T(8,128)S(1)}, f32[512,512]{1,0:T(8,128)S(1)}, u32[]{:S(2)}, u32[]{:S(2)}) %collective-permute-start.33) | collective-permute-done | bytes 1048608 | tf_op jit(solution)/shard_map/ppermute | solution.py:88
  196.3 5.1 %diagonal.1 = f32[2,512,512]{2,1,0:T(8,128)} custom-call(f32[2,512]{1,0:T(2,128)S(1)} %copy-done.15, f32[2,512,512]{2,1,0:T(8,128)S(1)} %copy-done, f32[512,512]{1,0:T(8,128)S(1)} %pad_maximum_fusion.rest_0_, f32[512,512]{1,0:T(8,128)S(1)} %collective-permute-done.33.rest_1_), custom_call_target="tpu_custom_call" | custom-call | flops 1677721600 | bytes 8388608 | tf_op jit(solution)/shard_map/diagonal/pallas_call | solution.py:495
  (111 shorter events, 26.4 us)
Async XLA Ops:
  0.6 7.2 %copy-start.13 = (s32[2,16]{1,0:T(2,128)S(1)}, s32[2,16]{1,0:T(2,128)}, u32[]{:S(2)}) copy-start(s32[2,16]{1,0:T(2,128)} %tiles_ref.7) | copy-start | bytes 388
  0.6 7.2 %copy-start.14 = (s32[2,16]{1,0:T(2,128)S(1)}, s32[2,16]{1,0:T(2,128)}, u32[]{:S(2)}) copy-start(s32[2,16]{1,0:T(2,128)} %valid_ref.3) | copy-start | bytes 388
  2.0 17.2 %collective-permute-start.3 = (f32[512,512]{1,0:T(8,128)S(1)}, f32[512,512]{1,0:T(8,128)}, u32[]{:S(2)}, u32[]{:S(2)}) collective-permute-start(f32[512,512]{1,0:T(8,128)S(1)} %slice.19.factor), channel_id=1, source_target_pairs={{0,8},{4,20},{9,1},{13,29},{18,26}} | collective-permute-start | bytes 3145736 | tf_op jit(solution)/shard_map/ppermute | solution.py:156
  13.9 8.4 %collective-permute-start.1 = (f32[512,512]{1,0:T(8,128)}, f32[512,512]{1,0:T(8,128)}, u32[]{:S(2)}, u32[]{:S(2)}) collective-permute-start(f32[512,512]{1,0:T(8,128)} %get-tuple-element.49), channel_id=1, source_target_pairs={{4,0},{0,4},{12,8},{8,12},{20,16},{16,20},{28,24},{24,28},{5,1},{1... | collective-permute-start | bytes 3145736 | tf_op jit(solution)/shard_map/ppermute | solution.py:88
  21.0 19.1 %copy-start.1 = (f32[512,512]{1,0:T(8,128)}, f32[512,512]{1,0:T(8,128)S(1)}, u32[]{:S(2)}) copy-start(f32[512,512]{1,0:T(8,128)S(1)} %get-tuple-element.53.factor) | copy-start | bytes 3145732
  21.0 13.6 %collective-permute-start.4 = (f32[512,512]{1,0:T(8,128)S(1)}, f32[512,512]{1,0:T(8,128)S(1)}, u32[]{:S(2)}, u32[]{:S(2)}) collective-permute-start(f32[512,512]{1,0:T(8,128)S(1)} %get-tuple-element.50), channel_id=1, source_target_pairs={{0,16},{8,24},{4,12},{20,28},{9,25},{1,17},{29,21},{22,30}} | collective-permute-start | bytes 3145736 | tf_op jit(solution)/shard_map/ppermute | solution.py:156
  23.8 21.3 %collective-permute-start.2 = (f32[512,512]{1,0:T(8,128)S(1)}, f32[512,512]{1,0:T(8,128)S(1)}, u32[]{:S(2)}, u32[]{:S(2)}) collective-permute-start(f32[512,512]{1,0:T(8,128)S(1)} %add.91), channel_id=1, source_target_pairs={{16,0},{24,8},{12,4},{28,20},{25,9},{17,1},{21,29},{30,22}} | collective-permute-start | bytes 3145736 | tf_op jit(solution)/shard_map/ppermute | solution.py:156
  34.8 11.8 %collective-permute-start.5 = (f32[512,512]{1,0:T(8,128)S(1)}, f32[512,512]{1,0:T(8,128)S(1)}, u32[]{:S(2)}, u32[]{:S(2)}) collective-permute-start(f32[512,512]{1,0:T(8,128)S(1)} %add.93.rest_0_), channel_id=1, source_target_pairs={{4,0},{0,4},{12,8},{8,12},{20,16},{16,20},{28,24},{24,28},{5,1},{1... | collective-permute-start | bytes 3145736 | tf_op jit(solution)/shard_map/ppermute | solution.py:88
  40.0 7.6 %copy-start.6 = (bf16[512,1024]{1,0:T(8,128)(2,1)S(1)}, bf16[512,1024]{1,0:T(8,128)(2,1)}, u32[]{:S(2)}) copy-start(bf16[512,1024]{1,0:T(8,128)(2,1)} %copy-done.5) | copy-start | bytes 3145732
  40.1 17.2 %collective-permute-start.8 = (f32[512,512]{1,0:T(8,128)S(1)}, f32[512,512]{1,0:T(8,128)S(1)}, u32[]{:S(2)}, u32[]{:S(2)}) collective-permute-start(f32[512,512]{1,0:T(8,128)S(1)} %get-tuple-element.53.factor), channel_id=1, source_target_pairs={{0,8},{4,20},{9,1},{13,29},{18,26}} | collective-permute-start | bytes 3145736 | tf_op jit(solution)/shard_map/ppermute | solution.py:156
  45.3 16.7 %collective-permute-start.6 = (f32[512,512]{1,0:T(8,128)S(1)}, f32[512,512]{1,0:T(8,128)S(1)}, u32[]{:S(2)}, u32[]{:S(2)}) collective-permute-start(f32[512,512]{1,0:T(8,128)S(1)} %add.92.mirror), channel_id=1, source_target_pairs={{8,0},{20,4},{1,9},{29,13},{26,18}} | collective-permute-start | bytes 3145736 | tf_op jit(solution)/shard_map/ppermute | solution.py:156
  46.6 18.6 %collective-permute-start = (f32[512,512]{1,0:T(8,128)S(1)}, f32[512,512]{1,0:T(8,128)S(1)}, u32[]{:S(2)}, u32[]{:S(2)}) collective-permute-start(f32[512,512]{1,0:T(8,128)S(1)} %get-tuple-element.45), channel_id=1, source_target_pairs={{4,0},{0,4},{12,8},{8,12},{20,16},{16,20},{28,24},{24,28},{5,1},{1... | collective-permute-start | bytes 3145736 | tf_op jit(solution)/shard_map/ppermute | solution.py:88
  47.7 9.6 %copy-start.16 = (f32[512,1024]{1,0:T(8,128)S(1)}, f32[512,1024]{1,0:T(8,128)}, u32[]{:S(2)}) copy-start(f32[512,1024]{1,0:T(8,128)} %param.7) | copy-start | bytes 6291460
  62.2 14.7 %copy-start.22 = (f32[256,512]{1,0:T(8,128)}, f32[256,512]{1,0:T(8,128)S(1)}, u32[]{:S(2)}) copy-start(f32[256,512]{1,0:T(8,128)S(1)} %get-tuple-element.57) | copy-start | bytes 1572868
  62.2 13.6 %collective-permute-start.9 = (f32[512,512]{1,0:T(8,128)S(1)}, f32[512,512]{1,0:T(8,128)S(1)}, u32[]{:S(2)}, u32[]{:S(2)}) collective-permute-start(f32[512,512]{1,0:T(8,128)S(1)} %broadcast_select_fusion), channel_id=1, source_target_pairs={{0,16},{8,24},{4,12},{20,28},{9,25},{1,17},{29,21},{22,30}} | collective-permute-start | bytes 3145736 | tf_op jit(solution)/shard_map/ppermute | solution.py:156
  63.6 11.8 %collective-permute-start.7 = (f32[256,512]{1,0:T(8,128)S(1)}, f32[256,512]{1,0:T(8,128)S(1)}, u32[]{:S(2)}, u32[]{:S(2)}) collective-permute-start(f32[256,512]{1,0:T(8,128)S(1)} %get-tuple-element.87), channel_id=1, source_target_pairs={{0,1},{3,2},{4,5},{7,6},{8,9},{11,10},{12,13},{15,14},{16,17},{19,... | collective-permute-start | bytes 1572872 | tf_op jit(solution)/shard_map/ppermute | solution.py:372
  65.4 17.6 %collective-permute-start.12 = (f32[512,512]{1,0:T(8,128)S(1)}, f32[512,512]{1,0:T(8,128)S(1)}, u32[]{:S(2)}, u32[]{:S(2)}) collective-permute-start(f32[512,512]{1,0:T(8,128)S(1)} %add.90), channel_id=1, source_target_pairs={{16,0},{24,8},{12,4},{28,20},{25,9},{17,1},{21,29},{30,22}} | collective-permute-start | bytes 3145736 | tf_op jit(solution)/shard_map/ppermute | solution.py:156
  76.0 19.2 %copy-start.17 = (f32[512,512]{1,0:T(8,128)}, f32[512,512]{1,0:T(8,128)S(1)}, u32[]{:S(2)}) copy-start(f32[512,512]{1,0:T(8,128)S(1)} %add.98.rest_0_) | copy-start | bytes 3145732
  76.0 20.6 %collective-permute-start.13 = (f32[512,512]{1,0:T(8,128)S(1)}, f32[512,512]{1,0:T(8,128)S(1)}, u32[]{:S(2)}, u32[]{:S(2)}) collective-permute-start(f32[512,512]{1,0:T(8,128)S(1)} %add.98.rest_0_), channel_id=1, source_target_pairs={{4,0},{0,4},{12,8},{8,12},{20,16},{16,20},{28,24},{24,28},{5,1},{1... | collective-permute-start | bytes 3145736 | tf_op jit(solution)/shard_map/ppermute | solution.py:88
  76.2 6.8 %copy-start.20 = (f32[256,512]{1,0:T(8,128)}, f32[256,512]{1,0:T(8,128)S(1)}, u32[]{:S(2)}) copy-start(f32[256,512]{1,0:T(8,128)S(1)} %add.96) | copy-start | bytes 1572868
  76.2 6.8 %collective-permute-start.10 = (f32[256,512]{1,0:T(8,128)S(1)}, f32[256,512]{1,0:T(8,128)S(1)}, u32[]{:S(2)}, u32[]{:S(2)}) collective-permute-start(f32[256,512]{1,0:T(8,128)S(1)} %add.96), channel_id=1, source_target_pairs={{1,2},{2,1},{5,6},{6,5},{9,10},{10,9},{13,14},{14,13},{17,18},{18,... | collective-permute-start | bytes 1572872 | tf_op jit(solution)/shard_map/ppermute | solution.py:408
  76.9 17.1 %collective-permute-start.11 = (f32[256,512]{1,0:T(8,128)S(1)}, f32[256,512]{1,0:T(8,128)}, u32[]{:S(2)}, u32[]{:S(2)}) collective-permute-start(f32[256,512]{1,0:T(8,128)S(1)} %get-tuple-element.57), channel_id=1, source_target_pairs={{0,1},{3,2},{4,5},{7,6},{8,9},{11,10},{12,13},{15,14},{16,17},{19,... | collective-permute-start | bytes 1572872 | tf_op jit(solution)/shard_map/ppermute | solution.py:372
  95.2 17.0 %collective-permute-start.14 = (f32[512,512]{1,0:T(8,128)}, f32[512,512]{1,0:T(8,128)}, u32[]{:S(2)}, u32[]{:S(2)}) collective-permute-start(f32[512,512]{1,0:T(8,128)} %add.97.mirror), channel_id=1, source_target_pairs={{8,0},{20,4},{1,9},{29,13},{26,18}} | collective-permute-start | bytes 3145736 | tf_op jit(solution)/shard_map/ppermute | solution.py:156
  103.0 16.3 %collective-permute-start.24 = (f32[512,512]{1,0:T(8,128)S(1)}, f32[512,512]{1,0:T(8,128)}, u32[]{:S(2)}, u32[]{:S(2)}) collective-permute-start(f32[512,512]{1,0:T(8,128)S(1)} %get-tuple-element.76), channel_id=1, source_target_pairs={{4,0},{0,4},{12,8},{8,12},{20,16},{16,20},{28,24},{24,28},{5,1},{1... | collective-permute-start | bytes 3145736 | tf_op jit(solution)/shard_map/ppermute | solution.py:88
  105.2 20.4 %collective-permute-start.18 = (f32[256,512]{1,0:T(8,128)}, f32[256,512]{1,0:T(8,128)}, u32[]{:S(2)}, u32[]{:S(2)}) collective-permute-start(f32[256,512]{1,0:T(8,128)} %add.103), channel_id=1, source_target_pairs={{1,2},{2,1},{5,6},{6,5},{9,10},{10,9},{13,14},{14,13},{17,18},{18,... | collective-permute-start | bytes 1572872 | tf_op jit(solution)/shard_map/ppermute | solution.py:384
  114.6 16.9 %collective-permute-start.15 = (f32[256,512]{1,0:T(8,128)}, f32[256,512]{1,0:T(8,128)}, u32[]{:S(2)}, u32[]{:S(2)}) collective-permute-start(f32[256,512]{1,0:T(8,128)} %get-tuple-element.85), channel_id=1, source_target_pairs={{0,1},{3,2},{4,5},{7,6},{8,9},{11,10},{12,13},{15,14},{16,17},{19,... | collective-permute-start | bytes 1572872 | tf_op jit(solution)/shard_map/ppermute | solution.py:372
  120.8 6.0 %copy-start.23 = (f32[256,512]{1,0:T(8,128)S(1)}, f32[256,512]{1,0:T(8,128)}, u32[]{:S(2)}) copy-start(f32[256,512]{1,0:T(8,128)} %get-tuple-element.72) | copy-start | bytes 1572868
  121.7 11.1 %collective-permute-start.25 = (f32[256,512]{1,0:T(8,128)}, f32[256,512]{1,0:T(8,128)}, u32[]{:S(2)}, u32[]{:S(2)}) collective-permute-start(f32[256,512]{1,0:T(8,128)} %dynamic-slice_bitcast_fusion), channel_id=1, source_target_pairs={{0,8},{1,9},{2,10},{3,11},{4,20},{5,21},{6,22},{7,23},{8,0},{9,1},... | collective-permute-start | bytes 1572872 | tf_op jit(solution)/shard_map/ppermute | solution.py:440
  124.2 14.1 %collective-permute-start.16 = (f32[256,512]{1,0:T(8,128)S(1)}, f32[256,512]{1,0:T(8,128)S(1)}, u32[]{:S(2)}, u32[]{:S(2)}) collective-permute-start(f32[256,512]{1,0:T(8,128)S(1)} %add.101.rest_0_), channel_id=1, source_target_pairs={{1,0},{2,3},{5,4},{6,7},{9,8},{10,11},{13,12},{14,15},{17,16},{18,... | collective-permute-start | bytes 1572872 | tf_op jit(solution)/shard_map/ppermute | solution.py:384
  126.8 14.9 %collective-permute-start.21 = (f32[256,512]{1,0:T(8,128)S(1)}, f32[256,512]{1,0:T(8,128)S(1)}, u32[]{:S(2)}, u32[]{:S(2)}) collective-permute-start(f32[256,512]{1,0:T(8,128)S(1)} %copy-done.23), channel_id=1, source_target_pairs={{0,1},{3,2},{4,5},{7,6},{8,9},{11,10},{12,13},{15,14},{16,17},{19,... | collective-permute-start | bytes 1572872 | tf_op jit(solution)/shard_map/ppermute | solution.py:372
  131.5 16.3 %collective-permute-start.19 = (f32[256,512]{1,0:T(8,128)S(1)}, f32[256,512]{1,0:T(8,128)S(1)}, u32[]{:S(2)}, u32[]{:S(2)}) collective-permute-start(f32[256,512]{1,0:T(8,128)S(1)} %add.104.rest_2_), channel_id=1, source_target_pairs={{1,0},{2,3},{5,4},{6,7},{9,8},{10,11},{13,12},{14,15},{17,16},{18,... | collective-permute-start | bytes 1572872 | tf_op jit(solution)/shard_map/ppermute | solution.py:384
  134.0 14.5 %collective-permute-start.26 = (f32[128,512]{1,0:T(8,128)S(1)}, f32[128,512]{1,0:T(8,128)S(1)}, u32[]{:S(2)}, u32[]{:S(2)}) collective-permute-start(f32[128,512]{1,0:T(8,128)S(1)} %dynamic-slice_bitcast_fusion.1), channel_id=1, source_target_pairs={{0,16},{1,17},{2,18},{3,19},{4,12},{5,13},{6,14},{7,15},{8,24},{9,... | collective-permute-start | bytes 786440 | tf_op jit(solution)/shard_map/ppermute | solution.py:440
  138.3 10.2 %copy-start.7 = (f32[256,512]{1,0:T(8,128)}, f32[256,512]{1,0:T(8,128)S(1)}, u32[]{:S(2)}) copy-start(f32[256,512]{1,0:T(8,128)S(1)} %collective-permute-done.16.rest_1_) | copy-start | bytes 1572868
  138.3 12.6 %collective-permute-start.17 = (f32[256,512]{1,0:T(8,128)S(1)}, f32[256,512]{1,0:T(8,128)S(1)}, u32[]{:S(2)}, u32[]{:S(2)}) collective-permute-start(f32[256,512]{1,0:T(8,128)S(1)} %add.100), channel_id=1, source_target_pairs={{1,2},{2,1},{5,6},{6,5},{9,10},{10,9},{13,14},{14,13},{17,18},{18,... | collective-permute-start | bytes 1572872 | tf_op jit(solution)/shard_map/ppermute | solution.py:384
  148.6 19.0 %copy-start = (f32[2,512,512]{2,1,0:T(8,128)S(1)}, f32[2,512,512]{2,1,0:T(8,128)}, u32[]{:S(2)}) copy-start(f32[2,512,512]{2,1,0:T(8,128)} %unit_ref.5) | copy-start | bytes 6291460
  148.6 5.7 %collective-permute-start.27 = (f32[128,512]{1,0:T(8,128)S(1)}, f32[128,512]{1,0:T(8,128)S(1)}, u32[]{:S(2)}, u32[]{:S(2)}) collective-permute-start(f32[128,512]{1,0:T(8,128)S(1)} %bitcast_add_fusion.1), channel_id=1, source_target_pairs={{0,1},{3,2},{4,5},{7,6},{8,9},{11,10},{12,13},{15,14},{16,17},{19,... | collective-permute-start | bytes 786440 | tf_op jit(solution)/shard_map/ppermute | solution.py:372
  150.2 4.9 %collective-permute-start.22 = (f32[256,512]{1,0:T(8,128)S(1)}, f32[256,512]{1,0:T(8,128)S(1)}, u32[]{:S(2)}, u32[]{:S(2)}) collective-permute-start(f32[256,512]{1,0:T(8,128)S(1)} %add.106), channel_id=1, source_target_pairs={{1,2},{2,1},{5,6},{6,5},{9,10},{10,9},{13,14},{14,13},{17,18},{18,... | collective-permute-start | bytes 1572872 | tf_op jit(solution)/shard_map/ppermute | solution.py:384
  151.0 14.4 %collective-permute-start.20 = (f32[256,512]{1,0:T(8,128)S(1)}, f32[256,512]{1,0:T(8,128)S(1)}, u32[]{:S(2)}, u32[]{:S(2)}) collective-permute-start(f32[256,512]{1,0:T(8,128)S(1)} %add.102.rest_0_), channel_id=1, source_target_pairs={{1,0},{2,3},{5,4},{6,7},{9,8},{10,11},{13,12},{14,15},{17,16},{18,... | collective-permute-start | bytes 1572872 | tf_op jit(solution)/shard_map/ppermute | solution.py:384
  154.4 1.6 collective-permute-start.28
  156.0 22.6 %collective-permute-start.29 = (f32[128,512]{1,0:T(8,128)S(1)}, f32[128,512]{1,0:T(8,128)}, u32[]{:S(2)}, u32[]{:S(2)}) collective-permute-start(f32[128,512]{1,0:T(8,128)S(1)} %add.115), channel_id=1, source_target_pairs={{1,0},{2,3},{5,4},{6,7},{9,8},{10,11},{13,12},{14,15},{17,16},{18,... | collective-permute-start | bytes 786440 | tf_op jit(solution)/shard_map/ppermute | solution.py:384
  166.2 21.0 %collective-permute-start.23 = (f32[256,512]{1,0:T(8,128)}, f32[256,512]{1,0:T(8,128)}, u32[]{:S(2)}, u32[]{:S(2)}) collective-permute-start(f32[256,512]{1,0:T(8,128)} %add.107.rest_2_), channel_id=1, source_target_pairs={{1,0},{2,3},{5,4},{6,7},{9,8},{10,11},{13,12},{14,15},{17,16},{18,... | collective-permute-start | bytes 1572872 | tf_op jit(solution)/shard_map/ppermute | solution.py:384
  169.6 17.6 %copy-start.3 = (f32[256,512]{1,0:T(8,128)S(1)}, f32[256,512]{1,0:T(8,128)}, u32[]{:S(2)}) copy-start(f32[256,512]{1,0:T(8,128)} %copy-done.2) | copy-start | bytes 1572868
  169.6 17.6 %copy-start.12 = (f32[256,512]{1,0:T(8,128)S(1)}, f32[256,512]{1,0:T(8,128)}, u32[]{:S(2)}) copy-start(f32[256,512]{1,0:T(8,128)} %copy-done.11) | copy-start | bytes 1572868
  179.6 11.0 %collective-permute-start.32 = (f32[128,512]{1,0:T(8,128)S(1)}, f32[128,512]{1,0:T(8,128)S(1)}, u32[]{:S(2)}, u32[]{:S(2)}) collective-permute-start(f32[128,512]{1,0:T(8,128)S(1)} %broadcast_select_fusion.2), channel_id=1, source_target_pairs={{0,24},{1,25},{2,26},{3,27},{8,16},{9,17},{10,18},{11,19},{16,8},{... | collective-permute-start | bytes 786440 | tf_op jit(solution)/shard_map/ppermute | solution.py:492
  182.3 10.5 %collective-permute-start.31 = (f32[128,512]{1,0:T(8,128)S(1)}, f32[128,512]{1,0:T(8,128)S(1)}, u32[]{:S(2)}, u32[]{:S(2)}) collective-permute-start(f32[128,512]{1,0:T(8,128)S(1)} %broadcast_select_fusion.2), channel_id=1, source_target_pairs={{0,8},{1,9},{2,10},{3,11},{8,0},{9,1},{10,2},{11,3},{16,24},{17,25... | collective-permute-start | bytes 786440 | tf_op jit(solution)/shard_map/ppermute | solution.py:492
  183.0 10.4 %collective-permute-start.30 = (f32[128,512]{1,0:T(8,128)S(1)}, f32[128,512]{1,0:T(8,128)S(1)}, u32[]{:S(2)}, u32[]{:S(2)}) collective-permute-start(f32[128,512]{1,0:T(8,128)S(1)} %broadcast_select_fusion.2), channel_id=1, source_target_pairs={{0,16},{1,17},{2,18},{3,19},{8,24},{9,25},{10,26},{11,27},{16,0},{... | collective-permute-start | bytes 786440 | tf_op jit(solution)/shard_map/ppermute | solution.py:492
  190.5 5.7 %copy-start.15 = (f32[2,512]{1,0:T(2,128)S(1)}, f32[2,512]{1,0:T(2,128)}, u32[]{:S(2)}) copy-start(f32[2,512]{1,0:T(2,128)} %pivot.1) | copy-start | bytes 12292
  193.5 2.7 %collective-permute-start.33 = (f32[512,512]{1,0:T(8,128)S(1)}, f32[512,512]{1,0:T(8,128)S(1)}, u32[]{:S(2)}, u32[]{:S(2)}) collective-permute-start(f32[512,512]{1,0:T(8,128)S(1)} %pad_maximum_fusion.rest_0_), channel_id=1, source_target_pairs={{4,0},{0,4},{12,8},{8,12},{20,16},{16,20},{28,24},{24,28},{5,1},{1... | collective-permute-start | bytes 3145736 | tf_op jit(solution)/shard_map/ppermute | solution.py:88
  (14 other events, 25.7 us)

commit v10 on v9

--- a/solution.py
+++ b/solution.py
@@ -403,13 +403,12 @@
             )
         if chunks and 0 not in entered:
             entered[0] = enter(chunks[0])
-            entered[0], got_out = lax.optimization_barrier((entered[0], got_out))
+            entered[0], got_out, got_back = lax.optimization_barrier(
+                (entered[0], got_out, got_back)
+            )
             if len(hops) > 1 and len(chunks) > 1:
                 second = lax.ppermute(plan.line_step(0, chunks[0], entered[0]), "col", hops[1])
                 entered[1] = enter(chunks[1], (entered[0],))
-                second, entered[1], got_back = lax.optimization_barrier(
-                    (second, entered[1], got_back)
-                )
         after = ()
         if phase % steps == 0 and phase < count:
             high, low, *parts = gather(out) if out == 0 else tiles[out]
@@ -424,7 +423,10 @@
             if turn < steps - 1:
                 mirror[back] = mirror[back] + got_back
             else:
-                sums, cross = forward(back, *tiles[back], mirror[back], held[back], cross)
+                x = mirror[back]
+                if second is not None and len(chunks) == plan.splits[0]:
+                    x, second, entered[1] = lax.optimization_barrier((x, second, entered[1]))
+                sums, cross = forward(back, *tiles[back], x, held[back], cross)
                 share = sums[0].shape[0]
                 after = tuple(
                     part + got_back[i * share:(i + 1) * share] for i, part in enumerate(sums)

time: 203 us -> 197 us (0.970)
  waiting for transfers between devices: 84.1 us -> 78.5 us
    ppermute x8, waiting for transfers between devices: 29.9 us -> 25 us  [issue(): out.append(lax.ppermute(x, axis, pairs))]
    ppermute x5, waiting for transfers between devices: 22.9 us -> 19.4 us  [enter(): return lax.ppermute(x, 'col', hops[0])]
    unnamed x56 -> x58, local copies, waits for them, and re-layouts: 9.25 us -> 7.69 us
  transfers between devices with their start and end apart: 34 -> 34, of which waited for: 18 -> 18; matrix products, arithmetic and copies ran while one was open for 9% -> 9% of each run, Pallas kernels for 13% -> 14%
where the time goes in v10:
time: 197 us; the launch traced here: 195 us
  waiting for transfers between devices  78.5 us (40%)
  starting transfers between devices  55.6 us (28%)
  Pallas kernels  32.2 us (16%)
  other arithmetic  17.9 us (9%)
  local copies, waits for them, and re-layouts  9.87 us (5%)
    ppermute x9, waiting for transfers between devices, run(): got = lax.ppermute(y, 'col', hops[hop])  27.6 us
    ppermute x8, waiting for transfers between devices, issue(): out.append(lax.ppermute(x, axis, pairs))  25 us
    ppermute x5, waiting for transfers between devices, enter(): return lax.ppermute(x, 'col', hops[0])  19.4 us
    ppermute x8, starting transfers between devices, issue(): out.append(lax.ppermute(x, axis, pairs))  18.9 us
    ppermute x5, starting transfers between devices, enter(): return lax.ppermute(x, 'col', hops[0])  17.9 us
    pallas_call x2, Pallas kernels, forward(): pl.pallas_call(functools.partial(forward_kernel, plan, member), in_specs=...  10.1 us
    ppermute x9, starting transfers between devices, run(): got = lax.ppermute(y, 'col', hops[hop])  9.97 us
    pallas_call x2, Pallas kernels, gather(): pl.pallas_call(functools.partial(gather_kernel, plan, member), in_specs=s...  9.28 us
  transfers between devices with their start and end apart: 34, of which 18 were waited for; matrix products, arithmetic and copies ran while one was open for 9% of the time, Pallas kernels for 14%

profile of v10, /device:TPU:0, one launch (start us, length us, event | category | flops | bytes accessed | tf_op | source)
XLA Modules:
  0.0 195.3 jit_solution(6113620295200411209)
XLA Ops:
  0.6 1.3 slice.19.factor
  2.0 5.8 %collective-permute-start.3 = (f32[512,512]{1,0:T(8,128)S(1)}, f32[512,512]{1,0:T(8,128)}, u32[]{:S(2)}, u32[]{:S(2)}) collective-permute-start(f32[512,512]{1,0:T(8,128)S(1)} %slice.19.factor), channel_id=1, source_target_pairs={{0,8},{4,20},{9,1},{13,29},{18,26}} | collective-permute-start | bytes 3145736 | tf_op jit(solution)/shard_map/ppermute | solution.py:156
  7.8 5.1 %gather_mirror.3 = (bf16[512,1024]{1,0:T(8,128)(2,1)S(1)}, bf16[512,1024]{1,0:T(8,128)(2,1)S(1)}, f32[512,512]{1,0:T(8,128)S(1)}, f32[512,512]{1,0:T(8,128)}) custom-call(s32[2,16]{1,0:T(2,128)S(1)} %copy-done.13, s32[2,16]{1,0:T(2,128)S(1)} %copy-done.14, f32[2048,4096]{1,0:T(8,128)} %front.3, f32[512,512]{1,0:T(8,128)S(1)} %slice.19.factor), custom_call_target="tpu_custom_call" | custom-call | flops 1677721600 | bytes 8388608 | tf_op jit(solution)/shard_map/gather_mirror/pallas_call | solution.py:333
  14.0 5.2 %collective-permute-done.3 = f32[512,512]{1,0:T(8,128)} collective-permute-done((f32[512,512]{1,0:T(8,128)S(1)}, f32[512,512]{1,0:T(8,128)}, u32[]{:S(2)}, u32[]{:S(2)}) %collective-permute-start.3) | collective-permute-done | bytes 1048608 | tf_op jit(solution)/shard_map/ppermute | solution.py:156
  19.1 1.9 broadcast_select_fusion.1
  21.0 1.4 collective-permute-start.4
  22.4 1.4 add.91
  23.8 1.3 collective-permute-start.2
  25.1 4.2 %gather_mirror.2 = (bf16[512,1024]{1,0:T(8,128)(2,1)S(1)}, bf16[512,1024]{1,0:T(8,128)(2,1)S(1)}, f32[512,512]{1,0:T(8,128)S(1)}, f32[512,512]{1,0:T(8,128)S(1)}) custom-call(s32[2,16]{1,0:T(2,128)S(1)} %copy-done.13, s32[2,16]{1,0:T(2,128)S(1)} %copy-done.14, f32[2048,4096]{1,0:T(8,128)} %front.3, f32[512,512]{1,0:T(8,128)S(1)} %get-tuple-element.54.factor), custom_call_target="tpu_custom_call" | custom-call | flops 1677721600 | bytes 8388608 | tf_op jit(solution)/shard_map/gather_mirror/pallas_call | solution.py:333
  29.3 5.3 %collective-permute-done.4 = f32[512,512]{1,0:T(8,128)S(1)} collective-permute-done((f32[512,512]{1,0:T(8,128)S(1)}, f32[512,512]{1,0:T(8,128)S(1)}, u32[]{:S(2)}, u32[]{:S(2)}) %collective-permute-start.4) | collective-permute-done | bytes 1048608 | tf_op jit(solution)/shard_map/ppermute | solution.py:156
  34.9 4.9 %collective-permute-start.8 = (f32[512,512]{1,0:T(8,128)S(1)}, f32[512,512]{1,0:T(8,128)S(1)}, u32[]{:S(2)}, u32[]{:S(2)}) collective-permute-start(f32[512,512]{1,0:T(8,128)S(1)} %get-tuple-element.54.factor), channel_id=1, source_target_pairs={{0,8},{4,20},{9,1},{13,29},{18,26}} | collective-permute-start | bytes 3145736 | tf_op jit(solution)/shard_map/ppermute | solution.py:156
  40.7 1.4 collective-permute-start.6
  43.4 4.8 %forward.2 = (f32[256,512]{1,0:T(8,128)S(1)}, f32[256,512]{1,0:T(8,128)S(1)}, f32[256,512]{1,0:T(8,128)S(1)}, f32[256,512]{1,0:T(8,128)S(1)}) custom-call(bf16[512,1024]{1,0:T(8,128)(2,1)S(1)} %get-tuple-element.47.high, bf16[512,1024]{1,0:T(8,128)(2,1)S(1)} %copy-done.6, f32[512,512]{1,0:T(8,128)S(1)} %slice.19.factor, f32[512,512]{1,0:T(8,128)} %copy-done.19, ...), custom_call_target="tpu_custom_call" | custom-call | flops 1677721600 | bytes 8388608 | tf_op jit(solution)/shard_map/forward/pallas_call | solution.py:351
  48.2 3.8 %collective-permute-done.8 = f32[512,512]{1,0:T(8,128)S(1)} collective-permute-done((f32[512,512]{1,0:T(8,128)S(1)}, f32[512,512]{1,0:T(8,128)S(1)}, u32[]{:S(2)}, u32[]{:S(2)}) %collective-permute-start.8) | collective-permute-done | bytes 1048608 | tf_op jit(solution)/shard_map/ppermute | solution.py:156
  52.2 5.5 %collective-permute-done.6 = f32[512,512]{1,0:T(8,128)S(1)} collective-permute-done((f32[512,512]{1,0:T(8,128)S(1)}, f32[512,512]{1,0:T(8,128)S(1)}, u32[]{:S(2)}, u32[]{:S(2)}) %collective-permute-start.6) | collective-permute-done | bytes 1048608 | tf_op jit(solution)/shard_map/ppermute | solution.py:156
  58.0 1.4 collective-permute-start.9
  59.4 1.3 collective-permute-start.10
  60.7 1.6 collective-permute-start.7
  62.2 9.3 %collective-permute-done.7 = f32[256,512]{1,0:T(8,128)S(1)} collective-permute-done((f32[256,512]{1,0:T(8,128)S(1)}, f32[256,512]{1,0:T(8,128)S(1)}, u32[]{:S(2)}, u32[]{:S(2)}) %collective-permute-start.7) | collective-permute-done | bytes 524320 | tf_op jit(solution)/shard_map/ppermute | solution.py:372
  71.6 4.5 %collective-permute-done.10 = f32[512,512]{1,0:T(8,128)S(1)} collective-permute-done((f32[512,512]{1,0:T(8,128)S(1)}, f32[512,512]{1,0:T(8,128)S(1)}, u32[]{:S(2)}, u32[]{:S(2)}) %collective-permute-start.10) | collective-permute-done | bytes 1048608 | tf_op jit(solution)/shard_map/ppermute | solution.py:156
  77.2 2.8 %collective-permute-start.12 = (f32[256,512]{1,0:T(8,128)S(1)}, f32[256,512]{1,0:T(8,128)S(1)}, u32[]{:S(2)}, u32[]{:S(2)}) collective-permute-start(f32[256,512]{1,0:T(8,128)S(1)} %get-tuple-element.60), channel_id=1, source_target_pairs={{0,1},{3,2},{4,5},{7,6},{8,9},{11,10},{12,13},{15,14},{16,17},{19,... | collective-permute-start | bytes 1572872 | tf_op jit(solution)/shard_map/ppermute | solution.py:372
  81.2 1.5 collective-permute-start.14
  82.7 9.1 %collective-permute-done.12 = f32[256,512]{1,0:T(8,128)S(1)} collective-permute-done((f32[256,512]{1,0:T(8,128)S(1)}, f32[256,512]{1,0:T(8,128)S(1)}, u32[]{:S(2)}, u32[]{:S(2)}) %collective-permute-start.12) | collective-permute-done | bytes 524320 | tf_op jit(solution)/shard_map/ppermute | solution.py:372
  92.9 5.3 %forward.3 = (f32[256,512]{1,0:T(8,128)S(1)}, f32[256,512]{1,0:T(8,128)S(1)}, f32[512,512]{1,0:T(8,128)S(1)}, f32[512,512]{1,0:T(8,128)S(1)}) custom-call(bf16[512,1024]{1,0:T(8,128)(2,1)S(1)} %get-tuple-element.43.high, bf16[512,1024]{1,0:T(8,128)(2,1)} %copy-done.4, f32[512,512]{1,0:T(8,128)} %copy-done.1, f32[512,512]{1,0:T(8,128)} %add.96.mirror, ...), custom_call_target="tpu_custom_call" | custom-call | flops 1677721600 | bytes 8388608 | tf_op jit(solution)/shard_map/forward/pallas_call | solution.py:351
  98.4 2.1 %add.103 = f32[256,512]{1,0:T(8,128)} add(f32[256,512]{1,0:T(8,128)} %copy-done.22, f32[256,512]{1,0:T(8,128)} %copy-done.28) | non-fusion elementwise | flops 131072 | bytes 1572864 | tf_op jit(solution)/shard_map/add | solution.py:101
  100.5 1.5 collective-permute-start.18
  101.9 2.4 %slice_add_fusion = (f32[256,512]{1,0:T(8,128)}, f32[256,512]{1,0:T(8,128)}) fusion(f32[256,512]{1,0:T(8,128)S(1)} %get-tuple-element.73, f32[512,512]{1,0:T(8,128)} %collective-permute-done.14, f32[256,512]{1,0:T(8,128)S(1)} %get-tuple-element.65), kind=kLoop, calls=%fused_computation.1 | loop fusion | flops 262144 | bytes 3145728 | tf_op jit(solution)/shard_map/add | solution.py:432
  104.3 7.4 %collective-permute-start.15 = (f32[256,512]{1,0:T(8,128)}, f32[256,512]{1,0:T(8,128)}, u32[]{:S(2)}, u32[]{:S(2)}) collective-permute-start(f32[256,512]{1,0:T(8,128)} %get-tuple-element.87), channel_id=1, source_target_pairs={{0,1},{3,2},{4,5},{7,6},{8,9},{11,10},{12,13},{15,14},{16,17},{19,... | collective-permute-start | bytes 1572872 | tf_op jit(solution)/shard_map/ppermute | solution.py:372
  111.7 1.6 add.108
  114.1 2.5 %collective-permute-start.25 = (f32[256,512]{1,0:T(8,128)}, f32[256,512]{1,0:T(8,128)}, u32[]{:S(2)}, u32[]{:S(2)}) collective-permute-start(f32[256,512]{1,0:T(8,128)} %dynamic-slice_bitcast_fusion), channel_id=1, source_target_pairs={{0,8},{1,9},{2,10},{3,11},{4,20},{5,21},{6,22},{7,23},{8,0},{9,1},... | collective-permute-start | bytes 1572872 | tf_op jit(solution)/shard_map/ppermute | solution.py:442
  116.7 1.3 collective-permute-start.16
  119.3 4.6 %collective-permute-start.21 = (f32[256,512]{1,0:T(8,128)S(1)}, f32[256,512]{1,0:T(8,128)S(1)}, u32[]{:S(2)}, u32[]{:S(2)}) collective-permute-start(f32[256,512]{1,0:T(8,128)S(1)} %copy-done.23), channel_id=1, source_target_pairs={{0,1},{3,2},{4,5},{7,6},{8,9},{11,10},{12,13},{15,14},{16,17},{19,... | collective-permute-start | bytes 1572872 | tf_op jit(solution)/shard_map/ppermute | solution.py:372
  123.9 1.3 collective-permute-start.19
  126.5 1.3 add.100
  127.8 5.6 %collective-permute-done.16.rest_1_ = f32[256,512]{1,0:T(8,128)S(1)} collective-permute-done((f32[256,512]{1,0:T(8,128)S(1)}, f32[256,512]{1,0:T(8,128)S(1)}, u32[]{:S(2)}, u32[]{:S(2)}) %collective-permute-start.16) | collective-permute-done | bytes 524320 | tf_op jit(solution)/shard_map/ppermute | solution.py:384
  134.2 7.3 %collective-permute-done.19.rest_3_ = f32[256,512]{1,0:T(8,128)S(1)} collective-permute-done((f32[256,512]{1,0:T(8,128)S(1)}, f32[256,512]{1,0:T(8,128)S(1)}, u32[]{:S(2)}, u32[]{:S(2)}) %collective-permute-start.19) | collective-permute-done | bytes 524320 | tf_op jit(solution)/shard_map/ppermute | solution.py:384
  142.4 1.6 collective-permute-start.27
  144.8 1.3 collective-permute-start.20
  149.5 1.3 collective-permute-start.29
  150.8 6.5 %collective-permute-done.20.rest_1_ = f32[256,512]{1,0:T(8,128)S(1)} collective-permute-done((f32[256,512]{1,0:T(8,128)S(1)}, f32[256,512]{1,0:T(8,128)S(1)}, u32[]{:S(2)}, u32[]{:S(2)}) %collective-permute-start.20) | collective-permute-done | bytes 524320 | tf_op jit(solution)/shard_map/ppermute | solution.py:384
  161.6 4.3 %place.2.rest_4_ = f32[2048,1024]{1,0:T(8,128)} custom-call(s32[2,16]{1,0:T(2,128)S(1)} %copy-done.13, f32[2,512,512]{2,1,0:T(8,128)S(1)} %copy-done, f32[256,512]{1,0:T(8,128)S(1)} %add.101.rest_0_, f32[256,512]{1,0:T(8,128)S(1)} %copy-done.8, f32[256,512]{1,0:T(8,128)S(1)} %add.104.rest_2_, f32[256,512]{1,0:T(8,128)S(1)} %copy-done.10), custom_call_target="tpu_custom_call" | custom-call | flops 1677721600 | bytes 8388608 | tf_op jit(solution)/shard_map/place/pallas_call | solution.py:450
  165.9 5.9 %collective-permute-done.29 = f32[128,512]{1,0:T(8,128)} collective-permute-done((f32[128,512]{1,0:T(8,128)S(1)}, f32[128,512]{1,0:T(8,128)}, u32[]{:S(2)}, u32[]{:S(2)}) %collective-permute-start.29) | collective-permute-done | bytes 262176 | tf_op jit(solution)/shard_map/ppermute | solution.py:384
  172.8 4.5 %collective-permute-start.32 = (f32[128,512]{1,0:T(8,128)S(1)}, f32[128,512]{1,0:T(8,128)S(1)}, u32[]{:S(2)}, u32[]{:S(2)}) collective-permute-start(f32[128,512]{1,0:T(8,128)S(1)} %broadcast_select_fusion.2), channel_id=1, source_target_pairs={{0,24},{1,25},{2,26},{3,27},{8,16},{9,17},{10,18},{11,19},{16,8},{... | collective-permute-start | bytes 786440 | tf_op jit(solution)/shard_map/ppermute | solution.py:494
  178.0 2.2 %collective-permute-done.23.rest_3_ = f32[256,512]{1,0:T(8,128)} collective-permute-done((f32[256,512]{1,0:T(8,128)}, f32[256,512]{1,0:T(8,128)}, u32[]{:S(2)}, u32[]{:S(2)}) %collective-permute-start.23) | collective-permute-done | bytes 524320 | tf_op jit(solution)/shard_map/ppermute | solution.py:384
  180.1 3.3 %place.3 = f32[2048,1024]{1,0:T(8,128)} custom-call(s32[2,16]{1,0:T(2,128)S(1)} %copy-done.13, f32[2,512,512]{2,1,0:T(8,128)S(1)} %copy-done, f32[256,512]{1,0:T(8,128)S(1)} %copy-done.3, f32[256,512]{1,0:T(8,128)S(1)} %copy-done.12, f32[256,512]{1,0:T(8,128)} %add.107.rest_2_, ...), custom_call_target="tpu_custom_call", output_to_operand_aliasing={{}: (6, {})} | custom-call | flops 1677721600 | bytes 8388608 | tf_op jit(solution)/shard_map/place/pallas_call | solution.py:450
  184.6 2.2 %collective-permute-done.31 = f32[128,512]{1,0:T(8,128)S(1)} collective-permute-done((f32[128,512]{1,0:T(8,128)S(1)}, f32[128,512]{1,0:T(8,128)S(1)}, u32[]{:S(2)}, u32[]{:S(2)}) %collective-permute-start.31) | collective-permute-done | bytes 262176 | tf_op jit(solution)/shard_map/ppermute | solution.py:494
  187.6 2.6 %collective-permute-done.33.rest_1_ = f32[512,512]{1,0:T(8,128)S(1)} collective-permute-done((f32[512,512]{1,0:T(8,128)S(1)}, f32[512,512]{1,0:T(8,128)S(1)}, u32[]{:S(2)}, u32[]{:S(2)}) %collective-permute-start.33) | collective-permute-done | bytes 1048608 | tf_op jit(solution)/shard_map/ppermute | solution.py:88
  190.2 5.1 %diagonal.1 = f32[2,512,512]{2,1,0:T(8,128)} custom-call(f32[2,512]{1,0:T(2,128)S(1)} %copy-done.15, f32[2,512,512]{2,1,0:T(8,128)S(1)} %copy-done, f32[512,512]{1,0:T(8,128)S(1)} %pad_maximum_fusion.rest_0_, f32[512,512]{1,0:T(8,128)S(1)} %collective-permute-done.33.rest_1_), custom_call_target="tpu_custom_call" | custom-call | flops 1677721600 | bytes 8388608 | tf_op jit(solution)/shard_map/diagonal/pallas_call | solution.py:497
  (113 shorter events, 24.4 us)
Async XLA Ops:
  0.6 7.2 %copy-start.13 = (s32[2,16]{1,0:T(2,128)S(1)}, s32[2,16]{1,0:T(2,128)}, u32[]{:S(2)}) copy-start(s32[2,16]{1,0:T(2,128)} %tiles_ref.7) | copy-start | bytes 388
  0.6 7.2 %copy-start.14 = (s32[2,16]{1,0:T(2,128)S(1)}, s32[2,16]{1,0:T(2,128)}, u32[]{:S(2)}) copy-start(s32[2,16]{1,0:T(2,128)} %valid_ref.3) | copy-start | bytes 388
  2.0 17.2 %collective-permute-start.3 = (f32[512,512]{1,0:T(8,128)S(1)}, f32[512,512]{1,0:T(8,128)}, u32[]{:S(2)}, u32[]{:S(2)}) collective-permute-start(f32[512,512]{1,0:T(8,128)S(1)} %slice.19.factor), channel_id=1, source_target_pairs={{0,8},{4,20},{9,1},{13,29},{18,26}} | collective-permute-start | bytes 3145736 | tf_op jit(solution)/shard_map/ppermute | solution.py:156
  14.0 8.4 %collective-permute-start.1 = (f32[512,512]{1,0:T(8,128)}, f32[512,512]{1,0:T(8,128)}, u32[]{:S(2)}, u32[]{:S(2)}) collective-permute-start(f32[512,512]{1,0:T(8,128)} %get-tuple-element.50), channel_id=1, source_target_pairs={{4,0},{0,4},{12,8},{8,12},{20,16},{16,20},{28,24},{24,28},{5,1},{1... | collective-permute-start | bytes 3145736 | tf_op jit(solution)/shard_map/ppermute | solution.py:88
  21.0 13.9 %copy-start.1 = (f32[512,512]{1,0:T(8,128)}, f32[512,512]{1,0:T(8,128)S(1)}, u32[]{:S(2)}) copy-start(f32[512,512]{1,0:T(8,128)S(1)} %get-tuple-element.54.factor) | copy-start | bytes 3145732
  21.0 13.6 %collective-permute-start.4 = (f32[512,512]{1,0:T(8,128)S(1)}, f32[512,512]{1,0:T(8,128)S(1)}, u32[]{:S(2)}, u32[]{:S(2)}) collective-permute-start(f32[512,512]{1,0:T(8,128)S(1)} %get-tuple-element.51), channel_id=1, source_target_pairs={{0,16},{8,24},{4,12},{20,28},{9,25},{1,17},{29,21},{22,30}} | collective-permute-start | bytes 3145736 | tf_op jit(solution)/shard_map/ppermute | solution.py:156
  23.8 16.7 %collective-permute-start.2 = (f32[512,512]{1,0:T(8,128)S(1)}, f32[512,512]{1,0:T(8,128)S(1)}, u32[]{:S(2)}, u32[]{:S(2)}) collective-permute-start(f32[512,512]{1,0:T(8,128)S(1)} %add.91), channel_id=1, source_target_pairs={{16,0},{24,8},{12,4},{28,20},{25,9},{17,1},{21,29},{30,22}} | collective-permute-start | bytes 3145736 | tf_op jit(solution)/shard_map/ppermute | solution.py:156
  29.2 11.4 %copy-start.4 = (bf16[512,1024]{1,0:T(8,128)(2,1)}, bf16[512,1024]{1,0:T(8,128)(2,1)S(1)}, u32[]{:S(2)}) copy-start(bf16[512,1024]{1,0:T(8,128)(2,1)S(1)} %get-tuple-element.44.low) | copy-start | bytes 3145732
  29.2 12.9 %collective-permute-start = (f32[512,512]{1,0:T(8,128)S(1)}, f32[512,512]{1,0:T(8,128)S(1)}, u32[]{:S(2)}, u32[]{:S(2)}) collective-permute-start(f32[512,512]{1,0:T(8,128)S(1)} %get-tuple-element.46), channel_id=1, source_target_pairs={{4,0},{0,4},{12,8},{8,12},{20,16},{16,20},{28,24},{24,28},{5,1},{1... | collective-permute-start | bytes 3145736 | tf_op jit(solution)/shard_map/ppermute | solution.py:88
  34.8 7.5 %copy-start.18 = (f32[512,512]{1,0:T(8,128)}, f32[512,512]{1,0:T(8,128)S(1)}, u32[]{:S(2)}) copy-start(f32[512,512]{1,0:T(8,128)S(1)} %add.93.rest_0_) | copy-start | bytes 3145732
  34.8 7.5 %collective-permute-start.5 = (f32[512,512]{1,0:T(8,128)S(1)}, f32[512,512]{1,0:T(8,128)S(1)}, u32[]{:S(2)}, u32[]{:S(2)}) collective-permute-start(f32[512,512]{1,0:T(8,128)S(1)} %add.93.rest_0_), channel_id=1, source_target_pairs={{4,0},{0,4},{12,8},{8,12},{20,16},{16,20},{28,24},{24,28},{5,1},{1... | collective-permute-start | bytes 3145736 | tf_op jit(solution)/shard_map/ppermute | solution.py:88
  34.9 17.1 %collective-permute-start.8 = (f32[512,512]{1,0:T(8,128)S(1)}, f32[512,512]{1,0:T(8,128)S(1)}, u32[]{:S(2)}, u32[]{:S(2)}) collective-permute-start(f32[512,512]{1,0:T(8,128)S(1)} %get-tuple-element.54.factor), channel_id=1, source_target_pairs={{0,8},{4,20},{9,1},{13,29},{18,26}} | collective-permute-start | bytes 3145736 | tf_op jit(solution)/shard_map/ppermute | solution.py:156
  40.7 17.1 %collective-permute-start.6 = (f32[512,512]{1,0:T(8,128)S(1)}, f32[512,512]{1,0:T(8,128)S(1)}, u32[]{:S(2)}, u32[]{:S(2)}) collective-permute-start(f32[512,512]{1,0:T(8,128)S(1)} %add.92.mirror), channel_id=1, source_target_pairs={{8,0},{20,4},{1,9},{29,13},{26,18}} | collective-permute-start | bytes 3145736 | tf_op jit(solution)/shard_map/ppermute | solution.py:156
  43.4 8.7 %copy-start.16 = (f32[512,1024]{1,0:T(8,128)S(1)}, f32[512,1024]{1,0:T(8,128)}, u32[]{:S(2)}) copy-start(f32[512,1024]{1,0:T(8,128)} %param.7) | copy-start | bytes 6291460
  58.0 19.2 %copy-start.22 = (f32[256,512]{1,0:T(8,128)}, f32[256,512]{1,0:T(8,128)S(1)}, u32[]{:S(2)}) copy-start(f32[256,512]{1,0:T(8,128)S(1)} %get-tuple-element.60) | copy-start | bytes 1572868
  58.0 13.6 %collective-permute-start.9 = (f32[512,512]{1,0:T(8,128)S(1)}, f32[512,512]{1,0:T(8,128)S(1)}, u32[]{:S(2)}, u32[]{:S(2)}) collective-permute-start(f32[512,512]{1,0:T(8,128)S(1)} %broadcast_select_fusion), channel_id=1, source_target_pairs={{0,16},{8,24},{4,12},{20,28},{9,25},{1,17},{29,21},{22,30}} | collective-permute-start | bytes 3145736 | tf_op jit(solution)/shard_map/ppermute | solution.py:156
  59.4 16.7 %collective-permute-start.10 = (f32[512,512]{1,0:T(8,128)S(1)}, f32[512,512]{1,0:T(8,128)S(1)}, u32[]{:S(2)}, u32[]{:S(2)}) collective-permute-start(f32[512,512]{1,0:T(8,128)S(1)} %add.90), channel_id=1, source_target_pairs={{16,0},{24,8},{12,4},{28,20},{25,9},{17,1},{21,29},{30,22}} | collective-permute-start | bytes 3145736 | tf_op jit(solution)/shard_map/ppermute | solution.py:156
  60.7 10.9 %collective-permute-start.7 = (f32[256,512]{1,0:T(8,128)S(1)}, f32[256,512]{1,0:T(8,128)S(1)}, u32[]{:S(2)}, u32[]{:S(2)}) collective-permute-start(f32[256,512]{1,0:T(8,128)S(1)} %get-tuple-element.89), channel_id=1, source_target_pairs={{0,1},{3,2},{4,5},{7,6},{8,9},{11,10},{12,13},{15,14},{16,17},{19,... | collective-permute-start | bytes 1572872 | tf_op jit(solution)/shard_map/ppermute | solution.py:372
  76.3 15.5 %collective-permute-start.13 = (f32[512,512]{1,0:T(8,128)S(1)}, f32[512,512]{1,0:T(8,128)S(1)}, u32[]{:S(2)}, u32[]{:S(2)}) collective-permute-start(f32[512,512]{1,0:T(8,128)S(1)} %add.98.rest_0_), channel_id=1, source_target_pairs={{4,0},{0,4},{12,8},{8,12},{20,16},{16,20},{28,24},{24,28},{5,1},{1... | collective-permute-start | bytes 3145736 | tf_op jit(solution)/shard_map/ppermute | solution.py:88
  76.4 21.8 %copy-start.20 = (f32[256,512]{1,0:T(8,128)}, f32[256,512]{1,0:T(8,128)S(1)}, u32[]{:S(2)}) copy-start(f32[256,512]{1,0:T(8,128)S(1)} %add.97) | copy-start | bytes 1572868
  76.5 6.2 %collective-permute-start.11 = (f32[256,512]{1,0:T(8,128)S(1)}, f32[256,512]{1,0:T(8,128)S(1)}, u32[]{:S(2)}, u32[]{:S(2)}) collective-permute-start(f32[256,512]{1,0:T(8,128)S(1)} %add.97), channel_id=1, source_target_pairs={{1,2},{2,1},{5,6},{6,5},{9,10},{10,9},{13,14},{14,13},{17,18},{18,... | collective-permute-start | bytes 1572872 | tf_op jit(solution)/shard_map/ppermute | solution.py:410
  77.2 14.6 %collective-permute-start.12 = (f32[256,512]{1,0:T(8,128)S(1)}, f32[256,512]{1,0:T(8,128)S(1)}, u32[]{:S(2)}, u32[]{:S(2)}) collective-permute-start(f32[256,512]{1,0:T(8,128)S(1)} %get-tuple-element.60), channel_id=1, source_target_pairs={{0,1},{3,2},{4,5},{7,6},{8,9},{11,10},{12,13},{15,14},{16,17},{19,... | collective-permute-start | bytes 1572872 | tf_op jit(solution)/shard_map/ppermute | solution.py:372
  81.2 20.7 %collective-permute-start.14 = (f32[512,512]{1,0:T(8,128)}, f32[512,512]{1,0:T(8,128)}, u32[]{:S(2)}, u32[]{:S(2)}) collective-permute-start(f32[512,512]{1,0:T(8,128)} %add.96.mirror), channel_id=1, source_target_pairs={{8,0},{20,4},{1,9},{29,13},{26,18}} | collective-permute-start | bytes 3145736 | tf_op jit(solution)/shard_map/ppermute | solution.py:156
  82.7 15.6 %copy-start.26 = (f32[256,512]{1,0:T(8,128)}, f32[256,512]{1,0:T(8,128)S(1)}, u32[]{:S(2)}) copy-start(f32[256,512]{1,0:T(8,128)S(1)} %collective-permute-done.11) | copy-start | bytes 1572868
  98.3 13.4 %collective-permute-start.24 = (f32[512,512]{1,0:T(8,128)S(1)}, f32[512,512]{1,0:T(8,128)}, u32[]{:S(2)}, u32[]{:S(2)}) collective-permute-start(f32[512,512]{1,0:T(8,128)S(1)} %get-tuple-element.78), channel_id=1, source_target_pairs={{4,0},{0,4},{12,8},{8,12},{20,16},{16,20},{28,24},{24,28},{5,1},{1... | collective-permute-start | bytes 3145736 | tf_op jit(solution)/shard_map/ppermute | solution.py:88
  100.5 17.6 %collective-permute-start.18 = (f32[256,512]{1,0:T(8,128)}, f32[256,512]{1,0:T(8,128)}, u32[]{:S(2)}, u32[]{:S(2)}) collective-permute-start(f32[256,512]{1,0:T(8,128)} %add.103), channel_id=1, source_target_pairs={{1,2},{2,1},{5,6},{6,5},{9,10},{10,9},{13,14},{14,13},{17,18},{18,... | collective-permute-start | bytes 1572872 | tf_op jit(solution)/shard_map/ppermute | solution.py:384
  104.3 19.6 %collective-permute-start.15 = (f32[256,512]{1,0:T(8,128)}, f32[256,512]{1,0:T(8,128)}, u32[]{:S(2)}, u32[]{:S(2)}) collective-permute-start(f32[256,512]{1,0:T(8,128)} %get-tuple-element.87), channel_id=1, source_target_pairs={{0,1},{3,2},{4,5},{7,6},{8,9},{11,10},{12,13},{15,14},{16,17},{19,... | collective-permute-start | bytes 1572872 | tf_op jit(solution)/shard_map/ppermute | solution.py:372
  114.1 11.1 %collective-permute-start.25 = (f32[256,512]{1,0:T(8,128)}, f32[256,512]{1,0:T(8,128)}, u32[]{:S(2)}, u32[]{:S(2)}) collective-permute-start(f32[256,512]{1,0:T(8,128)} %dynamic-slice_bitcast_fusion), channel_id=1, source_target_pairs={{0,8},{1,9},{2,10},{3,11},{4,20},{5,21},{6,22},{7,23},{8,0},{9,1},... | collective-permute-start | bytes 1572872 | tf_op jit(solution)/shard_map/ppermute | solution.py:442
  116.7 16.8 %collective-permute-start.16 = (f32[256,512]{1,0:T(8,128)S(1)}, f32[256,512]{1,0:T(8,128)S(1)}, u32[]{:S(2)}, u32[]{:S(2)}) collective-permute-start(f32[256,512]{1,0:T(8,128)S(1)} %add.101.rest_0_), channel_id=1, source_target_pairs={{1,0},{2,3},{5,4},{6,7},{9,8},{10,11},{13,12},{14,15},{17,16},{18,... | collective-permute-start | bytes 1572872 | tf_op jit(solution)/shard_map/ppermute | solution.py:384
  119.3 14.8 %collective-permute-start.21 = (f32[256,512]{1,0:T(8,128)S(1)}, f32[256,512]{1,0:T(8,128)S(1)}, u32[]{:S(2)}, u32[]{:S(2)}) collective-permute-start(f32[256,512]{1,0:T(8,128)S(1)} %copy-done.23), channel_id=1, source_target_pairs={{0,1},{3,2},{4,5},{7,6},{8,9},{11,10},{12,13},{15,14},{16,17},{19,... | collective-permute-start | bytes 1572872 | tf_op jit(solution)/shard_map/ppermute | solution.py:372
  123.9 17.6 %collective-permute-start.19 = (f32[256,512]{1,0:T(8,128)S(1)}, f32[256,512]{1,0:T(8,128)S(1)}, u32[]{:S(2)}, u32[]{:S(2)}) collective-permute-start(f32[256,512]{1,0:T(8,128)S(1)} %add.104.rest_2_), channel_id=1, source_target_pairs={{1,0},{2,3},{5,4},{6,7},{9,8},{10,11},{13,12},{14,15},{17,16},{18,... | collective-permute-start | bytes 1572872 | tf_op jit(solution)/shard_map/ppermute | solution.py:384
  126.4 15.9 %collective-permute-start.26 = (f32[128,512]{1,0:T(8,128)S(1)}, f32[128,512]{1,0:T(8,128)S(1)}, u32[]{:S(2)}, u32[]{:S(2)}) collective-permute-start(f32[128,512]{1,0:T(8,128)S(1)} %dynamic-slice_bitcast_fusion.1), channel_id=1, source_target_pairs={{0,16},{1,17},{2,18},{3,19},{4,12},{5,13},{6,14},{7,15},{8,24},{9,... | collective-permute-start | bytes 786440 | tf_op jit(solution)/shard_map/ppermute | solution.py:442
  133.5 8.9 %copy-start.7 = (f32[256,512]{1,0:T(8,128)}, f32[256,512]{1,0:T(8,128)S(1)}, u32[]{:S(2)}) copy-start(f32[256,512]{1,0:T(8,128)S(1)} %collective-permute-done.16.rest_1_) | copy-start | bytes 1572868
  133.5 11.3 %collective-permute-start.17 = (f32[256,512]{1,0:T(8,128)S(1)}, f32[256,512]{1,0:T(8,128)S(1)}, u32[]{:S(2)}, u32[]{:S(2)}) collective-permute-start(f32[256,512]{1,0:T(8,128)S(1)} %add.100), channel_id=1, source_target_pairs={{1,2},{2,1},{5,6},{6,5},{9,10},{10,9},{13,14},{14,13},{17,18},{18,... | collective-permute-start | bytes 1572872 | tf_op jit(solution)/shard_map/ppermute | solution.py:384
  142.4 17.1 %copy-start = (f32[2,512,512]{2,1,0:T(8,128)S(1)}, f32[2,512,512]{2,1,0:T(8,128)}, u32[]{:S(2)}) copy-start(f32[2,512,512]{2,1,0:T(8,128)} %unit_ref.5) | copy-start | bytes 6291460
  142.4 5.5 %collective-permute-start.27 = (f32[128,512]{1,0:T(8,128)S(1)}, f32[128,512]{1,0:T(8,128)S(1)}, u32[]{:S(2)}, u32[]{:S(2)}) collective-permute-start(f32[128,512]{1,0:T(8,128)S(1)} %bitcast_add_fusion.1), channel_id=1, source_target_pairs={{0,1},{3,2},{4,5},{7,6},{8,9},{11,10},{12,13},{15,14},{16,17},{19,... | collective-permute-start | bytes 786440 | tf_op jit(solution)/shard_map/ppermute | solution.py:372
  144.0 4.6 %collective-permute-start.22 = (f32[256,512]{1,0:T(8,128)S(1)}, f32[256,512]{1,0:T(8,128)S(1)}, u32[]{:S(2)}, u32[]{:S(2)}) collective-permute-start(f32[256,512]{1,0:T(8,128)S(1)} %add.106), channel_id=1, source_target_pairs={{1,2},{2,1},{5,6},{6,5},{9,10},{10,9},{13,14},{14,13},{17,18},{18,... | collective-permute-start | bytes 1572872 | tf_op jit(solution)/shard_map/ppermute | solution.py:384
  144.8 12.6 %collective-permute-start.20 = (f32[256,512]{1,0:T(8,128)S(1)}, f32[256,512]{1,0:T(8,128)S(1)}, u32[]{:S(2)}, u32[]{:S(2)}) collective-permute-start(f32[256,512]{1,0:T(8,128)S(1)} %add.102.rest_0_), channel_id=1, source_target_pairs={{1,0},{2,3},{5,4},{6,7},{9,8},{10,11},{13,12},{14,15},{17,16},{18,... | collective-permute-start | bytes 1572872 | tf_op jit(solution)/shard_map/ppermute | solution.py:384
  147.9 1.6 collective-permute-start.28
  149.5 22.3 %collective-permute-start.29 = (f32[128,512]{1,0:T(8,128)S(1)}, f32[128,512]{1,0:T(8,128)}, u32[]{:S(2)}, u32[]{:S(2)}) collective-permute-start(f32[128,512]{1,0:T(8,128)S(1)} %add.115), channel_id=1, source_target_pairs={{1,0},{2,3},{5,4},{6,7},{9,8},{10,11},{13,12},{14,15},{17,16},{18,... | collective-permute-start | bytes 786440 | tf_op jit(solution)/shard_map/ppermute | solution.py:384
  158.2 22.0 %collective-permute-start.23 = (f32[256,512]{1,0:T(8,128)}, f32[256,512]{1,0:T(8,128)}, u32[]{:S(2)}, u32[]{:S(2)}) collective-permute-start(f32[256,512]{1,0:T(8,128)} %add.107.rest_2_), channel_id=1, source_target_pairs={{1,0},{2,3},{5,4},{6,7},{9,8},{10,11},{13,12},{14,15},{17,16},{18,... | collective-permute-start | bytes 1572872 | tf_op jit(solution)/shard_map/ppermute | solution.py:384
  161.6 18.6 %copy-start.3 = (f32[256,512]{1,0:T(8,128)S(1)}, f32[256,512]{1,0:T(8,128)}, u32[]{:S(2)}) copy-start(f32[256,512]{1,0:T(8,128)} %copy-done.2) | copy-start | bytes 1572868
  161.6 18.6 %copy-start.12 = (f32[256,512]{1,0:T(8,128)S(1)}, f32[256,512]{1,0:T(8,128)}, u32[]{:S(2)}) copy-start(f32[256,512]{1,0:T(8,128)} %copy-done.11) | copy-start | bytes 1572868
  172.8 11.7 %collective-permute-start.32 = (f32[128,512]{1,0:T(8,128)S(1)}, f32[128,512]{1,0:T(8,128)S(1)}, u32[]{:S(2)}, u32[]{:S(2)}) collective-permute-start(f32[128,512]{1,0:T(8,128)S(1)} %broadcast_select_fusion.2), channel_id=1, source_target_pairs={{0,24},{1,25},{2,26},{3,27},{8,16},{9,17},{10,18},{11,19},{16,8},{... | collective-permute-start | bytes 786440 | tf_op jit(solution)/shard_map/ppermute | solution.py:494
  177.3 9.4 %collective-permute-start.31 = (f32[128,512]{1,0:T(8,128)S(1)}, f32[128,512]{1,0:T(8,128)S(1)}, u32[]{:S(2)}, u32[]{:S(2)}) collective-permute-start(f32[128,512]{1,0:T(8,128)S(1)} %broadcast_select_fusion.2), channel_id=1, source_target_pairs={{0,8},{1,9},{2,10},{3,11},{8,0},{9,1},{10,2},{11,3},{16,24},{17,25... | collective-permute-start | bytes 786440 | tf_op jit(solution)/shard_map/ppermute | solution.py:494
  177.3 10.1 %collective-permute-start.30 = (f32[128,512]{1,0:T(8,128)S(1)}, f32[128,512]{1,0:T(8,128)S(1)}, u32[]{:S(2)}, u32[]{:S(2)}) collective-permute-start(f32[128,512]{1,0:T(8,128)S(1)} %broadcast_select_fusion.2), channel_id=1, source_target_pairs={{0,16},{1,17},{2,18},{3,19},{8,24},{9,25},{10,26},{11,27},{16,0},{... | collective-permute-start | bytes 786440 | tf_op jit(solution)/shard_map/ppermute | solution.py:494
  183.5 6.7 %copy-start.15 = (f32[2,512]{1,0:T(2,128)S(1)}, f32[2,512]{1,0:T(2,128)}, u32[]{:S(2)}) copy-start(f32[2,512]{1,0:T(2,128)} %pivot.1) | copy-start | bytes 12292
  187.5 2.7 %collective-permute-start.33 = (f32[512,512]{1,0:T(8,128)S(1)}, f32[512,512]{1,0:T(8,128)S(1)}, u32[]{:S(2)}, u32[]{:S(2)}) collective-permute-start(f32[512,512]{1,0:T(8,128)S(1)} %pad_maximum_fusion.rest_0_), channel_id=1, source_target_pairs={{4,0},{0,4},{12,8},{8,12},{20,16},{16,20},{28,24},{24,28},{5,1},{1... | collective-permute-start | bytes 3145736 | tf_op jit(solution)/shard_map/ppermute | solution.py:88
  (15 other events, 34.6 us)

commit v11 on v10

--- a/solution.py
+++ b/solution.py
@@ -471,23 +471,27 @@
         if i > 2:
             entered[i] = enter(chunks[i], (brought[i - 2][min(1, middle)],))
         if i == 1 and last > 1:
-            entered[2] = enter(chunks[2])
+            entered[2] = enter(chunks[2], (ends[0],))
         ties = [()] * middle
         if i < 2 and i < last and middle:
             if 1 not in entered:
                 entered[1] = enter(chunks[1], (entered[0],))
             ties[-1] = (entered[i + 1],)
         elif i > 1 and middle:
-            ties = [(brought[i - 2][hop + 1],) for hop in range(1, middle)]
+            ties = [
+                (brought[i - 2][hop + 1],) if i > 2 else () for hop in range(1, middle)
+            ]
             ties.append((brought[i - 1][-1],))
         chunks[i], ends[i], sent[i], brought[i] = run(
             chunks[i], entered[i], ties, second if i == 0 else None
         )
-    update, got, _, _ = run(update, enter(update), [(x,) for x in sent[last]])
-    for member in range(members):
+    column = place(0, column)
+    ties = [(x,) for x in sent[last]]
+    if middle:
+        ties[-1] += (column,)
+    update, got, _, _ = run(update, enter(update), ties)
+    for member in range(1, members):
         column = place(member, column)
-        if member == 0:
-            got, _ = lax.optimization_barrier((got, column))
 
     x = update
     x = jnp.where(plan.at_end(), got, x)

time: 197 us -> 199 us (1.010)
  waiting for transfers between devices: 78.5 us -> 93.1 us
  starting transfers between devices: 55.6 us -> 47.1 us
  local copies, waits for them, and re-layouts: 9.87 us -> 6.43 us
    ppermute x5, waiting for transfers between devices: 19.4 us -> 31.5 us  [enter(): return lax.ppermute(x, 'col', hops[0])]
    ppermute x5, starting transfers between devices: 17.9 us -> 10.1 us  [enter(): return lax.ppermute(x, 'col', hops[0])]
    ppermute x9, waiting for transfers between devices: 27.6 us -> 33.9 us  [run(): got = lax.ppermute(y, 'col', hops[hop])]
    ppermute x3, waiting for transfers between devices: 3.92 us -> 0.01 us  [shards(): lax.ppermute(x, both, plan.offset_pairs(r))]
    unnamed x58 -> x40, local copies, waits for them, and re-layouts: 7.69 us -> 5.05 us
  transfers between devices with their start and end apart: 34 -> 34, of which waited for: 18 -> 17; matrix products, arithmetic and copies ran while one was open for 9% -> 8% of each run, Pallas kernels for 14% -> 14%
where the time goes in v11:
time: 199 us; the launch traced here: 198 us
  waiting for transfers between devices  93.1 us (47%)
  starting transfers between devices  47.1 us (24%)
  Pallas kernels  33 us (17%)
  other arithmetic  17 us (9%)
  local copies, waits for them, and re-layouts  6.43 us (3%)
    ppermute x9, waiting for transfers between devices, run(): got = lax.ppermute(y, 'col', hops[hop])  33.9 us
    ppermute x5, waiting for transfers between devices, enter(): return lax.ppermute(x, 'col', hops[0])  31.5 us
    ppermute x8, waiting for transfers between devices, issue(): out.append(lax.ppermute(x, axis, pairs))  25 us
    ppermute x8, starting transfers between devices, issue(): out.append(lax.ppermute(x, axis, pairs))  18.9 us
    pallas_call x2, Pallas kernels, forward(): pl.pallas_call(functools.partial(forward_kernel, plan, member), in_specs=...  11.1 us
    ppermute x5, starting transfers between devices, enter(): return lax.ppermute(x, 'col', hops[0])  10.1 us
    ppermute x9, starting transfers between devices, run(): got = lax.ppermute(y, 'col', hops[hop])  10.1 us
    pallas_call x2, Pallas kernels, gather(): pl.pallas_call(functools.partial(gather_kernel, plan, member), in_specs=s...  9.26 us
  transfers between devices with their start and end apart: 34, of which 17 were waited for; matrix products, arithmetic and copies ran while one was open for 8% of the time, Pallas kernels for 14%

profile of v11, /device:TPU:0, one launch (start us, length us, event | category | flops | bytes accessed | tf_op | source)
XLA Modules:
  0.0 197.9 jit_solution(11941544089879233590)
XLA Ops:
  0.6 1.3 slice.19.factor
  2.0 5.8 %collective-permute-start.3 = (f32[512,512]{1,0:T(8,128)S(1)}, f32[512,512]{1,0:T(8,128)}, u32[]{:S(2)}, u32[]{:S(2)}) collective-permute-start(f32[512,512]{1,0:T(8,128)S(1)} %slice.19.factor), channel_id=1, source_target_pairs={{0,8},{4,20},{9,1},{13,29},{18,26}} | collective-permute-start | bytes 3145736 | tf_op jit(solution)/shard_map/ppermute | solution.py:156
  7.8 5.1 %gather_mirror.3 = (bf16[512,1024]{1,0:T(8,128)(2,1)S(1)}, bf16[512,1024]{1,0:T(8,128)(2,1)S(1)}, f32[512,512]{1,0:T(8,128)S(1)}, f32[512,512]{1,0:T(8,128)}) custom-call(s32[2,16]{1,0:T(2,128)S(1)} %copy-done.9, s32[2,16]{1,0:T(2,128)S(1)} %copy-done.10, f32[2048,4096]{1,0:T(8,128)} %front.3, f32[512,512]{1,0:T(8,128)S(1)} %slice.19.factor), custom_call_target="tpu_custom_call" | custom-call | flops 1677721600 | bytes 8388608 | tf_op jit(solution)/shard_map/gather_mirror/pallas_call | solution.py:333
  13.9 5.2 %collective-permute-done.3 = f32[512,512]{1,0:T(8,128)} collective-permute-done((f32[512,512]{1,0:T(8,128)S(1)}, f32[512,512]{1,0:T(8,128)}, u32[]{:S(2)}, u32[]{:S(2)}) %collective-permute-start.3) | collective-permute-done | bytes 1048608 | tf_op jit(solution)/shard_map/ppermute | solution.py:156
  19.1 1.9 broadcast_select_fusion.1
  21.0 1.4 collective-permute-start.4
  22.4 1.4 add.91
  23.8 1.3 collective-permute-start.2
  25.1 4.1 %gather_mirror.2 = (bf16[512,1024]{1,0:T(8,128)(2,1)S(1)}, bf16[512,1024]{1,0:T(8,128)(2,1)S(1)}, f32[512,512]{1,0:T(8,128)S(1)}, f32[512,512]{1,0:T(8,128)S(1)}) custom-call(s32[2,16]{1,0:T(2,128)S(1)} %copy-done.9, s32[2,16]{1,0:T(2,128)S(1)} %copy-done.10, f32[2048,4096]{1,0:T(8,128)} %front.3, f32[512,512]{1,0:T(8,128)S(1)} %get-tuple-element.53.factor), custom_call_target="tpu_custom_call" | custom-call | flops 1677721600 | bytes 8388608 | tf_op jit(solution)/shard_map/gather_mirror/pallas_call | solution.py:333
  29.3 5.3 %collective-permute-done.4 = f32[512,512]{1,0:T(8,128)S(1)} collective-permute-done((f32[512,512]{1,0:T(8,128)S(1)}, f32[512,512]{1,0:T(8,128)S(1)}, u32[]{:S(2)}, u32[]{:S(2)}) %collective-permute-start.4) | collective-permute-done | bytes 1048608 | tf_op jit(solution)/shard_map/ppermute | solution.py:156
  34.9 4.9 %collective-permute-start.8 = (f32[512,512]{1,0:T(8,128)S(1)}, f32[512,512]{1,0:T(8,128)S(1)}, u32[]{:S(2)}, u32[]{:S(2)}) collective-permute-start(f32[512,512]{1,0:T(8,128)S(1)} %get-tuple-element.53.factor), channel_id=1, source_target_pairs={{0,8},{4,20},{9,1},{13,29},{18,26}} | collective-permute-start | bytes 3145736 | tf_op jit(solution)/shard_map/ppermute | solution.py:156
  40.7 1.4 collective-permute-start.6
  43.4 4.8 %forward.2 = (f32[256,512]{1,0:T(8,128)S(1)}, f32[256,512]{1,0:T(8,128)S(1)}, f32[256,512]{1,0:T(8,128)S(1)}, f32[256,512]{1,0:T(8,128)S(1)}) custom-call(bf16[512,1024]{1,0:T(8,128)(2,1)S(1)} %get-tuple-element.46.high, bf16[512,1024]{1,0:T(8,128)(2,1)S(1)} %copy-done.4, f32[512,512]{1,0:T(8,128)S(1)} %slice.19.factor, f32[512,512]{1,0:T(8,128)} %copy-done.15, ...), custom_call_target="tpu_custom_call" | custom-call | flops 1677721600 | bytes 8388608 | tf_op jit(solution)/shard_map/forward/pallas_call | solution.py:351
  48.2 3.8 %collective-permute-done.8 = f32[512,512]{1,0:T(8,128)S(1)} collective-permute-done((f32[512,512]{1,0:T(8,128)S(1)}, f32[512,512]{1,0:T(8,128)S(1)}, u32[]{:S(2)}, u32[]{:S(2)}) %collective-permute-start.8) | collective-permute-done | bytes 1048608 | tf_op jit(solution)/shard_map/ppermute | solution.py:156
  52.2 5.5 %collective-permute-done.6 = f32[512,512]{1,0:T(8,128)S(1)} collective-permute-done((f32[512,512]{1,0:T(8,128)S(1)}, f32[512,512]{1,0:T(8,128)S(1)}, u32[]{:S(2)}, u32[]{:S(2)}) %collective-permute-start.6) | collective-permute-done | bytes 1048608 | tf_op jit(solution)/shard_map/ppermute | solution.py:156
  58.0 1.4 collective-permute-start.9
  59.4 1.3 collective-permute-start.10
  60.7 1.6 collective-permute-start.7
  62.2 9.3 %collective-permute-done.7 = f32[256,512]{1,0:T(8,128)S(1)} collective-permute-done((f32[256,512]{1,0:T(8,128)S(1)}, f32[256,512]{1,0:T(8,128)S(1)}, u32[]{:S(2)}, u32[]{:S(2)}) %collective-permute-start.7) | collective-permute-done | bytes 524320 | tf_op jit(solution)/shard_map/ppermute | solution.py:372
  71.6 4.5 %collective-permute-done.10 = f32[512,512]{1,0:T(8,128)S(1)} collective-permute-done((f32[512,512]{1,0:T(8,128)S(1)}, f32[512,512]{1,0:T(8,128)S(1)}, u32[]{:S(2)}, u32[]{:S(2)}) %collective-permute-start.10) | collective-permute-done | bytes 1048608 | tf_op jit(solution)/shard_map/ppermute | solution.py:156
  77.2 2.8 %collective-permute-start.12 = (f32[256,512]{1,0:T(8,128)S(1)}, f32[256,512]{1,0:T(8,128)S(1)}, u32[]{:S(2)}, u32[]{:S(2)}) collective-permute-start(f32[256,512]{1,0:T(8,128)S(1)} %get-tuple-element.59), channel_id=1, source_target_pairs={{0,1},{3,2},{4,5},{7,6},{8,9},{11,10},{12,13},{15,14},{16,17},{19,... | collective-permute-start | bytes 1572872 | tf_op jit(solution)/shard_map/ppermute | solution.py:372
  81.2 1.5 collective-permute-start.14
  82.7 9.1 %collective-permute-done.12 = f32[256,512]{1,0:T(8,128)S(1)} collective-permute-done((f32[256,512]{1,0:T(8,128)S(1)}, f32[256,512]{1,0:T(8,128)S(1)}, u32[]{:S(2)}, u32[]{:S(2)}) %collective-permute-start.12) | collective-permute-done | bytes 524320 | tf_op jit(solution)/shard_map/ppermute | solution.py:372
  92.9 6.3 %forward.3 = (f32[256,512]{1,0:T(8,128)S(1)}, f32[256,512]{1,0:T(8,128)S(1)}, f32[512,512]{1,0:T(8,128)S(1)}, f32[512,512]{1,0:T(8,128)}) custom-call(bf16[512,1024]{1,0:T(8,128)(2,1)S(1)} %get-tuple-element.42.high, bf16[512,1024]{1,0:T(8,128)(2,1)} %copy-done.2, f32[512,512]{1,0:T(8,128)} %copy-done.1, f32[512,512]{1,0:T(8,128)} %add.96.mirror, ...), custom_call_target="tpu_custom_call" | custom-call | flops 1677721600 | bytes 8388608 | tf_op jit(solution)/shard_map/forward/pallas_call | solution.py:351
  99.3 1.3 collective-permute-start.15
  100.6 2.1 %add.103 = f32[256,512]{1,0:T(8,128)} add(f32[256,512]{1,0:T(8,128)} %copy-done.16, f32[256,512]{1,0:T(8,128)} %copy-done.19) | non-fusion elementwise | flops 131072 | bytes 1572864 | tf_op jit(solution)/shard_map/add | solution.py:101
  102.7 1.5 collective-permute-start.18
  104.2 2.4 %slice_add_fusion = (f32[256,512]{1,0:T(8,128)}, f32[256,512]{1,0:T(8,128)}) fusion(f32[256,512]{1,0:T(8,128)S(1)} %get-tuple-element.72, f32[512,512]{1,0:T(8,128)} %collective-permute-done.14, f32[256,512]{1,0:T(8,128)S(1)} %get-tuple-element.64), kind=kLoop, calls=%fused_computation.1 | loop fusion | flops 262144 | bytes 3145728 | tf_op jit(solution)/shard_map/add | solution.py:432
  106.6 9.1 %collective-permute-done.15.rest_1_ = f32[256,512]{1,0:T(8,128)S(1)} collective-permute-done((f32[256,512]{1,0:T(8,128)S(1)}, f32[256,512]{1,0:T(8,128)S(1)}, u32[]{:S(2)}, u32[]{:S(2)}) %collective-permute-start.15) | collective-permute-done | bytes 524320 | tf_op jit(solution)/shard_map/ppermute | solution.py:384
  115.7 2.2 %collective-permute-start.16 = (f32[256,512]{1,0:T(8,128)}, f32[256,512]{1,0:T(8,128)}, u32[]{:S(2)}, u32[]{:S(2)}) collective-permute-start(f32[256,512]{1,0:T(8,128)} %get-tuple-element.69), channel_id=1, source_target_pairs={{0,1},{3,2},{4,5},{7,6},{8,9},{11,10},{12,13},{15,14},{16,17},{19,... | collective-permute-start | bytes 1572872 | tf_op jit(solution)/shard_map/ppermute | solution.py:372
  117.9 1.5 add.108
  119.4 2.5 %collective-permute-start.25 = (f32[256,512]{1,0:T(8,128)S(1)}, f32[256,512]{1,0:T(8,128)S(1)}, u32[]{:S(2)}, u32[]{:S(2)}) collective-permute-start(f32[256,512]{1,0:T(8,128)S(1)} %dynamic-slice_bitcast_fusion), channel_id=1, source_target_pairs={{0,8},{1,9},{2,10},{3,11},{4,20},{5,21},{6,22},{7,23},{8,0},{9,1},... | collective-permute-start | bytes 1572872 | tf_op jit(solution)/shard_map/ppermute | solution.py:442
  123.3 1.7 collective-permute-start.21
  125.0 4.7 %collective-permute-done.16 = f32[256,512]{1,0:T(8,128)} collective-permute-done((f32[256,512]{1,0:T(8,128)}, f32[256,512]{1,0:T(8,128)}, u32[]{:S(2)}, u32[]{:S(2)}) %collective-permute-start.16) | collective-permute-done | bytes 524320 | tf_op jit(solution)/shard_map/ppermute | solution.py:372
  134.1 5.8 %collective-permute-done.21 = f32[256,512]{1,0:T(8,128)S(1)} collective-permute-done((f32[256,512]{1,0:T(8,128)}, f32[256,512]{1,0:T(8,128)S(1)}, u32[]{:S(2)}, u32[]{:S(2)}) %collective-permute-start.21) | collective-permute-done | bytes 524320 | tf_op jit(solution)/shard_map/ppermute | solution.py:372
  141.0 2.5 %collective-permute-done.19.rest_3_ = f32[256,512]{1,0:T(8,128)S(1)} collective-permute-done((f32[256,512]{1,0:T(8,128)S(1)}, f32[256,512]{1,0:T(8,128)S(1)}, u32[]{:S(2)}, u32[]{:S(2)}) %collective-permute-start.19) | collective-permute-done | bytes 524320 | tf_op jit(solution)/shard_map/ppermute | solution.py:384
  143.6 1.8 collective-permute-start.27
  146.2 1.3 collective-permute-start.20
  147.5 2.6 %collective-permute-done.27 = f32[128,512]{1,0:T(8,128)S(1)} collective-permute-done((f32[128,512]{1,0:T(8,128)S(1)}, f32[128,512]{1,0:T(8,128)S(1)}, u32[]{:S(2)}, u32[]{:S(2)}) %collective-permute-start.27) | collective-permute-done | bytes 262176 | tf_op jit(solution)/shard_map/ppermute | solution.py:372
  150.9 4.4 %place.2.rest_4_ = f32[2048,1024]{1,0:T(8,128)} custom-call(s32[2,16]{1,0:T(2,128)S(1)} %copy-done.9, f32[2,512,512]{2,1,0:T(8,128)S(1)} %copy-done, f32[256,512]{1,0:T(8,128)S(1)} %add.100.rest_0_, f32[256,512]{1,0:T(8,128)S(1)} %copy-done.6, f32[256,512]{1,0:T(8,128)S(1)} %add.104.rest_2_, f32[256,512]{1,0:T(8,128)S(1)} %collective-permute-done.19.rest_3_), custom_call_target="tpu_custom_call" | custom-call | flops 1677721600 | bytes 8388608 | tf_op jit(solution)/shard_map/place/pallas_call | solution.py:450
  155.4 1.3 collective-permute-start.29
  156.7 6.4 %collective-permute-done.20.rest_1_ = f32[256,512]{1,0:T(8,128)S(1)} collective-permute-done((f32[256,512]{1,0:T(8,128)S(1)}, f32[256,512]{1,0:T(8,128)S(1)}, u32[]{:S(2)}, u32[]{:S(2)}) %collective-permute-start.20) | collective-permute-done | bytes 524320 | tf_op jit(solution)/shard_map/ppermute | solution.py:384
  165.2 11.5 %collective-permute-done.29 = f32[128,512]{1,0:T(8,128)} collective-permute-done((f32[128,512]{1,0:T(8,128)S(1)}, f32[128,512]{1,0:T(8,128)}, u32[]{:S(2)}, u32[]{:S(2)}) %collective-permute-start.29) | collective-permute-done | bytes 262176 | tf_op jit(solution)/shard_map/ppermute | solution.py:384
  178.8 2.5 %collective-permute-start.30 = (f32[128,512]{1,0:T(8,128)S(1)}, f32[128,512]{1,0:T(8,128)S(1)}, u32[]{:S(2)}, u32[]{:S(2)}) collective-permute-start(f32[128,512]{1,0:T(8,128)S(1)} %broadcast_select_fusion.2), channel_id=1, source_target_pairs={{0,16},{1,17},{2,18},{3,19},{8,24},{9,25},{10,26},{11,27},{16,0},{... | collective-permute-start | bytes 786440 | tf_op jit(solution)/shard_map/ppermute | solution.py:498
  181.3 4.4 %collective-permute-done.23.rest_3_ = f32[256,512]{1,0:T(8,128)} collective-permute-done((f32[256,512]{1,0:T(8,128)S(1)}, f32[256,512]{1,0:T(8,128)}, u32[]{:S(2)}, u32[]{:S(2)}) %collective-permute-start.23) | collective-permute-done | bytes 524320 | tf_op jit(solution)/shard_map/ppermute | solution.py:384
  186.7 3.2 %place.3 = f32[2048,1024]{1,0:T(8,128)} custom-call(s32[2,16]{1,0:T(2,128)S(1)} %copy-done.9, f32[2,512,512]{2,1,0:T(8,128)S(1)} %copy-done, f32[256,512]{1,0:T(8,128)S(1)} %add.102.rest_0_, f32[256,512]{1,0:T(8,128)S(1)} %copy-done.8, f32[256,512]{1,0:T(8,128)S(1)} %add.107.rest_2_, ...), custom_call_target="tpu_custom_call", output_to_operand_aliasing={{}: (6, {})} | custom-call | flops 1677721600 | bytes 8388608 | tf_op jit(solution)/shard_map/place/pallas_call | solution.py:450
  190.1 2.6 %collective-permute-done.33.rest_1_ = f32[512,512]{1,0:T(8,128)S(1)} collective-permute-done((f32[512,512]{1,0:T(8,128)S(1)}, f32[512,512]{1,0:T(8,128)S(1)}, u32[]{:S(2)}, u32[]{:S(2)}) %collective-permute-start.33) | collective-permute-done | bytes 1048608 | tf_op jit(solution)/shard_map/ppermute | solution.py:88
  192.8 5.1 %diagonal.1 = f32[2,512,512]{2,1,0:T(8,128)} custom-call(f32[2,512]{1,0:T(2,128)S(1)} %copy-done.11, f32[2,512,512]{2,1,0:T(8,128)S(1)} %copy-done, f32[512,512]{1,0:T(8,128)S(1)} %pad_maximum_fusion.rest_0_, f32[512,512]{1,0:T(8,128)S(1)} %collective-permute-done.33.rest_1_), custom_call_target="tpu_custom_call" | custom-call | flops 1677721600 | bytes 8388608 | tf_op jit(solution)/shard_map/diagonal/pallas_call | solution.py:501
  (95 shorter events, 21.3 us)
Async XLA Ops:
  0.6 7.2 %copy-start.9 = (s32[2,16]{1,0:T(2,128)S(1)}, s32[2,16]{1,0:T(2,128)}, u32[]{:S(2)}) copy-start(s32[2,16]{1,0:T(2,128)} %tiles_ref.7) | copy-start | bytes 388
  0.6 7.2 %copy-start.10 = (s32[2,16]{1,0:T(2,128)S(1)}, s32[2,16]{1,0:T(2,128)}, u32[]{:S(2)}) copy-start(s32[2,16]{1,0:T(2,128)} %valid_ref.3) | copy-start | bytes 388
  2.0 17.2 %collective-permute-start.3 = (f32[512,512]{1,0:T(8,128)S(1)}, f32[512,512]{1,0:T(8,128)}, u32[]{:S(2)}, u32[]{:S(2)}) collective-permute-start(f32[512,512]{1,0:T(8,128)S(1)} %slice.19.factor), channel_id=1, source_target_pairs={{0,8},{4,20},{9,1},{13,29},{18,26}} | collective-permute-start | bytes 3145736 | tf_op jit(solution)/shard_map/ppermute | solution.py:156
  13.9 8.4 %collective-permute-start.1 = (f32[512,512]{1,0:T(8,128)}, f32[512,512]{1,0:T(8,128)}, u32[]{:S(2)}, u32[]{:S(2)}) collective-permute-start(f32[512,512]{1,0:T(8,128)} %get-tuple-element.49), channel_id=1, source_target_pairs={{4,0},{0,4},{12,8},{8,12},{20,16},{16,20},{28,24},{24,28},{5,1},{1... | collective-permute-start | bytes 3145736 | tf_op jit(solution)/shard_map/ppermute | solution.py:88
  21.0 13.9 %copy-start.1 = (f32[512,512]{1,0:T(8,128)}, f32[512,512]{1,0:T(8,128)S(1)}, u32[]{:S(2)}) copy-start(f32[512,512]{1,0:T(8,128)S(1)} %get-tuple-element.53.factor) | copy-start | bytes 3145732
  21.0 13.6 %collective-permute-start.4 = (f32[512,512]{1,0:T(8,128)S(1)}, f32[512,512]{1,0:T(8,128)S(1)}, u32[]{:S(2)}, u32[]{:S(2)}) collective-permute-start(f32[512,512]{1,0:T(8,128)S(1)} %get-tuple-element.50), channel_id=1, source_target_pairs={{0,16},{8,24},{4,12},{20,28},{9,25},{1,17},{29,21},{22,30}} | collective-permute-start | bytes 3145736 | tf_op jit(solution)/shard_map/ppermute | solution.py:156
  23.8 16.7 %collective-permute-start.2 = (f32[512,512]{1,0:T(8,128)S(1)}, f32[512,512]{1,0:T(8,128)S(1)}, u32[]{:S(2)}, u32[]{:S(2)}) collective-permute-start(f32[512,512]{1,0:T(8,128)S(1)} %add.91), channel_id=1, source_target_pairs={{16,0},{24,8},{12,4},{28,20},{25,9},{17,1},{21,29},{30,22}} | collective-permute-start | bytes 3145736 | tf_op jit(solution)/shard_map/ppermute | solution.py:156
  29.2 11.5 %copy-start.2 = (bf16[512,1024]{1,0:T(8,128)(2,1)}, bf16[512,1024]{1,0:T(8,128)(2,1)S(1)}, u32[]{:S(2)}) copy-start(bf16[512,1024]{1,0:T(8,128)(2,1)S(1)} %get-tuple-element.43.low) | copy-start | bytes 3145732
  29.2 12.9 %collective-permute-start = (f32[512,512]{1,0:T(8,128)S(1)}, f32[512,512]{1,0:T(8,128)S(1)}, u32[]{:S(2)}, u32[]{:S(2)}) collective-permute-start(f32[512,512]{1,0:T(8,128)S(1)} %get-tuple-element.45), channel_id=1, source_target_pairs={{4,0},{0,4},{12,8},{8,12},{20,16},{16,20},{28,24},{24,28},{5,1},{1... | collective-permute-start | bytes 3145736 | tf_op jit(solution)/shard_map/ppermute | solution.py:88
  34.8 7.6 %copy-start.14 = (f32[512,512]{1,0:T(8,128)}, f32[512,512]{1,0:T(8,128)S(1)}, u32[]{:S(2)}) copy-start(f32[512,512]{1,0:T(8,128)S(1)} %add.93.rest_0_) | copy-start | bytes 3145732
  34.8 7.6 %collective-permute-start.5 = (f32[512,512]{1,0:T(8,128)S(1)}, f32[512,512]{1,0:T(8,128)S(1)}, u32[]{:S(2)}, u32[]{:S(2)}) collective-permute-start(f32[512,512]{1,0:T(8,128)S(1)} %add.93.rest_0_), channel_id=1, source_target_pairs={{4,0},{0,4},{12,8},{8,12},{20,16},{16,20},{28,24},{24,28},{5,1},{1... | collective-permute-start | bytes 3145736 | tf_op jit(solution)/shard_map/ppermute | solution.py:88
  34.9 17.1 %collective-permute-start.8 = (f32[512,512]{1,0:T(8,128)S(1)}, f32[512,512]{1,0:T(8,128)S(1)}, u32[]{:S(2)}, u32[]{:S(2)}) collective-permute-start(f32[512,512]{1,0:T(8,128)S(1)} %get-tuple-element.53.factor), channel_id=1, source_target_pairs={{0,8},{4,20},{9,1},{13,29},{18,26}} | collective-permute-start | bytes 3145736 | tf_op jit(solution)/shard_map/ppermute | solution.py:156
  40.7 2.7 %copy-start.15 = (f32[512,512]{1,0:T(8,128)}, f32[512,512]{1,0:T(8,128)S(1)}, u32[]{:S(2)}) copy-start(f32[512,512]{1,0:T(8,128)S(1)} %add.92.mirror) | copy-start | bytes 3145732
  40.7 2.7 %copy-start.4 = (bf16[512,1024]{1,0:T(8,128)(2,1)S(1)}, bf16[512,1024]{1,0:T(8,128)(2,1)}, u32[]{:S(2)}) copy-start(bf16[512,1024]{1,0:T(8,128)(2,1)} %copy-done.3) | copy-start | bytes 3145732
  40.7 17.1 %collective-permute-start.6 = (f32[512,512]{1,0:T(8,128)S(1)}, f32[512,512]{1,0:T(8,128)S(1)}, u32[]{:S(2)}, u32[]{:S(2)}) collective-permute-start(f32[512,512]{1,0:T(8,128)S(1)} %add.92.mirror), channel_id=1, source_target_pairs={{8,0},{20,4},{1,9},{29,13},{26,18}} | collective-permute-start | bytes 3145736 | tf_op jit(solution)/shard_map/ppermute | solution.py:156
  43.4 8.7 %copy-start.12 = (f32[512,1024]{1,0:T(8,128)S(1)}, f32[512,1024]{1,0:T(8,128)}, u32[]{:S(2)}) copy-start(f32[512,1024]{1,0:T(8,128)} %param.7) | copy-start | bytes 6291460
  58.0 19.2 %copy-start.16 = (f32[256,512]{1,0:T(8,128)}, f32[256,512]{1,0:T(8,128)S(1)}, u32[]{:S(2)}) copy-start(f32[256,512]{1,0:T(8,128)S(1)} %get-tuple-element.59) | copy-start | bytes 1572868
  58.0 13.6 %collective-permute-start.9 = (f32[512,512]{1,0:T(8,128)S(1)}, f32[512,512]{1,0:T(8,128)S(1)}, u32[]{:S(2)}, u32[]{:S(2)}) collective-permute-start(f32[512,512]{1,0:T(8,128)S(1)} %broadcast_select_fusion), channel_id=1, source_target_pairs={{0,16},{8,24},{4,12},{20,28},{9,25},{1,17},{29,21},{22,30}} | collective-permute-start | bytes 3145736 | tf_op jit(solution)/shard_map/ppermute | solution.py:156
  59.4 16.7 %collective-permute-start.10 = (f32[512,512]{1,0:T(8,128)S(1)}, f32[512,512]{1,0:T(8,128)S(1)}, u32[]{:S(2)}, u32[]{:S(2)}) collective-permute-start(f32[512,512]{1,0:T(8,128)S(1)} %add.90), channel_id=1, source_target_pairs={{16,0},{24,8},{12,4},{28,20},{25,9},{17,1},{21,29},{30,22}} | collective-permute-start | bytes 3145736 | tf_op jit(solution)/shard_map/ppermute | solution.py:156
  60.7 10.9 %collective-permute-start.7 = (f32[256,512]{1,0:T(8,128)S(1)}, f32[256,512]{1,0:T(8,128)S(1)}, u32[]{:S(2)}, u32[]{:S(2)}) collective-permute-start(f32[256,512]{1,0:T(8,128)S(1)} %get-tuple-element.87), channel_id=1, source_target_pairs={{0,1},{3,2},{4,5},{7,6},{8,9},{11,10},{12,13},{15,14},{16,17},{19,... | collective-permute-start | bytes 1572872 | tf_op jit(solution)/shard_map/ppermute | solution.py:372
  76.3 4.9 %copy-start.13 = (f32[512,512]{1,0:T(8,128)}, f32[512,512]{1,0:T(8,128)S(1)}, u32[]{:S(2)}) copy-start(f32[512,512]{1,0:T(8,128)S(1)} %add.98.rest_0_) | copy-start | bytes 3145732
  76.3 15.5 %collective-permute-start.13 = (f32[512,512]{1,0:T(8,128)S(1)}, f32[512,512]{1,0:T(8,128)S(1)}, u32[]{:S(2)}, u32[]{:S(2)}) collective-permute-start(f32[512,512]{1,0:T(8,128)S(1)} %add.98.rest_0_), channel_id=1, source_target_pairs={{4,0},{0,4},{12,8},{8,12},{20,16},{16,20},{28,24},{24,28},{5,1},{1... | collective-permute-start | bytes 3145736 | tf_op jit(solution)/shard_map/ppermute | solution.py:88
  76.4 6.2 %collective-permute-start.11 = (f32[256,512]{1,0:T(8,128)S(1)}, f32[256,512]{1,0:T(8,128)S(1)}, u32[]{:S(2)}, u32[]{:S(2)}) collective-permute-start(f32[256,512]{1,0:T(8,128)S(1)} %add.97), channel_id=1, source_target_pairs={{1,2},{2,1},{5,6},{6,5},{9,10},{10,9},{13,14},{14,13},{17,18},{18,... | collective-permute-start | bytes 1572872 | tf_op jit(solution)/shard_map/ppermute | solution.py:410
  77.2 14.6 %collective-permute-start.12 = (f32[256,512]{1,0:T(8,128)S(1)}, f32[256,512]{1,0:T(8,128)S(1)}, u32[]{:S(2)}, u32[]{:S(2)}) collective-permute-start(f32[256,512]{1,0:T(8,128)S(1)} %get-tuple-element.59), channel_id=1, source_target_pairs={{0,1},{3,2},{4,5},{7,6},{8,9},{11,10},{12,13},{15,14},{16,17},{19,... | collective-permute-start | bytes 1572872 | tf_op jit(solution)/shard_map/ppermute | solution.py:372
  81.2 23.0 %collective-permute-start.14 = (f32[512,512]{1,0:T(8,128)}, f32[512,512]{1,0:T(8,128)}, u32[]{:S(2)}, u32[]{:S(2)}) collective-permute-start(f32[512,512]{1,0:T(8,128)} %add.96.mirror), channel_id=1, source_target_pairs={{8,0},{20,4},{1,9},{29,13},{26,18}} | collective-permute-start | bytes 3145736 | tf_op jit(solution)/shard_map/ppermute | solution.py:156
  99.2 18.7 %collective-permute-start.24 = (f32[512,512]{1,0:T(8,128)}, f32[512,512]{1,0:T(8,128)}, u32[]{:S(2)}, u32[]{:S(2)}) collective-permute-start(f32[512,512]{1,0:T(8,128)} %get-tuple-element.77), channel_id=1, source_target_pairs={{4,0},{0,4},{12,8},{8,12},{20,16},{16,20},{28,24},{24,28},{5,1},{1... | collective-permute-start | bytes 3145736 | tf_op jit(solution)/shard_map/ppermute | solution.py:88
  99.3 16.4 %collective-permute-start.15 = (f32[256,512]{1,0:T(8,128)S(1)}, f32[256,512]{1,0:T(8,128)S(1)}, u32[]{:S(2)}, u32[]{:S(2)}) collective-permute-start(f32[256,512]{1,0:T(8,128)S(1)} %add.100.rest_0_), channel_id=1, source_target_pairs={{1,0},{2,3},{5,4},{6,7},{9,8},{10,11},{13,12},{14,15},{17,16},{18,... | collective-permute-start | bytes 1572872 | tf_op jit(solution)/shard_map/ppermute | solution.py:384
  102.7 19.3 %collective-permute-start.18 = (f32[256,512]{1,0:T(8,128)}, f32[256,512]{1,0:T(8,128)}, u32[]{:S(2)}, u32[]{:S(2)}) collective-permute-start(f32[256,512]{1,0:T(8,128)} %add.103), channel_id=1, source_target_pairs={{1,2},{2,1},{5,6},{6,5},{9,10},{10,9},{13,14},{14,13},{17,18},{18,... | collective-permute-start | bytes 1572872 | tf_op jit(solution)/shard_map/ppermute | solution.py:384
  115.7 3.8 %copy-start.5 = (f32[256,512]{1,0:T(8,128)}, f32[256,512]{1,0:T(8,128)S(1)}, u32[]{:S(2)}) copy-start(f32[256,512]{1,0:T(8,128)S(1)} %collective-permute-done.15.rest_1_) | copy-start | bytes 1572868
  115.7 14.1 %collective-permute-start.16 = (f32[256,512]{1,0:T(8,128)}, f32[256,512]{1,0:T(8,128)}, u32[]{:S(2)}, u32[]{:S(2)}) collective-permute-start(f32[256,512]{1,0:T(8,128)} %get-tuple-element.69), channel_id=1, source_target_pairs={{0,1},{3,2},{4,5},{7,6},{8,9},{11,10},{12,13},{15,14},{16,17},{19,... | collective-permute-start | bytes 1572872 | tf_op jit(solution)/shard_map/ppermute | solution.py:372
  119.4 11.6 %collective-permute-start.25 = (f32[256,512]{1,0:T(8,128)S(1)}, f32[256,512]{1,0:T(8,128)S(1)}, u32[]{:S(2)}, u32[]{:S(2)}) collective-permute-start(f32[256,512]{1,0:T(8,128)S(1)} %dynamic-slice_bitcast_fusion), channel_id=1, source_target_pairs={{0,8},{1,9},{2,10},{3,11},{4,20},{5,21},{6,22},{7,23},{8,0},{9,1},... | collective-permute-start | bytes 1572872 | tf_op jit(solution)/shard_map/ppermute | solution.py:442
  123.3 16.6 %collective-permute-start.21 = (f32[256,512]{1,0:T(8,128)}, f32[256,512]{1,0:T(8,128)S(1)}, u32[]{:S(2)}, u32[]{:S(2)}) collective-permute-start(f32[256,512]{1,0:T(8,128)} %get-tuple-element.73), channel_id=1, source_target_pairs={{0,1},{3,2},{4,5},{7,6},{8,9},{11,10},{12,13},{15,14},{16,17},{19,... | collective-permute-start | bytes 1572872 | tf_op jit(solution)/shard_map/ppermute | solution.py:372
  129.7 13.8 %collective-permute-start.19 = (f32[256,512]{1,0:T(8,128)S(1)}, f32[256,512]{1,0:T(8,128)S(1)}, u32[]{:S(2)}, u32[]{:S(2)}) collective-permute-start(f32[256,512]{1,0:T(8,128)S(1)} %add.104.rest_2_), channel_id=1, source_target_pairs={{1,0},{2,3},{5,4},{6,7},{9,8},{10,11},{13,12},{14,15},{17,16},{18,... | collective-permute-start | bytes 1572872 | tf_op jit(solution)/shard_map/ppermute | solution.py:384
  131.2 12.4 %collective-permute-start.26 = (f32[128,512]{1,0:T(8,128)S(1)}, f32[128,512]{1,0:T(8,128)S(1)}, u32[]{:S(2)}, u32[]{:S(2)}) collective-permute-start(f32[128,512]{1,0:T(8,128)S(1)} %dynamic-slice_bitcast_fusion.1), channel_id=1, source_target_pairs={{0,16},{1,17},{2,18},{3,19},{4,12},{5,13},{6,14},{7,15},{8,24},{9,... | collective-permute-start | bytes 786440 | tf_op jit(solution)/shard_map/ppermute | solution.py:442
  133.3 17.6 %copy-start = (f32[2,512,512]{2,1,0:T(8,128)S(1)}, f32[2,512,512]{2,1,0:T(8,128)}, u32[]{:S(2)}) copy-start(f32[2,512,512]{2,1,0:T(8,128)} %unit_ref.5) | copy-start | bytes 6291460
  133.3 17.6 %copy-start.6 = (f32[256,512]{1,0:T(8,128)S(1)}, f32[256,512]{1,0:T(8,128)}, u32[]{:S(2)}) copy-start(f32[256,512]{1,0:T(8,128)} %copy-done.5) | copy-start | bytes 1572868
  133.3 12.8 %collective-permute-start.17 = (f32[256,512]{1,0:T(8,128)S(1)}, f32[256,512]{1,0:T(8,128)S(1)}, u32[]{:S(2)}, u32[]{:S(2)}) collective-permute-start(f32[256,512]{1,0:T(8,128)S(1)} %add.101), channel_id=1, source_target_pairs={{1,2},{2,1},{5,6},{6,5},{9,10},{10,9},{13,14},{14,13},{17,18},{18,... | collective-permute-start | bytes 1572872 | tf_op jit(solution)/shard_map/ppermute | solution.py:384
  143.6 6.6 %collective-permute-start.27 = (f32[128,512]{1,0:T(8,128)S(1)}, f32[128,512]{1,0:T(8,128)S(1)}, u32[]{:S(2)}, u32[]{:S(2)}) collective-permute-start(f32[128,512]{1,0:T(8,128)S(1)} %bitcast_add_fusion.1), channel_id=1, source_target_pairs={{0,1},{3,2},{4,5},{7,6},{8,9},{11,10},{12,13},{15,14},{16,17},{19,... | collective-permute-start | bytes 786440 | tf_op jit(solution)/shard_map/ppermute | solution.py:372
  145.4 9.8 %collective-permute-start.22 = (f32[256,512]{1,0:T(8,128)S(1)}, f32[256,512]{1,0:T(8,128)S(1)}, u32[]{:S(2)}, u32[]{:S(2)}) collective-permute-start(f32[256,512]{1,0:T(8,128)S(1)} %add.106), channel_id=1, source_target_pairs={{1,2},{2,1},{5,6},{6,5},{9,10},{10,9},{13,14},{14,13},{17,18},{18,... | collective-permute-start | bytes 1572872 | tf_op jit(solution)/shard_map/ppermute | solution.py:384
  146.2 16.9 %collective-permute-start.20 = (f32[256,512]{1,0:T(8,128)S(1)}, f32[256,512]{1,0:T(8,128)S(1)}, u32[]{:S(2)}, u32[]{:S(2)}) collective-permute-start(f32[256,512]{1,0:T(8,128)S(1)} %add.102.rest_0_), channel_id=1, source_target_pairs={{1,0},{2,3},{5,4},{6,7},{9,8},{10,11},{13,12},{14,15},{17,16},{18,... | collective-permute-start | bytes 1572872 | tf_op jit(solution)/shard_map/ppermute | solution.py:384
  150.2 5.2 %collective-permute-start.28 = (f32[128,512]{1,0:T(8,128)S(1)}, f32[128,512]{1,0:T(8,128)S(1)}, u32[]{:S(2)}, u32[]{:S(2)}) collective-permute-start(f32[128,512]{1,0:T(8,128)S(1)} %add.114), channel_id=1, source_target_pairs={{1,2},{2,1},{5,6},{6,5},{9,10},{10,9},{13,14},{14,13},{17,18},{18,... | collective-permute-start | bytes 786440 | tf_op jit(solution)/shard_map/ppermute | solution.py:384
  155.4 21.3 %collective-permute-start.29 = (f32[128,512]{1,0:T(8,128)S(1)}, f32[128,512]{1,0:T(8,128)}, u32[]{:S(2)}, u32[]{:S(2)}) collective-permute-start(f32[128,512]{1,0:T(8,128)S(1)} %add.115), channel_id=1, source_target_pairs={{1,0},{2,3},{5,4},{6,7},{9,8},{10,11},{13,12},{14,15},{17,16},{18,... | collective-permute-start | bytes 786440 | tf_op jit(solution)/shard_map/ppermute | solution.py:384
  163.9 21.7 %collective-permute-start.23 = (f32[256,512]{1,0:T(8,128)S(1)}, f32[256,512]{1,0:T(8,128)}, u32[]{:S(2)}, u32[]{:S(2)}) collective-permute-start(f32[256,512]{1,0:T(8,128)S(1)} %add.107.rest_2_), channel_id=1, source_target_pairs={{1,0},{2,3},{5,4},{6,7},{9,8},{10,11},{13,12},{14,15},{17,16},{18,... | collective-permute-start | bytes 1572872 | tf_op jit(solution)/shard_map/ppermute | solution.py:384
  177.7 12.2 %collective-permute-start.32 = (f32[128,512]{1,0:T(8,128)S(1)}, f32[128,512]{1,0:T(8,128)S(1)}, u32[]{:S(2)}, u32[]{:S(2)}) collective-permute-start(f32[128,512]{1,0:T(8,128)S(1)} %broadcast_select_fusion.2), channel_id=1, source_target_pairs={{0,24},{1,25},{2,26},{3,27},{8,16},{9,17},{10,18},{11,19},{16,8},{... | collective-permute-start | bytes 786440 | tf_op jit(solution)/shard_map/ppermute | solution.py:498
  177.8 12.2 %collective-permute-start.31 = (f32[128,512]{1,0:T(8,128)S(1)}, f32[128,512]{1,0:T(8,128)S(1)}, u32[]{:S(2)}, u32[]{:S(2)}) collective-permute-start(f32[128,512]{1,0:T(8,128)S(1)} %broadcast_select_fusion.2), channel_id=1, source_target_pairs={{0,8},{1,9},{2,10},{3,11},{8,0},{9,1},{10,2},{11,3},{16,24},{17,25... | collective-permute-start | bytes 786440 | tf_op jit(solution)/shard_map/ppermute | solution.py:498
  178.8 11.2 %collective-permute-start.30 = (f32[128,512]{1,0:T(8,128)S(1)}, f32[128,512]{1,0:T(8,128)S(1)}, u32[]{:S(2)}, u32[]{:S(2)}) collective-permute-start(f32[128,512]{1,0:T(8,128)S(1)} %broadcast_select_fusion.2), channel_id=1, source_target_pairs={{0,16},{1,17},{2,18},{3,19},{8,24},{9,25},{10,26},{11,27},{16,0},{... | collective-permute-start | bytes 786440 | tf_op jit(solution)/shard_map/ppermute | solution.py:498
  189.9 2.9 %copy-start.11 = (f32[2,512]{1,0:T(2,128)S(1)}, f32[2,512]{1,0:T(2,128)}, u32[]{:S(2)}) copy-start(f32[2,512]{1,0:T(2,128)} %pivot.1) | copy-start | bytes 12292
  190.1 2.7 %collective-permute-start.33 = (f32[512,512]{1,0:T(8,128)S(1)}, f32[512,512]{1,0:T(8,128)S(1)}, u32[]{:S(2)}, u32[]{:S(2)}) collective-permute-start(f32[512,512]{1,0:T(8,128)S(1)} %pad_maximum_fusion.rest_0_), channel_id=1, source_target_pairs={{4,0},{0,4},{12,8},{8,12},{20,16},{16,20},{28,24},{24,28},{5,1},{1... | collective-permute-start | bytes 3145736 | tf_op jit(solution)/shard_map/ppermute | solution.py:88
  (6 other events, 5.8 us)

commit v12 on v8

--- a/solution.py
+++ b/solution.py
@@ -472,16 +472,18 @@
             ties = [(brought[i - 2][hop + 1],) for hop in range(1, middle)]
             ties.append((brought[i - 1][-1],))
         chunks[i], ends[i], sent[i], brought[i] = run(chunks[i], entered[i], ties)
-    update, got, _, _ = run(update, enter(update), [(x,) for x in sent[last]])
-    for member in range(members):
+    column = place(0, column)
+    ties = [(x,) for x in sent[last]]
+    if middle:
+        ties[-1] += (column,)
+    update, got, _, _ = run(update, enter(update), ties)
+    for member in range(1, members):
         column = place(member, column)
-        if member == 0:
-            got, _ = lax.optimization_barrier((got, column))
 
     x = update
     x = jnp.where(plan.at_end(), got, x)
     pieces = [x] + [lax.ppermute(x, both, plan.offset_pairs(r)) for r in range(1, 1 << steps)]
-    x, _ = lax.optimization_barrier((jnp.concatenate(pieces), column))
+    x, _ = lax.optimization_barrier((jnp.concatenate(pieces), tuple(ends.values())))
     parts = [x] + [plan.swap(x, shift) for shift in range(1, lanes)]
     diagonal = pl.pallas_call(
         functools.partial(diagonal_kernel, plan),

time: 193 us -> 191 us (0.990)
  waiting for transfers between devices: 67.8 us -> 73.4 us
  local copies, waits for them, and re-layouts: 10.4 us -> 5.16 us
    ppermute x3, waiting for transfers between devices: 0.01 us -> 6.59 us  [shards(): lax.ppermute(x, both, plan.offset_pairs(r))]
    unnamed x48 -> x34, local copies, waits for them, and re-layouts: 8.26 us -> 3.78 us
    ppermute x6, waiting for transfers between devices: 2.66 us -> 0.02 us  [swap(): return lax.ppermute(x, 'row', pairs)]
  transfers between devices with their start and end apart: 34 -> 34, of which waited for: 16 -> 16; matrix products, arithmetic and copies ran while one was open for 10% -> 9% of each run, Pallas kernels for 14% -> 14%
where the time goes in v12:
time: 191 us; the launch traced here: 190 us
  waiting for transfers between devices  73.4 us (38%)
  starting transfers between devices  59.6 us (31%)
  Pallas kernels  32 us (17%)
  other arithmetic  19 us (10%)
  local copies, waits for them, and re-layouts  5.16 us (3%)
    ppermute x5, starting transfers between devices, enter(): return lax.ppermute(x, 'col', hops[0])  24.7 us
    ppermute x8, waiting for transfers between devices, issue(): out.append(lax.ppermute(x, axis, pairs))  24.2 us
    ppermute x10, waiting for transfers between devices, run(): got = lax.ppermute(y, 'col', hops[hop])  22.9 us
    ppermute x5, waiting for transfers between devices, enter(): return lax.ppermute(x, 'col', hops[0])  19.6 us
    ppermute x8, starting transfers between devices, issue(): out.append(lax.ppermute(x, axis, pairs))  18.9 us
    ppermute x10, starting transfers between devices, run(): got = lax.ppermute(y, 'col', hops[hop])  11.6 us
    pallas_call x2, Pallas kernels, forward(): pl.pallas_call(functools.partial(forward_kernel, plan, member), in_specs=...  10.1 us
    pallas_call x2, Pallas kernels, gather(): pl.pallas_call(functools.partial(gather_kernel, plan, member), in_specs=s...  9.27 us
  transfers between devices with their start and end apart: 34, of which 16 were waited for; matrix products, arithmetic and copies ran while one was open for 9% of the time, Pallas kernels for 14%

profile of v12, /device:TPU:0, one launch (start us, length us, event | category | flops | bytes accessed | tf_op | source)
XLA Modules:
  0.0 190.5 jit_solution(6584188224316218751)
XLA Ops:
  0.6 1.3 slice.19.factor
  2.0 5.8 %collective-permute-start.3 = (f32[512,512]{1,0:T(8,128)S(1)}, f32[512,512]{1,0:T(8,128)}, u32[]{:S(2)}, u32[]{:S(2)}) collective-permute-start(f32[512,512]{1,0:T(8,128)S(1)} %slice.19.factor), channel_id=1, source_target_pairs={{0,8},{4,20},{9,1},{13,29},{18,26}} | collective-permute-start | bytes 3145736 | tf_op jit(solution)/shard_map/ppermute | solution.py:156
  7.8 5.1 %gather_mirror.3 = (bf16[512,1024]{1,0:T(8,128)(2,1)S(1)}, bf16[512,1024]{1,0:T(8,128)(2,1)S(1)}, f32[512,512]{1,0:T(8,128)S(1)}, f32[512,512]{1,0:T(8,128)}) custom-call(s32[2,16]{1,0:T(2,128)S(1)} %copy-done.5, s32[2,16]{1,0:T(2,128)S(1)} %copy-done.6, f32[2048,4096]{1,0:T(8,128)} %front.3, f32[512,512]{1,0:T(8,128)S(1)} %slice.19.factor), custom_call_target="tpu_custom_call" | custom-call | flops 1677721600 | bytes 8388608 | tf_op jit(solution)/shard_map/gather_mirror/pallas_call | solution.py:333
  13.9 5.2 %collective-permute-done.3 = f32[512,512]{1,0:T(8,128)} collective-permute-done((f32[512,512]{1,0:T(8,128)S(1)}, f32[512,512]{1,0:T(8,128)}, u32[]{:S(2)}, u32[]{:S(2)}) %collective-permute-start.3) | collective-permute-done | bytes 1048608 | tf_op jit(solution)/shard_map/ppermute | solution.py:156
  19.1 1.9 broadcast_select_fusion.1
  21.0 1.4 collective-permute-start.4
  22.4 1.4 add.90
  23.8 1.3 collective-permute-start.2
  25.1 4.1 %gather_mirror.2 = (bf16[512,1024]{1,0:T(8,128)(2,1)S(1)}, bf16[512,1024]{1,0:T(8,128)(2,1)S(1)}, f32[512,512]{1,0:T(8,128)S(1)}, f32[512,512]{1,0:T(8,128)S(1)}) custom-call(s32[2,16]{1,0:T(2,128)S(1)} %copy-done.5, s32[2,16]{1,0:T(2,128)S(1)} %copy-done.6, f32[2048,4096]{1,0:T(8,128)} %front.3, f32[512,512]{1,0:T(8,128)S(1)} %get-tuple-element.50.factor), custom_call_target="tpu_custom_call" | custom-call | flops 1677721600 | bytes 8388608 | tf_op jit(solution)/shard_map/gather_mirror/pallas_call | solution.py:333
  29.3 5.3 %collective-permute-done.4 = f32[512,512]{1,0:T(8,128)S(1)} collective-permute-done((f32[512,512]{1,0:T(8,128)S(1)}, f32[512,512]{1,0:T(8,128)S(1)}, u32[]{:S(2)}, u32[]{:S(2)}) %collective-permute-start.4) | collective-permute-done | bytes 1048608 | tf_op jit(solution)/shard_map/ppermute | solution.py:156
  34.9 4.9 %collective-permute-start.8 = (f32[512,512]{1,0:T(8,128)S(1)}, f32[512,512]{1,0:T(8,128)S(1)}, u32[]{:S(2)}, u32[]{:S(2)}) collective-permute-start(f32[512,512]{1,0:T(8,128)S(1)} %get-tuple-element.50.factor), channel_id=1, source_target_pairs={{0,8},{4,20},{9,1},{13,29},{18,26}} | collective-permute-start | bytes 3145736 | tf_op jit(solution)/shard_map/ppermute | solution.py:156
  40.7 1.4 collective-permute-start.6
  43.4 4.8 %forward.2 = (f32[256,512]{1,0:T(8,128)S(1)}, f32[256,512]{1,0:T(8,128)S(1)}, f32[256,512]{1,0:T(8,128)S(1)}, f32[256,512]{1,0:T(8,128)S(1)}) custom-call(bf16[512,1024]{1,0:T(8,128)(2,1)S(1)} %get-tuple-element.43.high, bf16[512,1024]{1,0:T(8,128)(2,1)S(1)} %copy-done.4, f32[512,512]{1,0:T(8,128)S(1)} %slice.19.factor, f32[512,512]{1,0:T(8,128)} %copy-done.11, ...), custom_call_target="tpu_custom_call" | custom-call | flops 1677721600 | bytes 8388608 | tf_op jit(solution)/shard_map/forward/pallas_call | solution.py:351
  48.2 3.8 %collective-permute-done.8 = f32[512,512]{1,0:T(8,128)S(1)} collective-permute-done((f32[512,512]{1,0:T(8,128)S(1)}, f32[512,512]{1,0:T(8,128)S(1)}, u32[]{:S(2)}, u32[]{:S(2)}) %collective-permute-start.8) | collective-permute-done | bytes 1048608 | tf_op jit(solution)/shard_map/ppermute | solution.py:156
  52.2 5.5 %collective-permute-done.6 = f32[512,512]{1,0:T(8,128)S(1)} collective-permute-done((f32[512,512]{1,0:T(8,128)S(1)}, f32[512,512]{1,0:T(8,128)S(1)}, u32[]{:S(2)}, u32[]{:S(2)}) %collective-permute-start.6) | collective-permute-done | bytes 1048608 | tf_op jit(solution)/shard_map/ppermute | solution.py:156
  58.8 1.3 collective-permute-start.9
  60.1 1.3 collective-permute-start.10
  61.4 1.6 collective-permute-start.7
  63.0 9.3 %collective-permute-done.7 = f32[256,512]{1,0:T(8,128)S(1)} collective-permute-done((f32[256,512]{1,0:T(8,128)S(1)}, f32[256,512]{1,0:T(8,128)S(1)}, u32[]{:S(2)}, u32[]{:S(2)}) %collective-permute-start.7) | collective-permute-done | bytes 524320 | tf_op jit(solution)/shard_map/ppermute | solution.py:372
  73.2 3.7 %collective-permute-done.10 = f32[512,512]{1,0:T(8,128)S(1)} collective-permute-done((f32[512,512]{1,0:T(8,128)S(1)}, f32[512,512]{1,0:T(8,128)S(1)}, u32[]{:S(2)}, u32[]{:S(2)}) %collective-permute-start.10) | collective-permute-done | bytes 1048608 | tf_op jit(solution)/shard_map/ppermute | solution.py:156
  78.4 1.5 collective-permute-start.12
  80.8 5.3 %forward.3 = (f32[256,512]{1,0:T(8,128)S(1)}, f32[256,512]{1,0:T(8,128)S(1)}, f32[512,512]{1,0:T(8,128)S(1)}, f32[512,512]{1,0:T(8,128)S(1)}) custom-call(bf16[512,1024]{1,0:T(8,128)(2,1)S(1)} %get-tuple-element.39.high, bf16[512,1024]{1,0:T(8,128)(2,1)} %copy-done.2, f32[512,512]{1,0:T(8,128)} %copy-done.1, f32[512,512]{1,0:T(8,128)} %add.95.mirror, ...), custom_call_target="tpu_custom_call" | custom-call | flops 1677721600 | bytes 8388608 | tf_op jit(solution)/shard_map/forward/pallas_call | solution.py:351
  86.7 5.8 %collective-permute-start.15 = (f32[256,512]{1,0:T(8,128)}, f32[256,512]{1,0:T(8,128)}, u32[]{:S(2)}, u32[]{:S(2)}) collective-permute-start(f32[256,512]{1,0:T(8,128)} %get-tuple-element.61), channel_id=1, source_target_pairs={{0,1},{3,2},{4,5},{7,6},{8,9},{11,10},{12,13},{15,14},{16,17},{19,... | collective-permute-start | bytes 1572872 | tf_op jit(solution)/shard_map/ppermute | solution.py:372
  92.4 2.1 %add.99 = f32[256,512]{1,0:T(8,128)} add(f32[256,512]{1,0:T(8,128)} %copy-done.13, f32[256,512]{1,0:T(8,128)} %copy-done.16) | non-fusion elementwise | flops 131072 | bytes 1572864 | tf_op jit(solution)/shard_map/add | solution.py:101
  94.5 1.5 collective-permute-start.14
  96.0 2.4 %slice_add_fusion = (f32[256,512]{1,0:T(8,128)}, f32[256,512]{1,0:T(8,128)}) fusion(f32[256,512]{1,0:T(8,128)S(1)} %get-tuple-element.66, f32[512,512]{1,0:T(8,128)} %collective-permute-done.12, f32[256,512]{1,0:T(8,128)S(1)} %get-tuple-element.58), kind=kLoop, calls=%fused_computation.1 | loop fusion | flops 262144 | bytes 3145728 | tf_op jit(solution)/shard_map/add | solution.py:423
  98.4 2.1 %collective-permute-start.13 = (f32[256,512]{1,0:T(8,128)}, f32[256,512]{1,0:T(8,128)}, u32[]{:S(2)}, u32[]{:S(2)}) collective-permute-start(f32[256,512]{1,0:T(8,128)} %get-tuple-element.79), channel_id=1, source_target_pairs={{0,1},{3,2},{4,5},{7,6},{8,9},{11,10},{12,13},{15,14},{16,17},{19,... | collective-permute-start | bytes 1572872 | tf_op jit(solution)/shard_map/ppermute | solution.py:372
  100.5 3.7 %collective-permute-done.15 = f32[256,512]{1,0:T(8,128)} collective-permute-done((f32[256,512]{1,0:T(8,128)}, f32[256,512]{1,0:T(8,128)}, u32[]{:S(2)}, u32[]{:S(2)}) %collective-permute-start.15) | collective-permute-done | bytes 524320 | tf_op jit(solution)/shard_map/ppermute | solution.py:372
  105.5 1.5 collective-permute-start.18
  106.9 1.5 add.107
  109.8 1.3 collective-permute-start.16
  111.2 13.8 %collective-permute-start.21 = (f32[256,512]{1,0:T(8,128)S(1)}, f32[256,512]{1,0:T(8,128)S(1)}, u32[]{:S(2)}, u32[]{:S(2)}) collective-permute-start(f32[256,512]{1,0:T(8,128)S(1)} %copy-done.12), channel_id=1, source_target_pairs={{0,1},{3,2},{4,5},{7,6},{8,9},{11,10},{12,13},{15,14},{16,17},{19,... | collective-permute-start | bytes 1572872 | tf_op jit(solution)/shard_map/ppermute | solution.py:372
  126.2 1.3 collective-permute-start.19
  129.8 4.8 %collective-permute-done.21 = f32[256,512]{1,0:T(8,128)S(1)} collective-permute-done((f32[256,512]{1,0:T(8,128)S(1)}, f32[256,512]{1,0:T(8,128)S(1)}, u32[]{:S(2)}, u32[]{:S(2)}) %collective-permute-start.21) | collective-permute-done | bytes 524320 | tf_op jit(solution)/shard_map/ppermute | solution.py:372
  134.8 5.2 %collective-permute-done.19.rest_3_ = f32[256,512]{1,0:T(8,128)S(1)} collective-permute-done((f32[256,512]{1,0:T(8,128)S(1)}, f32[256,512]{1,0:T(8,128)S(1)}, u32[]{:S(2)}, u32[]{:S(2)}) %collective-permute-start.19) | collective-permute-done | bytes 524320 | tf_op jit(solution)/shard_map/ppermute | solution.py:381
  140.0 1.5 collective-permute-start.27
  142.3 1.3 collective-permute-start.20
  143.6 1.8 collective-permute-done.27
  146.1 4.3 %place.2.rest_4_ = f32[2048,1024]{1,0:T(8,128)} custom-call(s32[2,16]{1,0:T(2,128)S(1)} %copy-done.5, f32[2,512,512]{2,1,0:T(8,128)S(1)} %copy-done, f32[256,512]{1,0:T(8,128)S(1)} %add.100.rest_0_, f32[256,512]{1,0:T(8,128)S(1)} %collective-permute-done.16.rest_1_, f32[256,512]{1,0:T(8,128)S(1)} %add.103.rest_2_, f32[256,512]{1,0:T(8,128)S(1)} %collective-permute-done.19.rest_3_), custom_call_target="tpu_custom_call" | custom-call | flops 1677721600 | bytes 8388608 | tf_op jit(solution)/shard_map/place/pallas_call | solution.py:441
  150.6 1.3 collective-permute-start.29
  151.9 4.8 %collective-permute-done.20.rest_1_ = f32[256,512]{1,0:T(8,128)} collective-permute-done((f32[256,512]{1,0:T(8,128)S(1)}, f32[256,512]{1,0:T(8,128)}, u32[]{:S(2)}, u32[]{:S(2)}) %collective-permute-start.20) | collective-permute-done | bytes 524320 | tf_op jit(solution)/shard_map/ppermute | solution.py:381
  158.0 12.9 %collective-permute-done.29 = f32[128,512]{1,0:T(8,128)} collective-permute-done((f32[128,512]{1,0:T(8,128)S(1)}, f32[128,512]{1,0:T(8,128)}, u32[]{:S(2)}, u32[]{:S(2)}) %collective-permute-start.29) | collective-permute-done | bytes 262176 | tf_op jit(solution)/shard_map/ppermute | solution.py:381
  171.9 1.8 collective-permute-start.31
  173.7 1.7 collective-permute-start.30
  175.4 3.9 %collective-permute-done.32 = f32[128,512]{1,0:T(8,128)S(1)} collective-permute-done((f32[128,512]{1,0:T(8,128)S(1)}, f32[128,512]{1,0:T(8,128)S(1)}, u32[]{:S(2)}, u32[]{:S(2)}) %collective-permute-start.32) | collective-permute-done | bytes 262176 | tf_op jit(solution)/shard_map/ppermute | solution.py:485
  179.3 1.5 collective-permute-done.31
  182.1 3.2 %place.3 = f32[2048,1024]{1,0:T(8,128)} custom-call(s32[2,16]{1,0:T(2,128)S(1)} %copy-done.5, f32[2,512,512]{2,1,0:T(8,128)S(1)} %copy-done, f32[256,512]{1,0:T(8,128)S(1)} %add.101.rest_0_, f32[256,512]{1,0:T(8,128)} %collective-permute-done.20.rest_1_, f32[256,512]{1,0:T(8,128)S(1)} %add.106.rest_2_, ...), custom_call_target="tpu_custom_call", output_to_operand_aliasing={{}: (6, {})} | custom-call | flops 1677721600 | bytes 8388608 | tf_op jit(solution)/shard_map/place/pallas_call | solution.py:441
  185.4 5.1 %diagonal.1 = f32[2,512,512]{2,1,0:T(8,128)} custom-call(f32[2,512]{1,0:T(2,128)S(1)} %copy-done.7, f32[2,512,512]{2,1,0:T(8,128)S(1)} %copy-done, f32[512,512]{1,0:T(8,128)S(1)} %pad_maximum_fusion.rest_0_, f32[512,512]{1,0:T(8,128)S(1)} %collective-permute-done.33.rest_1_), custom_call_target="tpu_custom_call" | custom-call | flops 1677721600 | bytes 8388608 | tf_op jit(solution)/shard_map/diagonal/pallas_call | solution.py:488
  (89 shorter events, 20.0 us)
Async XLA Ops:
  0.6 7.2 %copy-start.5 = (s32[2,16]{1,0:T(2,128)S(1)}, s32[2,16]{1,0:T(2,128)}, u32[]{:S(2)}) copy-start(s32[2,16]{1,0:T(2,128)} %tiles_ref.7) | copy-start | bytes 388
  0.6 7.2 %copy-start.6 = (s32[2,16]{1,0:T(2,128)S(1)}, s32[2,16]{1,0:T(2,128)}, u32[]{:S(2)}) copy-start(s32[2,16]{1,0:T(2,128)} %valid_ref.3) | copy-start | bytes 388
  2.0 17.2 %collective-permute-start.3 = (f32[512,512]{1,0:T(8,128)S(1)}, f32[512,512]{1,0:T(8,128)}, u32[]{:S(2)}, u32[]{:S(2)}) collective-permute-start(f32[512,512]{1,0:T(8,128)S(1)} %slice.19.factor), channel_id=1, source_target_pairs={{0,8},{4,20},{9,1},{13,29},{18,26}} | collective-permute-start | bytes 3145736 | tf_op jit(solution)/shard_map/ppermute | solution.py:156
  12.9 1.0 copy-start.3
  13.9 8.4 %collective-permute-start.1 = (f32[512,512]{1,0:T(8,128)}, f32[512,512]{1,0:T(8,128)}, u32[]{:S(2)}, u32[]{:S(2)}) collective-permute-start(f32[512,512]{1,0:T(8,128)} %get-tuple-element.46), channel_id=1, source_target_pairs={{4,0},{0,4},{12,8},{8,12},{20,16},{16,20},{28,24},{24,28},{5,1},{1... | collective-permute-start | bytes 3145736 | tf_op jit(solution)/shard_map/ppermute | solution.py:88
  21.0 13.9 %copy-start.1 = (f32[512,512]{1,0:T(8,128)}, f32[512,512]{1,0:T(8,128)S(1)}, u32[]{:S(2)}) copy-start(f32[512,512]{1,0:T(8,128)S(1)} %get-tuple-element.50.factor) | copy-start | bytes 3145732
  21.0 13.6 %collective-permute-start.4 = (f32[512,512]{1,0:T(8,128)S(1)}, f32[512,512]{1,0:T(8,128)S(1)}, u32[]{:S(2)}, u32[]{:S(2)}) collective-permute-start(f32[512,512]{1,0:T(8,128)S(1)} %get-tuple-element.47), channel_id=1, source_target_pairs={{0,16},{8,24},{4,12},{20,28},{9,25},{1,17},{29,21},{22,30}} | collective-permute-start | bytes 3145736 | tf_op jit(solution)/shard_map/ppermute | solution.py:156
  23.8 16.7 %collective-permute-start.2 = (f32[512,512]{1,0:T(8,128)S(1)}, f32[512,512]{1,0:T(8,128)S(1)}, u32[]{:S(2)}, u32[]{:S(2)}) collective-permute-start(f32[512,512]{1,0:T(8,128)S(1)} %add.90), channel_id=1, source_target_pairs={{16,0},{24,8},{12,4},{28,20},{25,9},{17,1},{21,29},{30,22}} | collective-permute-start | bytes 3145736 | tf_op jit(solution)/shard_map/ppermute | solution.py:156
  29.2 11.5 %copy-start.2 = (bf16[512,1024]{1,0:T(8,128)(2,1)}, bf16[512,1024]{1,0:T(8,128)(2,1)S(1)}, u32[]{:S(2)}) copy-start(bf16[512,1024]{1,0:T(8,128)(2,1)S(1)} %get-tuple-element.40.low) | copy-start | bytes 3145732
  29.2 12.9 %collective-permute-start = (f32[512,512]{1,0:T(8,128)S(1)}, f32[512,512]{1,0:T(8,128)S(1)}, u32[]{:S(2)}, u32[]{:S(2)}) collective-permute-start(f32[512,512]{1,0:T(8,128)S(1)} %get-tuple-element.42), channel_id=1, source_target_pairs={{4,0},{0,4},{12,8},{8,12},{20,16},{16,20},{28,24},{24,28},{5,1},{1... | collective-permute-start | bytes 3145736 | tf_op jit(solution)/shard_map/ppermute | solution.py:88
  34.8 7.6 %copy-start.10 = (f32[512,512]{1,0:T(8,128)}, f32[512,512]{1,0:T(8,128)S(1)}, u32[]{:S(2)}) copy-start(f32[512,512]{1,0:T(8,128)S(1)} %add.92.rest_0_) | copy-start | bytes 3145732
  34.8 7.6 %collective-permute-start.5 = (f32[512,512]{1,0:T(8,128)S(1)}, f32[512,512]{1,0:T(8,128)S(1)}, u32[]{:S(2)}, u32[]{:S(2)}) collective-permute-start(f32[512,512]{1,0:T(8,128)S(1)} %add.92.rest_0_), channel_id=1, source_target_pairs={{4,0},{0,4},{12,8},{8,12},{20,16},{16,20},{28,24},{24,28},{5,1},{1... | collective-permute-start | bytes 3145736 | tf_op jit(solution)/shard_map/ppermute | solution.py:88
  34.9 17.1 %collective-permute-start.8 = (f32[512,512]{1,0:T(8,128)S(1)}, f32[512,512]{1,0:T(8,128)S(1)}, u32[]{:S(2)}, u32[]{:S(2)}) collective-permute-start(f32[512,512]{1,0:T(8,128)S(1)} %get-tuple-element.50.factor), channel_id=1, source_target_pairs={{0,8},{4,20},{9,1},{13,29},{18,26}} | collective-permute-start | bytes 3145736 | tf_op jit(solution)/shard_map/ppermute | solution.py:156
  40.7 2.7 %copy-start.11 = (f32[512,512]{1,0:T(8,128)}, f32[512,512]{1,0:T(8,128)S(1)}, u32[]{:S(2)}) copy-start(f32[512,512]{1,0:T(8,128)S(1)} %add.91.mirror) | copy-start | bytes 3145732
  40.7 2.7 %copy-start.4 = (bf16[512,1024]{1,0:T(8,128)(2,1)S(1)}, bf16[512,1024]{1,0:T(8,128)(2,1)}, u32[]{:S(2)}) copy-start(bf16[512,1024]{1,0:T(8,128)(2,1)} %copy-done.3) | copy-start | bytes 3145732
  40.7 17.1 %collective-permute-start.6 = (f32[512,512]{1,0:T(8,128)S(1)}, f32[512,512]{1,0:T(8,128)S(1)}, u32[]{:S(2)}, u32[]{:S(2)}) collective-permute-start(f32[512,512]{1,0:T(8,128)S(1)} %add.91.mirror), channel_id=1, source_target_pairs={{8,0},{20,4},{1,9},{29,13},{26,18}} | collective-permute-start | bytes 3145736 | tf_op jit(solution)/shard_map/ppermute | solution.py:156
  43.4 8.7 %copy-start.8 = (f32[512,1024]{1,0:T(8,128)S(1)}, f32[512,1024]{1,0:T(8,128)}, u32[]{:S(2)}) copy-start(f32[512,1024]{1,0:T(8,128)} %param.7) | copy-start | bytes 6291460
  58.8 13.6 %copy-start.13 = (f32[256,512]{1,0:T(8,128)}, f32[256,512]{1,0:T(8,128)S(1)}, u32[]{:S(2)}) copy-start(f32[256,512]{1,0:T(8,128)S(1)} %get-tuple-element.81) | copy-start | bytes 1572868
  58.8 13.6 %collective-permute-start.9 = (f32[512,512]{1,0:T(8,128)S(1)}, f32[512,512]{1,0:T(8,128)S(1)}, u32[]{:S(2)}, u32[]{:S(2)}) collective-permute-start(f32[512,512]{1,0:T(8,128)S(1)} %broadcast_select_fusion), channel_id=1, source_target_pairs={{0,16},{8,24},{4,12},{20,28},{9,25},{1,17},{29,21},{22,30}} | collective-permute-start | bytes 3145736 | tf_op jit(solution)/shard_map/ppermute | solution.py:156
  60.1 16.7 %collective-permute-start.10 = (f32[512,512]{1,0:T(8,128)S(1)}, f32[512,512]{1,0:T(8,128)S(1)}, u32[]{:S(2)}, u32[]{:S(2)}) collective-permute-start(f32[512,512]{1,0:T(8,128)S(1)} %add.89), channel_id=1, source_target_pairs={{16,0},{24,8},{12,4},{28,20},{25,9},{17,1},{21,29},{30,22}} | collective-permute-start | bytes 3145736 | tf_op jit(solution)/shard_map/ppermute | solution.py:156
  61.4 10.9 %collective-permute-start.7 = (f32[256,512]{1,0:T(8,128)S(1)}, f32[256,512]{1,0:T(8,128)S(1)}, u32[]{:S(2)}, u32[]{:S(2)}) collective-permute-start(f32[256,512]{1,0:T(8,128)S(1)} %get-tuple-element.81), channel_id=1, source_target_pairs={{0,1},{3,2},{4,5},{7,6},{8,9},{11,10},{12,13},{15,14},{16,17},{19,... | collective-permute-start | bytes 1572872 | tf_op jit(solution)/shard_map/ppermute | solution.py:372
  77.0 2.8 %copy-start.9 = (f32[512,512]{1,0:T(8,128)}, f32[512,512]{1,0:T(8,128)S(1)}, u32[]{:S(2)}) copy-start(f32[512,512]{1,0:T(8,128)S(1)} %add.96.rest_0_) | copy-start | bytes 3145732
  77.1 2.8 %collective-permute-start.11 = (f32[512,512]{1,0:T(8,128)S(1)}, f32[512,512]{1,0:T(8,128)S(1)}, u32[]{:S(2)}, u32[]{:S(2)}) collective-permute-start(f32[512,512]{1,0:T(8,128)S(1)} %add.96.rest_0_), channel_id=1, source_target_pairs={{4,0},{0,4},{12,8},{8,12},{20,16},{16,20},{28,24},{24,28},{5,1},{1... | collective-permute-start | bytes 3145736 | tf_op jit(solution)/shard_map/ppermute | solution.py:88
  78.4 17.6 %collective-permute-start.12 = (f32[512,512]{1,0:T(8,128)}, f32[512,512]{1,0:T(8,128)}, u32[]{:S(2)}, u32[]{:S(2)}) collective-permute-start(f32[512,512]{1,0:T(8,128)} %add.95.mirror), channel_id=1, source_target_pairs={{8,0},{20,4},{1,9},{29,13},{26,18}} | collective-permute-start | bytes 3145736 | tf_op jit(solution)/shard_map/ppermute | solution.py:156
  86.2 20.8 %collective-permute-start.24 = (f32[512,512]{1,0:T(8,128)S(1)}, f32[512,512]{1,0:T(8,128)}, u32[]{:S(2)}, u32[]{:S(2)}) collective-permute-start(f32[512,512]{1,0:T(8,128)S(1)} %get-tuple-element.71), channel_id=1, source_target_pairs={{4,0},{0,4},{12,8},{8,12},{20,16},{16,20},{28,24},{24,28},{5,1},{1... | collective-permute-start | bytes 3145736 | tf_op jit(solution)/shard_map/ppermute | solution.py:88
  86.7 17.5 %collective-permute-start.15 = (f32[256,512]{1,0:T(8,128)}, f32[256,512]{1,0:T(8,128)}, u32[]{:S(2)}, u32[]{:S(2)}) collective-permute-start(f32[256,512]{1,0:T(8,128)} %get-tuple-element.61), channel_id=1, source_target_pairs={{0,1},{3,2},{4,5},{7,6},{8,9},{11,10},{12,13},{15,14},{16,17},{19,... | collective-permute-start | bytes 1572872 | tf_op jit(solution)/shard_map/ppermute | solution.py:372
  94.5 14.0 %collective-permute-start.14 = (f32[256,512]{1,0:T(8,128)}, f32[256,512]{1,0:T(8,128)}, u32[]{:S(2)}, u32[]{:S(2)}) collective-permute-start(f32[256,512]{1,0:T(8,128)} %add.99), channel_id=1, source_target_pairs={{1,2},{2,1},{5,6},{6,5},{9,10},{10,9},{13,14},{14,13},{17,18},{18,... | collective-permute-start | bytes 1572872 | tf_op jit(solution)/shard_map/ppermute | solution.py:381
  98.4 27.8 %collective-permute-start.13 = (f32[256,512]{1,0:T(8,128)}, f32[256,512]{1,0:T(8,128)}, u32[]{:S(2)}, u32[]{:S(2)}) collective-permute-start(f32[256,512]{1,0:T(8,128)} %get-tuple-element.79), channel_id=1, source_target_pairs={{0,1},{3,2},{4,5},{7,6},{8,9},{11,10},{12,13},{15,14},{16,17},{19,... | collective-permute-start | bytes 1572872 | tf_op jit(solution)/shard_map/ppermute | solution.py:372
  105.5 5.7 %collective-permute-start.18 = (f32[256,512]{1,0:T(8,128)S(1)}, f32[256,512]{1,0:T(8,128)}, u32[]{:S(2)}, u32[]{:S(2)}) collective-permute-start(f32[256,512]{1,0:T(8,128)S(1)} %add.102), channel_id=1, source_target_pairs={{1,2},{2,1},{5,6},{6,5},{9,10},{10,9},{13,14},{14,13},{17,18},{18,... | collective-permute-start | bytes 1572872 | tf_op jit(solution)/shard_map/ppermute | solution.py:381
  108.4 2.8 %copy-start.12 = (f32[256,512]{1,0:T(8,128)S(1)}, f32[256,512]{1,0:T(8,128)}, u32[]{:S(2)}) copy-start(f32[256,512]{1,0:T(8,128)} %get-tuple-element.67) | copy-start | bytes 1572868
  108.5 19.0 %collective-permute-start.25 = (f32[256,512]{1,0:T(8,128)S(1)}, f32[256,512]{1,0:T(8,128)S(1)}, u32[]{:S(2)}, u32[]{:S(2)}) collective-permute-start(f32[256,512]{1,0:T(8,128)S(1)} %dynamic-slice_bitcast_fusion), channel_id=1, source_target_pairs={{0,8},{1,9},{2,10},{3,11},{4,20},{5,21},{6,22},{7,23},{8,0},{9,1},... | collective-permute-start | bytes 1572872 | tf_op jit(solution)/shard_map/ppermute | solution.py:433
  109.8 19.1 %collective-permute-start.16 = (f32[256,512]{1,0:T(8,128)S(1)}, f32[256,512]{1,0:T(8,128)S(1)}, u32[]{:S(2)}, u32[]{:S(2)}) collective-permute-start(f32[256,512]{1,0:T(8,128)S(1)} %add.100.rest_0_), channel_id=1, source_target_pairs={{1,0},{2,3},{5,4},{6,7},{9,8},{10,11},{13,12},{14,15},{17,16},{18,... | collective-permute-start | bytes 1572872 | tf_op jit(solution)/shard_map/ppermute | solution.py:381
  111.2 23.5 %collective-permute-start.21 = (f32[256,512]{1,0:T(8,128)S(1)}, f32[256,512]{1,0:T(8,128)S(1)}, u32[]{:S(2)}, u32[]{:S(2)}) collective-permute-start(f32[256,512]{1,0:T(8,128)S(1)} %copy-done.12), channel_id=1, source_target_pairs={{0,1},{3,2},{4,5},{7,6},{8,9},{11,10},{12,13},{15,14},{16,17},{19,... | collective-permute-start | bytes 1572872 | tf_op jit(solution)/shard_map/ppermute | solution.py:372
  126.2 13.8 %collective-permute-start.19 = (f32[256,512]{1,0:T(8,128)S(1)}, f32[256,512]{1,0:T(8,128)S(1)}, u32[]{:S(2)}, u32[]{:S(2)}) collective-permute-start(f32[256,512]{1,0:T(8,128)S(1)} %add.103.rest_2_), channel_id=1, source_target_pairs={{1,0},{2,3},{5,4},{6,7},{9,8},{10,11},{13,12},{14,15},{17,16},{18,... | collective-permute-start | bytes 1572872 | tf_op jit(solution)/shard_map/ppermute | solution.py:381
  127.6 12.4 %collective-permute-start.26 = (f32[128,512]{1,0:T(8,128)S(1)}, f32[128,512]{1,0:T(8,128)S(1)}, u32[]{:S(2)}, u32[]{:S(2)}) collective-permute-start(f32[128,512]{1,0:T(8,128)S(1)} %dynamic-slice_bitcast_fusion.1), channel_id=1, source_target_pairs={{0,16},{1,17},{2,18},{3,19},{4,12},{5,13},{6,14},{7,15},{8,24},{9,... | collective-permute-start | bytes 786440 | tf_op jit(solution)/shard_map/ppermute | solution.py:433
  129.0 17.1 %copy-start = (f32[2,512,512]{2,1,0:T(8,128)S(1)}, f32[2,512,512]{2,1,0:T(8,128)}, u32[]{:S(2)}) copy-start(f32[2,512,512]{2,1,0:T(8,128)} %unit_ref.5) | copy-start | bytes 6291460
  129.0 13.2 %collective-permute-start.17 = (f32[256,512]{1,0:T(8,128)S(1)}, f32[256,512]{1,0:T(8,128)S(1)}, u32[]{:S(2)}, u32[]{:S(2)}) collective-permute-start(f32[256,512]{1,0:T(8,128)S(1)} %add.98), channel_id=1, source_target_pairs={{1,2},{2,1},{5,6},{6,5},{9,10},{10,9},{13,14},{14,13},{17,18},{18,... | collective-permute-start | bytes 1572872 | tf_op jit(solution)/shard_map/ppermute | solution.py:381
  140.0 5.3 %collective-permute-start.27 = (f32[128,512]{1,0:T(8,128)S(1)}, f32[128,512]{1,0:T(8,128)S(1)}, u32[]{:S(2)}, u32[]{:S(2)}) collective-permute-start(f32[128,512]{1,0:T(8,128)S(1)} %bitcast_add_fusion.1), channel_id=1, source_target_pairs={{0,1},{3,2},{4,5},{7,6},{8,9},{11,10},{12,13},{15,14},{16,17},{19,... | collective-permute-start | bytes 786440 | tf_op jit(solution)/shard_map/ppermute | solution.py:372
  141.5 8.9 %collective-permute-start.22 = (f32[256,512]{1,0:T(8,128)S(1)}, f32[256,512]{1,0:T(8,128)S(1)}, u32[]{:S(2)}, u32[]{:S(2)}) collective-permute-start(f32[256,512]{1,0:T(8,128)S(1)} %add.105), channel_id=1, source_target_pairs={{1,2},{2,1},{5,6},{6,5},{9,10},{10,9},{13,14},{14,13},{17,18},{18,... | collective-permute-start | bytes 1572872 | tf_op jit(solution)/shard_map/ppermute | solution.py:381
  142.3 14.4 %collective-permute-start.20 = (f32[256,512]{1,0:T(8,128)S(1)}, f32[256,512]{1,0:T(8,128)}, u32[]{:S(2)}, u32[]{:S(2)}) collective-permute-start(f32[256,512]{1,0:T(8,128)S(1)} %add.101.rest_0_), channel_id=1, source_target_pairs={{1,0},{2,3},{5,4},{6,7},{9,8},{10,11},{13,12},{14,15},{17,16},{18,... | collective-permute-start | bytes 1572872 | tf_op jit(solution)/shard_map/ppermute | solution.py:381
  145.4 5.1 %collective-permute-start.28 = (f32[128,512]{1,0:T(8,128)S(1)}, f32[128,512]{1,0:T(8,128)S(1)}, u32[]{:S(2)}, u32[]{:S(2)}) collective-permute-start(f32[128,512]{1,0:T(8,128)S(1)} %add.113), channel_id=1, source_target_pairs={{1,2},{2,1},{5,6},{6,5},{9,10},{10,9},{13,14},{14,13},{17,18},{18,... | collective-permute-start | bytes 786440 | tf_op jit(solution)/shard_map/ppermute | solution.py:381
  150.6 20.2 %collective-permute-start.29 = (f32[128,512]{1,0:T(8,128)S(1)}, f32[128,512]{1,0:T(8,128)}, u32[]{:S(2)}, u32[]{:S(2)}) collective-permute-start(f32[128,512]{1,0:T(8,128)S(1)} %add.114), channel_id=1, source_target_pairs={{1,0},{2,3},{5,4},{6,7},{9,8},{10,11},{13,12},{14,15},{17,16},{18,... | collective-permute-start | bytes 786440 | tf_op jit(solution)/shard_map/ppermute | solution.py:381
  156.7 25.4 %collective-permute-start.23 = (f32[256,512]{1,0:T(8,128)S(1)}, f32[256,512]{1,0:T(8,128)S(1)}, u32[]{:S(2)}, u32[]{:S(2)}) collective-permute-start(f32[256,512]{1,0:T(8,128)S(1)} %add.106.rest_2_), channel_id=1, source_target_pairs={{1,0},{2,3},{5,4},{6,7},{9,8},{10,11},{13,12},{14,15},{17,16},{18,... | collective-permute-start | bytes 1572872 | tf_op jit(solution)/shard_map/ppermute | solution.py:381
  171.8 7.4 %collective-permute-start.32 = (f32[128,512]{1,0:T(8,128)S(1)}, f32[128,512]{1,0:T(8,128)S(1)}, u32[]{:S(2)}, u32[]{:S(2)}) collective-permute-start(f32[128,512]{1,0:T(8,128)S(1)} %broadcast_select_fusion.2), channel_id=1, source_target_pairs={{0,24},{1,25},{2,26},{3,27},{8,16},{9,17},{10,18},{11,19},{16,8},{... | collective-permute-start | bytes 786440 | tf_op jit(solution)/shard_map/ppermute | solution.py:485
  171.9 8.9 %collective-permute-start.31 = (f32[128,512]{1,0:T(8,128)S(1)}, f32[128,512]{1,0:T(8,128)S(1)}, u32[]{:S(2)}, u32[]{:S(2)}) collective-permute-start(f32[128,512]{1,0:T(8,128)S(1)} %broadcast_select_fusion.2), channel_id=1, source_target_pairs={{0,8},{1,9},{2,10},{3,11},{8,0},{9,1},{10,2},{11,3},{16,24},{17,25... | collective-permute-start | bytes 786440 | tf_op jit(solution)/shard_map/ppermute | solution.py:485
  173.7 8.3 %collective-permute-start.30 = (f32[128,512]{1,0:T(8,128)S(1)}, f32[128,512]{1,0:T(8,128)S(1)}, u32[]{:S(2)}, u32[]{:S(2)}) collective-permute-start(f32[128,512]{1,0:T(8,128)S(1)} %broadcast_select_fusion.2), channel_id=1, source_target_pairs={{0,16},{1,17},{2,18},{3,19},{8,24},{9,25},{10,26},{11,27},{16,0},{... | collective-permute-start | bytes 786440 | tf_op jit(solution)/shard_map/ppermute | solution.py:485
  182.0 3.3 %copy-start.7 = (f32[2,512]{1,0:T(2,128)S(1)}, f32[2,512]{1,0:T(2,128)}, u32[]{:S(2)}) copy-start(f32[2,512]{1,0:T(2,128)} %pivot.1) | copy-start | bytes 12292
  182.1 3.3 %collective-permute-start.33 = (f32[512,512]{1,0:T(8,128)S(1)}, f32[512,512]{1,0:T(8,128)S(1)}, u32[]{:S(2)}, u32[]{:S(2)}) collective-permute-start(f32[512,512]{1,0:T(8,128)S(1)} %pad_maximum_fusion.rest_0_), channel_id=1, source_target_pairs={{4,0},{0,4},{12,8},{8,12},{20,16},{16,20},{28,24},{24,28},{5,1},{1... | collective-permute-start | bytes 3145736 | tf_op jit(solution)/shard_map/ppermute | solution.py:88
  (3 other events, 2.8 us)

commit v13 on v12

--- a/solution.py
+++ b/solution.py
@@ -264,7 +264,12 @@
     share = plan.depth // splits
     for i in range(splits):
         x = jnp.where(at_end, sums[2 * i + 1][...], sums[2 * i][...])
-        stack[i * share:(i + 1) * share, :] = -product(split(x), right)
+        left, part = split(x), width // 2
+        rows = slice(i * share, (i + 1) * share)
+        stack[rows, :part] = -product(left, tuple(y[:, :part] for y in right))
+        stack[rows, part:] = -product(
+            tuple(y[:, part:] for y in left), tuple(y[part:, part:] for y in right)
+        )
     copies = []
     for a in range(plan.na):
         t = jnp.clip(
@@ -309,8 +314,17 @@
         x = jnp.concatenate([cross[other, rows, :] for other in range(lanes)])
         x = jnp.where(row == col, pivot[member:member + 1, :], 0.0) + x + x.T
         inverse = split(unit_inverse(unit_ref, member))
-        half = product(split(x), inverse)
-        out[member] = product(inverse, split(half), contract=0)
+        left, part = split(x), width // 2
+        lower = tuple(y[part:, :part] for y in inverse)
+        upper = tuple(y[:part, :part] for y in inverse)
+        corner = tuple(y[part:, part:] for y in inverse)
+        right = tuple(y[:, part:] for y in left)
+        half = jnp.concatenate(
+            [product(left, tuple(y[:, :part] for y in inverse)), product(right, corner)], axis=1
+        )
+        top, bottom = split(half[:part, :]), split(half[part:, :])
+        out[member, :part, :] = product(upper, top, contract=0) + product(lower, bottom, contract=0)
+        out[member, part:, :] = product(corner, bottom, contract=0)
 
 
 def reverse(pairs):

time: 191 us -> 191 us (level)
  no operation moved by 1% of the time
where the time goes in v13:
time: 191 us; the launch traced here: 190 us
  waiting for transfers between devices  73.5 us (38%)
  starting transfers between devices  59.6 us (31%)
  Pallas kernels  31.4 us (16%)
  other arithmetic  19 us (10%)
  local copies, waits for them, and re-layouts  5.16 us (3%)
    ppermute x5, starting transfers between devices, enter(): return lax.ppermute(x, 'col', hops[0])  24.7 us
    ppermute x8, waiting for transfers between devices, issue(): out.append(lax.ppermute(x, axis, pairs))  24.2 us
    ppermute x10, waiting for transfers between devices, run(): got = lax.ppermute(y, 'col', hops[hop])  23 us
    ppermute x5, waiting for transfers between devices, enter(): return lax.ppermute(x, 'col', hops[0])  19.6 us
    ppermute x8, starting transfers between devices, issue(): out.append(lax.ppermute(x, axis, pairs))  18.9 us
    ppermute x10, starting transfers between devices, run(): got = lax.ppermute(y, 'col', hops[hop])  11.6 us
    pallas_call x2, Pallas kernels, forward(): pl.pallas_call(functools.partial(forward_kernel, plan, member), in_specs=...  10.1 us
    pallas_call x2, Pallas kernels, gather(): pl.pallas_call(functools.partial(gather_kernel, plan, member), in_specs=s...  9.27 us
  transfers between devices with their start and end apart: 34, of which 16 were waited for; matrix products, arithmetic and copies ran while one was open for 9% of the time, Pallas kernels for 14%

profile of v13, /device:TPU:0, one launch (start us, length us, event | category | flops | bytes accessed | tf_op | source)
XLA Modules:
  0.0 190.0 jit_solution(13424369094481320619)
XLA Ops:
  0.6 1.3 slice.19.factor
  2.0 5.8 %collective-permute-start.3 = (f32[512,512]{1,0:T(8,128)S(1)}, f32[512,512]{1,0:T(8,128)}, u32[]{:S(2)}, u32[]{:S(2)}) collective-permute-start(f32[512,512]{1,0:T(8,128)S(1)} %slice.19.factor), channel_id=1, source_target_pairs={{0,8},{4,20},{9,1},{13,29},{18,26}} | collective-permute-start | bytes 3145736 | tf_op jit(solution)/shard_map/ppermute | solution.py:156
  7.8 5.1 %gather_mirror.3 = (bf16[512,1024]{1,0:T(8,128)(2,1)S(1)}, bf16[512,1024]{1,0:T(8,128)(2,1)S(1)}, f32[512,512]{1,0:T(8,128)S(1)}, f32[512,512]{1,0:T(8,128)}) custom-call(s32[2,16]{1,0:T(2,128)S(1)} %copy-done.5, s32[2,16]{1,0:T(2,128)S(1)} %copy-done.6, f32[2048,4096]{1,0:T(8,128)} %front.3, f32[512,512]{1,0:T(8,128)S(1)} %slice.19.factor), custom_call_target="tpu_custom_call" | custom-call | flops 1677721600 | bytes 8388608 | tf_op jit(solution)/shard_map/gather_mirror/pallas_call | solution.py:347
  13.9 5.2 %collective-permute-done.3 = f32[512,512]{1,0:T(8,128)} collective-permute-done((f32[512,512]{1,0:T(8,128)S(1)}, f32[512,512]{1,0:T(8,128)}, u32[]{:S(2)}, u32[]{:S(2)}) %collective-permute-start.3) | collective-permute-done | bytes 1048608 | tf_op jit(solution)/shard_map/ppermute | solution.py:156
  19.1 1.9 broadcast_select_fusion.1
  21.0 1.4 collective-permute-start.4
  22.4 1.4 add.90
  23.8 1.3 collective-permute-start.2
  25.1 4.1 %gather_mirror.2 = (bf16[512,1024]{1,0:T(8,128)(2,1)S(1)}, bf16[512,1024]{1,0:T(8,128)(2,1)S(1)}, f32[512,512]{1,0:T(8,128)S(1)}, f32[512,512]{1,0:T(8,128)S(1)}) custom-call(s32[2,16]{1,0:T(2,128)S(1)} %copy-done.5, s32[2,16]{1,0:T(2,128)S(1)} %copy-done.6, f32[2048,4096]{1,0:T(8,128)} %front.3, f32[512,512]{1,0:T(8,128)S(1)} %get-tuple-element.50.factor), custom_call_target="tpu_custom_call" | custom-call | flops 1677721600 | bytes 8388608 | tf_op jit(solution)/shard_map/gather_mirror/pallas_call | solution.py:347
  29.3 5.3 %collective-permute-done.4 = f32[512,512]{1,0:T(8,128)S(1)} collective-permute-done((f32[512,512]{1,0:T(8,128)S(1)}, f32[512,512]{1,0:T(8,128)S(1)}, u32[]{:S(2)}, u32[]{:S(2)}) %collective-permute-start.4) | collective-permute-done | bytes 1048608 | tf_op jit(solution)/shard_map/ppermute | solution.py:156
  34.9 4.9 %collective-permute-start.8 = (f32[512,512]{1,0:T(8,128)S(1)}, f32[512,512]{1,0:T(8,128)S(1)}, u32[]{:S(2)}, u32[]{:S(2)}) collective-permute-start(f32[512,512]{1,0:T(8,128)S(1)} %get-tuple-element.50.factor), channel_id=1, source_target_pairs={{0,8},{4,20},{9,1},{13,29},{18,26}} | collective-permute-start | bytes 3145736 | tf_op jit(solution)/shard_map/ppermute | solution.py:156
  40.7 1.4 collective-permute-start.6
  43.4 4.8 %forward.2 = (f32[256,512]{1,0:T(8,128)S(1)}, f32[256,512]{1,0:T(8,128)S(1)}, f32[256,512]{1,0:T(8,128)S(1)}, f32[256,512]{1,0:T(8,128)S(1)}) custom-call(bf16[512,1024]{1,0:T(8,128)(2,1)S(1)} %get-tuple-element.43.high, bf16[512,1024]{1,0:T(8,128)(2,1)S(1)} %copy-done.4, f32[512,512]{1,0:T(8,128)S(1)} %slice.19.factor, f32[512,512]{1,0:T(8,128)} %copy-done.11, ...), custom_call_target="tpu_custom_call" | custom-call | flops 1677721600 | bytes 8388608 | tf_op jit(solution)/shard_map/forward/pallas_call | solution.py:365
  48.2 3.8 %collective-permute-done.8 = f32[512,512]{1,0:T(8,128)S(1)} collective-permute-done((f32[512,512]{1,0:T(8,128)S(1)}, f32[512,512]{1,0:T(8,128)S(1)}, u32[]{:S(2)}, u32[]{:S(2)}) %collective-permute-start.8) | collective-permute-done | bytes 1048608 | tf_op jit(solution)/shard_map/ppermute | solution.py:156
  52.2 5.5 %collective-permute-done.6 = f32[512,512]{1,0:T(8,128)S(1)} collective-permute-done((f32[512,512]{1,0:T(8,128)S(1)}, f32[512,512]{1,0:T(8,128)S(1)}, u32[]{:S(2)}, u32[]{:S(2)}) %collective-permute-start.6) | collective-permute-done | bytes 1048608 | tf_op jit(solution)/shard_map/ppermute | solution.py:156
  58.8 1.3 collective-permute-start.9
  60.1 1.3 collective-permute-start.10
  61.4 1.6 collective-permute-start.7
  63.0 9.3 %collective-permute-done.7 = f32[256,512]{1,0:T(8,128)S(1)} collective-permute-done((f32[256,512]{1,0:T(8,128)S(1)}, f32[256,512]{1,0:T(8,128)S(1)}, u32[]{:S(2)}, u32[]{:S(2)}) %collective-permute-start.7) | collective-permute-done | bytes 524320 | tf_op jit(solution)/shard_map/ppermute | solution.py:386
  73.2 3.7 %collective-permute-done.10 = f32[512,512]{1,0:T(8,128)S(1)} collective-permute-done((f32[512,512]{1,0:T(8,128)S(1)}, f32[512,512]{1,0:T(8,128)S(1)}, u32[]{:S(2)}, u32[]{:S(2)}) %collective-permute-start.10) | collective-permute-done | bytes 1048608 | tf_op jit(solution)/shard_map/ppermute | solution.py:156
  78.4 1.5 collective-permute-start.12
  80.8 5.3 %forward.3 = (f32[256,512]{1,0:T(8,128)S(1)}, f32[256,512]{1,0:T(8,128)S(1)}, f32[512,512]{1,0:T(8,128)S(1)}, f32[512,512]{1,0:T(8,128)S(1)}) custom-call(bf16[512,1024]{1,0:T(8,128)(2,1)S(1)} %get-tuple-element.39.high, bf16[512,1024]{1,0:T(8,128)(2,1)} %copy-done.2, f32[512,512]{1,0:T(8,128)} %copy-done.1, f32[512,512]{1,0:T(8,128)} %add.95.mirror, ...), custom_call_target="tpu_custom_call" | custom-call | flops 1677721600 | bytes 8388608 | tf_op jit(solution)/shard_map/forward/pallas_call | solution.py:365
  86.7 5.8 %collective-permute-start.15 = (f32[256,512]{1,0:T(8,128)}, f32[256,512]{1,0:T(8,128)}, u32[]{:S(2)}, u32[]{:S(2)}) collective-permute-start(f32[256,512]{1,0:T(8,128)} %get-tuple-element.61), channel_id=1, source_target_pairs={{0,1},{3,2},{4,5},{7,6},{8,9},{11,10},{12,13},{15,14},{16,17},{19,... | collective-permute-start | bytes 1572872 | tf_op jit(solution)/shard_map/ppermute | solution.py:386
  92.4 2.1 %add.99 = f32[256,512]{1,0:T(8,128)} add(f32[256,512]{1,0:T(8,128)} %copy-done.13, f32[256,512]{1,0:T(8,128)} %copy-done.16) | non-fusion elementwise | flops 131072 | bytes 1572864 | tf_op jit(solution)/shard_map/add | solution.py:101
  94.5 1.5 collective-permute-start.14
  96.0 2.4 %slice_add_fusion = (f32[256,512]{1,0:T(8,128)}, f32[256,512]{1,0:T(8,128)}) fusion(f32[256,512]{1,0:T(8,128)S(1)} %get-tuple-element.66, f32[512,512]{1,0:T(8,128)} %collective-permute-done.12, f32[256,512]{1,0:T(8,128)S(1)} %get-tuple-element.58), kind=kLoop, calls=%fused_computation.1 | loop fusion | flops 262144 | bytes 3145728 | tf_op jit(solution)/shard_map/add | solution.py:437
  98.4 2.1 %collective-permute-start.13 = (f32[256,512]{1,0:T(8,128)}, f32[256,512]{1,0:T(8,128)}, u32[]{:S(2)}, u32[]{:S(2)}) collective-permute-start(f32[256,512]{1,0:T(8,128)} %get-tuple-element.79), channel_id=1, source_target_pairs={{0,1},{3,2},{4,5},{7,6},{8,9},{11,10},{12,13},{15,14},{16,17},{19,... | collective-permute-start | bytes 1572872 | tf_op jit(solution)/shard_map/ppermute | solution.py:386
  100.5 3.7 %collective-permute-done.15 = f32[256,512]{1,0:T(8,128)} collective-permute-done((f32[256,512]{1,0:T(8,128)}, f32[256,512]{1,0:T(8,128)}, u32[]{:S(2)}, u32[]{:S(2)}) %collective-permute-start.15) | collective-permute-done | bytes 524320 | tf_op jit(solution)/shard_map/ppermute | solution.py:386
  105.5 1.5 collective-permute-start.18
  106.9 1.5 add.107
  109.8 1.3 collective-permute-start.16
  111.2 13.8 %collective-permute-start.21 = (f32[256,512]{1,0:T(8,128)S(1)}, f32[256,512]{1,0:T(8,128)S(1)}, u32[]{:S(2)}, u32[]{:S(2)}) collective-permute-start(f32[256,512]{1,0:T(8,128)S(1)} %copy-done.12), channel_id=1, source_target_pairs={{0,1},{3,2},{4,5},{7,6},{8,9},{11,10},{12,13},{15,14},{16,17},{19,... | collective-permute-start | bytes 1572872 | tf_op jit(solution)/shard_map/ppermute | solution.py:386
  126.2 1.3 collective-permute-start.19
  129.8 4.8 %collective-permute-done.21 = f32[256,512]{1,0:T(8,128)S(1)} collective-permute-done((f32[256,512]{1,0:T(8,128)S(1)}, f32[256,512]{1,0:T(8,128)S(1)}, u32[]{:S(2)}, u32[]{:S(2)}) %collective-permute-start.21) | collective-permute-done | bytes 524320 | tf_op jit(solution)/shard_map/ppermute | solution.py:386
  134.8 5.2 %collective-permute-done.19.rest_3_ = f32[256,512]{1,0:T(8,128)S(1)} collective-permute-done((f32[256,512]{1,0:T(8,128)S(1)}, f32[256,512]{1,0:T(8,128)S(1)}, u32[]{:S(2)}, u32[]{:S(2)}) %collective-permute-start.19) | collective-permute-done | bytes 524320 | tf_op jit(solution)/shard_map/ppermute | solution.py:395
  140.0 1.5 collective-permute-start.27
  142.3 1.3 collective-permute-start.20
  143.6 1.8 collective-permute-done.27
  146.1 4.2 %place.2.rest_4_ = f32[2048,1024]{1,0:T(8,128)} custom-call(s32[2,16]{1,0:T(2,128)S(1)} %copy-done.5, f32[2,512,512]{2,1,0:T(8,128)S(1)} %copy-done, f32[256,512]{1,0:T(8,128)S(1)} %add.100.rest_0_, f32[256,512]{1,0:T(8,128)S(1)} %collective-permute-done.16.rest_1_, f32[256,512]{1,0:T(8,128)S(1)} %add.103.rest_2_, f32[256,512]{1,0:T(8,128)S(1)} %collective-permute-done.19.rest_3_), custom_call_target="tpu_custom_call" | custom-call | flops 1677721600 | bytes 8388608 | tf_op jit(solution)/shard_map/place/pallas_call | solution.py:455
  150.4 1.3 collective-permute-start.29
  151.8 4.9 %collective-permute-done.20.rest_1_ = f32[256,512]{1,0:T(8,128)} collective-permute-done((f32[256,512]{1,0:T(8,128)S(1)}, f32[256,512]{1,0:T(8,128)}, u32[]{:S(2)}, u32[]{:S(2)}) %collective-permute-start.20) | collective-permute-done | bytes 524320 | tf_op jit(solution)/shard_map/ppermute | solution.py:395
  158.0 12.9 %collective-permute-done.29 = f32[128,512]{1,0:T(8,128)} collective-permute-done((f32[128,512]{1,0:T(8,128)S(1)}, f32[128,512]{1,0:T(8,128)}, u32[]{:S(2)}, u32[]{:S(2)}) %collective-permute-start.29) | collective-permute-done | bytes 262176 | tf_op jit(solution)/shard_map/ppermute | solution.py:395
  171.9 1.8 collective-permute-start.31
  173.7 1.7 collective-permute-start.30
  175.4 3.9 %collective-permute-done.32 = f32[128,512]{1,0:T(8,128)S(1)} collective-permute-done((f32[128,512]{1,0:T(8,128)S(1)}, f32[128,512]{1,0:T(8,128)S(1)}, u32[]{:S(2)}, u32[]{:S(2)}) %collective-permute-start.32) | collective-permute-done | bytes 262176 | tf_op jit(solution)/shard_map/ppermute | solution.py:499
  179.3 1.5 collective-permute-done.31
  182.1 3.1 %place.3 = f32[2048,1024]{1,0:T(8,128)} custom-call(s32[2,16]{1,0:T(2,128)S(1)} %copy-done.5, f32[2,512,512]{2,1,0:T(8,128)S(1)} %copy-done, f32[256,512]{1,0:T(8,128)S(1)} %add.101.rest_0_, f32[256,512]{1,0:T(8,128)} %collective-permute-done.20.rest_1_, f32[256,512]{1,0:T(8,128)S(1)} %add.106.rest_2_, ...), custom_call_target="tpu_custom_call", output_to_operand_aliasing={{}: (6, {})} | custom-call | flops 1677721600 | bytes 8388608 | tf_op jit(solution)/shard_map/place/pallas_call | solution.py:455
  185.2 4.8 %diagonal.1 = f32[2,512,512]{2,1,0:T(8,128)} custom-call(f32[2,512]{1,0:T(2,128)S(1)} %copy-done.7, f32[2,512,512]{2,1,0:T(8,128)S(1)} %copy-done, f32[512,512]{1,0:T(8,128)S(1)} %pad_maximum_fusion.rest_0_, f32[512,512]{1,0:T(8,128)S(1)} %collective-permute-done.33.rest_1_), custom_call_target="tpu_custom_call" | custom-call | flops 1677721600 | bytes 8388608 | tf_op jit(solution)/shard_map/diagonal/pallas_call | solution.py:502
  (89 shorter events, 20.0 us)
Async XLA Ops:
  0.6 7.2 %copy-start.5 = (s32[2,16]{1,0:T(2,128)S(1)}, s32[2,16]{1,0:T(2,128)}, u32[]{:S(2)}) copy-start(s32[2,16]{1,0:T(2,128)} %tiles_ref.7) | copy-start | bytes 388
  0.6 7.2 %copy-start.6 = (s32[2,16]{1,0:T(2,128)S(1)}, s32[2,16]{1,0:T(2,128)}, u32[]{:S(2)}) copy-start(s32[2,16]{1,0:T(2,128)} %valid_ref.3) | copy-start | bytes 388
  2.0 17.2 %collective-permute-start.3 = (f32[512,512]{1,0:T(8,128)S(1)}, f32[512,512]{1,0:T(8,128)}, u32[]{:S(2)}, u32[]{:S(2)}) collective-permute-start(f32[512,512]{1,0:T(8,128)S(1)} %slice.19.factor), channel_id=1, source_target_pairs={{0,8},{4,20},{9,1},{13,29},{18,26}} | collective-permute-start | bytes 3145736 | tf_op jit(solution)/shard_map/ppermute | solution.py:156
  12.9 1.0 copy-start.3
  13.9 8.4 %collective-permute-start.1 = (f32[512,512]{1,0:T(8,128)}, f32[512,512]{1,0:T(8,128)}, u32[]{:S(2)}, u32[]{:S(2)}) collective-permute-start(f32[512,512]{1,0:T(8,128)} %get-tuple-element.46), channel_id=1, source_target_pairs={{4,0},{0,4},{12,8},{8,12},{20,16},{16,20},{28,24},{24,28},{5,1},{1... | collective-permute-start | bytes 3145736 | tf_op jit(solution)/shard_map/ppermute | solution.py:88
  21.0 13.9 %copy-start.1 = (f32[512,512]{1,0:T(8,128)}, f32[512,512]{1,0:T(8,128)S(1)}, u32[]{:S(2)}) copy-start(f32[512,512]{1,0:T(8,128)S(1)} %get-tuple-element.50.factor) | copy-start | bytes 3145732
  21.0 13.6 %collective-permute-start.4 = (f32[512,512]{1,0:T(8,128)S(1)}, f32[512,512]{1,0:T(8,128)S(1)}, u32[]{:S(2)}, u32[]{:S(2)}) collective-permute-start(f32[512,512]{1,0:T(8,128)S(1)} %get-tuple-element.47), channel_id=1, source_target_pairs={{0,16},{8,24},{4,12},{20,28},{9,25},{1,17},{29,21},{22,30}} | collective-permute-start | bytes 3145736 | tf_op jit(solution)/shard_map/ppermute | solution.py:156
  23.8 16.7 %collective-permute-start.2 = (f32[512,512]{1,0:T(8,128)S(1)}, f32[512,512]{1,0:T(8,128)S(1)}, u32[]{:S(2)}, u32[]{:S(2)}) collective-permute-start(f32[512,512]{1,0:T(8,128)S(1)} %add.90), channel_id=1, source_target_pairs={{16,0},{24,8},{12,4},{28,20},{25,9},{17,1},{21,29},{30,22}} | collective-permute-start | bytes 3145736 | tf_op jit(solution)/shard_map/ppermute | solution.py:156
  29.2 11.5 %copy-start.2 = (bf16[512,1024]{1,0:T(8,128)(2,1)}, bf16[512,1024]{1,0:T(8,128)(2,1)S(1)}, u32[]{:S(2)}) copy-start(bf16[512,1024]{1,0:T(8,128)(2,1)S(1)} %get-tuple-element.40.low) | copy-start | bytes 3145732
  29.2 12.9 %collective-permute-start = (f32[512,512]{1,0:T(8,128)S(1)}, f32[512,512]{1,0:T(8,128)S(1)}, u32[]{:S(2)}, u32[]{:S(2)}) collective-permute-start(f32[512,512]{1,0:T(8,128)S(1)} %get-tuple-element.42), channel_id=1, source_target_pairs={{4,0},{0,4},{12,8},{8,12},{20,16},{16,20},{28,24},{24,28},{5,1},{1... | collective-permute-start | bytes 3145736 | tf_op jit(solution)/shard_map/ppermute | solution.py:88
  34.8 7.6 %copy-start.10 = (f32[512,512]{1,0:T(8,128)}, f32[512,512]{1,0:T(8,128)S(1)}, u32[]{:S(2)}) copy-start(f32[512,512]{1,0:T(8,128)S(1)} %add.92.rest_0_) | copy-start | bytes 3145732
  34.8 7.6 %collective-permute-start.5 = (f32[512,512]{1,0:T(8,128)S(1)}, f32[512,512]{1,0:T(8,128)S(1)}, u32[]{:S(2)}, u32[]{:S(2)}) collective-permute-start(f32[512,512]{1,0:T(8,128)S(1)} %add.92.rest_0_), channel_id=1, source_target_pairs={{4,0},{0,4},{12,8},{8,12},{20,16},{16,20},{28,24},{24,28},{5,1},{1... | collective-permute-start | bytes 3145736 | tf_op jit(solution)/shard_map/ppermute | solution.py:88
  34.9 17.1 %collective-permute-start.8 = (f32[512,512]{1,0:T(8,128)S(1)}, f32[512,512]{1,0:T(8,128)S(1)}, u32[]{:S(2)}, u32[]{:S(2)}) collective-permute-start(f32[512,512]{1,0:T(8,128)S(1)} %get-tuple-element.50.factor), channel_id=1, source_target_pairs={{0,8},{4,20},{9,1},{13,29},{18,26}} | collective-permute-start | bytes 3145736 | tf_op jit(solution)/shard_map/ppermute | solution.py:156
  40.7 2.7 %copy-start.11 = (f32[512,512]{1,0:T(8,128)}, f32[512,512]{1,0:T(8,128)S(1)}, u32[]{:S(2)}) copy-start(f32[512,512]{1,0:T(8,128)S(1)} %add.91.mirror) | copy-start | bytes 3145732
  40.7 2.7 %copy-start.4 = (bf16[512,1024]{1,0:T(8,128)(2,1)S(1)}, bf16[512,1024]{1,0:T(8,128)(2,1)}, u32[]{:S(2)}) copy-start(bf16[512,1024]{1,0:T(8,128)(2,1)} %copy-done.3) | copy-start | bytes 3145732
  40.7 17.1 %collective-permute-start.6 = (f32[512,512]{1,0:T(8,128)S(1)}, f32[512,512]{1,0:T(8,128)S(1)}, u32[]{:S(2)}, u32[]{:S(2)}) collective-permute-start(f32[512,512]{1,0:T(8,128)S(1)} %add.91.mirror), channel_id=1, source_target_pairs={{8,0},{20,4},{1,9},{29,13},{26,18}} | collective-permute-start | bytes 3145736 | tf_op jit(solution)/shard_map/ppermute | solution.py:156
  43.4 8.7 %copy-start.8 = (f32[512,1024]{1,0:T(8,128)S(1)}, f32[512,1024]{1,0:T(8,128)}, u32[]{:S(2)}) copy-start(f32[512,1024]{1,0:T(8,128)} %param.7) | copy-start | bytes 6291460
  58.8 13.6 %copy-start.13 = (f32[256,512]{1,0:T(8,128)}, f32[256,512]{1,0:T(8,128)S(1)}, u32[]{:S(2)}) copy-start(f32[256,512]{1,0:T(8,128)S(1)} %get-tuple-element.81) | copy-start | bytes 1572868
  58.8 13.6 %collective-permute-start.9 = (f32[512,512]{1,0:T(8,128)S(1)}, f32[512,512]{1,0:T(8,128)S(1)}, u32[]{:S(2)}, u32[]{:S(2)}) collective-permute-start(f32[512,512]{1,0:T(8,128)S(1)} %broadcast_select_fusion), channel_id=1, source_target_pairs={{0,16},{8,24},{4,12},{20,28},{9,25},{1,17},{29,21},{22,30}} | collective-permute-start | bytes 3145736 | tf_op jit(solution)/shard_map/ppermute | solution.py:156
  60.1 16.7 %collective-permute-start.10 = (f32[512,512]{1,0:T(8,128)S(1)}, f32[512,512]{1,0:T(8,128)S(1)}, u32[]{:S(2)}, u32[]{:S(2)}) collective-permute-start(f32[512,512]{1,0:T(8,128)S(1)} %add.89), channel_id=1, source_target_pairs={{16,0},{24,8},{12,4},{28,20},{25,9},{17,1},{21,29},{30,22}} | collective-permute-start | bytes 3145736 | tf_op jit(solution)/shard_map/ppermute | solution.py:156
  61.4 10.9 %collective-permute-start.7 = (f32[256,512]{1,0:T(8,128)S(1)}, f32[256,512]{1,0:T(8,128)S(1)}, u32[]{:S(2)}, u32[]{:S(2)}) collective-permute-start(f32[256,512]{1,0:T(8,128)S(1)} %get-tuple-element.81), channel_id=1, source_target_pairs={{0,1},{3,2},{4,5},{7,6},{8,9},{11,10},{12,13},{15,14},{16,17},{19,... | collective-permute-start | bytes 1572872 | tf_op jit(solution)/shard_map/ppermute | solution.py:386
  77.0 2.8 %copy-start.9 = (f32[512,512]{1,0:T(8,128)}, f32[512,512]{1,0:T(8,128)S(1)}, u32[]{:S(2)}) copy-start(f32[512,512]{1,0:T(8,128)S(1)} %add.96.rest_0_) | copy-start | bytes 3145732
  77.1 2.8 %collective-permute-start.11 = (f32[512,512]{1,0:T(8,128)S(1)}, f32[512,512]{1,0:T(8,128)S(1)}, u32[]{:S(2)}, u32[]{:S(2)}) collective-permute-start(f32[512,512]{1,0:T(8,128)S(1)} %add.96.rest_0_), channel_id=1, source_target_pairs={{4,0},{0,4},{12,8},{8,12},{20,16},{16,20},{28,24},{24,28},{5,1},{1... | collective-permute-start | bytes 3145736 | tf_op jit(solution)/shard_map/ppermute | solution.py:88
  78.4 17.6 %collective-permute-start.12 = (f32[512,512]{1,0:T(8,128)}, f32[512,512]{1,0:T(8,128)}, u32[]{:S(2)}, u32[]{:S(2)}) collective-permute-start(f32[512,512]{1,0:T(8,128)} %add.95.mirror), channel_id=1, source_target_pairs={{8,0},{20,4},{1,9},{29,13},{26,18}} | collective-permute-start | bytes 3145736 | tf_op jit(solution)/shard_map/ppermute | solution.py:156
  86.2 20.8 %collective-permute-start.24 = (f32[512,512]{1,0:T(8,128)S(1)}, f32[512,512]{1,0:T(8,128)}, u32[]{:S(2)}, u32[]{:S(2)}) collective-permute-start(f32[512,512]{1,0:T(8,128)S(1)} %get-tuple-element.71), channel_id=1, source_target_pairs={{4,0},{0,4},{12,8},{8,12},{20,16},{16,20},{28,24},{24,28},{5,1},{1... | collective-permute-start | bytes 3145736 | tf_op jit(solution)/shard_map/ppermute | solution.py:88
  86.7 17.5 %collective-permute-start.15 = (f32[256,512]{1,0:T(8,128)}, f32[256,512]{1,0:T(8,128)}, u32[]{:S(2)}, u32[]{:S(2)}) collective-permute-start(f32[256,512]{1,0:T(8,128)} %get-tuple-element.61), channel_id=1, source_target_pairs={{0,1},{3,2},{4,5},{7,6},{8,9},{11,10},{12,13},{15,14},{16,17},{19,... | collective-permute-start | bytes 1572872 | tf_op jit(solution)/shard_map/ppermute | solution.py:386
  94.5 14.0 %collective-permute-start.14 = (f32[256,512]{1,0:T(8,128)}, f32[256,512]{1,0:T(8,128)}, u32[]{:S(2)}, u32[]{:S(2)}) collective-permute-start(f32[256,512]{1,0:T(8,128)} %add.99), channel_id=1, source_target_pairs={{1,2},{2,1},{5,6},{6,5},{9,10},{10,9},{13,14},{14,13},{17,18},{18,... | collective-permute-start | bytes 1572872 | tf_op jit(solution)/shard_map/ppermute | solution.py:395
  98.4 27.8 %collective-permute-start.13 = (f32[256,512]{1,0:T(8,128)}, f32[256,512]{1,0:T(8,128)}, u32[]{:S(2)}, u32[]{:S(2)}) collective-permute-start(f32[256,512]{1,0:T(8,128)} %get-tuple-element.79), channel_id=1, source_target_pairs={{0,1},{3,2},{4,5},{7,6},{8,9},{11,10},{12,13},{15,14},{16,17},{19,... | collective-permute-start | bytes 1572872 | tf_op jit(solution)/shard_map/ppermute | solution.py:386
  105.5 5.7 %collective-permute-start.18 = (f32[256,512]{1,0:T(8,128)S(1)}, f32[256,512]{1,0:T(8,128)}, u32[]{:S(2)}, u32[]{:S(2)}) collective-permute-start(f32[256,512]{1,0:T(8,128)S(1)} %add.102), channel_id=1, source_target_pairs={{1,2},{2,1},{5,6},{6,5},{9,10},{10,9},{13,14},{14,13},{17,18},{18,... | collective-permute-start | bytes 1572872 | tf_op jit(solution)/shard_map/ppermute | solution.py:395
  108.4 2.8 %copy-start.12 = (f32[256,512]{1,0:T(8,128)S(1)}, f32[256,512]{1,0:T(8,128)}, u32[]{:S(2)}) copy-start(f32[256,512]{1,0:T(8,128)} %get-tuple-element.67) | copy-start | bytes 1572868
  108.5 19.0 %collective-permute-start.25 = (f32[256,512]{1,0:T(8,128)S(1)}, f32[256,512]{1,0:T(8,128)S(1)}, u32[]{:S(2)}, u32[]{:S(2)}) collective-permute-start(f32[256,512]{1,0:T(8,128)S(1)} %dynamic-slice_bitcast_fusion), channel_id=1, source_target_pairs={{0,8},{1,9},{2,10},{3,11},{4,20},{5,21},{6,22},{7,23},{8,0},{9,1},... | collective-permute-start | bytes 1572872 | tf_op jit(solution)/shard_map/ppermute | solution.py:447
  109.8 19.1 %collective-permute-start.16 = (f32[256,512]{1,0:T(8,128)S(1)}, f32[256,512]{1,0:T(8,128)S(1)}, u32[]{:S(2)}, u32[]{:S(2)}) collective-permute-start(f32[256,512]{1,0:T(8,128)S(1)} %add.100.rest_0_), channel_id=1, source_target_pairs={{1,0},{2,3},{5,4},{6,7},{9,8},{10,11},{13,12},{14,15},{17,16},{18,... | collective-permute-start | bytes 1572872 | tf_op jit(solution)/shard_map/ppermute | solution.py:395
  111.2 23.5 %collective-permute-start.21 = (f32[256,512]{1,0:T(8,128)S(1)}, f32[256,512]{1,0:T(8,128)S(1)}, u32[]{:S(2)}, u32[]{:S(2)}) collective-permute-start(f32[256,512]{1,0:T(8,128)S(1)} %copy-done.12), channel_id=1, source_target_pairs={{0,1},{3,2},{4,5},{7,6},{8,9},{11,10},{12,13},{15,14},{16,17},{19,... | collective-permute-start | bytes 1572872 | tf_op jit(solution)/shard_map/ppermute | solution.py:386
  126.2 13.8 %collective-permute-start.19 = (f32[256,512]{1,0:T(8,128)S(1)}, f32[256,512]{1,0:T(8,128)S(1)}, u32[]{:S(2)}, u32[]{:S(2)}) collective-permute-start(f32[256,512]{1,0:T(8,128)S(1)} %add.103.rest_2_), channel_id=1, source_target_pairs={{1,0},{2,3},{5,4},{6,7},{9,8},{10,11},{13,12},{14,15},{17,16},{18,... | collective-permute-start | bytes 1572872 | tf_op jit(solution)/shard_map/ppermute | solution.py:395
  127.6 12.4 %collective-permute-start.26 = (f32[128,512]{1,0:T(8,128)S(1)}, f32[128,512]{1,0:T(8,128)S(1)}, u32[]{:S(2)}, u32[]{:S(2)}) collective-permute-start(f32[128,512]{1,0:T(8,128)S(1)} %dynamic-slice_bitcast_fusion.1), channel_id=1, source_target_pairs={{0,16},{1,17},{2,18},{3,19},{4,12},{5,13},{6,14},{7,15},{8,24},{9,... | collective-permute-start | bytes 786440 | tf_op jit(solution)/shard_map/ppermute | solution.py:447
  129.0 17.1 %copy-start = (f32[2,512,512]{2,1,0:T(8,128)S(1)}, f32[2,512,512]{2,1,0:T(8,128)}, u32[]{:S(2)}) copy-start(f32[2,512,512]{2,1,0:T(8,128)} %unit_ref.5) | copy-start | bytes 6291460
  129.0 13.2 %collective-permute-start.17 = (f32[256,512]{1,0:T(8,128)S(1)}, f32[256,512]{1,0:T(8,128)S(1)}, u32[]{:S(2)}, u32[]{:S(2)}) collective-permute-start(f32[256,512]{1,0:T(8,128)S(1)} %add.98), channel_id=1, source_target_pairs={{1,2},{2,1},{5,6},{6,5},{9,10},{10,9},{13,14},{14,13},{17,18},{18,... | collective-permute-start | bytes 1572872 | tf_op jit(solution)/shard_map/ppermute | solution.py:395
  140.0 5.3 %collective-permute-start.27 = (f32[128,512]{1,0:T(8,128)S(1)}, f32[128,512]{1,0:T(8,128)S(1)}, u32[]{:S(2)}, u32[]{:S(2)}) collective-permute-start(f32[128,512]{1,0:T(8,128)S(1)} %bitcast_add_fusion.1), channel_id=1, source_target_pairs={{0,1},{3,2},{4,5},{7,6},{8,9},{11,10},{12,13},{15,14},{16,17},{19,... | collective-permute-start | bytes 786440 | tf_op jit(solution)/shard_map/ppermute | solution.py:386
  141.5 8.8 %collective-permute-start.22 = (f32[256,512]{1,0:T(8,128)S(1)}, f32[256,512]{1,0:T(8,128)S(1)}, u32[]{:S(2)}, u32[]{:S(2)}) collective-permute-start(f32[256,512]{1,0:T(8,128)S(1)} %add.105), channel_id=1, source_target_pairs={{1,2},{2,1},{5,6},{6,5},{9,10},{10,9},{13,14},{14,13},{17,18},{18,... | collective-permute-start | bytes 1572872 | tf_op jit(solution)/shard_map/ppermute | solution.py:395
  142.3 14.4 %collective-permute-start.20 = (f32[256,512]{1,0:T(8,128)S(1)}, f32[256,512]{1,0:T(8,128)}, u32[]{:S(2)}, u32[]{:S(2)}) collective-permute-start(f32[256,512]{1,0:T(8,128)S(1)} %add.101.rest_0_), channel_id=1, source_target_pairs={{1,0},{2,3},{5,4},{6,7},{9,8},{10,11},{13,12},{14,15},{17,16},{18,... | collective-permute-start | bytes 1572872 | tf_op jit(solution)/shard_map/ppermute | solution.py:395
  145.4 5.0 %collective-permute-start.28 = (f32[128,512]{1,0:T(8,128)S(1)}, f32[128,512]{1,0:T(8,128)S(1)}, u32[]{:S(2)}, u32[]{:S(2)}) collective-permute-start(f32[128,512]{1,0:T(8,128)S(1)} %add.113), channel_id=1, source_target_pairs={{1,2},{2,1},{5,6},{6,5},{9,10},{10,9},{13,14},{14,13},{17,18},{18,... | collective-permute-start | bytes 786440 | tf_op jit(solution)/shard_map/ppermute | solution.py:395
  150.4 20.4 %collective-permute-start.29 = (f32[128,512]{1,0:T(8,128)S(1)}, f32[128,512]{1,0:T(8,128)}, u32[]{:S(2)}, u32[]{:S(2)}) collective-permute-start(f32[128,512]{1,0:T(8,128)S(1)} %add.114), channel_id=1, source_target_pairs={{1,0},{2,3},{5,4},{6,7},{9,8},{10,11},{13,12},{14,15},{17,16},{18,... | collective-permute-start | bytes 786440 | tf_op jit(solution)/shard_map/ppermute | solution.py:395
  156.7 25.4 %collective-permute-start.23 = (f32[256,512]{1,0:T(8,128)S(1)}, f32[256,512]{1,0:T(8,128)S(1)}, u32[]{:S(2)}, u32[]{:S(2)}) collective-permute-start(f32[256,512]{1,0:T(8,128)S(1)} %add.106.rest_2_), channel_id=1, source_target_pairs={{1,0},{2,3},{5,4},{6,7},{9,8},{10,11},{13,12},{14,15},{17,16},{18,... | collective-permute-start | bytes 1572872 | tf_op jit(solution)/shard_map/ppermute | solution.py:395
  171.8 7.4 %collective-permute-start.32 = (f32[128,512]{1,0:T(8,128)S(1)}, f32[128,512]{1,0:T(8,128)S(1)}, u32[]{:S(2)}, u32[]{:S(2)}) collective-permute-start(f32[128,512]{1,0:T(8,128)S(1)} %broadcast_select_fusion.2), channel_id=1, source_target_pairs={{0,24},{1,25},{2,26},{3,27},{8,16},{9,17},{10,18},{11,19},{16,8},{... | collective-permute-start | bytes 786440 | tf_op jit(solution)/shard_map/ppermute | solution.py:499
  171.9 8.9 %collective-permute-start.31 = (f32[128,512]{1,0:T(8,128)S(1)}, f32[128,512]{1,0:T(8,128)S(1)}, u32[]{:S(2)}, u32[]{:S(2)}) collective-permute-start(f32[128,512]{1,0:T(8,128)S(1)} %broadcast_select_fusion.2), channel_id=1, source_target_pairs={{0,8},{1,9},{2,10},{3,11},{8,0},{9,1},{10,2},{11,3},{16,24},{17,25... | collective-permute-start | bytes 786440 | tf_op jit(solution)/shard_map/ppermute | solution.py:499
  173.7 8.3 %collective-permute-start.30 = (f32[128,512]{1,0:T(8,128)S(1)}, f32[128,512]{1,0:T(8,128)S(1)}, u32[]{:S(2)}, u32[]{:S(2)}) collective-permute-start(f32[128,512]{1,0:T(8,128)S(1)} %broadcast_select_fusion.2), channel_id=1, source_target_pairs={{0,16},{1,17},{2,18},{3,19},{8,24},{9,25},{10,26},{11,27},{16,0},{... | collective-permute-start | bytes 786440 | tf_op jit(solution)/shard_map/ppermute | solution.py:499
  182.0 3.2 %copy-start.7 = (f32[2,512]{1,0:T(2,128)S(1)}, f32[2,512]{1,0:T(2,128)}, u32[]{:S(2)}) copy-start(f32[2,512]{1,0:T(2,128)} %pivot.1) | copy-start | bytes 12292
  182.1 3.2 %collective-permute-start.33 = (f32[512,512]{1,0:T(8,128)S(1)}, f32[512,512]{1,0:T(8,128)S(1)}, u32[]{:S(2)}, u32[]{:S(2)}) collective-permute-start(f32[512,512]{1,0:T(8,128)S(1)} %pad_maximum_fusion.rest_0_), channel_id=1, source_target_pairs={{4,0},{0,4},{12,8},{8,12},{20,16},{16,20},{28,24},{24,28},{5,1},{1... | collective-permute-start | bytes 3145736 | tf_op jit(solution)/shard_map/ppermute | solution.py:88
  (3 other events, 2.8 us)
